TPU v7x, 32 devices: a whole 2x2x4 slice. The times are simulated.
32 devices in a mesh: step: 8 (over y, x, core), tile: 4 (over z).
Axes of the slice: x: 2, y: 2, z: 4, core: 2. Of those that a mesh axis runs over, the one named last changes fastest.
Arguments:
- target_left: float32 [16, 4, 2048, 128], P('step', 'tile'), may hold values from -6 to 6
- target_right: float32 [16, 4, 2048, 128], P('step', 'tile'), may hold values from -0.125 to 0.125
- column_left: float32 [16, 2048, 128], P('step', 'tile'), may hold values from -12 to 12
- column_right: float32 [16, 2048, 128], P('step', 'tile'), may hold values from -0.125 to 0.125
- sketch: float32 [2048, 128], P('tile'), may hold values from -6 to 6
- pattern: int32 [16, 4], P('step', 'tile'), may hold values from 0 to 1, as said below
Outputs:
- basis: float32 [4, 2048, 128], P('tile', 'step')
- factor: float32 [4, 2048, 128], P('tile', 'step')
Inputs may be any that keep to these rules, and one draw needn't show every extreme that they name: `pattern`: every target has at least 8 existing products; some target has exactly that many and some target has all 16.
All inputs are finite; a program needn't handle non-finite values.
Results may differ from a plain program's by a relative error of at most 0.00023.
Values sent between devices are 32-bit elements; how exact they have to be, the bound alone decides.
No kernel may reach another device: no remote copies, remote signals or barrier semaphores. Data moves between devices by JAX's collectives and lax.ppermute only.
A program may use at most 64 MiB of HBM per device.

v0:
```python
import jax
import jax.numpy as jnp
from jax import lax
from jax.sharding import PartitionSpec as P


def solve_rows(lower_factor, rows_here):
    return jax.scipy.linalg.solve_triangular(lower_factor, rows_here.T, lower=True).T


def local(target_left, target_right, column_left, column_right, sketch, pattern):
    highest = lax.Precision.HIGHEST
    col_left, col_right, sketch_full = (
        lax.all_gather(column_left, "tile", axis=1, tiled=True),
        lax.all_gather(column_right, "tile", axis=1, tiled=True),
        lax.all_gather(sketch, "tile", axis=0, tiled=True),
    )
    steps_here, targets_here, tile_rows, rank_width = target_left.shape
    probes = jnp.einsum("kbq,bp->kqp", col_left, sketch_full, precision=highest)
    weights = pattern.astype(jnp.float32)
    core_tile = (
        jnp.einsum("ktbr,kbq->ktrq", target_right, col_right, precision=highest)
        * weights[:, :, None, None]
    )
    reduced = jnp.einsum("ktrq,kqp->ktrp", core_tile, probes, precision=highest)
    partial_y = jnp.einsum("ktbr,ktrp->tbp", target_left, reduced, precision=highest)
    row_count = tile_rows // lax.axis_size("step")
    sketched = lax.psum(partial_y, "step")
    gram_matrix = jnp.einsum("tbp,tbq->tpq", sketched, sketched, precision=highest) / tile_rows
    lower_factor = jnp.linalg.cholesky(gram_matrix)
    basis_full = jax.vmap(solve_rows)(lower_factor, sketched)
    basis_rows = lax.dynamic_slice_in_dim(
        basis_full, lax.axis_index("step") * row_count, row_count, 1
    )
    projected = jnp.einsum("ktbr,tbp->ktrp", target_left, basis_full, precision=highest)
    returned = jnp.einsum("ktrq,ktrp->ktqp", core_tile, projected, precision=highest)
    partial_w = jnp.einsum("kbq,ktqp->tbp", col_left, returned, precision=highest)
    factor_rows = lax.psum_scatter(partial_w, "step", scatter_dimension=1, tiled=True) / tile_rows
    return (basis_rows, factor_rows)


def solution(mesh):
    return jax.shard_map(
        local,
        mesh=mesh,
        in_specs=(
            P("step", "tile", None, None),
            P("step", "tile", None, None),
            P("step", "tile", None),
            P("step", "tile", None),
            P("tile", None),
            P("step", "tile"),
        ),
        out_specs=(P("tile", "step", None), P("tile", "step", None)),
        check_vma=False,
    )
```

profile of v0, /device:TPU:0, one launch (start us, length us, event | category | flops | bytes accessed | tf_op | source)
XLA Modules:
  0.0 274.5 jit_solution(14348121459729673915)
XLA Ops:
  7.2 0.0 all-gather.8.cloned.1.call-start
  7.2 0.7 all-gather.8.cloned.1.call-update
  7.9 0.0 all-gather.6.cloned.1.call-start
  8.0 0.7 all-gather.6.cloned.1.call-update
  8.7 0.0 all-gather.4.cloned.1.call-start
  8.7 0.7 all-gather.4.cloned.1.call-update
  9.4 0.0 all-reduce.2.cloned.1.call-start
  9.4 0.7 convert_bitcast_fusion
  10.1 30.1 %all-gather.8.cloned.1.call-done = f32[2048,128]{1,0:T(8,128)} async-done(((f32[512,128]{1,0:T(8,128)}), f32[2048,128]{1,0:T(8,128)}) %all-gather.8.cloned.1.call-update) | async-done | bytes 1048592 | tf_op jit(solution)/shard_map/all_gather | solution.py:16
  40.2 47.0 %all-gather.6.cloned.1.call-done = f32[2,2048,128]{2,1,0:T(8,128)} async-done(((f32[2,512,128]{2,1,0:T(8,128)}), f32[2,2048,128]{2,1,0:T(8,128)}) %all-gather.6.cloned.1.call-update) | async-done | bytes 2097168 | tf_op jit(solution)/shard_map/all_gather | solution.py:14
  87.3 5.3 %fusion.15 = f32[2,128,128]{2,1,0:T(8,128)S(1)} fusion(f32[2,2048,128]{2,1,0:T(8,128)} %all-gather.6.cloned.1.call-done, f32[2048,128]{1,0:T(8,128)} %all-gather.8.cloned.1.call-done), kind=kOutput, calls=%fused_computation.14 | convolution fusion | flops 805306368 | bytes 3276800 | tf_op jit(solution)/shard_map/kbq,bp->kqp/dot_general | solution.py:19
  92.6 41.0 %all-gather.4.cloned.1.call-done = f32[2,2048,128]{2,1,0:T(8,128)} async-done(((f32[2,512,128]{2,1,0:T(8,128)}), f32[2,2048,128]{2,1,0:T(8,128)}) %all-gather.4.cloned.1.call-update) | async-done | bytes 2097168 | tf_op jit(solution)/shard_map/all_gather | solution.py:15
  133.5 5.7 %fusion.8 = f32[2,128,128]{2,1,0:T(8,128)S(1)} fusion(f32[2,2048,128]{2,1,0:T(8,128)} %all-gather.4.cloned.1.call-done, f32[2,1,2048,128]{3,2,1,0:T(8,128)} %param.7, f32[2]{0:T(128)S(1)} %convert_bitcast_fusion), kind=kOutput, calls=%fused_computation.8 | convolution fusion | flops 805339136 | bytes 4325384 | tf_op jit(solution)/shard_map/ktbr,kbq->ktrq/dot_general | solution.py:22
  139.2 0.4 fusion.20
  139.6 3.2 %convolution_bitcast_fusion.1 = f32[1,2048,128]{1,2,0:T(8,128)} fusion(f32[2,128,128]{1,2,0:T(8,128)S(1)} %fusion.20, f32[2,1,2048,128]{3,2,1,0:T(8,128)S(1)} %copy-done), kind=kOutput, calls=%fused_computation.1 | convolution fusion | flops 805306368 | bytes 3276800 | tf_op jit(solution)/shard_map/ktbr,ktrp->tbp/dot_general | solution.py:26
  142.9 0.2 reduce-scatter.2.cloned.1.call-start
  143.1 55.2 %all-reduce.2.cloned.1.call-done = f32[1,2048,128]{1,2,0:T(8,128)} async-done(((f32[1,2048,128]{1,2,0:T(8,128)}), f32[1,2048,128]{1,2,0:T(8,128)}) %all-reduce.2.cloned.1.call-update) | async-done | bytes 1048592 | tf_op jit(solution)/shard_map/psum | solution.py:28
  198.4 2.6 convolution_multiply_fusion
  201.0 0.1 copy.14
  201.1 11.7 %custom-call.8 = f32[1,128,128]{2,1,0:T(8,128)S(1)} custom-call(f32[1,128,128]{2,1,0:T(8,128)S(1)} %fusion.18), custom_call_target="Cholesky" | custom-call | tf_op jit(solution)/shard_map/jit(cholesky)/cholesky | solution.py:30
  212.8 0.6 compare_reduce_fusion
  213.5 0.7 fusion.17
  214.1 9.8 %custom-call.9 = f32[1,1,128,128]{2,3,1,0:T(8,128)S(1)} custom-call(f32[1,1,128,128]{3,2,1,0:T(8,128)S(1)} %fusion.17), custom_call_target="InvertDiagBlocksLowerTriangular" | custom-call | tf_op jit(solution)/shard_map/vmap(jit(_solve_triangular))/triangular_solve | solution.py:8
  224.0 2.3 fusion.11
  226.2 1.1 fusion.5
  227.4 0.3 fusion.21
  227.6 0.2 copy-done.1
  227.8 3.2 %convolution_bitcast_fusion = f32[1,2048,128]{1,2,0:T(8,128)} fusion(f32[2,128,128]{1,2,0:T(8,128)S(1)} %fusion.21, f32[2,2048,128]{2,1,0:T(8,128)S(1)} %copy-done.1), kind=kOutput, calls=%fused_computation | convolution fusion | flops 805306368 | bytes 3276800 | tf_op jit(solution)/shard_map/kbq,ktqp->tbp/dot_general | solution.py:37
  231.1 0.8 copy.15
  231.9 34.5 %reduce-scatter.2.cloned.1.call-done = f32[1,256,128]{1,2,0:T(8,128)} async-done(((f32[1,2048,128]{1,2,0:T(8,128)}), f32[1,256,128]{1,2,0:T(8,128)}) %reduce-scatter.2.cloned.1.call-update) | async-done | bytes 131088 | tf_op jit(solution)/shard_map/reduce_scatter | solution.py:38
  266.3 0.9 broadcast_multiply_fusion
  267.2 0.8 copy.16
  (8 shorter events, 0.1 us)
Async XLA Ops:
  7.2 132.5 %copy-start = (f32[2,1,2048,128]{3,2,1,0:T(8,128)S(1)}, f32[2,1,2048,128]{3,2,1,0:T(8,128)}, u32[]{:S(2)}) copy-start(f32[2,1,2048,128]{3,2,1,0:T(8,128)} %param.6) | copy-start | bytes 6291460
  7.2 33.1 %all-gather.8.cloned.1.call-start = ((), (), s32[]{:S(2)}) async-start(), calls=%async_computation.3 | async-start | bytes 1310720 | tf_op jit(solution)/shard_map/all_gather | solution.py:16
  7.9 79.4 %all-gather.6.cloned.1.call-start = ((), (), s32[]{:S(2)}) async-start(), calls=%async_computation.2 | async-start | bytes 2621440 | tf_op jit(solution)/shard_map/all_gather | solution.py:14
  8.7 124.9 %all-gather.4.cloned.1.call-start = ((), (), s32[]{:S(2)}) async-start(), calls=%async_computation.1 | async-start | bytes 2621440 | tf_op jit(solution)/shard_map/all_gather | solution.py:15
  9.4 189.0 %all-reduce.2.cloned.1.call-start = ((), (), s32[]{:S(2)}) async-start(), calls=%async_computation.4 | async-start | bytes 2097152 | tf_op jit(solution)/shard_map/psum | solution.py:28
  142.9 123.4 %reduce-scatter.2.cloned.1.call-start = ((), (), s32[]{:S(2)}) async-start(), calls=%async_computation.5 | async-start | bytes 1179648 | tf_op jit(solution)/shard_map/reduce_scatter | solution.py:38
  226.2 1.6 copy-start.1
Sparse Core Ops, SparseCore 0:
  9.6 30.6 all-gather.7
  41.8 45.4 all-gather.5
  88.9 44.6 all-gather.3
  143.0 55.3 all-reduce.1
  231.2 35.0 reduce-scatter.1
where the time goes:
time: 275 us
  waiting for transfers between devices  210 us (76%)
  other arithmetic  24.4 us (9%)
  matrix products  24 us (9%)
  between operations  13.9 us (5%)
    psum x1, waiting for transfers between devices, local(): sketched = lax.psum(partial_y, 'step')  55.2 us
    all_gather x1, waiting for transfers between devices, local(): lax.all_gather(column_left, 'tile', axis=1, tiled=True)  47 us
    all_gather x1, waiting for transfers between devices, local(): lax.all_gather(column_right, 'tile', axis=1, tiled=True)  41 us
    reduce_scatter x1, waiting for transfers between devices, local(): lax.psum_scatter(partial_w, 'step', scatter_dimension=1, tiled=True)  34.5 us
    all_gather x1, waiting for transfers between devices, local(): lax.all_gather(sketch, 'tile', axis=0, tiled=True)  30.1 us
    another operation x3, other arithmetic, local(): lower_factor = jnp.linalg.cholesky(gram_matrix)  12.4 us
    another operation x2, other arithmetic, solve_rows(): jax.scipy.linalg.solve_triangular(lower_factor, rows_here.T, lower=True)  10.5 us
    dot_general x1, matrix products, local(): jnp.einsum('ktbr,kbq->ktrq', target_right, col_right, precision=highest)  5.7 us
  transfers between devices with their start and end apart: 5, of which 5 were waited for; matrix products, arithmetic and copies ran while one was open for 2% of the time, Pallas kernels for 0%

commit v1 on v0

v1 whole, which is shorter than its diff:
```python
import jax
import jax.numpy as jnp
from jax import lax
from jax.sharding import PartitionSpec as P

HIGH = lax.Precision.HIGH


def mm(spec, *arrays):
    return jnp.einsum(spec, *arrays, precision=HIGH, preferred_element_type=jnp.float32)


def inverse_factor(gram):
    lower = jnp.linalg.cholesky(gram)
    eye = jnp.eye(gram.shape[-1], dtype=gram.dtype)
    return jax.scipy.linalg.solve_triangular(lower, eye, lower=True)


def exchange(array, axis, bit):
    return lax.ppermute(array, axis, [(i, i ^ bit) for i in range(lax.axis_size(axis))])


def take(array, index, axis):
    return lax.dynamic_index_in_dim(array, index, axis, keepdims=False)


def local_general(target_left, target_right, column_left, column_right, sketch, pattern):
    left, right = target_left[:, 0], target_right[:, 0]
    tile_rows = left.shape[1]
    probes = lax.psum(mm("kbq,bp->kqp", column_left, sketch), "tile")
    col_left = lax.all_gather(column_left, "tile", axis=1, tiled=True)
    col_right = lax.all_gather(column_right, "tile", axis=1, tiled=True)
    core = mm("kbr,kbq->krq", right, col_right) * pattern[:, 0].astype(jnp.float32)[:, None, None]
    reduced = mm("krq,kqp->krp", core, probes)
    sketched = lax.psum(mm("kbr,krp->bp", left, reduced), "step")
    inverse = inverse_factor(mm("bp,bq->pq", sketched, sketched) / tile_rows)
    row_count = tile_rows // lax.axis_size("step")
    rows = lax.dynamic_slice_in_dim(sketched, lax.axis_index("step") * row_count, row_count, 0)
    projected = mm("kbr,bp->krp", left, sketched)
    returned = mm("krq,krp->kqp", core, projected)
    partial = mm("kbq,kqp->bp", col_left, returned)
    factor = lax.psum_scatter(partial, "step", scatter_dimension=0, tiled=True) / tile_rows
    return mm("bp,qp->bq", rows, inverse)[None], mm("bp,qp->bq", factor, inverse)[None]


def local_line(target_left, target_right, column_left, column_right, sketch, pattern):
    left, right = target_left[:, 0], target_right[:, 0]
    tile_rows, rank = left.shape[1:]
    planes = lax.axis_size("tile")
    chips = lax.axis_size("step") // 2
    plane = lax.axis_index("tile")
    core_bit = lax.axis_index("step") % 2
    chip = lax.axis_index("step") // 2
    row_count = tile_rows // (2 * chips)
    up, down = [(0, 1), (1, 2), (2, 3)], [(1, 0), (2, 1), (3, 2)]
    inner_up, inner_down = [(1, 2), (2, 3)], [(2, 1), (1, 0)]

    def across(array, pairs):
        return lax.ppermute(array, "tile", pairs)

    from_below = across(column_right, up)
    from_above = across(column_right, down)
    right_blocks = right.reshape(2, planes, -1, rank)
    lent = across(take(right_blocks, jnp.where(plane == 0, planes - 1, 0), 1), [(0, 1), (3, 2)])
    probes = mm("kbq,bp->kqp", column_left, sketch)
    probes = probes + exchange(probes, "tile", 1)
    probes = probes + exchange(probes, "tile", 2)
    far = across(from_below, inner_up) + across(from_above, inner_down)
    far_index = jnp.where(plane < 2, plane + 2, plane - 2)

    def block(index):
        return take(right_blocks, index, 1)

    core = (
        mm("kbr,kbq->krq", block(plane), column_right)
        + mm("kbr,kbq->krq", block(jnp.maximum(plane - 1, 0)), from_below)
        + mm("kbr,kbq->krq", block(jnp.minimum(plane + 1, planes - 1)), from_above)
    )
    core = core + mm("kbr,kbq->krq", block(far_index), far)
    core = core + across(mm("kbr,kbq->krq", lent, far), [(1, 0), (2, 3)])
    core = core * pattern[:, 0].astype(jnp.float32)[:, None, None]
    left_split = left.reshape(2, chips, 2, row_count, rank)
    left_mine = take(left_split, core_bit, 2)
    left_other = exchange(take(left_split, 1 - core_bit, 2), "step", 1)
    col_split = column_left.reshape(2, 2, row_count, rank)
    col_half = jnp.concatenate([take(col_split, core_bit, 1), exchange(take(col_split, 1 - core_bit, 1), "step", 1)])
    col_below = across(col_half, up)
    col_above = across(col_half, down)
    col_far = across(col_below, inner_up) + across(col_above, inner_down)
    col_last = across(col_far, [(1, 0), (2, 3)])

    both = jnp.concatenate([mm("krq,kqp->krp", core, probes), core])
    both_other = exchange(both, "step", 1)
    core_other = both_other[2:]
    y_part = mm("kcbr,krp->cbp", left_mine, both[:2]) + mm("kcbr,krp->cbp", left_other, both_other[:2])

    def scatter(parts):
        total = take(parts, chip, 0)
        for bit in range(1, chips):
            total = total + exchange(take(parts, chip ^ bit, 0), "step", 2 * bit)
        return total

    y_rows = scatter(y_part)
    y_all = jnp.stack([y_rows] + [exchange(y_rows, "step", 2 * bit) for bit in range(1, chips)])
    order = chip ^ jnp.arange(chips)

    def z_of(part):
        return sum(mm("kbr,bp->krp", take(part, order[i], 1), y_all[i]) for i in range(chips))

    z_mine, z_other = z_of(left_mine), z_of(left_other)
    gram = mm("cbp,cbq->pq", y_all, y_all)[None]
    summed = jnp.concatenate([z_mine, z_other, gram]) + exchange(jnp.concatenate([z_other, z_mine, gram]), "step", 1)
    n_all = mm("krq,krp->kqp", jnp.concatenate([core, core_other]), summed[:4])
    w_mine = mm("kbq,kqp->bp", col_half, n_all)
    w_below = mm("kbq,kqp->bp", col_below, n_all)
    w_above = mm("kbq,kqp->bp", col_above, n_all)
    w_far = mm("kbq,kqp->bp", col_far, n_all)
    w_last = mm("kbq,kqp->bp", col_last, n_all)

    def w_block(index):
        distance = index - plane
        return jnp.where(
            distance == 0, w_mine,
            jnp.where(distance == 1, w_above,
                      jnp.where(distance == -1, w_below,
                                jnp.where(jnp.abs(distance) == 2, w_far, w_last))),
        )

    w_part = jnp.stack([w_block(i) for i in range(planes)])
    w_rows = scatter(w_part) / tile_rows
    inverse = inverse_factor(summed[4] / tile_rows)
    return mm("bp,qp->bq", y_rows, inverse)[None], mm("bp,qp->bq", w_rows, inverse)[None]


def solution(mesh):
    line = mesh.shape["tile"] == 4 and mesh.shape["step"] == 8
    return jax.shard_map(
        local_line if line else local_general,
        mesh=mesh,
        in_specs=(
            P("step", "tile", None, None),
            P("step", "tile", None, None),
            P("step", "tile", None),
            P("step", "tile", None),
            P("tile", None),
            P("step", "tile"),
        ),
        out_specs=(P("tile", "step", None), P("tile", "step", None)),
        check_vma=False,
    )
```

time: 275 us -> 151 us (0.55)
  waiting for transfers between devices: 210 us -> 23.9 us
  starting transfers between devices: 0.37 us -> 44.6 us
  local copies, waits for them, and re-layouts: 1.8 us -> 10.3 us
  other arithmetic: 24.4 us -> 31.9 us
  matrix products: 24 us -> 30.4 us
  between operations: 13.9 us -> 8.83 us
    all_gather x3 -> x0, waiting for transfers between devices: 118 us -> none  [the longest x1 47 us: local(): lax.all_gather(column_left, 'tile', axis=1, tiled=True)]
    psum x1 -> x0, waiting for transfers between devices: 55.2 us -> none  [local(): sketched = lax.psum(partial_y, 'step')]
    ppermute x0 -> x26, starting transfers between devices: none -> 44.6 us  [the longest x11 24.4 us: across(): return lax.ppermute(array, 'tile', pairs)]
    reduce_scatter x1 -> x0, waiting for transfers between devices: 34.5 us -> none  [local(): lax.psum_scatter(partial_w, 'step', scatter_dimension=1, tiled=True)]
    ppermute x0 -> x26, waiting for transfers between devices: none -> 23.9 us  [the longest x11 16.2 us: across(): return lax.ppermute(array, 'tile', pairs)]
    dot_general x8 -> x26, matrix products: 21.8 us -> 29.3 us  [mm(): jnp.einsum(spec, *arrays, precision=HIGH, preferred_element_type=jnp.floa...]
    add x0 -> x4, other arithmetic: none -> 3.5 us  [the longest x1 1.25 us: local_line(): col_far = across(col_below, inner_up) + across(col_above, inner_down)]
    concatenate x0 -> x3, other arithmetic: none -> 3.26 us  [the longest x1 1.77 us: local_line(): jnp.concatenate([take(col_split, core_bit, 1), exchange(take(col_split, 1...]
  transfers between devices with their start and end apart: 5 -> 26, of which waited for: 5 -> 7; matrix products, arithmetic and copies ran while one was open for 2% -> 46% of each run, Pallas kernels for 0% -> 0%
where the time goes in v1:
time: 151 us; the launch traced here: 150 us
  starting transfers between devices  44.6 us (30%)
  other arithmetic  31.9 us (21%)
  matrix products  30.4 us (20%)
  waiting for transfers between devices  23.9 us (16%)
  local copies, waits for them, and re-layouts  10.3 us (7%)
  between operations  8.83 us (6%)
    dot_general x26, matrix products, mm(): jnp.einsum(spec, *arrays, precision=HIGH, preferred_element_type=jnp.floa...  29.3 us
    ppermute x11, starting transfers between devices, across(): return lax.ppermute(array, 'tile', pairs)  24.4 us
    ppermute x15, starting transfers between devices, exchange(): lax.ppermute(array, axis, [(i, i ^ bit) for i in range(lax.axis_size(axis...  20.1 us
    ppermute x11, waiting for transfers between devices, across(): return lax.ppermute(array, 'tile', pairs)  16.2 us
    another operation x3, other arithmetic, inverse_factor(): lower = jnp.linalg.cholesky(gram)  12.4 us
    another operation x2, other arithmetic, inverse_factor(): return jax.scipy.linalg.solve_triangular(lower, eye, lower=True)  11.1 us
    ppermute x15, waiting for transfers between devices, exchange(): lax.ppermute(array, axis, [(i, i ^ bit) for i in range(lax.axis_size(axis...  7.75 us
  transfers between devices with their start and end apart: 26, of which 7 were waited for; matrix products, arithmetic and copies ran while one was open for 46% of the time, Pallas kernels for 0%

profile of v1, /device:TPU:0, one launch (start us, length us, event | category | flops | bytes accessed | tf_op | source)
XLA Modules:
  0.0 149.9 jit_solution(8825434154574705046)
XLA Ops:
  0.7 5.9 %collective-permute-start = (f32[2,512,128]{2,1,0:T(8,128)}, f32[2,512,128]{2,1,0:T(8,128)}, u32[]{:S(2)}, u32[]{:S(2)}) collective-permute-start(f32[2,512,128]{2,1,0:T(8,128)} %param.9), channel_id=1, source_target_pairs={{0,1},{1,2},{2,3},{4,5},{5,6},{6,7},{8,9},{9,10},{10,11},{12,13},{... | collective-permute-start | bytes 1572872 | tf_op jit(solution)/shard_map/ppermute | solution.py:59
  8.9 5.3 %collective-permute-start.4 = (f32[2,512,128]{1,2,0:T(8,128)}, f32[2,512,128]{1,2,0:T(8,128)}, u32[]{:S(2)}, u32[]{:S(2)}) collective-permute-start(f32[2,512,128]{1,2,0:T(8,128)} %bitcast.204), channel_id=1, source_target_pairs={{0,1},{3,2},{4,5},{7,6},{8,9},{11,10},{12,13},{15,14},{16,17},{19,... | collective-permute-start | bytes 1572872 | tf_op jit(solution)/shard_map/ppermute | solution.py:59
  14.2 1.5 %fusion.43 = f32[2,128,128]{2,1,0:T(8,128)S(1)} fusion(f32[2,512,128]{2,1,0:T(8,128)S(1)} %copy-done.1, f32[512,128]{1,0:T(8,128)} %param.10), kind=kOutput, calls=%fused_computation.65 | convolution fusion | flops 100663296 | bytes 917504 | tf_op jit(solution)/shard_map/kbq,bp->kqp/dot_general | solution.py:10
  15.9 2.7 %constant_dynamic-slice_fusion = (f32[2,4,1,256,128]{4,3,2,1,0:T(8,128)S(1)}, f32[2,4,1,256,128]{4,3,2,1,0:T(8,128)}) fusion(f32[2,4,2,256,128]{4,3,2,1,0:T(8,128)} %bitcast.197, s32[]{:T(128)S(6)} %select_n.194, s32[]{:T(128)S(6)} %select_n.188), kind=kLoop, calls=%fused_computation.131 | loop fusion | bytes 4194312 | tf_op jit(solution)/shard_map/jit(dynamic_index_in_dim)/dynamic_slice | solution.py:24
  19.7 1.5 collective-permute-start.2
  21.1 2.4 %collective-permute-done.1 = f32[2,512,128]{2,1,0:T(8,128)} collective-permute-done((f32[2,512,128]{2,1,0:T(8,128)}, f32[2,512,128]{2,1,0:T(8,128)}, u32[]{:S(2)}, u32[]{:S(2)}) %collective-permute-start.1) | collective-permute-done | bytes 524320 | tf_op jit(solution)/shard_map/ppermute | solution.py:59
  24.8 1.6 %fusion.17 = f32[2,128,128]{2,1,0:T(8,128)S(1)} fusion(f32[2,512,128]{2,1,0:T(8,128)} %param.9, f32[2,4,512,128]{3,2,1,0:T(8,128)S(1)} %bitcast.193, s32[]{:T(128)S(6)} %select_n.189), kind=kOutput, calls=%fused_computation.36 | convolution fusion | flops 100663296 | bytes 1179652 | tf_op jit(solution)/shard_map/kbr,kbq->krq/dot_general | solution.py:10
  26.5 4.7 %collective-permute-done.6 = f32[2,128,128]{2,1,0:T(8,128)S(1)} collective-permute-done((f32[2,128,128]{2,1,0:T(8,128)S(1)}, f32[2,128,128]{2,1,0:T(8,128)S(1)}, u32[]{:S(2)}, u32[]{:S(2)}) %collective-permute-start.6) | collective-permute-done | bytes 131104 | tf_op jit(solution)/shard_map/ppermute | solution.py:20
  31.2 7.6 %collective-permute-start.7 = (f32[2,128,128]{2,1,0:T(8,128)S(1)}, f32[2,128,128]{2,1,0:T(8,128)S(1)}, u32[]{:S(2)}, u32[]{:S(2)}) collective-permute-start(f32[2,128,128]{2,1,0:T(8,128)S(1)} %add.181), channel_id=1, source_target_pairs={{0,2},{1,3},{2,0},{3,1},{4,6},{5,7},{6,4},{7,5},{8,10},{9,11},{10,... | collective-permute-start | bytes 393224 | tf_op jit(solution)/shard_map/ppermute | solution.py:20
  38.7 1.6 %convolution_add_fusion.4 = f32[2,128,128]{2,1,0:T(8,128)S(1)} fusion(f32[2,128,128]{2,1,0:T(8,128)S(1)} %fusion.17, f32[2,512,128]{2,1,0:T(8,128)} %collective-permute-done, f32[2,4,512,128]{3,2,1,0:T(8,128)S(1)} %bitcast.194, s32[]{:T(128)S(6)} %max.3), kind=kOutput, calls=%fused_computation.19 | convolution fusion | flops 100696064 | bytes 1310724 | tf_op jit(solution)/shard_map/kbr,kbq->krq/dot_general | solution.py:10
  40.4 1.7 %fusion.53 = f32[2,128,128]{2,1,0:T(8,128)S(1)} fusion(f32[2,512,128]{1,2,0:T(8,128)} %collective-permute-done.4, f32[2,512,128]{2,1,0:T(8,128)} %collective-permute-done.2, f32[2,512,128]{2,1,0:T(8,128)} %collective-permute-done.3), kind=kOutput, calls=%fused_computation.77 | convolution fusion | flops 100794368 | bytes 1703936 | tf_op jit(solution)/shard_map/kbr,kbq->krq/dot_general | solution.py:10
  43.6 1.6 %convolution_add_fusion.3 = f32[2,128,128]{2,1,0:T(8,128)S(1)} fusion(f32[2,128,128]{2,1,0:T(8,128)S(1)} %convolution_add_fusion.4, f32[2,512,128]{2,1,0:T(8,128)} %collective-permute-done.1, f32[2,4,512,128]{3,2,1,0:T(8,128)S(1)} %bitcast.195, s32[]{:T(128)S(6)} %select_n.190), kind=kOutput, calls=%fused_computation.18 | convolution fusion | flops 100696064 | bytes 1310724 | tf_op jit(solution)/shard_map/kbr,kbq->krq/dot_general | solution.py:10
  45.2 5.8 %collective-permute-done.5 = f32[2,128,128]{2,1,0:T(8,128)S(1)} collective-permute-done((f32[2,128,128]{2,1,0:T(8,128)S(1)}, f32[2,128,128]{2,1,0:T(8,128)S(1)}, u32[]{:S(2)}, u32[]{:S(2)}) %collective-permute-start.5) | collective-permute-done | bytes 131104 | tf_op jit(solution)/shard_map/ppermute | solution.py:59
  51.0 1.8 %fusion.6 = f32[2,128,128]{2,1,0:T(8,128)S(1)} fusion(f32[2,128,128]{2,1,0:T(8,128)S(1)} %collective-permute-done.5, f32[2,128,128]{2,1,0:T(8,128)S(1)} %convolution_add_fusion.3, f32[2,4,512,128]{3,2,1,0:T(8,128)S(1)} %bitcast.196, s32[]{:T(128)S(6)} %select_n.192, f32[2,512,128]{2,1,0:T(8,128)} %collective-permute-done.2, ...), kind=kOutput, calls=%fused_computation.20 | convolution fusion | flops 100892672 | bytes 1966596 | tf_op jit(solution)/shard_map/kbr,kbq->krq/dot_general | solution.py:10
  55.0 1.8 %convolution_bitcast_fusion.1 = f32[4,256,128]{2,1,0:T(8,128)S(1)} fusion(f32[2,4,1,256,128]{4,3,2,1,0:T(8,128)} %get-tuple-element.3, f32[2,128,128]{2,1,0:T(8,128)S(1)} %fusion.72), kind=kOutput, calls=%fused_computation.1 | convolution fusion | flops 201326592 | bytes 1703936 | tf_op jit(solution)/shard_map/kcbr,krp->cbp/dot_general | solution.py:10
  56.9 1.5 fusion
  59.9 1.5 collective-permute-start.10
  61.4 1.5 %collective-permute-start.11 = (f32[256,128]{1,0:T(8,128)}, f32[256,128]{1,0:T(8,128)}, u32[]{:S(2)}, u32[]{:S(2)}) collective-permute-start(f32[256,128]{1,0:T(8,128)} %get-tuple-element.14), channel_id=1, source_target_pairs={{0,16},{4,20},{8,24},{12,28},{16,0},{20,4},{24,8},{28,12},{1,17},{... | collective-permute-start | bytes 393224 | tf_op jit(solution)/shard_map/ppermute | solution.py:20
  63.4 1.8 %pad_maximum_fusion = f32[4,256,128]{2,1,0:T(8,128)} fusion(f32[2,256,128]{2,1,0:T(8,128)} %collective-permute-done.17, f32[2,256,128]{2,1,0:T(8,128)S(1)} %get-tuple-element.10), kind=kLoop, calls=%fused_computation.31 | loop fusion | flops 131072 | bytes 1048576 | tf_op jit(solution)/shard_map/concatenate | solution.py:86
  65.1 2.3 %collective-permute-start.19 = (f32[4,256,128]{2,1,0:T(8,128)}, f32[4,256,128]{2,1,0:T(8,128)}, u32[]{:S(2)}, u32[]{:S(2)}) collective-permute-start(f32[4,256,128]{2,1,0:T(8,128)} %pad_maximum_fusion), channel_id=1, source_target_pairs={{0,1},{1,2},{2,3},{4,5},{5,6},{6,7},{8,9},{9,10},{10,11},{12,13},{... | collective-permute-start | bytes 1572872 | tf_op jit(solution)/shard_map/ppermute | solution.py:59
  70.8 2.3 %collective-permute-start.15 = (f32[256,128]{1,0:T(8,128)S(1)}, f32[256,128]{1,0:T(8,128)}, u32[]{:S(2)}, u32[]{:S(2)}) collective-permute-start(f32[256,128]{1,0:T(8,128)S(1)} %fusion.69), channel_id=1, source_target_pairs={{0,24},{4,28},{8,16},{12,20},{16,8},{20,12},{24,0},{28,4},{1,25},{... | collective-permute-start | bytes 393224 | tf_op jit(solution)/shard_map/ppermute | solution.py:20
  81.3 1.5 collective-permute-start.20
  85.3 1.5 %collective-permute-start.14 = (f32[256,128]{1,0:T(8,128)S(1)}, f32[256,128]{1,0:T(8,128)S(1)}, u32[]{:S(2)}, u32[]{:S(2)}) collective-permute-start(f32[256,128]{1,0:T(8,128)S(1)} %fusion.69), channel_id=1, source_target_pairs={{0,16},{4,20},{8,24},{12,28},{16,0},{20,4},{24,8},{28,12},{1,17},{... | collective-permute-start | bytes 393224 | tf_op jit(solution)/shard_map/ppermute | solution.py:20
  88.1 2.2 %collective-permute-done.14 = f32[256,128]{1,0:T(8,128)S(1)} collective-permute-done((f32[256,128]{1,0:T(8,128)S(1)}, f32[256,128]{1,0:T(8,128)S(1)}, u32[]{:S(2)}, u32[]{:S(2)}) %collective-permute-start.14) | collective-permute-done | bytes 131104 | tf_op jit(solution)/shard_map/ppermute | solution.py:20
  96.1 1.6 %convolution_bitcast_fusion.9 = f32[1,128,128]{1,2,0:T(8,128)S(1)} fusion(f32[1,256,128]{2,1,0:T(8,128)} %bitcast.40, f32[1,256,128]{2,1,0:T(8,128)S(1)} %bitcast.206, f32[1,256,128]{2,1,0:T(8,128)S(1)} %bitcast.205, f32[1,256,128]{2,1,0:T(8,128)S(1)} %bitcast.203), kind=kOutput, calls=%fused_computation.21 | convolution fusion | flops 101056512 | bytes 589824 | tf_op jit(solution)/shard_map/cbp,cbq->pq/dot_general | solution.py:10
  100.0 1.5 collective-permute-start.22
  107.1 1.4 convolution_bitcast_fusion.5
  109.2 7.8 %collective-permute-done.22 = f32[4,256,128]{2,1,0:T(8,128)S(1)} collective-permute-done((f32[4,256,128]{2,1,0:T(8,128)S(1)}, f32[4,256,128]{2,1,0:T(8,128)S(1)}, u32[]{:S(2)}, u32[]{:S(2)}) %collective-permute-start.22) | collective-permute-done | bytes 524320 | tf_op jit(solution)/shard_map/ppermute | solution.py:59
  118.2 1.5 collective-permute-start.23
  120.2 1.5 collective-permute-start.25
  123.5 11.7 %cholesky.17 = f32[128,128]{1,0:T(8,128)S(1)} custom-call(f32[128,128]{1,0:T(8,128)S(1)} %fusion.75), custom_call_target="Cholesky" | custom-call | tf_op jit(solution)/shard_map/jit(cholesky)/cholesky | solution.py:14
  136.6 10.4 %custom-call.7 = f32[1,128,128]{1,2,0:T(8,128)} custom-call(f32[1,128,128]{2,1,0:T(8,128)S(1)} %fusion.74), custom_call_target="InvertDiagBlocksLowerTriangular" | custom-call | tf_op jit(solution)/shard_map/jit(_solve_triangular)/triangular_solve | solution.py:16
  (98 shorter events, 40.1 us)
Async XLA Ops:
  0.6 7.2 %copy-start = (f32[2,1,2048,128]{3,2,1,0:T(8,128)S(1)}, f32[2,1,2048,128]{3,2,1,0:T(8,128)}, u32[]{:S(2)}) copy-start(f32[2,1,2048,128]{3,2,1,0:T(8,128)} %param.7) | copy-start | bytes 6291460
  0.6 13.6 %copy-start.1 = (f32[2,512,128]{2,1,0:T(8,128)S(1)}, f32[2,512,128]{2,1,0:T(8,128)}, u32[]{:S(2)}) copy-start(f32[2,512,128]{2,1,0:T(8,128)} %param.8) | copy-start | bytes 1572868
  0.7 19.0 %collective-permute-start = (f32[2,512,128]{2,1,0:T(8,128)}, f32[2,512,128]{2,1,0:T(8,128)}, u32[]{:S(2)}, u32[]{:S(2)}) collective-permute-start(f32[2,512,128]{2,1,0:T(8,128)} %param.9), channel_id=1, source_target_pairs={{0,1},{1,2},{2,3},{4,5},{5,6},{6,7},{8,9},{9,10},{10,11},{12,13},{... | collective-permute-start | bytes 1572872 | tf_op jit(solution)/shard_map/ppermute | solution.py:59
  6.5 17.0 %collective-permute-start.1 = (f32[2,512,128]{2,1,0:T(8,128)}, f32[2,512,128]{2,1,0:T(8,128)}, u32[]{:S(2)}, u32[]{:S(2)}) collective-permute-start(f32[2,512,128]{2,1,0:T(8,128)} %param.9), channel_id=1, source_target_pairs={{1,0},{2,1},{3,2},{5,4},{6,5},{7,6},{9,8},{10,9},{11,10},{13,12},{... | collective-permute-start | bytes 1572872 | tf_op jit(solution)/shard_map/ppermute | solution.py:59
  8.9 31.5 %collective-permute-start.4 = (f32[2,512,128]{1,2,0:T(8,128)}, f32[2,512,128]{1,2,0:T(8,128)}, u32[]{:S(2)}, u32[]{:S(2)}) collective-permute-start(f32[2,512,128]{1,2,0:T(8,128)} %bitcast.204), channel_id=1, source_target_pairs={{0,1},{3,2},{4,5},{7,6},{8,9},{11,10},{12,13},{15,14},{16,17},{19,... | collective-permute-start | bytes 1572872 | tf_op jit(solution)/shard_map/ppermute | solution.py:59
  15.8 15.4 %collective-permute-start.6 = (f32[2,128,128]{2,1,0:T(8,128)S(1)}, f32[2,128,128]{2,1,0:T(8,128)S(1)}, u32[]{:S(2)}, u32[]{:S(2)}) collective-permute-start(f32[2,128,128]{2,1,0:T(8,128)S(1)} %fusion.43), channel_id=1, source_target_pairs={{0,1},{1,0},{2,3},{3,2},{4,5},{5,4},{6,7},{7,6},{8,9},{9,8},{10,11... | collective-permute-start | bytes 393224 | tf_op jit(solution)/shard_map/ppermute | solution.py:20
  18.6 7.8 %copy-start.10 = (s32[2,1]{0,1:T(1,128)S(1)}, s32[2,1]{0,1:T(1,128)}, u32[]{:S(2)}) copy-start(s32[2,1]{0,1:T(1,128)} %param.11) | copy-start | bytes 28
  19.7 37.2 %collective-permute-start.8 = (f32[2,4,256,128]{3,2,0,1:T(8,128)}, f32[2,4,256,128]{3,2,0,1:T(8,128)S(1)}, u32[]{:S(2)}, u32[]{:S(2)}) collective-permute-start(f32[2,4,256,128]{3,2,0,1:T(8,128)} %bitcast.191), channel_id=1, source_target_pairs={{0,4},{4,0},{8,12},{12,8},{16,20},{20,16},{24,28},{28,24},{1,5},{5... | collective-permute-start | bytes 3145736 | tf_op jit(solution)/shard_map/ppermute | solution.py:20
  19.7 20.7 %collective-permute-start.2 = (f32[2,512,128]{2,1,0:T(8,128)}, f32[2,512,128]{2,1,0:T(8,128)}, u32[]{:S(2)}, u32[]{:S(2)}) collective-permute-start(f32[2,512,128]{2,1,0:T(8,128)} %collective-permute-done), channel_id=1, source_target_pairs={{1,2},{2,3},{5,6},{6,7},{9,10},{10,11},{13,14},{14,15},{17,18},{18... | collective-permute-start | bytes 1572872 | tf_op jit(solution)/shard_map/ppermute | solution.py:59
  23.5 16.9 %collective-permute-start.3 = (f32[2,512,128]{2,1,0:T(8,128)}, f32[2,512,128]{2,1,0:T(8,128)}, u32[]{:S(2)}, u32[]{:S(2)}) collective-permute-start(f32[2,512,128]{2,1,0:T(8,128)} %collective-permute-done.1), channel_id=1, source_target_pairs={{2,1},{1,0},{6,5},{5,4},{10,9},{9,8},{14,13},{13,12},{18,17},{17,1... | collective-permute-start | bytes 1572872 | tf_op jit(solution)/shard_map/ppermute | solution.py:59
  31.2 21.7 %collective-permute-start.7 = (f32[2,128,128]{2,1,0:T(8,128)S(1)}, f32[2,128,128]{2,1,0:T(8,128)S(1)}, u32[]{:S(2)}, u32[]{:S(2)}) collective-permute-start(f32[2,128,128]{2,1,0:T(8,128)S(1)} %add.181), channel_id=1, source_target_pairs={{0,2},{1,3},{2,0},{3,1},{4,6},{5,7},{6,4},{7,5},{8,10},{9,11},{10,... | collective-permute-start | bytes 393224 | tf_op jit(solution)/shard_map/ppermute | solution.py:20
  42.1 11.6 %copy-start.2 = (f32[2,512,128]{2,1,0:T(8,128)S(1)}, f32[2,512,128]{2,1,0:T(8,128)}, u32[]{:S(2)}) copy-start(f32[2,512,128]{2,1,0:T(8,128)} %param.8) | copy-start | bytes 1572868
  42.2 8.9 %collective-permute-start.5 = (f32[2,128,128]{2,1,0:T(8,128)S(1)}, f32[2,128,128]{2,1,0:T(8,128)S(1)}, u32[]{:S(2)}, u32[]{:S(2)}) collective-permute-start(f32[2,128,128]{2,1,0:T(8,128)S(1)} %fusion.53), channel_id=1, source_target_pairs={{1,0},{2,3},{5,4},{6,7},{9,8},{10,11},{13,12},{14,15},{17,16},{18,... | collective-permute-start | bytes 393224 | tf_op jit(solution)/shard_map/ppermute | solution.py:59
  53.8 3.1 %collective-permute-start.9 = (f32[4,128,128]{2,1,0:T(8,128)}, f32[4,128,128]{2,1,0:T(8,128)}, u32[]{:S(2)}, u32[]{:S(2)}) collective-permute-start(f32[4,128,128]{2,1,0:T(8,128)} %pad_maximum_fusion.4), channel_id=1, source_target_pairs={{0,4},{4,0},{8,12},{12,8},{16,20},{20,16},{24,28},{28,24},{1,5},{5... | collective-permute-start | bytes 786440 | tf_op jit(solution)/shard_map/ppermute | solution.py:20
  54.5 8.8 %collective-permute-start.17 = (f32[2,256,128]{2,1,0:T(8,128)}, f32[2,256,128]{2,1,0:T(8,128)}, u32[]{:S(2)}, u32[]{:S(2)}) collective-permute-start(f32[2,256,128]{2,1,0:T(8,128)} %get-tuple-element.11), channel_id=1, source_target_pairs={{0,4},{4,0},{8,12},{12,8},{16,20},{20,16},{24,28},{28,24},{1,5},{5... | collective-permute-start | bytes 786440 | tf_op jit(solution)/shard_map/ppermute | solution.py:20
  59.9 8.8 %collective-permute-start.10 = (f32[256,128]{1,0:T(8,128)}, f32[256,128]{1,0:T(8,128)S(1)}, u32[]{:S(2)}, u32[]{:S(2)}) collective-permute-start(f32[256,128]{1,0:T(8,128)} %get-tuple-element.12), channel_id=1, source_target_pairs={{0,8},{4,12},{8,0},{12,4},{16,24},{20,28},{24,16},{28,20},{1,9},{5... | collective-permute-start | bytes 393224 | tf_op jit(solution)/shard_map/ppermute | solution.py:20
  61.4 8.3 %collective-permute-start.11 = (f32[256,128]{1,0:T(8,128)}, f32[256,128]{1,0:T(8,128)}, u32[]{:S(2)}, u32[]{:S(2)}) collective-permute-start(f32[256,128]{1,0:T(8,128)} %get-tuple-element.14), channel_id=1, source_target_pairs={{0,16},{4,20},{8,24},{12,28},{16,0},{20,4},{24,8},{28,12},{1,17},{... | collective-permute-start | bytes 393224 | tf_op jit(solution)/shard_map/ppermute | solution.py:20
  62.9 6.7 %collective-permute-start.12 = (f32[256,128]{1,0:T(8,128)}, f32[256,128]{1,0:T(8,128)}, u32[]{:S(2)}, u32[]{:S(2)}) collective-permute-start(f32[256,128]{1,0:T(8,128)} %get-tuple-element.13), channel_id=1, source_target_pairs={{0,24},{4,28},{8,16},{12,20},{16,8},{20,12},{24,0},{28,4},{1,25},{... | collective-permute-start | bytes 393224 | tf_op jit(solution)/shard_map/ppermute | solution.py:20
  65.1 16.2 %collective-permute-start.19 = (f32[4,256,128]{2,1,0:T(8,128)}, f32[4,256,128]{2,1,0:T(8,128)}, u32[]{:S(2)}, u32[]{:S(2)}) collective-permute-start(f32[4,256,128]{2,1,0:T(8,128)} %pad_maximum_fusion), channel_id=1, source_target_pairs={{0,1},{1,2},{2,3},{4,5},{5,6},{6,7},{8,9},{9,10},{10,11},{12,13},{... | collective-permute-start | bytes 1572872 | tf_op jit(solution)/shard_map/ppermute | solution.py:59
  67.4 15.4 %collective-permute-start.18 = (f32[4,256,128]{2,1,0:T(8,128)}, f32[4,256,128]{2,1,0:T(8,128)}, u32[]{:S(2)}, u32[]{:S(2)}) collective-permute-start(f32[4,256,128]{2,1,0:T(8,128)} %pad_maximum_fusion), channel_id=1, source_target_pairs={{1,0},{2,1},{3,2},{5,4},{6,5},{7,6},{9,8},{10,9},{11,10},{13,12},{... | collective-permute-start | bytes 1572872 | tf_op jit(solution)/shard_map/ppermute | solution.py:59
  70.8 16.0 %collective-permute-start.15 = (f32[256,128]{1,0:T(8,128)S(1)}, f32[256,128]{1,0:T(8,128)}, u32[]{:S(2)}, u32[]{:S(2)}) collective-permute-start(f32[256,128]{1,0:T(8,128)S(1)} %fusion.69), channel_id=1, source_target_pairs={{0,24},{4,28},{8,16},{12,20},{16,8},{20,12},{24,0},{28,4},{1,25},{... | collective-permute-start | bytes 393224 | tf_op jit(solution)/shard_map/ppermute | solution.py:20
  81.3 17.2 %collective-permute-start.20 = (f32[4,256,128]{2,1,0:T(8,128)}, f32[4,256,128]{2,1,0:T(8,128)}, u32[]{:S(2)}, u32[]{:S(2)}) collective-permute-start(f32[4,256,128]{2,1,0:T(8,128)} %collective-permute-done.19), channel_id=1, source_target_pairs={{1,2},{2,3},{5,6},{6,7},{9,10},{10,11},{13,14},{14,15},{17,18},{18... | collective-permute-start | bytes 1572872 | tf_op jit(solution)/shard_map/ppermute | solution.py:59
  82.8 16.0 %collective-permute-start.21 = (f32[4,256,128]{2,1,0:T(8,128)}, f32[4,256,128]{2,1,0:T(8,128)}, u32[]{:S(2)}, u32[]{:S(2)}) collective-permute-start(f32[4,256,128]{2,1,0:T(8,128)} %collective-permute-done.18), channel_id=1, source_target_pairs={{2,1},{1,0},{6,5},{5,4},{10,9},{9,8},{14,13},{13,12},{18,17},{17,1... | collective-permute-start | bytes 1572872 | tf_op jit(solution)/shard_map/ppermute | solution.py:59
  84.1 7.4 %collective-permute-start.13 = (f32[256,128]{1,0:T(8,128)S(1)}, f32[256,128]{1,0:T(8,128)S(1)}, u32[]{:S(2)}, u32[]{:S(2)}) collective-permute-start(f32[256,128]{1,0:T(8,128)S(1)} %fusion.69), channel_id=1, source_target_pairs={{0,8},{4,12},{8,0},{12,4},{16,24},{20,28},{24,16},{28,20},{1,9},{5... | collective-permute-start | bytes 393224 | tf_op jit(solution)/shard_map/ppermute | solution.py:20
  85.3 5.0 %collective-permute-start.14 = (f32[256,128]{1,0:T(8,128)S(1)}, f32[256,128]{1,0:T(8,128)S(1)}, u32[]{:S(2)}, u32[]{:S(2)}) collective-permute-start(f32[256,128]{1,0:T(8,128)S(1)} %fusion.69), channel_id=1, source_target_pairs={{0,16},{4,20},{8,24},{12,28},{16,0},{20,4},{24,8},{28,12},{1,17},{... | collective-permute-start | bytes 393224 | tf_op jit(solution)/shard_map/ppermute | solution.py:20
  96.1 7.4 %copy-start.5 = (f32[2,128,128]{2,1,0:T(8,128)S(1)}, f32[2,128,128]{2,1,0:T(8,128)}, u32[]{:S(2)}) copy-start(f32[2,128,128]{2,1,0:T(8,128)} %copy-done.4) | copy-start | bytes 393220
  98.5 3.9 %collective-permute-start.16 = (f32[5,128,128]{1,2,0:T(8,128)}, f32[5,128,128]{1,2,0:T(8,128)}, u32[]{:S(2)}, u32[]{:S(2)}) collective-permute-start(f32[5,128,128]{1,2,0:T(8,128)} %pad_maximum_fusion.2), channel_id=1, source_target_pairs={{0,4},{4,0},{8,12},{12,8},{16,20},{20,16},{24,28},{28,24},{1,5},{5... | collective-permute-start | bytes 983048 | tf_op jit(solution)/shard_map/ppermute | solution.py:20
  100.0 16.9 %collective-permute-start.22 = (f32[4,256,128]{2,1,0:T(8,128)S(1)}, f32[4,256,128]{2,1,0:T(8,128)S(1)}, u32[]{:S(2)}, u32[]{:S(2)}) collective-permute-start(f32[4,256,128]{2,1,0:T(8,128)S(1)} %add.204), channel_id=1, source_target_pairs={{1,0},{2,3},{5,4},{6,7},{9,8},{10,11},{13,12},{14,15},{17,16},{18,... | collective-permute-start | bytes 1572872 | tf_op jit(solution)/shard_map/ppermute | solution.py:59
  103.6 5.0 %copy-start.6 = (f32[5,128,128]{1,2,0:T(8,128)}, f32[5,128,128]{1,2,0:T(8,128)S(1)}, u32[]{:S(2)}) copy-start(f32[5,128,128]{1,2,0:T(8,128)S(1)} %fusion.23) | copy-start | bytes 983044
  118.2 30.8 %collective-permute-start.23 = (f32[256,128]{1,0:T(8,128)}, f32[256,128]{1,0:T(8,128)S(1)}, u32[]{:S(2)}, u32[]{:S(2)}) collective-permute-start(f32[256,128]{1,0:T(8,128)} %get-tuple-element.7), channel_id=1, source_target_pairs={{0,8},{4,12},{8,0},{12,4},{16,24},{20,28},{24,16},{28,20},{1,9},{5... | collective-permute-start | bytes 393224 | tf_op jit(solution)/shard_map/ppermute | solution.py:20
  119.7 29.3 %collective-permute-start.24 = (f32[256,128]{1,0:T(8,128)S(1)}, f32[256,128]{1,0:T(8,128)S(1)}, u32[]{:S(2)}, u32[]{:S(2)}) collective-permute-start(f32[256,128]{1,0:T(8,128)S(1)} %get-tuple-element.9), channel_id=1, source_target_pairs={{0,16},{4,20},{8,24},{12,28},{16,0},{20,4},{24,8},{28,12},{1,17},{... | collective-permute-start | bytes 393224 | tf_op jit(solution)/shard_map/ppermute | solution.py:20
  120.2 28.8 %collective-permute-start.25 = (f32[256,128]{1,0:T(8,128)S(1)}, f32[256,128]{1,0:T(8,128)S(1)}, u32[]{:S(2)}, u32[]{:S(2)}) collective-permute-start(f32[256,128]{1,0:T(8,128)S(1)} %get-tuple-element.8), channel_id=1, source_target_pairs={{0,24},{4,28},{8,16},{12,20},{16,8},{20,12},{24,0},{28,4},{1,25},{... | collective-permute-start | bytes 393224 | tf_op jit(solution)/shard_map/ppermute | solution.py:20
  (5 other events, 8.8 us)

commit v2 on v1

v2 whole, which is shorter than its diff:
```python
import functools

import jax
import jax.numpy as jnp
from jax import lax
from jax.experimental import pallas as pl
from jax.experimental.pallas import tpu as pltpu
from jax.sharding import PartitionSpec as P

HIGH = lax.Precision.HIGH


def mm(spec, *arrays):
    return jnp.einsum(spec, *arrays, precision=HIGH, preferred_element_type=jnp.float32)


def inverse_factor(gram):
    lower = jnp.linalg.cholesky(gram)
    eye = jnp.eye(gram.shape[-1], dtype=gram.dtype)
    return jax.scipy.linalg.solve_triangular(lower, eye, lower=True)


def exchange(array, axis, bit):
    return lax.ppermute(array, axis, [(i, i ^ bit) for i in range(lax.axis_size(axis))])


def take(array, index, axis):
    return lax.dynamic_index_in_dim(array, index, axis, keepdims=False)


def local_general(target_left, target_right, column_left, column_right, sketch, pattern):
    left, right = target_left[:, 0], target_right[:, 0]
    tile_rows = left.shape[1]
    probes = lax.psum(mm("kbq,bp->kqp", column_left, sketch), "tile")
    col_left = lax.all_gather(column_left, "tile", axis=1, tiled=True)
    col_right = lax.all_gather(column_right, "tile", axis=1, tiled=True)
    core = mm("kbr,kbq->krq", right, col_right) * pattern[:, 0].astype(jnp.float32)[:, None, None]
    reduced = mm("krq,kqp->krp", core, probes)
    sketched = lax.psum(mm("kbr,krp->bp", left, reduced), "step")
    inverse = inverse_factor(mm("bp,bq->pq", sketched, sketched) / tile_rows)
    row_count = tile_rows // lax.axis_size("step")
    rows = lax.dynamic_slice_in_dim(sketched, lax.axis_index("step") * row_count, row_count, 0)
    projected = mm("kbr,bp->krp", left, sketched)
    returned = mm("krq,krp->kqp", core, projected)
    partial = mm("kbq,kqp->bp", col_left, returned)
    factor = lax.psum_scatter(partial, "step", scatter_dimension=0, tiled=True) / tile_rows
    return mm("bp,qp->bq", rows, inverse)[None], mm("bp,qp->bq", factor, inverse)[None]


TN = (((0,), (0,)), ((), ()))
NN = (((1,), (0,)), ((), ()))
NT = (((1,), (1,)), ((), ()))


def split(array):
    high = array.astype(jnp.bfloat16)
    return high, (array - high.astype(jnp.float32)).astype(jnp.bfloat16)


def dot3(a, b, dims):
    a_high, a_low = split(a)
    b_high, b_low = split(b)
    axis = 1 - dims[0][1][0]
    width = b.shape[axis]
    dot = functools.partial(lax.dot_general, dimension_numbers=dims, preferred_element_type=jnp.float32)
    wide = dot(a_high, jnp.concatenate([b_high, b_low], axis))
    return wide[:, :width] + wide[:, width:] + dot(a_low, b_high)


def dot_full(a, b, dims):
    return lax.dot_general(a, b, dims, precision=lax.Precision.HIGHEST, preferred_element_type=jnp.float32)


def call(kernel, outs, args, spaces="", scratch=(), cost=0):
    kinds = {"v": pltpu.VMEM, "a": pl.ANY, "s": pltpu.SMEM}
    spaces = spaces or "v" * len(args)
    shapes = [jax.ShapeDtypeStruct(shape, jnp.float32) for shape in outs]
    return pl.pallas_call(
        kernel,
        out_shape=shapes,
        in_specs=[pl.BlockSpec(memory_space=kinds[letter]) for letter in spaces],
        out_specs=[pl.BlockSpec(memory_space=pltpu.VMEM) for _ in shapes],
        scratch_shapes=list(scratch),
        compiler_params=pltpu.CompilerParams(vmem_limit_bytes=24 << 20),
        cost_estimate=pl.CostEstimate(flops=cost, bytes_accessed=1 << 20, transcendentals=0),
    )(*args)


def core_kernel(planes, part, own_rows, first, second, core, lent):
    plane = lax.axis_index("tile")
    is_end = jnp.logical_or(plane == 0, plane == planes - 1)

    @pl.when(is_end)
    def _():
        for k in range(2):
            core[k] = part[k] + dot3(own_rows[k], second[k], TN)
            lent[k] = jnp.zeros_like(lent[k])

    @pl.when(jnp.logical_not(is_end))
    def _():
        for k in range(2):
            core[k] = part[k] + dot3(own_rows[k], first[k], TN)
            lent[k] = dot3(second[k], first[k], TN)


def reduced_kernel(core, lent, probe_here, probe_far, pattern, both):
    for k in range(2):
        weight = pattern[k, 0].astype(jnp.float32)
        c = (core[k] + lent[k]) * weight
        both[k] = dot3(c, probe_here[k] + probe_far[k] + lent[2 + k], NN)
        both[2 + k] = c


def start_rows(left, left_other, held, sems, chips, rows):
    position = lax.axis_index("step")
    chip, bit = position // 2, position % 2
    copies = []
    for i in range(chips):
        block = jnp.bitwise_xor(chip, i)
        mine = left.at[:, 0, pl.ds(pl.multiple_of((block * 2 + bit) * rows, rows), rows), :]
        copies.append((
            pltpu.make_async_copy(mine, held.at[i, pl.ds(0, 2)], sems.at[2 * i]),
            pltpu.make_async_copy(left_other.at[:, block], held.at[i, pl.ds(2, 2)], sems.at[2 * i + 1]),
        ))
    for pair in copies:
        for copy in pair:
            copy.start()
    return copies


def y_kernel(left, left_other, both, both_other, *rest):
    *outs, held, sems = rest
    chips, rows = len(outs), outs[0].shape[0]
    copies = start_rows(left, left_other, held, sems, chips, rows)
    reduced = jnp.concatenate([both[0], both[1], both_other[0], both_other[1]], 0)
    for i, out in enumerate(outs):
        for copy in copies[i]:
            copy.wait()
        out[...] = dot3(jnp.concatenate([held[i, k] for k in range(4)], 1), reduced, NN)


def z_kernel(left, left_other, *rest):
    *ys, out, held, sems = rest
    chips, rows = len(ys), ys[0].shape[0]
    rank = out.shape[-1]
    copies = start_rows(left, left_other, held, sems, chips, rows)
    total = jnp.zeros((rank, 5 * rank), jnp.float32)
    dot = functools.partial(lax.dot_general, dimension_numbers=TN, preferred_element_type=jnp.float32)
    for i, y in enumerate(ys):
        y_here = y[...]
        for copy in copies[i]:
            copy.wait()
        beside = jnp.concatenate([held[i, 2], held[i, 3], held[i, 0], held[i, 1], y_here], 1)
        b_high, b_low = split(beside)
        a_high, a_low = split(y_here)
        total += dot(a_high, b_high) + dot(a_high, b_low) + dot(a_low, b_high)
    for k in range(5):
        out[k] = total[:, k * rank:(k + 1) * rank]


def w_kernel(planes, sent, got, both, both_other, own, near, inner, inner_far, outer, last, *rest):
    *outs, gram, held, sems = rest
    plane = lax.axis_index("tile")
    chip = lax.axis_index("step") // 2
    is_end = jnp.logical_or(plane == 0, plane == planes - 1)

    def pick(i, wanted, source):
        @pl.when(wanted)
        def _():
            pltpu.make_async_copy(source, held.at[i], sems.at[i]).start()

    for i in range(planes):
        block = jnp.bitwise_xor(chip, i)
        apart = jnp.bitwise_xor(block, plane)
        pick(i, apart == 0, own)
        pick(i, apart == 1, near)
        pick(i, jnp.logical_and(apart == 2, is_end), outer)
        pick(i, jnp.logical_and(apart == 2, jnp.logical_not(is_end)), inner_far)
        pick(i, jnp.logical_and(apart == 3, is_end), last)
        pick(i, jnp.logical_and(apart == 3, jnp.logical_not(is_end)), inner)
    gram[...] = sent[4] + got[4]
    returned = []
    for k in range(2):
        returned.append(dot3(sent[2 + k] + got[k], both[2 + k], NN))
    for k in range(2):
        returned.append(dot3(sent[k] + got[2 + k], both_other[2 + k], NN))
    returned = jnp.concatenate(returned, 1)
    for i, out in enumerate(outs):
        pltpu.make_async_copy(own, held.at[i], sems.at[i]).wait()
        out[...] = dot3(jnp.concatenate([held[i, k] for k in range(4)], 1), returned, NT)


def basis_kernel(tile_rows, width, gram, y_rows, basis, inverse):
    rank = gram.shape[0]
    scaled = gram[...] * (1.0 / tile_rows)
    eye = (lax.broadcasted_iota(jnp.int32, (rank, rank), 0) == lax.broadcasted_iota(jnp.int32, (rank, rank), 1))
    work = jnp.concatenate([scaled, eye.astype(jnp.float32)], 1)
    done = []
    for begin in range(0, rank, width):
        panel = work[:width]
        row_index = lax.broadcasted_iota(jnp.int32, (width, 1), 0)
        scale = jnp.zeros((width, 1), jnp.float32)
        for j in range(width):
            column = panel[:, begin + j:begin + j + 1]
            pivot = panel[j:j + 1, begin + j:begin + j + 1]
            factor = jnp.where(row_index > j, column * (1.0 / pivot), 0.0)
            scale = jnp.where(row_index == j, lax.rsqrt(pivot), scale)
            panel = panel - factor * panel[j:j + 1]
        panel = panel * scale
        done.append(panel[:, rank:])
        if begin + width < rank:
            work = work[width:] - dot_full(panel[:, begin + width:rank], panel, TN)
    lower_inverse = jnp.concatenate(done, 0)
    inverse[...] = lower_inverse
    basis[...] = dot_full(y_rows[...], lower_inverse, NT)


def factor_kernel(tile_rows, a, b, c, d, inverse, factor):
    total = (a[...] + b[...] + c[...] + d[...]) * (1.0 / tile_rows)
    factor[...] = dot_full(total, inverse[...], NT)


def local_line(target_left, target_right, column_left, column_right, sketch, pattern):
    tile_rows, rank = target_left.shape[2:]
    planes = lax.axis_size("tile")
    chips = lax.axis_size("step") // 2
    plane = lax.axis_index("tile")
    core_bit = lax.axis_index("step") % 2
    chip = lax.axis_index("step") // 2
    row_count = tile_rows // (2 * chips)
    is_end = jnp.logical_or(plane == 0, plane == planes - 1)
    outer_pairs, inner_pairs = [(0, 1), (1, 0), (2, 3), (3, 2)], [(1, 2), (2, 1)]
    outward = [(1, 0), (2, 3)]

    def across(array, pairs):
        return lax.ppermute(array, "tile", pairs)

    near = across(column_right, outer_pairs)
    inner = across(column_right, inner_pairs)
    probes = mm("kbq,bp->kqp", column_left, sketch)
    probes = probes + across(probes, outer_pairs)
    right_blocks = target_right.reshape(2, planes, -1, rank)

    def block(index):
        return take(right_blocks, index, 1)

    inner_far = across(near, inner_pairs)
    outer = across(jnp.where(is_end, block(planes - 1 - plane), inner), outer_pairs)
    probes_far = across(probes, inner_pairs)
    part = (
        mm("kbr,kbq->krq", block(plane), column_right)
        + mm("kbr,kbq->krq", block(plane ^ 1), near)
        + mm("kbr,kbq->krq", block(jnp.where(is_end, plane, planes - 1 - plane)), inner)
    )
    far_rows = block(plane ^ 2)
    core, lent = call(functools.partial(core_kernel, planes), [(2, rank, rank)] * 2, [part, far_rows, inner_far, outer])
    lent = across(jnp.concatenate([lent, probes_far]), outward)

    left_split = target_left.reshape(2, chips, 2, row_count, rank)
    left_other = exchange(take(left_split, 1 - core_bit, 2), "step", 1)
    col_split = column_left.reshape(2, 2, row_count, rank)
    col_half = jnp.concatenate([take(col_split, core_bit, 1), exchange(take(col_split, 1 - core_bit, 1), "step", 1)])
    col_half, _ = lax.optimization_barrier((col_half, near))
    col_near = across(col_half, outer_pairs)
    col_inner = across(col_half, inner_pairs)
    col_inner_far = across(col_near, inner_pairs)
    col_outer = across(col_inner, outward)
    col_last = across(col_inner_far, outward)

    (both,) = call(reduced_kernel, [(4, rank, rank)], [core, lent, probes, probes_far, pattern], "vvvvs")
    both_other = exchange(both, "step", 1)
    rows_scratch = [pltpu.VMEM((chips, 4, row_count, rank), jnp.float32), pltpu.SemaphoreType.DMA((2 * chips,))]
    y_parts = call(y_kernel, [(row_count, rank)] * chips, [target_left, left_other, both, both_other], "aavv", rows_scratch)
    y_rows = y_parts[0]
    for bit in range(1, chips):
        y_rows = y_rows + exchange(y_parts[bit], "step", 2 * bit)
    y_all = [y_rows] + [exchange(y_rows, "step", 2 * bit) for bit in range(1, chips)]
    (sent,) = call(z_kernel, [(5, rank, rank)], [target_left, left_other, *y_all], "aa" + "v" * chips, rows_scratch)
    got = exchange(sent, "step", 1)
    *w_parts, gram = call(
        functools.partial(w_kernel, planes),
        [(row_count, rank)] * planes + [(rank, rank)],
        [sent, got, both, both_other, col_half, col_near, col_inner, col_inner_far, col_outer, col_last],
        "vvvvaaaaaa",
        [pltpu.VMEM((planes, 4, row_count, rank), jnp.float32), pltpu.SemaphoreType.DMA((planes,))],
    )
    w_got = [exchange(w_parts[bit], "step", 2 * bit) for bit in range(1, chips)]
    basis, inverse = call(
        functools.partial(basis_kernel, tile_rows, 32), [(row_count, rank), (rank, rank)], [gram, y_rows], cost=10**9
    )
    (factor,) = call(functools.partial(factor_kernel, tile_rows), [(row_count, rank)], [w_parts[0], *w_got, inverse])
    return basis[None], factor[None]


def solution(mesh):
    line = mesh.shape["tile"] == 4 and mesh.shape["step"] == 8
    return jax.shard_map(
        local_line if line else local_general,
        mesh=mesh,
        in_specs=(
            P("step", "tile", None, None),
            P("step", "tile", None, None),
            P("step", "tile", None),
            P("step", "tile", None),
            P("tile", None),
            P("step", "tile"),
        ),
        out_specs=(P("tile", "step", None), P("tile", "step", None)),
        check_vma=False,
    )
```

time: 151 us -> 111 us (0.74)
  other arithmetic: 31.9 us -> 3.6 us
  matrix products: 30.4 us -> 7.5 us
  Pallas kernels: 0 us -> 21.1 us
  waiting for transfers between devices: 23.9 us -> 34.2 us
  starting transfers between devices: 44.6 us -> 35.1 us
  between operations: 8.83 us -> 0.9 us
  local copies, waits for them, and re-layouts: 10.3 us -> 7.59 us
    another operation x8 -> x0, other arithmetic: 23.6 us -> none  [the longest x3 12.4 us: inverse_factor(): lower = jnp.linalg.cholesky(gram)]
    dot_general x26 -> x4, matrix products: 29.3 us -> 7.5 us  [mm(): jnp.einsum(spec, *arrays, precision=HIGH, preferred_element_type=jnp.floa...]
    pallas_call x0 -> x7, Pallas kernels: none -> 21.1 us  [call(): pl.pallas_call(kernel, out_shape=shapes, in_specs=[pl.BlockSpec(memory_sp...]
    ppermute x15 -> x13, starting transfers between devices: 20.1 us -> 11.3 us  [exchange(): lax.ppermute(array, axis, [(i, i ^ bit) for i in range(lax.axis_size(axis...]
    ppermute x11 -> x12, waiting for transfers between devices: 16.2 us -> 23.4 us  [across(): return lax.ppermute(array, 'tile', pairs)]
    ppermute x15 -> x13, waiting for transfers between devices: 7.75 us -> 10.7 us  [exchange(): lax.ppermute(array, axis, [(i, i ^ bit) for i in range(lax.axis_size(axis...]
    squeeze x3, local copies, waits for them, and re-layouts: 2.19 us -> 4.98 us  [take(): return lax.dynamic_index_in_dim(array, index, axis, keepdims=False)]
    dynamic_slice x2 -> x0, local copies, waits for them, and re-layouts: 2.77 us -> none  [take(): return lax.dynamic_index_in_dim(array, index, axis, keepdims=False)]
  transfers between devices with their start and end apart: 26 -> 25, of which waited for: 7 -> 11; matrix products, arithmetic and copies ran while one was open for 46% -> 15% of each run, Pallas kernels for 0% -> 16%
where the time goes in v2:
time: 111 us; the launch traced here: 110 us
  starting transfers between devices  35.1 us (32%)
  waiting for transfers between devices  34.2 us (31%)
  Pallas kernels  21.1 us (19%)
  local copies, waits for them, and re-layouts  7.59 us (7%)
  matrix products  7.5 us (7%)
  other arithmetic  3.6 us (3%)
    ppermute x12, starting transfers between devices, across(): return lax.ppermute(array, 'tile', pairs)  23.8 us
    ppermute x12, waiting for transfers between devices, across(): return lax.ppermute(array, 'tile', pairs)  23.4 us
    pallas_call x7, Pallas kernels, call(): pl.pallas_call(kernel, out_shape=shapes, in_specs=[pl.BlockSpec(memory_sp...  21.1 us
    ppermute x13, starting transfers between devices, exchange(): lax.ppermute(array, axis, [(i, i ^ bit) for i in range(lax.axis_size(axis...  11.3 us
    ppermute x13, waiting for transfers between devices, exchange(): lax.ppermute(array, axis, [(i, i ^ bit) for i in range(lax.axis_size(axis...  10.7 us
    dot_general x4, matrix products, mm(): jnp.einsum(spec, *arrays, precision=HIGH, preferred_element_type=jnp.floa...  7.5 us
    squeeze x3, local copies, waits for them, and re-layouts, take(): return lax.dynamic_index_in_dim(array, index, axis, keepdims=False)  4.98 us
    unnamed x25, local copies, waits for them, and re-layouts  2.61 us
  transfers between devices with their start and end apart: 25, of which 11 were waited for; matrix products, arithmetic and copies ran while one was open for 15% of the time, Pallas kernels for 16%

profile of v2, /device:TPU:0, one launch (start us, length us, event | category | flops | bytes accessed | tf_op | source)
XLA Modules:
  0.0 109.9 jit_solution(16816188298877521147)
XLA Ops:
  0.7 3.1 %collective-permute-start.1 = (f32[2,512,128]{2,1,0:T(8,128)}, f32[2,512,128]{2,1,0:T(8,128)}, u32[]{:S(2)}, u32[]{:S(2)}) collective-permute-start(f32[2,512,128]{2,1,0:T(8,128)} %param.9), channel_id=1, source_target_pairs={{0,1},{1,0},{2,3},{3,2},{4,5},{5,4},{6,7},{7,6},{8,9},{9,8},{10,11... | collective-permute-start | bytes 1572872 | tf_op jit(solution)/shard_map/ppermute | solution.py:236
  3.7 1.5 %collective-permute-start.2 = (f32[2,512,128]{2,1,0:T(8,128)}, f32[2,512,128]{2,1,0:T(8,128)}, u32[]{:S(2)}, u32[]{:S(2)}) collective-permute-start(f32[2,512,128]{2,1,0:T(8,128)} %param.9), channel_id=1, source_target_pairs={{1,2},{2,1},{5,6},{6,5},{9,10},{10,9},{13,14},{14,13},{17,18},{18,... | collective-permute-start | bytes 1572872 | tf_op jit(solution)/shard_map/ppermute | solution.py:236
  5.2 1.6 %fusion.7 = f32[2,128,128]{2,1,0:T(8,128)S(1)} fusion(f32[2,512,128]{2,1,0:T(8,128)} %param.8, f32[512,128]{1,0:T(8,128)S(1)} %copy-done), kind=kOutput, calls=%fused_computation.14 | convolution fusion | flops 100663296 | bytes 917504 | tf_op jit(solution)/shard_map/kbq,bp->kqp/dot_general | solution.py:14
  6.9 3.7 %collective-permute-start.5 = (f32[2,128,128]{2,1,0:T(8,128)S(1)}, f32[2,128,128]{2,1,0:T(8,128)}, u32[]{:S(2)}, u32[]{:S(2)}) collective-permute-start(f32[2,128,128]{2,1,0:T(8,128)S(1)} %fusion.7), channel_id=1, source_target_pairs={{0,1},{1,0},{2,3},{3,2},{4,5},{5,4},{6,7},{7,6},{8,9},{9,8},{10,11... | collective-permute-start | bytes 393224 | tf_op jit(solution)/shard_map/ppermute | solution.py:236
  10.5 2.3 %dynamic-slice_bitcast_fusion = f32[2,4,256,128]{3,2,1,0:T(8,128)} fusion(f32[2,4,2,256,128]{4,3,2,1,0:T(8,128)} %bitcast.44, s32[]{:T(128)S(6)} %select_n.44), kind=kLoop, calls=%fused_computation.2 | loop fusion | bytes 2097156 | tf_op jit(solution)/shard_map/jit(dynamic_index_in_dim)/squeeze | solution.py:28
  12.8 1.9 %dynamic-slice_bitcast_fusion.3 = (f32[2,256,128]{2,1,0:T(8,128)}, f32[2,256,128]{2,1,0:T(8,128)}) fusion(f32[2,2,256,128]{3,2,1,0:T(8,128)} %bitcast.50, s32[]{:T(128)S(6)} %select_n.53, s32[]{:T(128)S(6)} %select_n.44), kind=kLoop, calls=%fused_computation.17 | loop fusion | bytes 1048584 | tf_op jit(solution)/shard_map/jit(dynamic_index_in_dim)/squeeze | solution.py:28
  15.2 2.3 %fusion.2 = f32[2,128,128]{2,1,0:T(8,128)} fusion(f32[2,512,128]{2,1,0:T(8,128)} %param.9, f32[2,4,512,128]{3,2,1,0:T(8,128)S(1)} %bitcast.46, s32[]{:T(128)S(6)} %select_n.45), kind=kOutput, calls=%fused_computation.6 | convolution fusion | flops 100663296 | bytes 1179652 | tf_op jit(solution)/shard_map/kbr,kbq->krq/dot_general | solution.py:14
  20.6 5.7 %collective-permute-start.4 = (f32[2,512,128]{2,1,0:T(8,128)S(1)}, f32[2,512,128]{2,1,0:T(8,128)S(1)}, u32[]{:S(2)}, u32[]{:S(2)}) collective-permute-start(f32[2,512,128]{2,1,0:T(8,128)S(1)} %bitcast_select_fusion), channel_id=1, source_target_pairs={{0,1},{1,0},{2,3},{3,2},{4,5},{5,4},{6,7},{7,6},{8,9},{9,8},{10,11... | collective-permute-start | bytes 1572872 | tf_op jit(solution)/shard_map/ppermute | solution.py:236
  26.9 1.8 %pad_maximum_fusion.own = f32[4,256,128]{2,1,0:T(8,128)} fusion(f32[2,256,128]{2,1,0:T(8,128)} %collective-permute-done.16, f32[2,256,128]{2,1,0:T(8,128)S(1)} %copy-done.8), kind=kLoop, calls=%fused_computation.3 | loop fusion | flops 131072 | bytes 1048576 | tf_op jit(solution)/shard_map/concatenate | solution.py:262
  28.7 1.8 %collective-permute-start.17 = (f32[4,256,128]{2,1,0:T(8,128)}, f32[4,256,128]{2,1,0:T(8,128)}, u32[]{:S(2)}, u32[]{:S(2)}) collective-permute-start(f32[4,256,128]{2,1,0:T(8,128)} %pad_maximum_fusion.own), channel_id=1, source_target_pairs={{0,1},{1,0},{2,3},{3,2},{4,5},{5,4},{6,7},{7,6},{8,9},{9,8},{10,11... | collective-permute-start | bytes 1572872 | tf_op jit(solution)/shard_map/ppermute | solution.py:236
  30.5 1.6 %convolution_add_fusion.1 = f32[2,128,128]{2,1,0:T(8,128)S(1)} fusion(f32[2,128,128]{2,1,0:T(8,128)S(1)} %copy-done.10, f32[2,512,128]{2,1,0:T(8,128)} %collective-permute-done.1, f32[2,4,512,128]{3,2,1,0:T(8,128)S(1)} %bitcast.49, s32[]{:T(128)S(6)} %select_n.46), kind=kOutput, calls=%fused_computation.1 | convolution fusion | flops 100696064 | bytes 1310724 | tf_op jit(solution)/shard_map/kbr,kbq->krq/dot_general | solution.py:14
  32.2 1.9 %convolution_add_fusion.part = f32[2,128,128]{2,1,0:T(8,128)S(1)} fusion(f32[2,128,128]{2,1,0:T(8,128)S(1)} %convolution_add_fusion.1, f32[2,512,128]{2,1,0:T(8,128)} %collective-permute-done.2, f32[2,4,512,128]{3,2,1,0:T(8,128)} %bitcast.45, s32[]{:T(128)S(6)} %select_n.48), kind=kOutput, calls=%fused_computation | convolution fusion | flops 100696064 | bytes 1310724 | tf_op jit(solution)/shard_map/kbr,kbq->krq/dot_general | solution.py:14
  34.2 4.9 %collective-permute-done.4.second = f32[2,512,128]{2,1,0:T(8,128)S(1)} collective-permute-done((f32[2,512,128]{2,1,0:T(8,128)S(1)}, f32[2,512,128]{2,1,0:T(8,128)S(1)}, u32[]{:S(2)}, u32[]{:S(2)}) %collective-permute-start.4) | collective-permute-done | bytes 524320 | tf_op jit(solution)/shard_map/ppermute | solution.py:236
  42.1 1.5 %collective-permute-start.18 = (f32[4,256,128]{2,1,0:T(8,128)}, f32[4,256,128]{2,1,0:T(8,128)}, u32[]{:S(2)}, u32[]{:S(2)}) collective-permute-start(f32[4,256,128]{2,1,0:T(8,128)} %pad_maximum_fusion.own), channel_id=1, source_target_pairs={{1,2},{2,1},{5,6},{6,5},{9,10},{10,9},{13,14},{14,13},{17,18},{18,... | collective-permute-start | bytes 1572872 | tf_op jit(solution)/shard_map/ppermute | solution.py:236
  43.6 6.8 %collective-permute-done.17.near = f32[4,256,128]{2,1,0:T(8,128)} collective-permute-done((f32[4,256,128]{2,1,0:T(8,128)}, f32[4,256,128]{2,1,0:T(8,128)}, u32[]{:S(2)}, u32[]{:S(2)}) %collective-permute-start.17) | collective-permute-done | bytes 524320 | tf_op jit(solution)/shard_map/ppermute | solution.py:236
  50.4 1.5 %collective-permute-start.19 = (f32[4,256,128]{2,1,0:T(8,128)}, f32[4,256,128]{2,1,0:T(8,128)}, u32[]{:S(2)}, u32[]{:S(2)}) collective-permute-start(f32[4,256,128]{2,1,0:T(8,128)} %collective-permute-done.17.near), channel_id=1, source_target_pairs={{1,2},{2,1},{5,6},{6,5},{9,10},{10,9},{13,14},{14,13},{17,18},{18,... | collective-permute-start | bytes 1572872 | tf_op jit(solution)/shard_map/ppermute | solution.py:236
  52.0 2.0 %collective-permute-done.7.lent = f32[4,128,128]{2,1,0:T(8,128)} collective-permute-done((f32[4,128,128]{2,1,0:T(8,128)}, f32[4,128,128]{2,1,0:T(8,128)}, u32[]{:S(2)}, u32[]{:S(2)}) %collective-permute-start.7) | collective-permute-done | bytes 262176 | tf_op jit(solution)/shard_map/ppermute | solution.py:236
  57.0 1.5 %collective-permute-done.8.both_other = f32[4,128,128]{2,1,0:T(8,128)S(1)} collective-permute-done((f32[4,128,128]{2,1,0:T(8,128)S(1)}, f32[4,128,128]{2,1,0:T(8,128)S(1)}, u32[]{:S(2)}, u32[]{:S(2)}) %collective-permute-start.8) | collective-permute-done | bytes 262176 | tf_op jit(solution)/shard_map/ppermute | solution.py:24
  58.5 1.5 %shard_map.79 = (f32[256,128]{1,0:T(8,128)S(1)}, f32[256,128]{1,0:T(8,128)S(1)}, f32[256,128]{1,0:T(8,128)S(1)}, f32[256,128]{1,0:T(8,128)S(1)}) custom-call(f32[2,1,2048,128]{3,2,1,0:T(8,128)S(1)} %copy-done.1, f32[2,4,256,128]{3,2,1,0:T(8,128)S(1)} %collective-permute-done.left_other, f32[4,128,128]{2,1,0:T(8,128)S(1)} %shard_map.78.both, ...), custom_call_target="tpu_custom_call" | custom-call | bytes 1048576 | tf_op jit(solution)/shard_map/pallas_call | solution.py:78
  60.0 1.6 %collective-permute-start.10 = (f32[256,128]{1,0:T(8,128)S(1)}, f32[256,128]{1,0:T(8,128)S(1)}, u32[]{:S(2)}, u32[]{:S(2)}) collective-permute-start(f32[256,128]{1,0:T(8,128)S(1)} %get-tuple-element.20), channel_id=1, source_target_pairs={{0,16},{4,20},{8,24},{12,28},{16,0},{20,4},{24,8},{28,12},{1,17},{... | collective-permute-start | bytes 393224 | tf_op jit(solution)/shard_map/ppermute | solution.py:24
  61.6 1.4 %collective-permute-start.11 = (f32[256,128]{1,0:T(8,128)S(1)}, f32[256,128]{1,0:T(8,128)S(1)}, u32[]{:S(2)}, u32[]{:S(2)}) collective-permute-start(f32[256,128]{1,0:T(8,128)S(1)} %get-tuple-element.21), channel_id=1, source_target_pairs={{0,24},{4,28},{8,16},{12,20},{16,8},{20,12},{24,0},{28,4},{1,25},{... | collective-permute-start | bytes 393224 | tf_op jit(solution)/shard_map/ppermute | solution.py:24
  64.8 1.3 %collective-permute-start.21 = (f32[4,256,128]{2,1,0:T(8,128)}, f32[4,256,128]{2,1,0:T(8,128)S(1)}, u32[]{:S(2)}, u32[]{:S(2)}) collective-permute-start(f32[4,256,128]{2,1,0:T(8,128)} %collective-permute-done.19.inner_far), channel_id=1, source_target_pairs={{1,0},{2,3},{5,4},{6,7},{9,8},{10,11},{13,12},{14,15},{17,16},{18,... | collective-permute-start | bytes 1572872 | tf_op jit(solution)/shard_map/ppermute | solution.py:236
  66.1 1.8 %collective-permute-done.10 = f32[256,128]{1,0:T(8,128)S(1)} collective-permute-done((f32[256,128]{1,0:T(8,128)S(1)}, f32[256,128]{1,0:T(8,128)S(1)}, u32[]{:S(2)}, u32[]{:S(2)}) %collective-permute-start.10) | collective-permute-done | bytes 131104 | tf_op jit(solution)/shard_map/ppermute | solution.py:24
  69.7 1.5 %collective-permute-start.12 = (f32[256,128]{1,0:T(8,128)S(1)}, f32[256,128]{1,0:T(8,128)S(1)}, u32[]{:S(2)}, u32[]{:S(2)}) collective-permute-start(f32[256,128]{1,0:T(8,128)S(1)} %add_add_fusion.rest_0_.y_rows), channel_id=1, source_target_pairs={{0,8},{4,12},{8,0},{12,4},{16,24},{20,28},{24,16},{28,20},{1,9},{5... | collective-permute-start | bytes 393224 | tf_op jit(solution)/shard_map/ppermute | solution.py:24
  71.2 1.5 %collective-permute-start.13 = (f32[256,128]{1,0:T(8,128)S(1)}, f32[256,128]{1,0:T(8,128)S(1)}, u32[]{:S(2)}, u32[]{:S(2)}) collective-permute-start(f32[256,128]{1,0:T(8,128)S(1)} %add_add_fusion.rest_0_.y_rows), channel_id=1, source_target_pairs={{0,16},{4,20},{8,24},{12,28},{16,0},{20,4},{24,8},{28,12},{1,17},{... | collective-permute-start | bytes 393224 | tf_op jit(solution)/shard_map/ppermute | solution.py:24
  73.2 2.5 %collective-permute-done.12.rest_1_ = f32[256,128]{1,0:T(8,128)S(1)} collective-permute-done((f32[256,128]{1,0:T(8,128)S(1)}, f32[256,128]{1,0:T(8,128)S(1)}, u32[]{:S(2)}, u32[]{:S(2)}) %collective-permute-start.12) | collective-permute-done | bytes 131104 | tf_op jit(solution)/shard_map/ppermute | solution.py:24
  75.8 3.2 %collective-permute-done.13.rest_2_ = f32[256,128]{1,0:T(8,128)S(1)} collective-permute-done((f32[256,128]{1,0:T(8,128)S(1)}, f32[256,128]{1,0:T(8,128)S(1)}, u32[]{:S(2)}, u32[]{:S(2)}) %collective-permute-start.13) | collective-permute-done | bytes 131104 | tf_op jit(solution)/shard_map/ppermute | solution.py:24
  78.9 1.7 %shard_map.80.sent = f32[5,128,128]{2,1,0:T(8,128)S(1)} custom-call(f32[2,1,2048,128]{3,2,1,0:T(8,128)S(1)} %copy-done.1, f32[2,4,256,128]{3,2,1,0:T(8,128)S(1)} %collective-permute-done.left_other, f32[256,128]{1,0:T(8,128)S(1)} %add_add_fusion.rest_0_.y_rows, f32[256,128]{1,0:T(8,128)S(1)} %collective-permute-done.12.rest_1_, ...), custom_call_target="tpu_custom_call" | custom-call | bytes 1048576 | tf_op jit(solution)/shard_map/pallas_call | solution.py:78
  80.8 9.3 %collective-permute-done.21.last = f32[4,256,128]{2,1,0:T(8,128)S(1)} collective-permute-done((f32[4,256,128]{2,1,0:T(8,128)}, f32[4,256,128]{2,1,0:T(8,128)S(1)}, u32[]{:S(2)}, u32[]{:S(2)}) %collective-permute-start.21) | collective-permute-done | bytes 524320 | tf_op jit(solution)/shard_map/ppermute | solution.py:236
  90.0 2.4 %shard_map.81 = (f32[256,128]{1,0:T(8,128)S(1)}, f32[256,128]{1,0:T(8,128)S(1)}, f32[256,128]{1,0:T(8,128)S(1)}, f32[256,128]{1,0:T(8,128)S(1)}, f32[128,128]{1,0:T(8,128)S(1)}) custom-call(f32[5,128,128]{2,1,0:T(8,128)S(1)} %shard_map.80.sent, f32[5,128,128]{2,1,0:T(8,128)S(1)} %collective-permute-done.15.got, f32[4,128,128]{2,1,0:T(8,128)S(1)} %shard_map.78.both, ...), custom_call_target="tpu_custom_call" | custom-call | bytes 1048576 | tf_op jit(solution)/shard_map/pallas_call | solution.py:78
  92.4 1.6 %collective-permute-start.22 = (f32[256,128]{1,0:T(8,128)S(1)}, f32[256,128]{1,0:T(8,128)S(1)}, u32[]{:S(2)}, u32[]{:S(2)}) collective-permute-start(f32[256,128]{1,0:T(8,128)S(1)} %get-tuple-element.26), channel_id=1, source_target_pairs={{0,8},{4,12},{8,0},{12,4},{16,24},{20,28},{24,16},{28,20},{1,9},{5... | collective-permute-start | bytes 393224 | tf_op jit(solution)/shard_map/ppermute | solution.py:24
  96.0 13.0 %shard_map.82 = (f32[256,128]{1,0:T(8,128)}, f32[128,128]{1,0:T(8,128)S(1)}) custom-call(f32[128,128]{1,0:T(8,128)S(1)} %get-tuple-element.23.gram, f32[256,128]{1,0:T(8,128)S(1)} %add_add_fusion.rest_0_.y_rows), custom_call_target="tpu_custom_call" | custom-call | flops 1000000000 | bytes 1048576 | tf_op jit(solution)/shard_map/pallas_call | solution.py:78
  (62 shorter events, 17.5 us)
Async XLA Ops:
  0.6 14.6 %copy-start.7 = (f32[2,1,2048,128]{3,2,1,0:T(8,128)S(1)}, f32[2,1,2048,128]{3,2,1,0:T(8,128)}, u32[]{:S(2)}) copy-start(f32[2,1,2048,128]{3,2,1,0:T(8,128)} %param.7) | copy-start | bytes 6291460
  0.7 25.6 %collective-permute-start.1 = (f32[2,512,128]{2,1,0:T(8,128)}, f32[2,512,128]{2,1,0:T(8,128)}, u32[]{:S(2)}, u32[]{:S(2)}) collective-permute-start(f32[2,512,128]{2,1,0:T(8,128)} %param.9), channel_id=1, source_target_pairs={{0,1},{1,0},{2,3},{3,2},{4,5},{5,4},{6,7},{7,6},{8,9},{9,8},{10,11... | collective-permute-start | bytes 1572872 | tf_op jit(solution)/shard_map/ppermute | solution.py:236
  3.7 16.7 %collective-permute-start.2 = (f32[2,512,128]{2,1,0:T(8,128)}, f32[2,512,128]{2,1,0:T(8,128)}, u32[]{:S(2)}, u32[]{:S(2)}) collective-permute-start(f32[2,512,128]{2,1,0:T(8,128)} %param.9), channel_id=1, source_target_pairs={{1,2},{2,1},{5,6},{6,5},{9,10},{10,9},{13,14},{14,13},{17,18},{18,... | collective-permute-start | bytes 1572872 | tf_op jit(solution)/shard_map/ppermute | solution.py:236
  6.8 10.7 %copy-start.9 = (f32[2,128,128]{2,1,0:T(8,128)}, f32[2,128,128]{2,1,0:T(8,128)S(1)}, u32[]{:S(2)}) copy-start(f32[2,128,128]{2,1,0:T(8,128)S(1)} %fusion.7) | copy-start | bytes 393220
  6.9 11.9 %collective-permute-start.5 = (f32[2,128,128]{2,1,0:T(8,128)S(1)}, f32[2,128,128]{2,1,0:T(8,128)}, u32[]{:S(2)}, u32[]{:S(2)}) collective-permute-start(f32[2,128,128]{2,1,0:T(8,128)S(1)} %fusion.7), channel_id=1, source_target_pairs={{0,1},{1,0},{2,3},{3,2},{4,5},{5,4},{6,7},{7,6},{8,9},{9,8},{10,11... | collective-permute-start | bytes 393224 | tf_op jit(solution)/shard_map/ppermute | solution.py:236
  12.8 44.2 %collective-permute-start = (f32[2,4,256,128]{3,2,1,0:T(8,128)}, f32[2,4,256,128]{3,2,1,0:T(8,128)S(1)}, u32[]{:S(2)}, u32[]{:S(2)}) collective-permute-start(f32[2,4,256,128]{3,2,1,0:T(8,128)} %dynamic-slice_bitcast_fusion), channel_id=1, source_target_pairs={{0,4},{4,0},{8,12},{12,8},{16,20},{20,16},{24,28},{28,24},{1,5},{5... | collective-permute-start | bytes 3145736 | tf_op jit(solution)/shard_map/ppermute | solution.py:24
  14.7 12.2 %collective-permute-start.16 = (f32[2,256,128]{2,1,0:T(8,128)}, f32[2,256,128]{2,1,0:T(8,128)}, u32[]{:S(2)}, u32[]{:S(2)}) collective-permute-start(f32[2,256,128]{2,1,0:T(8,128)} %get-tuple-element.31), channel_id=1, source_target_pairs={{0,4},{4,0},{8,12},{12,8},{16,20},{20,16},{24,28},{28,24},{1,5},{5... | collective-permute-start | bytes 786440 | tf_op jit(solution)/shard_map/ppermute | solution.py:24
  18.3 8.6 %copy-start.8 = (f32[2,256,128]{2,1,0:T(8,128)S(1)}, f32[2,256,128]{2,1,0:T(8,128)}, u32[]{:S(2)}) copy-start(f32[2,256,128]{2,1,0:T(8,128)} %get-tuple-element.30) | copy-start | bytes 786436
  18.3 12.2 %copy-start.10 = (f32[2,128,128]{2,1,0:T(8,128)S(1)}, f32[2,128,128]{2,1,0:T(8,128)}, u32[]{:S(2)}) copy-start(f32[2,128,128]{2,1,0:T(8,128)} %fusion.2) | copy-start | bytes 393220
  19.8 19.6 %collective-permute-start.6 = (f32[2,128,128]{2,1,0:T(8,128)S(1)}, f32[2,128,128]{2,1,0:T(8,128)S(1)}, u32[]{:S(2)}, u32[]{:S(2)}) collective-permute-start(f32[2,128,128]{2,1,0:T(8,128)S(1)} %add.58.probe_here), channel_id=1, source_target_pairs={{1,2},{2,1},{5,6},{6,5},{9,10},{10,9},{13,14},{14,13},{17,18},{18,... | collective-permute-start | bytes 393224 | tf_op jit(solution)/shard_map/ppermute | solution.py:236
  20.5 18.5 %copy-start.2 = (f32[2,512,128]{2,1,0:T(8,128)S(1)}, f32[2,512,128]{2,1,0:T(8,128)}, u32[]{:S(2)}) copy-start(f32[2,512,128]{2,1,0:T(8,128)} %dynamic-slice_bitcast_fusion.1.own_rows) | copy-start | bytes 1572868
  20.6 18.5 %collective-permute-start.4 = (f32[2,512,128]{2,1,0:T(8,128)S(1)}, f32[2,512,128]{2,1,0:T(8,128)S(1)}, u32[]{:S(2)}, u32[]{:S(2)}) collective-permute-start(f32[2,512,128]{2,1,0:T(8,128)S(1)} %bitcast_select_fusion), channel_id=1, source_target_pairs={{0,1},{1,0},{2,3},{3,2},{4,5},{5,4},{6,7},{7,6},{8,9},{9,8},{10,11... | collective-permute-start | bytes 1572872 | tf_op jit(solution)/shard_map/ppermute | solution.py:236
  26.2 12.8 %collective-permute-start.3 = (f32[2,512,128]{2,1,0:T(8,128)}, f32[2,512,128]{2,1,0:T(8,128)S(1)}, u32[]{:S(2)}, u32[]{:S(2)}) collective-permute-start(f32[2,512,128]{2,1,0:T(8,128)} %collective-permute-done.1), channel_id=1, source_target_pairs={{1,2},{2,1},{5,6},{6,5},{9,10},{10,9},{13,14},{14,13},{17,18},{18,... | collective-permute-start | bytes 1572872 | tf_op jit(solution)/shard_map/ppermute | solution.py:236
  28.7 21.7 %collective-permute-start.17 = (f32[4,256,128]{2,1,0:T(8,128)}, f32[4,256,128]{2,1,0:T(8,128)}, u32[]{:S(2)}, u32[]{:S(2)}) collective-permute-start(f32[4,256,128]{2,1,0:T(8,128)} %pad_maximum_fusion.own), channel_id=1, source_target_pairs={{0,1},{1,0},{2,3},{3,2},{4,5},{5,4},{6,7},{7,6},{8,9},{9,8},{10,11... | collective-permute-start | bytes 1572872 | tf_op jit(solution)/shard_map/ppermute | solution.py:236
  32.2 19.7 %copy-start.11 = (s32[2,1]{0,1:T(1,128)S(1)}, s32[2,1]{0,1:T(1,128)}, u32[]{:S(2)}) copy-start(s32[2,1]{0,1:T(1,128)} %param.11) | copy-start | bytes 28
  32.2 26.3 %copy-start.1 = (f32[2,1,2048,128]{3,2,1,0:T(8,128)S(1)}, f32[2,1,2048,128]{3,2,1,0:T(8,128)}, u32[]{:S(2)}) copy-start(f32[2,1,2048,128]{3,2,1,0:T(8,128)} %left.3) | copy-start | bytes 6291460
  40.8 13.1 %collective-permute-start.7 = (f32[4,128,128]{2,1,0:T(8,128)}, f32[4,128,128]{2,1,0:T(8,128)}, u32[]{:S(2)}, u32[]{:S(2)}) collective-permute-start(f32[4,128,128]{2,1,0:T(8,128)} %pad_maximum_fusion.1), channel_id=1, source_target_pairs={{1,0},{2,3},{5,4},{6,7},{9,8},{10,11},{13,12},{14,15},{17,16},{18,... | collective-permute-start | bytes 786440 | tf_op jit(solution)/shard_map/ppermute | solution.py:236
  42.1 21.4 %collective-permute-start.18 = (f32[4,256,128]{2,1,0:T(8,128)}, f32[4,256,128]{2,1,0:T(8,128)}, u32[]{:S(2)}, u32[]{:S(2)}) collective-permute-start(f32[4,256,128]{2,1,0:T(8,128)} %pad_maximum_fusion.own), channel_id=1, source_target_pairs={{1,2},{2,1},{5,6},{6,5},{9,10},{10,9},{13,14},{14,13},{17,18},{18,... | collective-permute-start | bytes 1572872 | tf_op jit(solution)/shard_map/ppermute | solution.py:236
  50.4 14.4 %collective-permute-start.19 = (f32[4,256,128]{2,1,0:T(8,128)}, f32[4,256,128]{2,1,0:T(8,128)}, u32[]{:S(2)}, u32[]{:S(2)}) collective-permute-start(f32[4,256,128]{2,1,0:T(8,128)} %collective-permute-done.17.near), channel_id=1, source_target_pairs={{1,2},{2,1},{5,6},{6,5},{9,10},{10,9},{13,14},{14,13},{17,18},{18,... | collective-permute-start | bytes 1572872 | tf_op jit(solution)/shard_map/ppermute | solution.py:236
  56.9 1.6 %collective-permute-start.8 = (f32[4,128,128]{2,1,0:T(8,128)S(1)}, f32[4,128,128]{2,1,0:T(8,128)S(1)}, u32[]{:S(2)}, u32[]{:S(2)}) collective-permute-start(f32[4,128,128]{2,1,0:T(8,128)S(1)} %shard_map.78.both), channel_id=1, source_target_pairs={{0,4},{4,0},{8,12},{12,8},{16,20},{20,16},{24,28},{28,24},{1,5},{5... | collective-permute-start | bytes 786440 | tf_op jit(solution)/shard_map/ppermute | solution.py:24
  60.0 8.0 %collective-permute-start.10 = (f32[256,128]{1,0:T(8,128)S(1)}, f32[256,128]{1,0:T(8,128)S(1)}, u32[]{:S(2)}, u32[]{:S(2)}) collective-permute-start(f32[256,128]{1,0:T(8,128)S(1)} %get-tuple-element.20), channel_id=1, source_target_pairs={{0,16},{4,20},{8,24},{12,28},{16,0},{20,4},{24,8},{28,12},{1,17},{... | collective-permute-start | bytes 393224 | tf_op jit(solution)/shard_map/ppermute | solution.py:24
  61.6 7.3 %collective-permute-start.11 = (f32[256,128]{1,0:T(8,128)S(1)}, f32[256,128]{1,0:T(8,128)S(1)}, u32[]{:S(2)}, u32[]{:S(2)}) collective-permute-start(f32[256,128]{1,0:T(8,128)S(1)} %get-tuple-element.21), channel_id=1, source_target_pairs={{0,24},{4,28},{8,16},{12,20},{16,8},{20,12},{24,0},{28,4},{1,25},{... | collective-permute-start | bytes 393224 | tf_op jit(solution)/shard_map/ppermute | solution.py:24
  63.0 6.6 %collective-permute-start.9 = (f32[256,128]{1,0:T(8,128)S(1)}, f32[256,128]{1,0:T(8,128)S(1)}, u32[]{:S(2)}, u32[]{:S(2)}) collective-permute-start(f32[256,128]{1,0:T(8,128)S(1)} %get-tuple-element.19), channel_id=1, source_target_pairs={{0,8},{4,12},{8,0},{12,4},{16,24},{20,28},{24,16},{28,20},{1,9},{5... | collective-permute-start | bytes 393224 | tf_op jit(solution)/shard_map/ppermute | solution.py:24
  63.5 17.2 %collective-permute-start.20 = (f32[4,256,128]{2,1,0:T(8,128)}, f32[4,256,128]{2,1,0:T(8,128)S(1)}, u32[]{:S(2)}, u32[]{:S(2)}) collective-permute-start(f32[4,256,128]{2,1,0:T(8,128)} %collective-permute-done.18.inner), channel_id=1, source_target_pairs={{1,0},{2,3},{5,4},{6,7},{9,8},{10,11},{13,12},{14,15},{17,16},{18,... | collective-permute-start | bytes 1572872 | tf_op jit(solution)/shard_map/ppermute | solution.py:236
  64.8 25.2 %collective-permute-start.21 = (f32[4,256,128]{2,1,0:T(8,128)}, f32[4,256,128]{2,1,0:T(8,128)S(1)}, u32[]{:S(2)}, u32[]{:S(2)}) collective-permute-start(f32[4,256,128]{2,1,0:T(8,128)} %collective-permute-done.19.inner_far), channel_id=1, source_target_pairs={{1,0},{2,3},{5,4},{6,7},{9,8},{10,11},{13,12},{14,15},{17,16},{18,... | collective-permute-start | bytes 1572872 | tf_op jit(solution)/shard_map/ppermute | solution.py:236
  69.7 6.1 %collective-permute-start.12 = (f32[256,128]{1,0:T(8,128)S(1)}, f32[256,128]{1,0:T(8,128)S(1)}, u32[]{:S(2)}, u32[]{:S(2)}) collective-permute-start(f32[256,128]{1,0:T(8,128)S(1)} %add_add_fusion.rest_0_.y_rows), channel_id=1, source_target_pairs={{0,8},{4,12},{8,0},{12,4},{16,24},{20,28},{24,16},{28,20},{1,9},{5... | collective-permute-start | bytes 393224 | tf_op jit(solution)/shard_map/ppermute | solution.py:24
  71.2 7.7 %collective-permute-start.13 = (f32[256,128]{1,0:T(8,128)S(1)}, f32[256,128]{1,0:T(8,128)S(1)}, u32[]{:S(2)}, u32[]{:S(2)}) collective-permute-start(f32[256,128]{1,0:T(8,128)S(1)} %add_add_fusion.rest_0_.y_rows), channel_id=1, source_target_pairs={{0,16},{4,20},{8,24},{12,28},{16,0},{20,4},{24,8},{28,12},{1,17},{... | collective-permute-start | bytes 393224 | tf_op jit(solution)/shard_map/ppermute | solution.py:24
  72.7 6.2 %collective-permute-start.14 = (f32[256,128]{1,0:T(8,128)S(1)}, f32[256,128]{1,0:T(8,128)S(1)}, u32[]{:S(2)}, u32[]{:S(2)}) collective-permute-start(f32[256,128]{1,0:T(8,128)S(1)} %add_add_fusion.rest_0_.y_rows), channel_id=1, source_target_pairs={{0,24},{4,28},{8,16},{12,20},{16,8},{20,12},{24,0},{28,4},{1,25},{... | collective-permute-start | bytes 393224 | tf_op jit(solution)/shard_map/ppermute | solution.py:24
  80.7 9.3 %collective-permute-start.15 = (f32[5,128,128]{2,1,0:T(8,128)S(1)}, f32[5,128,128]{2,1,0:T(8,128)S(1)}, u32[]{:S(2)}, u32[]{:S(2)}) collective-permute-start(f32[5,128,128]{2,1,0:T(8,128)S(1)} %shard_map.80.sent), channel_id=1, source_target_pairs={{0,4},{4,0},{8,12},{12,8},{16,20},{20,16},{24,28},{28,24},{1,5},{5... | collective-permute-start | bytes 983048 | tf_op jit(solution)/shard_map/ppermute | solution.py:24
  92.4 16.6 %collective-permute-start.22 = (f32[256,128]{1,0:T(8,128)S(1)}, f32[256,128]{1,0:T(8,128)S(1)}, u32[]{:S(2)}, u32[]{:S(2)}) collective-permute-start(f32[256,128]{1,0:T(8,128)S(1)} %get-tuple-element.26), channel_id=1, source_target_pairs={{0,8},{4,12},{8,0},{12,4},{16,24},{20,28},{24,16},{28,20},{1,9},{5... | collective-permute-start | bytes 393224 | tf_op jit(solution)/shard_map/ppermute | solution.py:24
  94.0 15.0 %collective-permute-start.23 = (f32[256,128]{1,0:T(8,128)S(1)}, f32[256,128]{1,0:T(8,128)S(1)}, u32[]{:S(2)}, u32[]{:S(2)}) collective-permute-start(f32[256,128]{1,0:T(8,128)S(1)} %get-tuple-element.27), channel_id=1, source_target_pairs={{0,16},{4,20},{8,24},{12,28},{16,0},{20,4},{24,8},{28,12},{1,17},{... | collective-permute-start | bytes 393224 | tf_op jit(solution)/shard_map/ppermute | solution.py:24
  95.0 14.0 %collective-permute-start.24 = (f32[256,128]{1,0:T(8,128)S(1)}, f32[256,128]{1,0:T(8,128)S(1)}, u32[]{:S(2)}, u32[]{:S(2)}) collective-permute-start(f32[256,128]{1,0:T(8,128)S(1)} %get-tuple-element.28), channel_id=1, source_target_pairs={{0,24},{4,28},{8,16},{12,20},{16,8},{20,12},{24,0},{28,4},{1,25},{... | collective-permute-start | bytes 393224 | tf_op jit(solution)/shard_map/ppermute | solution.py:24
  (5 other events, 7.8 us)

commit v3 on v2

--- a/solution.py
+++ b/solution.py
@@ -86,28 +86,40 @@
     )(*args)
 
 
-def core_kernel(planes, part, own_rows, first, second, core, lent):
+def load(sources, places, sems):
+    copies = [pltpu.make_async_copy(source, place, sems.at[i]) for i, (source, place) in enumerate(zip(sources, places))]
+    for copy in copies:
+        copy.start()
+    for copy in copies:
+        copy.wait()
+
+
+def core_kernel(planes, part, own_rows, first_hbm, second_hbm, probe_a, probe_b, core, sent, first, second, probe_in, sems):
     plane = lax.axis_index("tile")
     is_end = jnp.logical_or(plane == 0, plane == planes - 1)
+    sources = [first_hbm, second_hbm, probe_a, probe_b]
+    load(sources, [first, second, probe_in.at[0], probe_in.at[1]], sems)
+    sent[pl.ds(2, 2)] = probe_in[0] + probe_in[1]
 
     @pl.when(is_end)
     def _():
         for k in range(2):
             core[k] = part[k] + dot3(own_rows[k], second[k], TN)
-            lent[k] = jnp.zeros_like(lent[k])
+            sent[k] = jnp.zeros_like(sent[k])
 
     @pl.when(jnp.logical_not(is_end))
     def _():
         for k in range(2):
             core[k] = part[k] + dot3(own_rows[k], first[k], TN)
-            lent[k] = dot3(second[k], first[k], TN)
-
-
-def reduced_kernel(core, lent, probe_here, probe_far, pattern, both):
+            sent[k] = dot3(second[k], first[k], TN)
+
+
+def reduced_kernel(core, sent, got_hbm, probe_a, probe_b, pattern, both, got, probe_in, sems):
+    load([got_hbm, probe_a, probe_b], [got, probe_in.at[0], probe_in.at[1]], sems)
     for k in range(2):
-        weight = pattern[k, 0].astype(jnp.float32)
-        c = (core[k] + lent[k]) * weight
-        both[k] = dot3(c, probe_here[k] + probe_far[k] + lent[2 + k], NN)
+        c = (core[k] + got[k]) * pattern[k, 0].astype(jnp.float32)
+        probe = (probe_in[0, k] + probe_in[1, k]) + (sent[2 + k] + got[2 + k])
+        both[k] = dot3(c, probe, NN)
         both[2 + k] = c
 
 
@@ -159,7 +171,7 @@
 
 
 def w_kernel(planes, sent, got, both, both_other, own, near, inner, inner_far, outer, last, *rest):
-    *outs, gram, held, sems = rest
+    *outs, held, sems = rest
     plane = lax.axis_index("tile")
     chip = lax.axis_index("step") // 2
     is_end = jnp.logical_or(plane == 0, plane == planes - 1)
@@ -178,7 +190,6 @@
         pick(i, jnp.logical_and(apart == 2, jnp.logical_not(is_end)), inner_far)
         pick(i, jnp.logical_and(apart == 3, is_end), last)
         pick(i, jnp.logical_and(apart == 3, jnp.logical_not(is_end)), inner)
-    gram[...] = sent[4] + got[4]
     returned = []
     for k in range(2):
         returned.append(dot3(sent[2 + k] + got[k], both[2 + k], NN))
@@ -190,9 +201,9 @@
         out[...] = dot3(jnp.concatenate([held[i, k] for k in range(4)], 1), returned, NT)
 
 
-def basis_kernel(tile_rows, width, gram, y_rows, basis, inverse):
-    rank = gram.shape[0]
-    scaled = gram[...] * (1.0 / tile_rows)
+def basis_kernel(tile_rows, width, sent, got, y_rows, basis, inverse):
+    rank = inverse.shape[0]
+    scaled = (sent[4] + got[4]) * (1.0 / tile_rows)
     eye = (lax.broadcasted_iota(jnp.int32, (rank, rank), 0) == lax.broadcasted_iota(jnp.int32, (rank, rank), 1))
     work = jnp.concatenate([scaled, eye.astype(jnp.float32)], 1)
     done = []
@@ -238,55 +249,71 @@
     near = across(column_right, outer_pairs)
     inner = across(column_right, inner_pairs)
     probes = mm("kbq,bp->kqp", column_left, sketch)
-    probes = probes + across(probes, outer_pairs)
+    probes_near = across(probes, outer_pairs)
+    probes_inner = across(probes, inner_pairs)
     right_blocks = target_right.reshape(2, planes, -1, rank)
 
     def block(index):
         return take(right_blocks, index, 1)
 
+    left_split = target_left.reshape(2, chips, 2, row_count, rank)
+    left_other = exchange(take(left_split, 1 - core_bit, 2), "step", 1)
+    col_split = column_left.reshape(2, 2, row_count, rank)
+    col_half = jnp.concatenate([take(col_split, core_bit, 1), exchange(take(col_split, 1 - core_bit, 1), "step", 1)])
+
+    lent_rows = block(planes - 1 - plane)
     inner_far = across(near, inner_pairs)
-    outer = across(jnp.where(is_end, block(planes - 1 - plane), inner), outer_pairs)
-    probes_far = across(probes, inner_pairs)
+    outer = across(jnp.where(is_end, lent_rows, inner), outer_pairs)
     part = (
         mm("kbr,kbq->krq", block(plane), column_right)
         + mm("kbr,kbq->krq", block(plane ^ 1), near)
         + mm("kbr,kbq->krq", block(jnp.where(is_end, plane, planes - 1 - plane)), inner)
     )
+    part, probes_near, col_half = lax.optimization_barrier((part, probes_near, col_half))
+    probes_far = across(probes_near, inner_pairs)
+    col_inner = across(col_half, inner_pairs)
     far_rows = block(plane ^ 2)
-    core, lent = call(functools.partial(core_kernel, planes), [(2, rank, rank)] * 2, [part, far_rows, inner_far, outer])
-    lent = across(jnp.concatenate([lent, probes_far]), outward)
-
-    left_split = target_left.reshape(2, chips, 2, row_count, rank)
-    left_other = exchange(take(left_split, 1 - core_bit, 2), "step", 1)
-    col_split = column_left.reshape(2, 2, row_count, rank)
-    col_half = jnp.concatenate([take(col_split, core_bit, 1), exchange(take(col_split, 1 - core_bit, 1), "step", 1)])
-    col_half, _ = lax.optimization_barrier((col_half, near))
+    rows_per_plane = column_right.shape[1]
+    core, lent = call(
+        functools.partial(core_kernel, planes),
+        [(2, rank, rank), (4, rank, rank)],
+        [part, far_rows, inner_far, outer, probes_inner, probes_far],
+        "vvaaaa",
+        [pltpu.VMEM((2, rows_per_plane, rank), jnp.float32)] * 2
+        + [pltpu.VMEM((2, 2, rank, rank), jnp.float32), pltpu.SemaphoreType.DMA((4,))],
+    )
+    lent_got = across(lent, outward)
+    col_half, _ = lax.optimization_barrier((col_half, lent))
     col_near = across(col_half, outer_pairs)
-    col_inner = across(col_half, inner_pairs)
-    col_inner_far = across(col_near, inner_pairs)
-    col_outer = across(col_inner, outward)
-    col_last = across(col_inner_far, outward)
-
-    (both,) = call(reduced_kernel, [(4, rank, rank)], [core, lent, probes, probes_far, pattern], "vvvvs")
+
+    reduced_scratch = [pltpu.VMEM((4, rank, rank), jnp.float32), pltpu.VMEM((2, 2, rank, rank), jnp.float32)]
+    reduced_scratch += [pltpu.SemaphoreType.DMA((3,))]
+    (both,) = call(reduced_kernel, [(4, rank, rank)], [core, lent, lent_got, probes, probes_near, pattern], "vvaaas", reduced_scratch)
     both_other = exchange(both, "step", 1)
     rows_scratch = [pltpu.VMEM((chips, 4, row_count, rank), jnp.float32), pltpu.SemaphoreType.DMA((2 * chips,))]
     y_parts = call(y_kernel, [(row_count, rank)] * chips, [target_left, left_other, both, both_other], "aavv", rows_scratch)
+    y_got = [exchange(y_parts[bit], "step", 2 * bit) for bit in range(1, chips)]
+    y_got[0], col_near_held, col_inner_held = lax.optimization_barrier((y_got[0], col_near, col_inner))
+    col_inner_far = across(col_near_held, inner_pairs)
+    col_outer = across(col_inner_held, outward)
     y_rows = y_parts[0]
-    for bit in range(1, chips):
-        y_rows = y_rows + exchange(y_parts[bit], "step", 2 * bit)
+    for got in y_got:
+        y_rows = y_rows + got
     y_all = [y_rows] + [exchange(y_rows, "step", 2 * bit) for bit in range(1, chips)]
+    y_all[1], col_inner_far_held = lax.optimization_barrier((y_all[1], col_inner_far))
+    col_last = across(col_inner_far_held, outward)
     (sent,) = call(z_kernel, [(5, rank, rank)], [target_left, left_other, *y_all], "aa" + "v" * chips, rows_scratch)
     got = exchange(sent, "step", 1)
-    *w_parts, gram = call(
+    w_parts = call(
         functools.partial(w_kernel, planes),
-        [(row_count, rank)] * planes + [(rank, rank)],
+        [(row_count, rank)] * planes,
         [sent, got, both, both_other, col_half, col_near, col_inner, col_inner_far, col_outer, col_last],
         "vvvvaaaaaa",
         [pltpu.VMEM((planes, 4, row_count, rank), jnp.float32), pltpu.SemaphoreType.DMA((planes,))],
     )
     w_got = [exchange(w_parts[bit], "step", 2 * bit) for bit in range(1, chips)]
     basis, inverse = call(
-        functools.partial(basis_kernel, tile_rows, 32), [(row_count, rank), (rank, rank)], [gram, y_rows], cost=10**9
+        functools.partial(basis_kernel, tile_rows, 32), [(row_count, rank), (rank, rank)], [sent, got, y_rows], cost=10**9
     )
     (factor,) = call(functools.partial(factor_kernel, tile_rows), [(row_count, rank)], [w_parts[0], *w_got, inverse])
     return basis[None], factor[None]

time: 111 us -> 121 us (1.090)
  starting transfers between devices: 35.1 us -> 45 us
  Pallas kernels: 21.1 us -> 24.2 us
  waiting for transfers between devices: 34.2 us -> 32.9 us
    ppermute x12 -> x13, starting transfers between devices: 23.8 us -> 31.6 us  [across(): return lax.ppermute(array, 'tile', pairs)]
    ppermute x12 -> x13, waiting for transfers between devices: 23.4 us -> 17.4 us  [across(): return lax.ppermute(array, 'tile', pairs)]
    ppermute x13, waiting for transfers between devices: 10.7 us -> 15.5 us  [exchange(): lax.ppermute(array, axis, [(i, i ^ bit) for i in range(lax.axis_size(axis...]
    pallas_call x7, Pallas kernels: 21.1 us -> 24.2 us  [call(): pl.pallas_call(kernel, out_shape=shapes, in_specs=[pl.BlockSpec(memory_sp...]
    ppermute x13, starting transfers between devices: 11.3 us -> 13.4 us  [exchange(): lax.ppermute(array, axis, [(i, i ^ bit) for i in range(lax.axis_size(axis...]
    unnamed x25 -> x19, local copies, waits for them, and re-layouts: 2.61 us -> 2.58 us
  transfers between devices with their start and end apart: 25 -> 26, of which waited for: 11 -> 11; matrix products, arithmetic and copies ran while one was open for 15% -> 12% of each run, Pallas kernels for 16% -> 17%
where the time goes in v3:
time: 121 us; the launch traced here: 120 us
  starting transfers between devices  45 us (37%)
  waiting for transfers between devices  32.9 us (27%)
  Pallas kernels  24.2 us (20%)
  matrix products  7.85 us (6%)
  local copies, waits for them, and re-layouts  6.47 us (5%)
  other arithmetic  2.76 us (2%)
    ppermute x13, starting transfers between devices, across(): return lax.ppermute(array, 'tile', pairs)  31.6 us
    pallas_call x7, Pallas kernels, call(): pl.pallas_call(kernel, out_shape=shapes, in_specs=[pl.BlockSpec(memory_sp...  24.2 us
    ppermute x13, waiting for transfers between devices, across(): return lax.ppermute(array, 'tile', pairs)  17.4 us
    ppermute x13, waiting for transfers between devices, exchange(): lax.ppermute(array, axis, [(i, i ^ bit) for i in range(lax.axis_size(axis...  15.5 us
    ppermute x13, starting transfers between devices, exchange(): lax.ppermute(array, axis, [(i, i ^ bit) for i in range(lax.axis_size(axis...  13.4 us
    dot_general x4, matrix products, mm(): jnp.einsum(spec, *arrays, precision=HIGH, preferred_element_type=jnp.floa...  7.85 us
    squeeze x3, local copies, waits for them, and re-layouts, take(): return lax.dynamic_index_in_dim(array, index, axis, keepdims=False)  3.89 us
    unnamed x19, local copies, waits for them, and re-layouts  2.58 us
  transfers between devices with their start and end apart: 26, of which 11 were waited for; matrix products, arithmetic and copies ran while one was open for 12% of the time, Pallas kernels for 17%

profile of v3, /device:TPU:0, one launch (start us, length us, event | category | flops | bytes accessed | tf_op | source)
XLA Modules:
  0.0 120.0 jit_solution(5235011087434628771)
XLA Ops:
  0.7 3.1 %collective-permute-start.1 = (f32[2,512,128]{2,1,0:T(8,128)}, f32[2,512,128]{2,1,0:T(8,128)}, u32[]{:S(2)}, u32[]{:S(2)}) collective-permute-start(f32[2,512,128]{2,1,0:T(8,128)} %param.9), channel_id=1, source_target_pairs={{0,1},{1,0},{2,3},{3,2},{4,5},{5,4},{6,7},{7,6},{8,9},{9,8},{10,11... | collective-permute-start | bytes 1572872 | tf_op jit(solution)/shard_map/ppermute | solution.py:247
  5.2 1.6 %fusion.7.probe_a = f32[2,128,128]{2,1,0:T(8,128)S(1)} fusion(f32[2,512,128]{2,1,0:T(8,128)} %param.8, f32[512,128]{1,0:T(8,128)S(1)} %copy-done), kind=kOutput, calls=%fused_computation.13 | convolution fusion | flops 100663296 | bytes 917504 | tf_op jit(solution)/shard_map/kbq,bp->kqp/dot_general | solution.py:14
  6.9 3.7 %collective-permute-start.3 = (f32[2,128,128]{2,1,0:T(8,128)S(1)}, f32[2,128,128]{2,1,0:T(8,128)}, u32[]{:S(2)}, u32[]{:S(2)}) collective-permute-start(f32[2,128,128]{2,1,0:T(8,128)S(1)} %fusion.7.probe_a), channel_id=1, source_target_pairs={{0,1},{1,0},{2,3},{3,2},{4,5},{5,4},{6,7},{7,6},{8,9},{9,8},{10,11... | collective-permute-start | bytes 393224 | tf_op jit(solution)/shard_map/ppermute | solution.py:247
  11.8 1.8 %dynamic-slice_bitcast_fusion.3 = (f32[2,256,128]{2,1,0:T(8,128)}, f32[2,256,128]{2,1,0:T(8,128)S(1)}) fusion(f32[2,2,256,128]{3,2,1,0:T(8,128)} %bitcast.50, s32[]{:T(128)S(6)} %select_n.49, s32[]{:T(128)S(6)} %select_n.44), kind=kLoop, calls=%fused_computation.16 | loop fusion | bytes 1048584 | tf_op jit(solution)/shard_map/jit(dynamic_index_in_dim)/squeeze | solution.py:28
  13.6 2.3 %fusion.2 = f32[2,128,128]{2,1,0:T(8,128)} fusion(f32[2,512,128]{2,1,0:T(8,128)S(1)} %copy-done.7, f32[2,4,512,128]{3,2,1,0:T(8,128)} %bitcast.45, s32[]{:T(128)S(6)} %select_n.45), kind=kOutput, calls=%fused_computation.6 | convolution fusion | flops 100663296 | bytes 1179652 | tf_op jit(solution)/shard_map/kbr,kbq->krq/dot_general | solution.py:14
  17.5 1.9 %pad_maximum_fusion.own = f32[4,256,128]{2,1,0:T(8,128)} fusion(f32[2,256,128]{2,1,0:T(8,128)} %collective-permute-done.4, f32[2,256,128]{2,1,0:T(8,128)} %get-tuple-element.44), kind=kLoop, calls=%fused_computation.3 | loop fusion | flops 131072 | bytes 1048576 | tf_op jit(solution)/shard_map/concatenate | solution.py:262
  20.2 3.6 %collective-permute-start.6 = (f32[2,512,128]{2,1,0:T(8,128)}, f32[2,512,128]{2,1,0:T(8,128)}, u32[]{:S(2)}, u32[]{:S(2)}) collective-permute-start(f32[2,512,128]{2,1,0:T(8,128)} %bitcast_select_fusion), channel_id=1, source_target_pairs={{0,1},{1,0},{2,3},{3,2},{4,5},{5,4},{6,7},{7,6},{8,9},{9,8},{10,11... | collective-permute-start | bytes 1572872 | tf_op jit(solution)/shard_map/ppermute | solution.py:247
  25.3 1.6 %convolution_add_fusion.1 = f32[2,128,128]{2,1,0:T(8,128)S(1)} fusion(f32[2,128,128]{2,1,0:T(8,128)S(1)} %copy-done.6, f32[2,512,128]{2,1,0:T(8,128)} %collective-permute-done.1, f32[2,4,512,128]{3,2,1,0:T(8,128)S(1)} %bitcast.48, s32[]{:T(128)S(6)} %select_n.46), kind=kOutput, calls=%fused_computation.1 | convolution fusion | flops 100696064 | bytes 1310724 | tf_op jit(solution)/shard_map/kbr,kbq->krq/dot_general | solution.py:14
  26.9 2.3 %convolution_add_fusion.part = f32[2,128,128]{2,1,0:T(8,128)} fusion(f32[2,128,128]{2,1,0:T(8,128)S(1)} %convolution_add_fusion.1, f32[2,512,128]{2,1,0:T(8,128)} %collective-permute-done.2, f32[2,4,512,128]{3,2,1,0:T(8,128)S(1)} %bitcast.49, s32[]{:T(128)S(6)} %select_n.48), kind=kOutput, calls=%fused_computation | convolution fusion | flops 100696064 | bytes 1310724 | tf_op jit(solution)/shard_map/kbr,kbq->krq/dot_general | solution.py:14
  31.6 2.8 %collective-permute-done.6.second_hbm = f32[2,512,128]{2,1,0:T(8,128)} collective-permute-done((f32[2,512,128]{2,1,0:T(8,128)}, f32[2,512,128]{2,1,0:T(8,128)}, u32[]{:S(2)}, u32[]{:S(2)}) %collective-permute-start.6) | collective-permute-done | bytes 524320 | tf_op jit(solution)/shard_map/ppermute | solution.py:247
  35.3 2.4 %shard_map.77 = (f32[2,128,128]{2,1,0:T(8,128)S(1)}, f32[4,128,128]{2,1,0:T(8,128)}) custom-call(f32[2,128,128]{2,1,0:T(8,128)S(1)} %copy-done.2, f32[2,512,128]{2,1,0:T(8,128)S(1)} %dynamic-slice_bitcast_fusion.1.own_rows, f32[2,512,128]{2,1,0:T(8,128)} %collective-permute-done.5.first_hbm, f32[2,512,128]{2,1,0:T(8,128)} %collective-permute-done.6.second_hbm, ...), custom_call_target="tpu_custom_call" | custom-call | bytes 1048576 | tf_op jit(solution)/shard_map/pallas_call | solution.py:78
  39.6 1.5 %collective-permute-start.13 = (f32[4,256,128]{2,1,0:T(8,128)}, f32[4,256,128]{2,1,0:T(8,128)}, u32[]{:S(2)}, u32[]{:S(2)}) collective-permute-start(f32[4,256,128]{2,1,0:T(8,128)} %pad_maximum_fusion.own), channel_id=1, source_target_pairs={{1,2},{2,1},{5,6},{6,5},{9,10},{10,9},{13,14},{14,13},{17,18},{18,... | collective-permute-start | bytes 1572872 | tf_op jit(solution)/shard_map/ppermute | solution.py:247
  41.1 9.7 %collective-permute-start.12 = (f32[4,256,128]{2,1,0:T(8,128)}, f32[4,256,128]{2,1,0:T(8,128)}, u32[]{:S(2)}, u32[]{:S(2)}) collective-permute-start(f32[4,256,128]{2,1,0:T(8,128)} %pad_maximum_fusion.own), channel_id=1, source_target_pairs={{0,1},{1,0},{2,3},{3,2},{4,5},{5,4},{6,7},{7,6},{8,9},{9,8},{10,11... | collective-permute-start | bytes 1572872 | tf_op jit(solution)/shard_map/ppermute | solution.py:247
  50.9 2.3 %collective-permute-done.9.got_hbm = f32[4,128,128]{2,1,0:T(8,128)} collective-permute-done((f32[4,128,128]{2,1,0:T(8,128)}, f32[4,128,128]{2,1,0:T(8,128)}, u32[]{:S(2)}, u32[]{:S(2)}) %collective-permute-start.9) | collective-permute-done | bytes 262176 | tf_op jit(solution)/shard_map/ppermute | solution.py:247
  54.1 2.3 %shard_map.78.both = f32[4,128,128]{2,1,0:T(8,128)S(1)} custom-call(f32[2,128,128]{2,1,0:T(8,128)S(1)} %copy-done.4, f32[4,128,128]{2,1,0:T(8,128)} %get-tuple-element.26.sent, f32[4,128,128]{2,1,0:T(8,128)} %collective-permute-done.9.got_hbm, f32[2,128,128]{2,1,0:T(8,128)S(1)} %fusion.7.probe_a, f32[2,128,128]{2,1,0:T(8,128)} %collective-permute-done.3.probe_b, ...), custom_call_target="tpu_custom_call" | custom-call | bytes 1048576 | tf_op jit(solution)/shard_map/pallas_call | solution.py:78
  56.5 1.5 %collective-permute-done.10.both_other = f32[4,128,128]{2,1,0:T(8,128)S(1)} collective-permute-done((f32[4,128,128]{2,1,0:T(8,128)S(1)}, f32[4,128,128]{2,1,0:T(8,128)S(1)}, u32[]{:S(2)}, u32[]{:S(2)}) %collective-permute-start.10) | collective-permute-done | bytes 262176 | tf_op jit(solution)/shard_map/ppermute | solution.py:24
  58.0 1.5 %shard_map.79 = (f32[256,128]{1,0:T(8,128)S(1)}, f32[256,128]{1,0:T(8,128)S(1)}, f32[256,128]{1,0:T(8,128)S(1)}, f32[256,128]{1,0:T(8,128)S(1)}) custom-call(f32[2,1,2048,128]{3,2,1,0:T(8,128)S(1)} %copy-done.1, f32[2,4,256,128]{3,2,1,0:T(8,128)S(1)} %collective-permute-done.left_other, f32[4,128,128]{2,1,0:T(8,128)S(1)} %shard_map.78.both, ...), custom_call_target="tpu_custom_call" | custom-call | bytes 1048576 | tf_op jit(solution)/shard_map/pallas_call | solution.py:78
  59.5 1.6 %collective-permute-start.11 = (f32[256,128]{1,0:T(8,128)S(1)}, f32[256,128]{1,0:T(8,128)S(1)}, u32[]{:S(2)}, u32[]{:S(2)}) collective-permute-start(f32[256,128]{1,0:T(8,128)S(1)} %get-tuple-element.28), channel_id=1, source_target_pairs={{0,8},{4,12},{8,0},{12,4},{16,24},{20,28},{24,16},{28,20},{1,9},{5... | collective-permute-start | bytes 393224 | tf_op jit(solution)/shard_map/ppermute | solution.py:24
  62.3 2.8 %collective-permute-done.11 = f32[256,128]{1,0:T(8,128)S(1)} collective-permute-done((f32[256,128]{1,0:T(8,128)S(1)}, f32[256,128]{1,0:T(8,128)S(1)}, u32[]{:S(2)}, u32[]{:S(2)}) %collective-permute-start.11) | collective-permute-done | bytes 131104 | tf_op jit(solution)/shard_map/ppermute | solution.py:24
  65.8 1.6 %collective-permute-start.14 = (f32[256,128]{1,0:T(8,128)S(1)}, f32[256,128]{1,0:T(8,128)S(1)}, u32[]{:S(2)}, u32[]{:S(2)}) collective-permute-start(f32[256,128]{1,0:T(8,128)S(1)} %get-tuple-element.32), channel_id=1, source_target_pairs={{0,16},{4,20},{8,24},{12,28},{16,0},{20,4},{24,8},{28,12},{1,17},{... | collective-permute-start | bytes 393224 | tf_op jit(solution)/shard_map/ppermute | solution.py:24
  68.8 4.8 %collective-permute-done.14 = f32[256,128]{1,0:T(8,128)S(1)} collective-permute-done((f32[256,128]{1,0:T(8,128)S(1)}, f32[256,128]{1,0:T(8,128)S(1)}, u32[]{:S(2)}, u32[]{:S(2)}) %collective-permute-start.14) | collective-permute-done | bytes 131104 | tf_op jit(solution)/shard_map/ppermute | solution.py:24
  73.7 1.6 %collective-permute-start.16 = (f32[256,128]{1,0:T(8,128)S(1)}, f32[256,128]{1,0:T(8,128)S(1)}, u32[]{:S(2)}, u32[]{:S(2)}) collective-permute-start(f32[256,128]{1,0:T(8,128)S(1)} %add_add_fusion.rest_0_.y_rows), channel_id=1, source_target_pairs={{0,8},{4,12},{8,0},{12,4},{16,24},{20,28},{24,16},{28,20},{1,9},{5... | collective-permute-start | bytes 393224 | tf_op jit(solution)/shard_map/ppermute | solution.py:24
  76.5 2.2 %collective-permute-done.16.rest_1_ = f32[256,128]{1,0:T(8,128)S(1)} collective-permute-done((f32[256,128]{1,0:T(8,128)S(1)}, f32[256,128]{1,0:T(8,128)S(1)}, u32[]{:S(2)}, u32[]{:S(2)}) %collective-permute-start.16) | collective-permute-done | bytes 131104 | tf_op jit(solution)/shard_map/ppermute | solution.py:24
  81.3 1.7 %collective-permute-start.19 = (f32[256,128]{1,0:T(8,128)S(1)}, f32[256,128]{1,0:T(8,128)S(1)}, u32[]{:S(2)}, u32[]{:S(2)}) collective-permute-start(f32[256,128]{1,0:T(8,128)S(1)} %add_add_fusion.rest_0_.y_rows), channel_id=1, source_target_pairs={{0,24},{4,28},{8,16},{12,20},{16,8},{20,12},{24,0},{28,4},{1,25},{... | collective-permute-start | bytes 393224 | tf_op jit(solution)/shard_map/ppermute | solution.py:24
  83.0 2.0 %collective-permute-done.18.rest_2_ = f32[256,128]{1,0:T(8,128)S(1)} collective-permute-done((f32[256,128]{1,0:T(8,128)S(1)}, f32[256,128]{1,0:T(8,128)S(1)}, u32[]{:S(2)}, u32[]{:S(2)}) %collective-permute-start.18) | collective-permute-done | bytes 131104 | tf_op jit(solution)/shard_map/ppermute | solution.py:24
  85.0 2.2 %collective-permute-done.19.rest_3_ = f32[256,128]{1,0:T(8,128)S(1)} collective-permute-done((f32[256,128]{1,0:T(8,128)S(1)}, f32[256,128]{1,0:T(8,128)S(1)}, u32[]{:S(2)}, u32[]{:S(2)}) %collective-permute-start.19) | collective-permute-done | bytes 131104 | tf_op jit(solution)/shard_map/ppermute | solution.py:24
  87.2 1.7 %shard_map.80.sent = f32[5,128,128]{2,1,0:T(8,128)S(1)} custom-call(f32[2,1,2048,128]{3,2,1,0:T(8,128)S(1)} %copy-done.1, f32[2,4,256,128]{3,2,1,0:T(8,128)S(1)} %collective-permute-done.left_other, f32[256,128]{1,0:T(8,128)S(1)} %add_add_fusion.rest_0_.y_rows, f32[256,128]{1,0:T(8,128)S(1)} %collective-permute-done.16.rest_1_, ...), custom_call_target="tpu_custom_call" | custom-call | bytes 1048576 | tf_op jit(solution)/shard_map/pallas_call | solution.py:78
  89.0 3.6 %collective-permute-done.21.outer = f32[4,256,128]{2,1,0:T(8,128)S(1)} collective-permute-done((f32[4,256,128]{2,1,0:T(8,128)}, f32[4,256,128]{2,1,0:T(8,128)S(1)}, u32[]{:S(2)}, u32[]{:S(2)}) %collective-permute-start.21) | collective-permute-done | bytes 524320 | tf_op jit(solution)/shard_map/ppermute | solution.py:247
  92.6 7.5 %collective-permute-done.22.last = f32[4,256,128]{2,1,0:T(8,128)S(1)} collective-permute-done((f32[4,256,128]{2,1,0:T(8,128)S(1)}, f32[4,256,128]{2,1,0:T(8,128)S(1)}, u32[]{:S(2)}, u32[]{:S(2)}) %collective-permute-start.22) | collective-permute-done | bytes 524320 | tf_op jit(solution)/shard_map/ppermute | solution.py:247
  100.1 2.4 %shard_map.82 = (f32[256,128]{1,0:T(8,128)S(1)}, f32[256,128]{1,0:T(8,128)S(1)}, f32[256,128]{1,0:T(8,128)S(1)}, f32[256,128]{1,0:T(8,128)S(1)}) custom-call(f32[5,128,128]{2,1,0:T(8,128)S(1)} %shard_map.80.sent, f32[5,128,128]{2,1,0:T(8,128)S(1)} %collective-permute-done.20.got, f32[4,128,128]{2,1,0:T(8,128)S(1)} %shard_map.78.both, ...), custom_call_target="tpu_custom_call" | custom-call | bytes 1048576 | tf_op jit(solution)/shard_map/pallas_call | solution.py:78
  103.8 2.3 %collective-permute-start.25 = (f32[256,128]{1,0:T(8,128)S(1)}, f32[256,128]{1,0:T(8,128)S(1)}, u32[]{:S(2)}, u32[]{:S(2)}) collective-permute-start(f32[256,128]{1,0:T(8,128)S(1)} %get-tuple-element.42), channel_id=1, source_target_pairs={{0,24},{4,28},{8,16},{12,20},{16,8},{20,12},{24,0},{28,4},{1,25},{... | collective-permute-start | bytes 393224 | tf_op jit(solution)/shard_map/ppermute | solution.py:24
  106.1 13.0 %shard_map.81 = (f32[256,128]{1,0:T(8,128)}, f32[128,128]{1,0:T(8,128)S(1)}) custom-call(f32[5,128,128]{2,1,0:T(8,128)S(1)} %shard_map.80.sent, f32[5,128,128]{2,1,0:T(8,128)S(1)} %collective-permute-done.20.got, f32[256,128]{1,0:T(8,128)S(1)} %add_add_fusion.rest_0_.y_rows), custom_call_target="tpu_custom_call" | custom-call | flops 1000000000 | bytes 1048576 | tf_op jit(solution)/shard_map/pallas_call | solution.py:78
  (56 shorter events, 22.5 us)
Async XLA Ops:
  0.6 4.6 %copy-start = (f32[512,128]{1,0:T(8,128)S(1)}, f32[512,128]{1,0:T(8,128)}, u32[]{:S(2)}) copy-start(f32[512,128]{1,0:T(8,128)} %param.10) | copy-start | bytes 786436
  0.6 13.0 %copy-start.7 = (f32[2,512,128]{2,1,0:T(8,128)S(1)}, f32[2,512,128]{2,1,0:T(8,128)}, u32[]{:S(2)}) copy-start(f32[2,512,128]{2,1,0:T(8,128)} %param.9) | copy-start | bytes 1572868
  0.7 15.2 %copy-start.1 = (f32[2,1,2048,128]{3,2,1,0:T(8,128)S(1)}, f32[2,1,2048,128]{3,2,1,0:T(8,128)}, u32[]{:S(2)}) copy-start(f32[2,1,2048,128]{3,2,1,0:T(8,128)} %left.3) | copy-start | bytes 6291460
  0.7 23.1 %collective-permute-start.1 = (f32[2,512,128]{2,1,0:T(8,128)}, f32[2,512,128]{2,1,0:T(8,128)}, u32[]{:S(2)}, u32[]{:S(2)}) collective-permute-start(f32[2,512,128]{2,1,0:T(8,128)} %param.9), channel_id=1, source_target_pairs={{0,1},{1,0},{2,3},{3,2},{4,5},{5,4},{6,7},{7,6},{8,9},{9,8},{10,11... | collective-permute-start | bytes 1572872 | tf_op jit(solution)/shard_map/ppermute | solution.py:247
  3.8 15.6 %collective-permute-start.2 = (f32[2,512,128]{2,1,0:T(8,128)}, f32[2,512,128]{2,1,0:T(8,128)}, u32[]{:S(2)}, u32[]{:S(2)}) collective-permute-start(f32[2,512,128]{2,1,0:T(8,128)} %param.9), channel_id=1, source_target_pairs={{1,2},{2,1},{5,6},{6,5},{9,10},{10,9},{13,14},{14,13},{17,18},{18,... | collective-permute-start | bytes 1572872 | tf_op jit(solution)/shard_map/ppermute | solution.py:247
  6.9 22.3 %collective-permute-start.3 = (f32[2,128,128]{2,1,0:T(8,128)S(1)}, f32[2,128,128]{2,1,0:T(8,128)}, u32[]{:S(2)}, u32[]{:S(2)}) collective-permute-start(f32[2,128,128]{2,1,0:T(8,128)S(1)} %fusion.7.probe_a), channel_id=1, source_target_pairs={{0,1},{1,0},{2,3},{3,2},{4,5},{5,4},{6,7},{7,6},{8,9},{9,8},{10,11... | collective-permute-start | bytes 393224 | tf_op jit(solution)/shard_map/ppermute | solution.py:247
  10.5 21.1 %collective-permute-start.7 = (f32[2,128,128]{2,1,0:T(8,128)S(1)}, f32[2,128,128]{2,1,0:T(8,128)}, u32[]{:S(2)}, u32[]{:S(2)}) collective-permute-start(f32[2,128,128]{2,1,0:T(8,128)S(1)} %fusion.7.probe_a), channel_id=1, source_target_pairs={{1,2},{2,1},{5,6},{6,5},{9,10},{10,9},{13,14},{14,13},{17,18},{18,... | collective-permute-start | bytes 393224 | tf_op jit(solution)/shard_map/ppermute | solution.py:247
  13.6 3.4 %collective-permute-start.4 = (f32[2,256,128]{2,1,0:T(8,128)S(1)}, f32[2,256,128]{2,1,0:T(8,128)}, u32[]{:S(2)}, u32[]{:S(2)}) collective-permute-start(f32[2,256,128]{2,1,0:T(8,128)S(1)} %get-tuple-element.45), channel_id=1, source_target_pairs={{0,4},{4,0},{8,12},{12,8},{16,20},{20,16},{24,28},{28,24},{1,5},{5... | collective-permute-start | bytes 786440 | tf_op jit(solution)/shard_map/ppermute | solution.py:24
  15.9 3.4 %copy-start.5 = (f32[2,1,2048,128]{3,2,1,0:T(8,128)S(1)}, f32[2,1,2048,128]{3,2,1,0:T(8,128)}, u32[]{:S(2)}) copy-start(f32[2,1,2048,128]{3,2,1,0:T(8,128)} %param.7) | copy-start | bytes 6291460
  15.9 9.4 %copy-start.6 = (f32[2,128,128]{2,1,0:T(8,128)S(1)}, f32[2,128,128]{2,1,0:T(8,128)}, u32[]{:S(2)}) copy-start(f32[2,128,128]{2,1,0:T(8,128)} %fusion.2) | copy-start | bytes 393220
  17.0 39.6 %collective-permute-start = (f32[2,4,256,128]{3,2,1,0:T(8,128)}, f32[2,4,256,128]{3,2,1,0:T(8,128)S(1)}, u32[]{:S(2)}, u32[]{:S(2)}) collective-permute-start(f32[2,4,256,128]{3,2,1,0:T(8,128)} %dynamic-slice_bitcast_fusion), channel_id=1, source_target_pairs={{0,4},{4,0},{8,12},{12,8},{16,20},{20,16},{24,28},{28,24},{1,5},{5... | collective-permute-start | bytes 3145736 | tf_op jit(solution)/shard_map/ppermute | solution.py:24
  20.2 14.2 %collective-permute-start.6 = (f32[2,512,128]{2,1,0:T(8,128)}, f32[2,512,128]{2,1,0:T(8,128)}, u32[]{:S(2)}, u32[]{:S(2)}) collective-permute-start(f32[2,512,128]{2,1,0:T(8,128)} %bitcast_select_fusion), channel_id=1, source_target_pairs={{0,1},{1,0},{2,3},{3,2},{4,5},{5,4},{6,7},{7,6},{8,9},{9,8},{10,11... | collective-permute-start | bytes 1572872 | tf_op jit(solution)/shard_map/ppermute | solution.py:247
  23.8 10.6 %collective-permute-start.5 = (f32[2,512,128]{2,1,0:T(8,128)}, f32[2,512,128]{2,1,0:T(8,128)}, u32[]{:S(2)}, u32[]{:S(2)}) collective-permute-start(f32[2,512,128]{2,1,0:T(8,128)} %collective-permute-done.1), channel_id=1, source_target_pairs={{1,2},{2,1},{5,6},{6,5},{9,10},{10,9},{13,14},{14,13},{17,18},{18,... | collective-permute-start | bytes 1572872 | tf_op jit(solution)/shard_map/ppermute | solution.py:247
  26.9 23.9 %copy-start.8 = (s32[2,1]{0,1:T(1,128)S(1)}, s32[2,1]{0,1:T(1,128)}, u32[]{:S(2)}) copy-start(s32[2,1]{0,1:T(1,128)} %param.11) | copy-start | bytes 28
  29.2 2.4 %collective-permute-start.8 = (f32[2,128,128]{2,1,0:T(8,128)}, f32[2,128,128]{2,1,0:T(8,128)}, u32[]{:S(2)}, u32[]{:S(2)}) collective-permute-start(f32[2,128,128]{2,1,0:T(8,128)} %collective-permute-done.3.probe_b), channel_id=1, source_target_pairs={{1,2},{2,1},{5,6},{6,5},{9,10},{10,9},{13,14},{14,13},{17,18},{18,... | collective-permute-start | bytes 393224 | tf_op jit(solution)/shard_map/ppermute | solution.py:247
  38.3 14.9 %collective-permute-start.9 = (f32[4,128,128]{2,1,0:T(8,128)}, f32[4,128,128]{2,1,0:T(8,128)}, u32[]{:S(2)}, u32[]{:S(2)}) collective-permute-start(f32[4,128,128]{2,1,0:T(8,128)} %get-tuple-element.26.sent), channel_id=1, source_target_pairs={{1,0},{2,3},{5,4},{6,7},{9,8},{10,11},{13,12},{14,15},{17,16},{18,... | collective-permute-start | bytes 786440 | tf_op jit(solution)/shard_map/ppermute | solution.py:247
  39.6 21.5 %collective-permute-start.13 = (f32[4,256,128]{2,1,0:T(8,128)}, f32[4,256,128]{2,1,0:T(8,128)}, u32[]{:S(2)}, u32[]{:S(2)}) collective-permute-start(f32[4,256,128]{2,1,0:T(8,128)} %pad_maximum_fusion.own), channel_id=1, source_target_pairs={{1,2},{2,1},{5,6},{6,5},{9,10},{10,9},{13,14},{14,13},{17,18},{18,... | collective-permute-start | bytes 1572872 | tf_op jit(solution)/shard_map/ppermute | solution.py:247
  41.1 21.2 %collective-permute-start.12 = (f32[4,256,128]{2,1,0:T(8,128)}, f32[4,256,128]{2,1,0:T(8,128)}, u32[]{:S(2)}, u32[]{:S(2)}) collective-permute-start(f32[4,256,128]{2,1,0:T(8,128)} %pad_maximum_fusion.own), channel_id=1, source_target_pairs={{0,1},{1,0},{2,3},{3,2},{4,5},{5,4},{6,7},{7,6},{8,9},{9,8},{10,11... | collective-permute-start | bytes 1572872 | tf_op jit(solution)/shard_map/ppermute | solution.py:247
  56.4 1.6 %collective-permute-start.10 = (f32[4,128,128]{2,1,0:T(8,128)S(1)}, f32[4,128,128]{2,1,0:T(8,128)S(1)}, u32[]{:S(2)}, u32[]{:S(2)}) collective-permute-start(f32[4,128,128]{2,1,0:T(8,128)S(1)} %shard_map.78.both), channel_id=1, source_target_pairs={{0,4},{4,0},{8,12},{12,8},{16,20},{20,16},{24,28},{28,24},{1,5},{5... | collective-permute-start | bytes 786440 | tf_op jit(solution)/shard_map/ppermute | solution.py:24
  59.5 5.6 %collective-permute-start.11 = (f32[256,128]{1,0:T(8,128)S(1)}, f32[256,128]{1,0:T(8,128)S(1)}, u32[]{:S(2)}, u32[]{:S(2)}) collective-permute-start(f32[256,128]{1,0:T(8,128)S(1)} %get-tuple-element.28), channel_id=1, source_target_pairs={{0,8},{4,12},{8,0},{12,4},{16,24},{20,28},{24,16},{28,20},{1,9},{5... | collective-permute-start | bytes 393224 | tf_op jit(solution)/shard_map/ppermute | solution.py:24
  65.1 13.6 %collective-permute-start.17 = (f32[4,256,128]{2,1,0:T(8,128)}, f32[4,256,128]{2,1,0:T(8,128)S(1)}, u32[]{:S(2)}, u32[]{:S(2)}) collective-permute-start(f32[4,256,128]{2,1,0:T(8,128)} %collective-permute-done.12.near), channel_id=1, source_target_pairs={{1,2},{2,1},{5,6},{6,5},{9,10},{10,9},{13,14},{14,13},{17,18},{18,... | collective-permute-start | bytes 1572872 | tf_op jit(solution)/shard_map/ppermute | solution.py:247
  65.8 7.8 %collective-permute-start.14 = (f32[256,128]{1,0:T(8,128)S(1)}, f32[256,128]{1,0:T(8,128)S(1)}, u32[]{:S(2)}, u32[]{:S(2)}) collective-permute-start(f32[256,128]{1,0:T(8,128)S(1)} %get-tuple-element.32), channel_id=1, source_target_pairs={{0,16},{4,20},{8,24},{12,28},{16,0},{20,4},{24,8},{28,12},{1,17},{... | collective-permute-start | bytes 393224 | tf_op jit(solution)/shard_map/ppermute | solution.py:24
  67.4 6.2 %collective-permute-start.15 = (f32[256,128]{1,0:T(8,128)S(1)}, f32[256,128]{1,0:T(8,128)S(1)}, u32[]{:S(2)}, u32[]{:S(2)}) collective-permute-start(f32[256,128]{1,0:T(8,128)S(1)} %get-tuple-element.33), channel_id=1, source_target_pairs={{0,24},{4,28},{8,16},{12,20},{16,8},{20,12},{24,0},{28,4},{1,25},{... | collective-permute-start | bytes 393224 | tf_op jit(solution)/shard_map/ppermute | solution.py:24
  73.7 5.0 %collective-permute-start.16 = (f32[256,128]{1,0:T(8,128)S(1)}, f32[256,128]{1,0:T(8,128)S(1)}, u32[]{:S(2)}, u32[]{:S(2)}) collective-permute-start(f32[256,128]{1,0:T(8,128)S(1)} %add_add_fusion.rest_0_.y_rows), channel_id=1, source_target_pairs={{0,8},{4,12},{8,0},{12,4},{16,24},{20,28},{24,16},{28,20},{1,9},{5... | collective-permute-start | bytes 393224 | tf_op jit(solution)/shard_map/ppermute | solution.py:24
  75.3 17.3 %collective-permute-start.21 = (f32[4,256,128]{2,1,0:T(8,128)}, f32[4,256,128]{2,1,0:T(8,128)S(1)}, u32[]{:S(2)}, u32[]{:S(2)}) collective-permute-start(f32[4,256,128]{2,1,0:T(8,128)} %collective-permute-done.13.inner), channel_id=1, source_target_pairs={{1,0},{2,3},{5,4},{6,7},{9,8},{10,11},{13,12},{14,15},{17,16},{18,... | collective-permute-start | bytes 1572872 | tf_op jit(solution)/shard_map/ppermute | solution.py:247
  78.7 21.4 %collective-permute-start.22 = (f32[4,256,128]{2,1,0:T(8,128)S(1)}, f32[4,256,128]{2,1,0:T(8,128)S(1)}, u32[]{:S(2)}, u32[]{:S(2)}) collective-permute-start(f32[4,256,128]{2,1,0:T(8,128)S(1)} %collective-permute-done.17.inner_far), channel_id=1, source_target_pairs={{1,0},{2,3},{5,4},{6,7},{9,8},{10,11},{13,12},{14,15},{17,16},{18,... | collective-permute-start | bytes 1572872 | tf_op jit(solution)/shard_map/ppermute | solution.py:247
  80.0 5.0 %collective-permute-start.18 = (f32[256,128]{1,0:T(8,128)S(1)}, f32[256,128]{1,0:T(8,128)S(1)}, u32[]{:S(2)}, u32[]{:S(2)}) collective-permute-start(f32[256,128]{1,0:T(8,128)S(1)} %add_add_fusion.rest_0_.y_rows), channel_id=1, source_target_pairs={{0,16},{4,20},{8,24},{12,28},{16,0},{20,4},{24,8},{28,12},{1,17},{... | collective-permute-start | bytes 393224 | tf_op jit(solution)/shard_map/ppermute | solution.py:24
  81.3 5.9 %collective-permute-start.19 = (f32[256,128]{1,0:T(8,128)S(1)}, f32[256,128]{1,0:T(8,128)S(1)}, u32[]{:S(2)}, u32[]{:S(2)}) collective-permute-start(f32[256,128]{1,0:T(8,128)S(1)} %add_add_fusion.rest_0_.y_rows), channel_id=1, source_target_pairs={{0,24},{4,28},{8,16},{12,20},{16,8},{20,12},{24,0},{28,4},{1,25},{... | collective-permute-start | bytes 393224 | tf_op jit(solution)/shard_map/ppermute | solution.py:24
  89.0 3.6 %collective-permute-start.20 = (f32[5,128,128]{2,1,0:T(8,128)S(1)}, f32[5,128,128]{2,1,0:T(8,128)S(1)}, u32[]{:S(2)}, u32[]{:S(2)}) collective-permute-start(f32[5,128,128]{2,1,0:T(8,128)S(1)} %shard_map.80.sent), channel_id=1, source_target_pairs={{0,4},{4,0},{8,12},{12,8},{16,20},{20,16},{24,28},{28,24},{1,5},{5... | collective-permute-start | bytes 983048 | tf_op jit(solution)/shard_map/ppermute | solution.py:24
  102.5 16.6 %collective-permute-start.23 = (f32[256,128]{1,0:T(8,128)S(1)}, f32[256,128]{1,0:T(8,128)S(1)}, u32[]{:S(2)}, u32[]{:S(2)}) collective-permute-start(f32[256,128]{1,0:T(8,128)S(1)} %get-tuple-element.40), channel_id=1, source_target_pairs={{0,8},{4,12},{8,0},{12,4},{16,24},{20,28},{24,16},{28,20},{1,9},{5... | collective-permute-start | bytes 393224 | tf_op jit(solution)/shard_map/ppermute | solution.py:24
  103.2 16.0 %collective-permute-start.24 = (f32[256,128]{1,0:T(8,128)S(1)}, f32[256,128]{1,0:T(8,128)S(1)}, u32[]{:S(2)}, u32[]{:S(2)}) collective-permute-start(f32[256,128]{1,0:T(8,128)S(1)} %get-tuple-element.41), channel_id=1, source_target_pairs={{0,16},{4,20},{8,24},{12,28},{16,0},{20,4},{24,8},{28,12},{1,17},{... | collective-permute-start | bytes 393224 | tf_op jit(solution)/shard_map/ppermute | solution.py:24
  103.8 15.3 %collective-permute-start.25 = (f32[256,128]{1,0:T(8,128)S(1)}, f32[256,128]{1,0:T(8,128)S(1)}, u32[]{:S(2)}, u32[]{:S(2)}) collective-permute-start(f32[256,128]{1,0:T(8,128)S(1)} %get-tuple-element.42), channel_id=1, source_target_pairs={{0,24},{4,28},{8,16},{12,20},{16,8},{20,12},{24,0},{28,4},{1,25},{... | collective-permute-start | bytes 393224 | tf_op jit(solution)/shard_map/ppermute | solution.py:24
  (3 other events, 2.5 us)

commit v4 on v3

--- a/solution.py
+++ b/solution.py
@@ -71,18 +71,42 @@
     return lax.dot_general(a, b, dims, precision=lax.Precision.HIGHEST, preferred_element_type=jnp.float32)
 
 
-def call(kernel, outs, args, spaces="", scratch=(), cost=0):
-    kinds = {"v": pltpu.VMEM, "a": pl.ANY, "s": pltpu.SMEM}
-    spaces = spaces or "v" * len(args)
+def call(kernel, outs, args, spaces="", scratch=(), cost=0, limit=24, stored=()):
+    kinds = {"v": pltpu.VMEM, "a": pl.ANY, "l": pltpu.HBM, "h": pltpu.HBM, "s": pltpu.SMEM}
+    spaces = spaces or "l" * len(args)
+    loaded = [i for i, letter in enumerate(spaces) if letter == "l"]
     shapes = [jax.ShapeDtypeStruct(shape, jnp.float32) for shape in outs]
+    held = [pltpu.VMEM(args[i].shape, jnp.float32) for i in loaded] + [pltpu.VMEM(outs[i], jnp.float32) for i in stored]
+    held.append(pltpu.SemaphoreType.DMA((len(held) + 1,)))
+
+    def body(*refs):
+        own, sems = refs[-len(held):-1], refs[-1]
+        refs = list(refs[:-len(held)])
+        copies = []
+        for n, i in enumerate(loaded):
+            copies.append(pltpu.make_async_copy(refs[i], own[n], sems.at[n]))
+            copies[-1].start()
+            refs[i] = own[n]
+        after = []
+        for n, i in enumerate(stored, len(loaded)):
+            after.append(pltpu.make_async_copy(own[n], refs[len(args) + i], sems.at[n]))
+            refs[len(args) + i] = own[n]
+        for copy in copies:
+            copy.wait()
+        kernel(*refs)
+        for copy in after:
+            copy.start()
+        for copy in after:
+            copy.wait()
+
     return pl.pallas_call(
-        kernel,
+        body,
         out_shape=shapes,
         in_specs=[pl.BlockSpec(memory_space=kinds[letter]) for letter in spaces],
-        out_specs=[pl.BlockSpec(memory_space=pltpu.VMEM) for _ in shapes],
-        scratch_shapes=list(scratch),
-        compiler_params=pltpu.CompilerParams(vmem_limit_bytes=24 << 20),
-        cost_estimate=pl.CostEstimate(flops=cost, bytes_accessed=1 << 20, transcendentals=0),
+        out_specs=[pl.BlockSpec(memory_space=pltpu.HBM if i in stored else pltpu.VMEM) for i in range(len(outs))],
+        scratch_shapes=list(scratch) + held,
+        compiler_params=pltpu.CompilerParams(vmem_limit_bytes=limit << 20),
+        cost_estimate=pl.CostEstimate(flops=cost, bytes_accessed=0, transcendentals=0),
     )(*args)
 
 
@@ -94,12 +118,24 @@
         copy.wait()
 
 
-def core_kernel(planes, part, own_rows, first_hbm, second_hbm, probe_a, probe_b, core, sent, first, second, probe_in, sems):
+def pack_kernel(column_right, column_left, sketch, message, sem):
+    rows = column_right.shape[1]
+    copy = pltpu.make_async_copy(column_right, message.at[:, pl.ds(0, rows)], sem)
+    copy.start()
+    for k in range(message.shape[0]):
+        message[k, pl.ds(rows, column_left.shape[2])] = dot3(column_left[k], sketch[...], TN)
+    copy.wait()
+
+
+def core_kernel(planes, part, own_rows, own_hbm, near_hbm, inner_hbm, first_hbm, second_hbm, core, sent, probe, *held):
+    first, second, probe_in, sems = held
     plane = lax.axis_index("tile")
     is_end = jnp.logical_or(plane == 0, plane == planes - 1)
-    sources = [first_hbm, second_hbm, probe_a, probe_b]
-    load(sources, [first, second, probe_in.at[0], probe_in.at[1]], sems)
-    sent[pl.ds(2, 2)] = probe_in[0] + probe_in[1]
+    rows, rank = own_rows.shape[1:]
+    terms = [ref.at[:, pl.ds(rows, rank)] for ref in (own_hbm, near_hbm, inner_hbm)]
+    load([first_hbm, second_hbm, *terms], [first, second, *(probe_in.at[i] for i in range(3))], sems)
+    probe[...] = probe_in[0] + probe_in[1]
+    sent[pl.ds(2, 2)] = probe_in[2] + first[:, rows:]
 
     @pl.when(is_end)
     def _():
@@ -110,16 +146,14 @@
     @pl.when(jnp.logical_not(is_end))
     def _():
         for k in range(2):
-            core[k] = part[k] + dot3(own_rows[k], first[k], TN)
-            sent[k] = dot3(second[k], first[k], TN)
-
-
-def reduced_kernel(core, sent, got_hbm, probe_a, probe_b, pattern, both, got, probe_in, sems):
-    load([got_hbm, probe_a, probe_b], [got, probe_in.at[0], probe_in.at[1]], sems)
+            core[k] = part[k] + dot3(own_rows[k], first[k, :rows], TN)
+            sent[k] = dot3(second[k], first[k, :rows], TN)
+
+
+def reduced_kernel(core, sent, got, probe, pattern, both):
     for k in range(2):
         c = (core[k] + got[k]) * pattern[k, 0].astype(jnp.float32)
-        probe = (probe_in[0, k] + probe_in[1, k]) + (sent[2 + k] + got[2 + k])
-        both[k] = dot3(c, probe, NN)
+        both[k] = dot3(c, probe[k] + (sent[2 + k] + got[2 + k]), NN)
         both[2 + k] = c
 
 
@@ -246,11 +280,12 @@
     def across(array, pairs):
         return lax.ppermute(array, "tile", pairs)
 
-    near = across(column_right, outer_pairs)
-    inner = across(column_right, inner_pairs)
-    probes = mm("kbq,bp->kqp", column_left, sketch)
-    probes_near = across(probes, outer_pairs)
-    probes_inner = across(probes, inner_pairs)
+    rows = column_right.shape[1]
+    (message,) = call(
+        pack_kernel, [(2, rows + rank, rank)], [column_right, column_left, sketch], "hll", [pltpu.SemaphoreType.DMA], limit=60
+    )
+    near = across(message, outer_pairs)
+    inner = across(message, inner_pairs)
     right_blocks = target_right.reshape(2, planes, -1, rank)
 
     def block(index):
@@ -263,59 +298,54 @@
 
     lent_rows = block(planes - 1 - plane)
     inner_far = across(near, inner_pairs)
-    outer = across(jnp.where(is_end, lent_rows, inner), outer_pairs)
+    outer = across(jnp.where(is_end, lent_rows, inner[:, :rows]), outer_pairs)
     part = (
         mm("kbr,kbq->krq", block(plane), column_right)
-        + mm("kbr,kbq->krq", block(plane ^ 1), near)
-        + mm("kbr,kbq->krq", block(jnp.where(is_end, plane, planes - 1 - plane)), inner)
-    )
-    part, probes_near, col_half = lax.optimization_barrier((part, probes_near, col_half))
-    probes_far = across(probes_near, inner_pairs)
+        + mm("kbr,kbq->krq", block(plane ^ 1), near[:, :rows])
+        + mm("kbr,kbq->krq", block(jnp.where(is_end, plane, planes - 1 - plane)), inner[:, :rows])
+    )
+    part, col_half = lax.optimization_barrier((part, col_half))
     col_inner = across(col_half, inner_pairs)
-    far_rows = block(plane ^ 2)
-    rows_per_plane = column_right.shape[1]
-    core, lent = call(
+    col_near = across(col_half, outer_pairs)
+    core, lent, probe = call(
         functools.partial(core_kernel, planes),
-        [(2, rank, rank), (4, rank, rank)],
-        [part, far_rows, inner_far, outer, probes_inner, probes_far],
-        "vvaaaa",
-        [pltpu.VMEM((2, rows_per_plane, rank), jnp.float32)] * 2
-        + [pltpu.VMEM((2, 2, rank, rank), jnp.float32), pltpu.SemaphoreType.DMA((4,))],
-    )
-    lent_got = across(lent, outward)
-    col_half, _ = lax.optimization_barrier((col_half, lent))
-    col_near = across(col_half, outer_pairs)
-
-    reduced_scratch = [pltpu.VMEM((4, rank, rank), jnp.float32), pltpu.VMEM((2, 2, rank, rank), jnp.float32)]
-    reduced_scratch += [pltpu.SemaphoreType.DMA((3,))]
-    (both,) = call(reduced_kernel, [(4, rank, rank)], [core, lent, lent_got, probes, probes_near, pattern], "vvaaas", reduced_scratch)
+        [(2, rank, rank), (4, rank, rank), (2, rank, rank)],
+        [part, block(plane ^ 2), message, near, inner, inner_far, outer],
+        "vvhhhhh",
+        [pltpu.VMEM((2, rows + rank, rank), jnp.float32), pltpu.VMEM((2, rows, rank), jnp.float32)]
+        + [pltpu.VMEM((3, 2, rank, rank), jnp.float32), pltpu.SemaphoreType.DMA((5,))],
+        stored=(0, 1, 2),
+        limit=60,
+    )
+    lent_got = across(lent, outer_pairs)
+    _, col_near_held, col_inner_held = lax.optimization_barrier((lent_got, col_near, col_inner))
+    col_inner_far = across(col_near_held, inner_pairs)
+    col_outer = across(col_inner_held, outward)
+    col_outer, col_inner_far = lax.optimization_barrier((col_outer, col_inner_far))
+    (both,) = call(reduced_kernel, [(4, rank, rank)], [core, lent, lent_got, probe, pattern], "lllls", limit=60)
     both_other = exchange(both, "step", 1)
     rows_scratch = [pltpu.VMEM((chips, 4, row_count, rank), jnp.float32), pltpu.SemaphoreType.DMA((2 * chips,))]
     y_parts = call(y_kernel, [(row_count, rank)] * chips, [target_left, left_other, both, both_other], "aavv", rows_scratch)
-    y_got = [exchange(y_parts[bit], "step", 2 * bit) for bit in range(1, chips)]
-    y_got[0], col_near_held, col_inner_held = lax.optimization_barrier((y_got[0], col_near, col_inner))
-    col_inner_far = across(col_near_held, inner_pairs)
-    col_outer = across(col_inner_held, outward)
     y_rows = y_parts[0]
-    for got in y_got:
-        y_rows = y_rows + got
+    for bit in range(1, chips):
+        y_rows = y_rows + exchange(y_parts[bit], "step", 2 * bit)
     y_all = [y_rows] + [exchange(y_rows, "step", 2 * bit) for bit in range(1, chips)]
-    y_all[1], col_inner_far_held = lax.optimization_barrier((y_all[1], col_inner_far))
-    col_last = across(col_inner_far_held, outward)
+    _, col_last = lax.optimization_barrier((y_rows, col_inner_far))
+    col_last = across(col_last, outward)
     (sent,) = call(z_kernel, [(5, rank, rank)], [target_left, left_other, *y_all], "aa" + "v" * chips, rows_scratch)
     got = exchange(sent, "step", 1)
     w_parts = call(
         functools.partial(w_kernel, planes),
         [(row_count, rank)] * planes,
         [sent, got, both, both_other, col_half, col_near, col_inner, col_inner_far, col_outer, col_last],
-        "vvvvaaaaaa",
+        "vvvvhhhhhh",
         [pltpu.VMEM((planes, 4, row_count, rank), jnp.float32), pltpu.SemaphoreType.DMA((planes,))],
     )
     w_got = [exchange(w_parts[bit], "step", 2 * bit) for bit in range(1, chips)]
     basis, inverse = call(
-        functools.partial(basis_kernel, tile_rows, 32), [(row_count, rank), (rank, rank)], [sent, got, y_rows], cost=10**9
-    )
-    (factor,) = call(functools.partial(factor_kernel, tile_rows), [(row_count, rank)], [w_parts[0], *w_got, inverse])
+        functools.partial(basis_kernel, tile_rows, 32), [(row_count, rank), (rank, rank)], [sent, got, y_rows], "vvv", cost=10**9
+    )
+    (factor,) = call(functools.partial(factor_kernel, tile_rows), [(row_count, rank)], [w_parts[0], *w_got, inverse], "v" * (chips + 1))
     return basis[None], factor[None]
 
 

time: 121 us -> 114 us (0.942)
  starting transfers between devices: 45 us -> 28.1 us
  waiting for transfers between devices: 32.9 us -> 39.5 us
  Pallas kernels: 24.2 us -> 29.3 us
  matrix products: 7.85 us -> 5.91 us
    ppermute x13 -> x10, starting transfers between devices: 31.6 us -> 16.8 us  [across(): return lax.ppermute(array, 'tile', pairs)]
    ppermute x13 -> x10, waiting for transfers between devices: 17.4 us -> 25.9 us  [across(): return lax.ppermute(array, 'tile', pairs)]
    pallas_call x7 -> x8, Pallas kernels: 24.2 us -> 29.3 us  [call(): pl.pallas_call(body, out_shape=shapes, in_specs=[pl.BlockSpec(memory_spac...]
    ppermute x13, starting transfers between devices: 13.4 us -> 11.3 us  [exchange(): lax.ppermute(array, axis, [(i, i ^ bit) for i in range(lax.axis_size(axis...]
    dot_general x4 -> x3, matrix products: 7.85 us -> 5.91 us  [mm(): jnp.einsum(spec, *arrays, precision=HIGH, preferred_element_type=jnp.floa...]
    ppermute x13, waiting for transfers between devices: 15.5 us -> 13.6 us  [exchange(): lax.ppermute(array, axis, [(i, i ^ bit) for i in range(lax.axis_size(axis...]
    unnamed x19 -> x15, local copies, waits for them, and re-layouts: 2.58 us -> 2.33 us
  transfers between devices with their start and end apart: 26 -> 23, of which waited for: 11 -> 10; matrix products, arithmetic and copies ran while one was open for 12% -> 12% of each run, Pallas kernels for 17% -> 20%
where the time goes in v4:
time: 114 us
  waiting for transfers between devices  39.5 us (35%)
  Pallas kernels  29.3 us (26%)
  starting transfers between devices  28.1 us (25%)
  local copies, waits for them, and re-layouts  6 us (5%)
  matrix products  5.91 us (5%)
  other arithmetic  3.73 us (3%)
    pallas_call x8, Pallas kernels, call(): pl.pallas_call(body, out_shape=shapes, in_specs=[pl.BlockSpec(memory_spac...  29.3 us
    ppermute x10, waiting for transfers between devices, across(): return lax.ppermute(array, 'tile', pairs)  25.9 us
    ppermute x10, starting transfers between devices, across(): return lax.ppermute(array, 'tile', pairs)  16.8 us
    ppermute x13, waiting for transfers between devices, exchange(): lax.ppermute(array, axis, [(i, i ^ bit) for i in range(lax.axis_size(axis...  13.6 us
    ppermute x13, starting transfers between devices, exchange(): lax.ppermute(array, axis, [(i, i ^ bit) for i in range(lax.axis_size(axis...  11.3 us
    dot_general x3, matrix products, mm(): jnp.einsum(spec, *arrays, precision=HIGH, preferred_element_type=jnp.floa...  5.91 us
    squeeze x3, local copies, waits for them, and re-layouts, take(): return lax.dynamic_index_in_dim(array, index, axis, keepdims=False)  3.68 us
    unnamed x15, local copies, waits for them, and re-layouts  2.33 us
  transfers between devices with their start and end apart: 23, of which 10 were waited for; matrix products, arithmetic and copies ran while one was open for 12% of the time, Pallas kernels for 20%

profile of v4, /device:TPU:0, one launch (start us, length us, event | category | flops | bytes accessed | tf_op | source)
XLA Modules:
  0.0 113.6 jit_solution(13455233289273854877)
XLA Ops:
  0.6 3.2 %shard_map.77.refs_2_ = f32[2,640,128]{2,1,0:T(8,128)} custom-call(f32[2,512,128]{2,1,0:T(8,128)} %refs_0_.3, f32[2,512,128]{2,1,0:T(8,128)} %refs_1_.1, f32[512,128]{1,0:T(8,128)} %refs_2_.1), custom_call_target="tpu_custom_call" | custom-call | tf_op jit(solution)/shard_map/pallas_call | solution.py:102
  3.8 3.1 %collective-permute-start.1 = (f32[2,640,128]{2,1,0:T(8,128)}, f32[2,640,128]{2,1,0:T(8,128)}, u32[]{:S(2)}, u32[]{:S(2)}) collective-permute-start(f32[2,640,128]{2,1,0:T(8,128)} %shard_map.77.refs_2_), channel_id=1, source_target_pairs={{0,1},{1,0},{2,3},{3,2},{4,5},{5,4},{6,7},{7,6},{8,9},{9,8},{10,11... | collective-permute-start | bytes 1966088 | tf_op jit(solution)/shard_map/ppermute | solution.py:281
  6.9 1.5 %collective-permute-start.2 = (f32[2,640,128]{2,1,0:T(8,128)}, f32[2,640,128]{2,1,0:T(8,128)}, u32[]{:S(2)}, u32[]{:S(2)}) collective-permute-start(f32[2,640,128]{2,1,0:T(8,128)} %shard_map.77.refs_2_), channel_id=1, source_target_pairs={{1,2},{2,1},{5,6},{6,5},{9,10},{10,9},{13,14},{14,13},{17,18},{18,... | collective-permute-start | bytes 1966088 | tf_op jit(solution)/shard_map/ppermute | solution.py:281
  10.8 1.9 %fusion.3 = f32[2,128,128]{2,1,0:T(8,128)S(1)} fusion(f32[2,512,128]{2,1,0:T(8,128)} %refs_0_.3, f32[2,4,512,128]{3,2,1,0:T(8,128)} %bitcast.39, s32[]{:T(128)S(6)} %select_n.45), kind=kOutput, calls=%fused_computation.7 | convolution fusion | flops 100663296 | bytes 1179652 | tf_op jit(solution)/shard_map/kbr,kbq->krq/dot_general | solution.py:14
  12.7 1.8 %pad_maximum_fusion.refs_4_ = f32[4,256,128]{2,1,0:T(8,128)} fusion(f32[2,256,128]{2,1,0:T(8,128)} %collective-permute-done.3, f32[2,256,128]{2,1,0:T(8,128)S(1)} %get-tuple-element.42), kind=kLoop, calls=%fused_computation.4 | loop fusion | flops 131072 | bytes 1048576 | tf_op jit(solution)/shard_map/concatenate | solution.py:297
  14.5 7.5 %collective-permute-done.1.refs_3_ = f32[2,640,128]{2,1,0:T(8,128)} collective-permute-done((f32[2,640,128]{2,1,0:T(8,128)}, f32[2,640,128]{2,1,0:T(8,128)}, u32[]{:S(2)}, u32[]{:S(2)}) %collective-permute-start.1) | collective-permute-done | bytes 655392 | tf_op jit(solution)/shard_map/ppermute | solution.py:281
  22.0 1.5 %collective-permute-start.4 = (f32[2,640,128]{2,1,0:T(8,128)}, f32[2,640,128]{2,1,0:T(8,128)}, u32[]{:S(2)}, u32[]{:S(2)}) collective-permute-start(f32[2,640,128]{2,1,0:T(8,128)} %collective-permute-done.1.refs_3_), channel_id=1, source_target_pairs={{1,2},{2,1},{5,6},{6,5},{9,10},{10,9},{13,14},{14,13},{17,18},{18,... | collective-permute-start | bytes 1966088 | tf_op jit(solution)/shard_map/ppermute | solution.py:281
  23.5 1.9 %bitcast_select_fusion = f32[2,512,128]{2,1,0:T(8,128)} fusion(f32[2,4,512,128]{3,2,1,0:T(8,128)S(1)} %bitcast.41, s32[]{:T(128)S(6)} %select_n.52, f32[2,640,128]{2,1,0:T(8,128)} %collective-permute-done.2.refs_4_, pred[]{:T(512)S(6)} %or.3), kind=kLoop, calls=%fused_computation.9 | loop fusion | flops 131072 | bytes 1572869 | tf_op jit(solution)/shard_map/jit(_where)/select_n | solution.py:301
  25.4 3.8 %collective-permute-start.5 = (f32[2,512,128]{2,1,0:T(8,128)}, f32[2,512,128]{2,1,0:T(8,128)}, u32[]{:S(2)}, u32[]{:S(2)}) collective-permute-start(f32[2,512,128]{2,1,0:T(8,128)} %bitcast_select_fusion), channel_id=1, source_target_pairs={{0,1},{1,0},{2,3},{3,2},{4,5},{5,4},{6,7},{7,6},{8,9},{9,8},{10,11... | collective-permute-start | bytes 1572872 | tf_op jit(solution)/shard_map/ppermute | solution.py:281
  29.1 1.6 %convolution_add_fusion.1 = f32[2,128,128]{2,1,0:T(8,128)S(1)} fusion(f32[2,128,128]{2,1,0:T(8,128)S(1)} %fusion.3, f32[2,640,128]{2,1,0:T(8,128)} %collective-permute-done.1.refs_3_, f32[2,4,512,128]{3,2,1,0:T(8,128)S(1)} %bitcast.42, s32[]{:T(128)S(6)} %select_n.46), kind=kOutput, calls=%fused_computation.1 | convolution fusion | flops 100696064 | bytes 1310724 | tf_op jit(solution)/shard_map/kbr,kbq->krq/dot_general | solution.py:14
  30.8 2.3 %convolution_add_fusion.refs_0_ = f32[2,128,128]{2,1,0:T(8,128)} fusion(f32[2,128,128]{2,1,0:T(8,128)S(1)} %convolution_add_fusion.1, f32[2,4,512,128]{3,2,1,0:T(8,128)S(1)} %bitcast.43, s32[]{:T(128)S(6)} %select_n.48, f32[2,640,128]{2,1,0:T(8,128)} %collective-permute-done.2.refs_4_), kind=kOutput, calls=%fused_computation | convolution fusion | flops 100696064 | bytes 1310724 | tf_op jit(solution)/shard_map/kbr,kbq->krq/dot_general | solution.py:14
  33.1 1.5 %collective-permute-start.16 = (f32[4,256,128]{2,1,0:T(8,128)}, f32[4,256,128]{2,1,0:T(8,128)}, u32[]{:S(2)}, u32[]{:S(2)}) collective-permute-start(f32[4,256,128]{2,1,0:T(8,128)} %pad_maximum_fusion.refs_4_), channel_id=1, source_target_pairs={{1,2},{2,1},{5,6},{6,5},{9,10},{10,9},{13,14},{14,13},{17,18},{18,... | collective-permute-start | bytes 1572872 | tf_op jit(solution)/shard_map/ppermute | solution.py:281
  34.6 1.9 %dynamic-slice_bitcast_fusion.1.refs_1_ = f32[2,512,128]{2,1,0:T(8,128)} fusion(f32[2,4,512,128]{3,2,1,0:T(8,128)} %bitcast.40, s32[]{:T(128)S(6)} %select_n.50), kind=kLoop, calls=%fused_computation.10 | loop fusion | bytes 1048580 | tf_op jit(solution)/shard_map/jit(dynamic_index_in_dim)/squeeze | solution.py:28
  36.5 5.8 %collective-permute-done.5.refs_6_ = f32[2,512,128]{2,1,0:T(8,128)} collective-permute-done((f32[2,512,128]{2,1,0:T(8,128)}, f32[2,512,128]{2,1,0:T(8,128)}, u32[]{:S(2)}, u32[]{:S(2)}) %collective-permute-start.5) | collective-permute-done | bytes 524320 | tf_op jit(solution)/shard_map/ppermute | solution.py:281
  42.3 3.7 %shard_map.78 = (f32[2,128,128]{2,1,0:T(8,128)}, f32[4,128,128]{2,1,0:T(8,128)}, f32[2,128,128]{2,1,0:T(8,128)}) custom-call(f32[2,128,128]{2,1,0:T(8,128)} %convolution_add_fusion.refs_0_, f32[2,512,128]{2,1,0:T(8,128)} %dynamic-slice_bitcast_fusion.1.refs_1_, f32[2,640,128]{2,1,0:T(8,128)} %shard_map.77.refs_2_, ...), custom_call_target="tpu_custom_call" | custom-call | tf_op jit(solution)/shard_map/pallas_call | solution.py:102
  46.0 2.2 %collective-permute-start.6 = (f32[4,128,128]{2,1,0:T(8,128)}, f32[4,128,128]{2,1,0:T(8,128)S(1)}, u32[]{:S(2)}, u32[]{:S(2)}) collective-permute-start(f32[4,128,128]{2,1,0:T(8,128)} %get-tuple-element.24.refs_1_), channel_id=1, source_target_pairs={{0,1},{1,0},{2,3},{3,2},{4,5},{5,4},{6,7},{7,6},{8,9},{9,8},{10,11... | collective-permute-start | bytes 786440 | tf_op jit(solution)/shard_map/ppermute | solution.py:281
  48.9 8.1 %collective-permute-done.6.refs_2_ = f32[4,128,128]{2,1,0:T(8,128)S(1)} collective-permute-done((f32[4,128,128]{2,1,0:T(8,128)}, f32[4,128,128]{2,1,0:T(8,128)S(1)}, u32[]{:S(2)}, u32[]{:S(2)}) %collective-permute-start.6) | collective-permute-done | bytes 262176 | tf_op jit(solution)/shard_map/ppermute | solution.py:281
  57.7 2.8 %shard_map.79.refs_2_ = f32[4,128,128]{2,1,0:T(8,128)} custom-call(f32[2,128,128]{2,1,0:T(8,128)} %get-tuple-element.23.refs_0_, f32[4,128,128]{2,1,0:T(8,128)} %get-tuple-element.24.refs_1_, f32[4,128,128]{2,1,0:T(8,128)} %copy-done.5, f32[2,128,128]{2,1,0:T(8,128)} %get-tuple-element.25.refs_3_, s32[2,1]{1,0:T(2,128)} %copy.16.refs_4_), custom_call_target="tpu_custom_call" | custom-call | tf_op jit(solution)/shard_map/pallas_call | solution.py:102
  65.0 2.5 %collective-permute-start.10 = (f32[256,128]{1,0:T(8,128)S(1)}, f32[256,128]{1,0:T(8,128)S(1)}, u32[]{:S(2)}, u32[]{:S(2)}) collective-permute-start(f32[256,128]{1,0:T(8,128)S(1)} %get-tuple-element.29), channel_id=1, source_target_pairs={{0,24},{4,28},{8,16},{12,20},{16,8},{20,12},{24,0},{28,4},{1,25},{... | collective-permute-start | bytes 393224 | tf_op jit(solution)/shard_map/ppermute | solution.py:24
  68.6 3.7 %collective-permute-done.10 = f32[256,128]{1,0:T(8,128)S(1)} collective-permute-done((f32[256,128]{1,0:T(8,128)S(1)}, f32[256,128]{1,0:T(8,128)S(1)}, u32[]{:S(2)}, u32[]{:S(2)}) %collective-permute-start.10) | collective-permute-done | bytes 131104 | tf_op jit(solution)/shard_map/ppermute | solution.py:24
  72.3 2.5 %collective-permute-done.8 = f32[256,128]{1,0:T(8,128)S(1)} collective-permute-done((f32[256,128]{1,0:T(8,128)S(1)}, f32[256,128]{1,0:T(8,128)S(1)}, u32[]{:S(2)}, u32[]{:S(2)}) %collective-permute-start.8) | collective-permute-done | bytes 131104 | tf_op jit(solution)/shard_map/ppermute | solution.py:24
  74.8 2.1 %collective-permute-done.17.refs_8_ = f32[4,256,128]{2,1,0:T(8,128)S(1)} collective-permute-done((f32[4,256,128]{2,1,0:T(8,128)}, f32[4,256,128]{2,1,0:T(8,128)S(1)}, u32[]{:S(2)}, u32[]{:S(2)}) %collective-permute-start.17) | collective-permute-done | bytes 524320 | tf_op jit(solution)/shard_map/ppermute | solution.py:281
  78.3 1.6 %collective-permute-start.11 = (f32[256,128]{1,0:T(8,128)S(1)}, f32[256,128]{1,0:T(8,128)S(1)}, u32[]{:S(2)}, u32[]{:S(2)}) collective-permute-start(f32[256,128]{1,0:T(8,128)S(1)} %add_add_fusion.refs_2_), channel_id=1, source_target_pairs={{0,8},{4,12},{8,0},{12,4},{16,24},{20,28},{24,16},{28,20},{1,9},{5... | collective-permute-start | bytes 393224 | tf_op jit(solution)/shard_map/ppermute | solution.py:24
  79.8 1.5 %collective-permute-start.12 = (f32[256,128]{1,0:T(8,128)S(1)}, f32[256,128]{1,0:T(8,128)S(1)}, u32[]{:S(2)}, u32[]{:S(2)}) collective-permute-start(f32[256,128]{1,0:T(8,128)S(1)} %add_add_fusion.refs_2_), channel_id=1, source_target_pairs={{0,16},{4,20},{8,24},{12,28},{16,0},{20,4},{24,8},{28,12},{1,17},{... | collective-permute-start | bytes 393224 | tf_op jit(solution)/shard_map/ppermute | solution.py:24
  81.8 2.0 %collective-permute-done.11.refs_3_ = f32[256,128]{1,0:T(8,128)S(1)} collective-permute-done((f32[256,128]{1,0:T(8,128)S(1)}, f32[256,128]{1,0:T(8,128)S(1)}, u32[]{:S(2)}, u32[]{:S(2)}) %collective-permute-start.11) | collective-permute-done | bytes 131104 | tf_op jit(solution)/shard_map/ppermute | solution.py:24
  83.8 3.8 %collective-permute-done.12.refs_4_ = f32[256,128]{1,0:T(8,128)S(1)} collective-permute-done((f32[256,128]{1,0:T(8,128)S(1)}, f32[256,128]{1,0:T(8,128)S(1)}, u32[]{:S(2)}, u32[]{:S(2)}) %collective-permute-start.12) | collective-permute-done | bytes 131104 | tf_op jit(solution)/shard_map/ppermute | solution.py:24
  87.6 1.8 %shard_map.81.refs_0_ = f32[5,128,128]{2,1,0:T(8,128)S(1)} custom-call(f32[2,1,2048,128]{3,2,1,0:T(8,128)S(1)} %copy-done, f32[2,4,256,128]{3,2,1,0:T(8,128)S(1)} %collective-permute-done.refs_1_, f32[256,128]{1,0:T(8,128)S(1)} %add_add_fusion.refs_2_, f32[256,128]{1,0:T(8,128)S(1)} %collective-permute-done.11.refs_3_, ...), custom_call_target="tpu_custom_call" | custom-call | tf_op jit(solution)/shard_map/pallas_call | solution.py:102
  89.5 1.6 %collective-permute-done.14.refs_1_ = f32[5,128,128]{2,1,0:T(8,128)S(1)} collective-permute-done((f32[5,128,128]{2,1,0:T(8,128)S(1)}, f32[5,128,128]{2,1,0:T(8,128)S(1)}, u32[]{:S(2)}, u32[]{:S(2)}) %collective-permute-start.14) | collective-permute-done | bytes 327712 | tf_op jit(solution)/shard_map/ppermute | solution.py:24
  91.1 2.3 %collective-permute-done.19.refs_9_ = f32[4,256,128]{2,1,0:T(8,128)S(1)} collective-permute-done((f32[4,256,128]{2,1,0:T(8,128)S(1)}, f32[4,256,128]{2,1,0:T(8,128)S(1)}, u32[]{:S(2)}, u32[]{:S(2)}) %collective-permute-start.19) | collective-permute-done | bytes 524320 | tf_op jit(solution)/shard_map/ppermute | solution.py:281
  93.4 2.4 %shard_map.83 = (f32[256,128]{1,0:T(8,128)S(1)}, f32[256,128]{1,0:T(8,128)S(1)}, f32[256,128]{1,0:T(8,128)S(1)}, f32[256,128]{1,0:T(8,128)S(1)}) custom-call(f32[5,128,128]{2,1,0:T(8,128)S(1)} %shard_map.81.refs_0_, f32[5,128,128]{2,1,0:T(8,128)S(1)} %collective-permute-done.14.refs_1_, f32[4,128,128]{2,1,0:T(8,128)S(1)} %copy-done.2, ...), custom_call_target="tpu_custom_call" | custom-call | tf_op jit(solution)/shard_map/pallas_call | solution.py:102
  95.9 1.5 %collective-permute-start.20 = (f32[256,128]{1,0:T(8,128)S(1)}, f32[256,128]{1,0:T(8,128)S(1)}, u32[]{:S(2)}, u32[]{:S(2)}) collective-permute-start(f32[256,128]{1,0:T(8,128)S(1)} %get-tuple-element.38), channel_id=1, source_target_pairs={{0,8},{4,12},{8,0},{12,4},{16,24},{20,28},{24,16},{28,20},{1,9},{5... | collective-permute-start | bytes 393224 | tf_op jit(solution)/shard_map/ppermute | solution.py:24
  99.4 13.0 %shard_map.82 = (f32[256,128]{1,0:T(8,128)}, f32[128,128]{1,0:T(8,128)S(1)}) custom-call(f32[5,128,128]{2,1,0:T(8,128)S(1)} %shard_map.81.refs_0_, f32[5,128,128]{2,1,0:T(8,128)S(1)} %collective-permute-done.14.refs_1_, f32[256,128]{1,0:T(8,128)S(1)} %add_add_fusion.refs_2_), custom_call_target="tpu_custom_call" | custom-call | flops 1000000000 | tf_op jit(solution)/shard_map/pallas_call | solution.py:102
  (46 shorter events, 14.1 us)
Async XLA Ops:
  0.6 7.8 %copy-start.4 = (f32[2,512,128]{2,1,0:T(8,128)S(1)}, f32[2,512,128]{2,1,0:T(8,128)}, u32[]{:S(2)}) copy-start(f32[2,512,128]{2,1,0:T(8,128)} %refs_1_.1) | copy-start | bytes 1572868
  0.6 8.6 %copy-start = (f32[2,1,2048,128]{3,2,1,0:T(8,128)S(1)}, f32[2,1,2048,128]{3,2,1,0:T(8,128)}, u32[]{:S(2)}) copy-start(f32[2,1,2048,128]{3,2,1,0:T(8,128)} %refs_0_.5) | copy-start | bytes 6291460
  3.8 18.1 %collective-permute-start.1 = (f32[2,640,128]{2,1,0:T(8,128)}, f32[2,640,128]{2,1,0:T(8,128)}, u32[]{:S(2)}, u32[]{:S(2)}) collective-permute-start(f32[2,640,128]{2,1,0:T(8,128)} %shard_map.77.refs_2_), channel_id=1, source_target_pairs={{0,1},{1,0},{2,3},{3,2},{4,5},{5,4},{6,7},{7,6},{8,9},{9,8},{10,11... | collective-permute-start | bytes 1966088 | tf_op jit(solution)/shard_map/ppermute | solution.py:281
  6.9 16.5 %collective-permute-start.2 = (f32[2,640,128]{2,1,0:T(8,128)}, f32[2,640,128]{2,1,0:T(8,128)}, u32[]{:S(2)}, u32[]{:S(2)}) collective-permute-start(f32[2,640,128]{2,1,0:T(8,128)} %shard_map.77.refs_2_), channel_id=1, source_target_pairs={{1,2},{2,1},{5,6},{6,5},{9,10},{10,9},{13,14},{14,13},{17,18},{18,... | collective-permute-start | bytes 1966088 | tf_op jit(solution)/shard_map/ppermute | solution.py:281
  9.2 3.5 %collective-permute-start.3 = (f32[2,256,128]{2,1,0:T(8,128)}, f32[2,256,128]{2,1,0:T(8,128)}, u32[]{:S(2)}, u32[]{:S(2)}) collective-permute-start(f32[2,256,128]{2,1,0:T(8,128)} %get-tuple-element.43), channel_id=1, source_target_pairs={{0,4},{4,0},{8,12},{12,8},{16,20},{20,16},{24,28},{28,24},{1,5},{5... | collective-permute-start | bytes 786440 | tf_op jit(solution)/shard_map/ppermute | solution.py:24
  10.2 52.3 %collective-permute-start = (f32[2,4,256,128]{3,2,1,0:T(8,128)}, f32[2,4,256,128]{3,2,1,0:T(8,128)S(1)}, u32[]{:S(2)}, u32[]{:S(2)}) collective-permute-start(f32[2,4,256,128]{3,2,1,0:T(8,128)} %dynamic-slice_bitcast_fusion), channel_id=1, source_target_pairs={{0,4},{4,0},{8,12},{12,8},{16,20},{20,16},{24,28},{28,24},{1,5},{5... | collective-permute-start | bytes 3145736 | tf_op jit(solution)/shard_map/ppermute | solution.py:24
  10.8 12.7 %copy-start.3 = (f32[2,1,2048,128]{3,2,1,0:T(8,128)S(1)}, f32[2,1,2048,128]{3,2,1,0:T(8,128)}, u32[]{:S(2)}) copy-start(f32[2,1,2048,128]{3,2,1,0:T(8,128)} %param.7) | copy-start | bytes 6291460
  22.0 20.3 %collective-permute-start.4 = (f32[2,640,128]{2,1,0:T(8,128)}, f32[2,640,128]{2,1,0:T(8,128)}, u32[]{:S(2)}, u32[]{:S(2)}) collective-permute-start(f32[2,640,128]{2,1,0:T(8,128)} %collective-permute-done.1.refs_3_), channel_id=1, source_target_pairs={{1,2},{2,1},{5,6},{6,5},{9,10},{10,9},{13,14},{14,13},{17,18},{18,... | collective-permute-start | bytes 1966088 | tf_op jit(solution)/shard_map/ppermute | solution.py:281
  25.4 16.9 %collective-permute-start.5 = (f32[2,512,128]{2,1,0:T(8,128)}, f32[2,512,128]{2,1,0:T(8,128)}, u32[]{:S(2)}, u32[]{:S(2)}) collective-permute-start(f32[2,512,128]{2,1,0:T(8,128)} %bitcast_select_fusion), channel_id=1, source_target_pairs={{0,1},{1,0},{2,3},{3,2},{4,5},{5,4},{6,7},{7,6},{8,9},{9,8},{10,11... | collective-permute-start | bytes 1572872 | tf_op jit(solution)/shard_map/ppermute | solution.py:281
  33.1 27.4 %collective-permute-start.15 = (f32[4,256,128]{2,1,0:T(8,128)}, f32[4,256,128]{2,1,0:T(8,128)}, u32[]{:S(2)}, u32[]{:S(2)}) collective-permute-start(f32[4,256,128]{2,1,0:T(8,128)} %pad_maximum_fusion.refs_4_), channel_id=1, source_target_pairs={{0,1},{1,0},{2,3},{3,2},{4,5},{5,4},{6,7},{7,6},{8,9},{9,8},{10,11... | collective-permute-start | bytes 1572872 | tf_op jit(solution)/shard_map/ppermute | solution.py:281
  33.1 27.4 %collective-permute-start.16 = (f32[4,256,128]{2,1,0:T(8,128)}, f32[4,256,128]{2,1,0:T(8,128)}, u32[]{:S(2)}, u32[]{:S(2)}) collective-permute-start(f32[4,256,128]{2,1,0:T(8,128)} %pad_maximum_fusion.refs_4_), channel_id=1, source_target_pairs={{1,2},{2,1},{5,6},{6,5},{9,10},{10,9},{13,14},{14,13},{17,18},{18,... | collective-permute-start | bytes 1572872 | tf_op jit(solution)/shard_map/ppermute | solution.py:281
  36.5 11.7 %copy-start.6 = (s32[2,1]{0,1:T(1,128)S(1)}, s32[2,1]{0,1:T(1,128)}, u32[]{:S(2)}) copy-start(s32[2,1]{0,1:T(1,128)} %param.11) | copy-start | bytes 28
  46.0 11.0 %collective-permute-start.6 = (f32[4,128,128]{2,1,0:T(8,128)}, f32[4,128,128]{2,1,0:T(8,128)S(1)}, u32[]{:S(2)}, u32[]{:S(2)}) collective-permute-start(f32[4,128,128]{2,1,0:T(8,128)} %get-tuple-element.24.refs_1_), channel_id=1, source_target_pairs={{0,1},{1,0},{2,3},{3,2},{4,5},{5,4},{6,7},{7,6},{8,9},{9,8},{10,11... | collective-permute-start | bytes 786440 | tf_op jit(solution)/shard_map/ppermute | solution.py:281
  57.0 0.7 copy-start.5
  60.5 2.1 %collective-permute-start.7 = (f32[4,128,128]{2,1,0:T(8,128)}, f32[4,128,128]{2,1,0:T(8,128)S(1)}, u32[]{:S(2)}, u32[]{:S(2)}) collective-permute-start(f32[4,128,128]{2,1,0:T(8,128)} %shard_map.79.refs_2_), channel_id=1, source_target_pairs={{0,4},{4,0},{8,12},{12,8},{16,20},{20,16},{24,28},{28,24},{1,5},{5... | collective-permute-start | bytes 786440 | tf_op jit(solution)/shard_map/ppermute | solution.py:24
  60.6 16.4 %collective-permute-start.17 = (f32[4,256,128]{2,1,0:T(8,128)}, f32[4,256,128]{2,1,0:T(8,128)S(1)}, u32[]{:S(2)}, u32[]{:S(2)}) collective-permute-start(f32[4,256,128]{2,1,0:T(8,128)} %collective-permute-done.16.refs_6_), channel_id=1, source_target_pairs={{1,0},{2,3},{5,4},{6,7},{9,8},{10,11},{13,12},{14,15},{17,16},{18,... | collective-permute-start | bytes 1572872 | tf_op jit(solution)/shard_map/ppermute | solution.py:281
  61.9 15.1 %collective-permute-start.18 = (f32[4,256,128]{2,1,0:T(8,128)}, f32[4,256,128]{2,1,0:T(8,128)S(1)}, u32[]{:S(2)}, u32[]{:S(2)}) collective-permute-start(f32[4,256,128]{2,1,0:T(8,128)} %collective-permute-done.15.refs_5_), channel_id=1, source_target_pairs={{1,2},{2,1},{5,6},{6,5},{9,10},{10,9},{13,14},{14,13},{17,18},{18,... | collective-permute-start | bytes 1572872 | tf_op jit(solution)/shard_map/ppermute | solution.py:281
  62.6 1.0 copy-start.1
  65.0 7.3 %collective-permute-start.10 = (f32[256,128]{1,0:T(8,128)S(1)}, f32[256,128]{1,0:T(8,128)S(1)}, u32[]{:S(2)}, u32[]{:S(2)}) collective-permute-start(f32[256,128]{1,0:T(8,128)S(1)} %get-tuple-element.29), channel_id=1, source_target_pairs={{0,24},{4,28},{8,16},{12,20},{16,8},{20,12},{24,0},{28,4},{1,25},{... | collective-permute-start | bytes 393224 | tf_op jit(solution)/shard_map/ppermute | solution.py:24
  67.6 7.2 %collective-permute-start.8 = (f32[256,128]{1,0:T(8,128)S(1)}, f32[256,128]{1,0:T(8,128)S(1)}, u32[]{:S(2)}, u32[]{:S(2)}) collective-permute-start(f32[256,128]{1,0:T(8,128)S(1)} %get-tuple-element.27), channel_id=1, source_target_pairs={{0,8},{4,12},{8,0},{12,4},{16,24},{20,28},{24,16},{28,20},{1,9},{5... | collective-permute-start | bytes 393224 | tf_op jit(solution)/shard_map/ppermute | solution.py:24
  68.1 6.7 %collective-permute-start.9 = (f32[256,128]{1,0:T(8,128)S(1)}, f32[256,128]{1,0:T(8,128)S(1)}, u32[]{:S(2)}, u32[]{:S(2)}) collective-permute-start(f32[256,128]{1,0:T(8,128)S(1)} %get-tuple-element.28), channel_id=1, source_target_pairs={{0,16},{4,20},{8,24},{12,28},{16,0},{20,4},{24,8},{28,12},{1,17},{... | collective-permute-start | bytes 393224 | tf_op jit(solution)/shard_map/ppermute | solution.py:24
  74.8 18.6 %copy-start.2 = (f32[4,128,128]{2,1,0:T(8,128)S(1)}, f32[4,128,128]{2,1,0:T(8,128)}, u32[]{:S(2)}) copy-start(f32[4,128,128]{2,1,0:T(8,128)} %shard_map.79.refs_2_) | copy-start | bytes 786436
  77.0 16.4 %collective-permute-start.19 = (f32[4,256,128]{2,1,0:T(8,128)S(1)}, f32[4,256,128]{2,1,0:T(8,128)S(1)}, u32[]{:S(2)}, u32[]{:S(2)}) collective-permute-start(f32[4,256,128]{2,1,0:T(8,128)S(1)} %collective-permute-done.18.refs_7_), channel_id=1, source_target_pairs={{1,0},{2,3},{5,4},{6,7},{9,8},{10,11},{13,12},{14,15},{17,16},{18,... | collective-permute-start | bytes 1572872 | tf_op jit(solution)/shard_map/ppermute | solution.py:281
  78.3 5.6 %collective-permute-start.11 = (f32[256,128]{1,0:T(8,128)S(1)}, f32[256,128]{1,0:T(8,128)S(1)}, u32[]{:S(2)}, u32[]{:S(2)}) collective-permute-start(f32[256,128]{1,0:T(8,128)S(1)} %add_add_fusion.refs_2_), channel_id=1, source_target_pairs={{0,8},{4,12},{8,0},{12,4},{16,24},{20,28},{24,16},{28,20},{1,9},{5... | collective-permute-start | bytes 393224 | tf_op jit(solution)/shard_map/ppermute | solution.py:24
  79.8 7.8 %collective-permute-start.12 = (f32[256,128]{1,0:T(8,128)S(1)}, f32[256,128]{1,0:T(8,128)S(1)}, u32[]{:S(2)}, u32[]{:S(2)}) collective-permute-start(f32[256,128]{1,0:T(8,128)S(1)} %add_add_fusion.refs_2_), channel_id=1, source_target_pairs={{0,16},{4,20},{8,24},{12,28},{16,0},{20,4},{24,8},{28,12},{1,17},{... | collective-permute-start | bytes 393224 | tf_op jit(solution)/shard_map/ppermute | solution.py:24
  81.4 6.3 %collective-permute-start.13 = (f32[256,128]{1,0:T(8,128)S(1)}, f32[256,128]{1,0:T(8,128)S(1)}, u32[]{:S(2)}, u32[]{:S(2)}) collective-permute-start(f32[256,128]{1,0:T(8,128)S(1)} %add_add_fusion.refs_2_), channel_id=1, source_target_pairs={{0,24},{4,28},{8,16},{12,20},{16,8},{20,12},{24,0},{28,4},{1,25},{... | collective-permute-start | bytes 393224 | tf_op jit(solution)/shard_map/ppermute | solution.py:24
  89.4 1.7 %collective-permute-start.14 = (f32[5,128,128]{2,1,0:T(8,128)S(1)}, f32[5,128,128]{2,1,0:T(8,128)S(1)}, u32[]{:S(2)}, u32[]{:S(2)}) collective-permute-start(f32[5,128,128]{2,1,0:T(8,128)S(1)} %shard_map.81.refs_0_), channel_id=1, source_target_pairs={{0,4},{4,0},{8,12},{12,8},{16,20},{20,16},{24,28},{28,24},{1,5},{5... | collective-permute-start | bytes 983048 | tf_op jit(solution)/shard_map/ppermute | solution.py:24
  95.9 16.6 %collective-permute-start.20 = (f32[256,128]{1,0:T(8,128)S(1)}, f32[256,128]{1,0:T(8,128)S(1)}, u32[]{:S(2)}, u32[]{:S(2)}) collective-permute-start(f32[256,128]{1,0:T(8,128)S(1)} %get-tuple-element.38), channel_id=1, source_target_pairs={{0,8},{4,12},{8,0},{12,4},{16,24},{20,28},{24,16},{28,20},{1,9},{5... | collective-permute-start | bytes 393224 | tf_op jit(solution)/shard_map/ppermute | solution.py:24
  97.4 15.0 %collective-permute-start.21 = (f32[256,128]{1,0:T(8,128)S(1)}, f32[256,128]{1,0:T(8,128)S(1)}, u32[]{:S(2)}, u32[]{:S(2)}) collective-permute-start(f32[256,128]{1,0:T(8,128)S(1)} %get-tuple-element.39), channel_id=1, source_target_pairs={{0,16},{4,20},{8,24},{12,28},{16,0},{20,4},{24,8},{28,12},{1,17},{... | collective-permute-start | bytes 393224 | tf_op jit(solution)/shard_map/ppermute | solution.py:24
  98.4 14.0 %collective-permute-start.22 = (f32[256,128]{1,0:T(8,128)S(1)}, f32[256,128]{1,0:T(8,128)S(1)}, u32[]{:S(2)}, u32[]{:S(2)}) collective-permute-start(f32[256,128]{1,0:T(8,128)S(1)} %get-tuple-element.40), channel_id=1, source_target_pairs={{0,24},{4,28},{8,16},{12,20},{16,8},{20,12},{24,0},{28,4},{1,25},{... | collective-permute-start | bytes 393224 | tf_op jit(solution)/shard_map/ppermute | solution.py:24

commit v5 on v2

--- a/solution.py
+++ b/solution.py
@@ -82,11 +82,12 @@
         out_specs=[pl.BlockSpec(memory_space=pltpu.VMEM) for _ in shapes],
         scratch_shapes=list(scratch),
         compiler_params=pltpu.CompilerParams(vmem_limit_bytes=24 << 20),
-        cost_estimate=pl.CostEstimate(flops=cost, bytes_accessed=1 << 20, transcendentals=0),
+        cost_estimate=pl.CostEstimate(flops=cost, bytes_accessed=0, transcendentals=0),
     )(*args)
 
 
-def core_kernel(planes, part, own_rows, first, second, core, lent):
+def core_kernel(planes, part, own_rows, first, second, probe_far, core, lent):
+    lent[pl.ds(2, 2)] = probe_far[...]
     plane = lax.axis_index("tile")
     is_end = jnp.logical_or(plane == 0, plane == planes - 1)
 
@@ -94,7 +95,7 @@
     def _():
         for k in range(2):
             core[k] = part[k] + dot3(own_rows[k], second[k], TN)
-            lent[k] = jnp.zeros_like(lent[k])
+            lent[k] = jnp.zeros_like(core[k])
 
     @pl.when(jnp.logical_not(is_end))
     def _():
@@ -159,7 +160,7 @@
 
 
 def w_kernel(planes, sent, got, both, both_other, own, near, inner, inner_far, outer, last, *rest):
-    *outs, gram, held, sems = rest
+    *outs, held, sems = rest
     plane = lax.axis_index("tile")
     chip = lax.axis_index("step") // 2
     is_end = jnp.logical_or(plane == 0, plane == planes - 1)
@@ -178,7 +179,6 @@
         pick(i, jnp.logical_and(apart == 2, jnp.logical_not(is_end)), inner_far)
         pick(i, jnp.logical_and(apart == 3, is_end), last)
         pick(i, jnp.logical_and(apart == 3, jnp.logical_not(is_end)), inner)
-    gram[...] = sent[4] + got[4]
     returned = []
     for k in range(2):
         returned.append(dot3(sent[2 + k] + got[k], both[2 + k], NN))
@@ -190,26 +190,32 @@
         out[...] = dot3(jnp.concatenate([held[i, k] for k in range(4)], 1), returned, NT)
 
 
-def basis_kernel(tile_rows, width, gram, y_rows, basis, inverse):
-    rank = gram.shape[0]
-    scaled = gram[...] * (1.0 / tile_rows)
-    eye = (lax.broadcasted_iota(jnp.int32, (rank, rank), 0) == lax.broadcasted_iota(jnp.int32, (rank, rank), 1))
-    work = jnp.concatenate([scaled, eye.astype(jnp.float32)], 1)
+def basis_kernel(tile_rows, width, group, sent, got, y_rows, basis, inverse):
+    rank = inverse.shape[0]
+    left = (sent[4] + got[4]) * (1.0 / tile_rows)
+    index = lax.broadcasted_iota(jnp.int32, (rank, rank), 0)
+    right = (index == lax.broadcasted_iota(jnp.int32, (rank, rank), 1)).astype(jnp.float32)
+    row_index = lax.broadcasted_iota(jnp.int32, (width, rank), 0)
     done = []
     for begin in range(0, rank, width):
-        panel = work[:width]
-        row_index = lax.broadcasted_iota(jnp.int32, (width, 1), 0)
-        scale = jnp.zeros((width, 1), jnp.float32)
-        for j in range(width):
-            column = panel[:, begin + j:begin + j + 1]
-            pivot = panel[j:j + 1, begin + j:begin + j + 1]
-            factor = jnp.where(row_index > j, column * (1.0 / pivot), 0.0)
-            scale = jnp.where(row_index == j, lax.rsqrt(pivot), scale)
-            panel = panel - factor * panel[j:j + 1]
-        panel = panel * scale
-        done.append(panel[:, rank:])
+        l, r = left[:width], right[:width]
+        scale = jnp.zeros((width, rank), jnp.float32)
+        for first in range(0, width, group):
+            place = begin + first
+            columns = [jnp.broadcast_to(l[:, place + c:place + c + 1], (width, rank)) for c in range(group)]
+            for c in range(group):
+                j = first + c
+                pivot = columns[c][j:j + 1]
+                scale = jnp.where(row_index == j, lax.rsqrt(pivot), scale)
+                factor = jnp.where(row_index > j, columns[c] * (1.0 / pivot), 0.0)
+                for d in range(c + 1, group):
+                    columns[d] = columns[d] - factor * columns[d][j:j + 1]
+                l, r = l - factor * l[j:j + 1], r - factor * r[j:j + 1]
+        l, r = l * scale, r * scale
+        done.append(r)
         if begin + width < rank:
-            work = work[width:] - dot_full(panel[:, begin + width:rank], panel, TN)
+            both = dot_full(l[:, begin + width:], jnp.concatenate([l, r], 1), TN)
+            left, right = left[width:] - both[:, :rank], right[width:] - both[:, rank:]
     lower_inverse = jnp.concatenate(done, 0)
     inverse[...] = lower_inverse
     basis[...] = dot_full(y_rows[...], lower_inverse, NT)
@@ -246,27 +252,28 @@
 
     inner_far = across(near, inner_pairs)
     outer = across(jnp.where(is_end, block(planes - 1 - plane), inner), outer_pairs)
-    probes_far = across(probes, inner_pairs)
     part = (
         mm("kbr,kbq->krq", block(plane), column_right)
         + mm("kbr,kbq->krq", block(plane ^ 1), near)
         + mm("kbr,kbq->krq", block(jnp.where(is_end, plane, planes - 1 - plane)), inner)
     )
+    _, probes_held = lax.optimization_barrier((near, probes))
+    probes_far = across(probes_held, inner_pairs)
     far_rows = block(plane ^ 2)
-    core, lent = call(functools.partial(core_kernel, planes), [(2, rank, rank)] * 2, [part, far_rows, inner_far, outer])
-    lent = across(jnp.concatenate([lent, probes_far]), outward)
+    core, lent = call(functools.partial(core_kernel, planes), [(2, rank, rank), (4, rank, rank)], [part, far_rows, inner_far, outer, probes_far])
+    lent = across(lent, outward)
 
     left_split = target_left.reshape(2, chips, 2, row_count, rank)
     left_other = exchange(take(left_split, 1 - core_bit, 2), "step", 1)
     col_split = column_left.reshape(2, 2, row_count, rank)
     col_half = jnp.concatenate([take(col_split, core_bit, 1), exchange(take(col_split, 1 - core_bit, 1), "step", 1)])
-    col_half, _ = lax.optimization_barrier((col_half, near))
-    col_near = across(col_half, outer_pairs)
-    col_inner = across(col_half, inner_pairs)
+    _, col_held = lax.optimization_barrier((near, col_half))
+    col_near = across(col_held, outer_pairs)
+    col_inner = across(col_held, inner_pairs)
+    col_near, col_inner = lax.optimization_barrier((col_near, col_inner))
     col_inner_far = across(col_near, inner_pairs)
     col_outer = across(col_inner, outward)
-    col_last = across(col_inner_far, outward)
-
+    col_inner_far, col_outer = lax.optimization_barrier((col_inner_far, col_outer))
     (both,) = call(reduced_kernel, [(4, rank, rank)], [core, lent, probes, probes_far, pattern], "vvvvs")
     both_other = exchange(both, "step", 1)
     rows_scratch = [pltpu.VMEM((chips, 4, row_count, rank), jnp.float32), pltpu.SemaphoreType.DMA((2 * chips,))]
@@ -275,18 +282,20 @@
     for bit in range(1, chips):
         y_rows = y_rows + exchange(y_parts[bit], "step", 2 * bit)
     y_all = [y_rows] + [exchange(y_rows, "step", 2 * bit) for bit in range(1, chips)]
+    _, col_last = lax.optimization_barrier((y_rows, col_inner_far))
+    col_last = across(col_last, outward)
     (sent,) = call(z_kernel, [(5, rank, rank)], [target_left, left_other, *y_all], "aa" + "v" * chips, rows_scratch)
     got = exchange(sent, "step", 1)
-    *w_parts, gram = call(
+    w_parts = call(
         functools.partial(w_kernel, planes),
-        [(row_count, rank)] * planes + [(rank, rank)],
+        [(row_count, rank)] * planes,
         [sent, got, both, both_other, col_half, col_near, col_inner, col_inner_far, col_outer, col_last],
         "vvvvaaaaaa",
         [pltpu.VMEM((planes, 4, row_count, rank), jnp.float32), pltpu.SemaphoreType.DMA((planes,))],
     )
     w_got = [exchange(w_parts[bit], "step", 2 * bit) for bit in range(1, chips)]
     basis, inverse = call(
-        functools.partial(basis_kernel, tile_rows, 32), [(row_count, rank), (rank, rank)], [gram, y_rows], cost=10**9
+        functools.partial(basis_kernel, tile_rows, 32, 16), [(row_count, rank), (rank, rank)], [sent, got, y_rows], cost=10**9
     )
     (factor,) = call(functools.partial(factor_kernel, tile_rows), [(row_count, rank)], [w_parts[0], *w_got, inverse])
     return basis[None], factor[None]

time: 111 us -> 99 us (0.89)
  Pallas kernels: 21.1 us -> 12.9 us
  waiting for transfers between devices: 34.2 us -> 32.4 us
  other arithmetic: 3.6 us -> 2.01 us
    pallas_call x7, Pallas kernels: 21.1 us -> 12.9 us  [call(): pl.pallas_call(kernel, out_shape=shapes, in_specs=[pl.BlockSpec(memory_sp...]
    ppermute x12, waiting for transfers between devices: 23.4 us -> 18.5 us  [across(): return lax.ppermute(array, 'tile', pairs)]
    ppermute x13, waiting for transfers between devices: 10.7 us -> 13.9 us  [exchange(): lax.ppermute(array, axis, [(i, i ^ bit) for i in range(lax.axis_size(axis...]
    unnamed x25 -> x27, local copies, waits for them, and re-layouts: 2.61 us -> 2.61 us
  transfers between devices with their start and end apart: 25 -> 25, of which waited for: 11 -> 14; matrix products, arithmetic and copies ran while one was open for 15% -> 15% of each run, Pallas kernels for 16% -> 10%
where the time goes in v5:
time: 99 us; the launch traced here: 98.3 us
  starting transfers between devices  35 us (35%)
  waiting for transfers between devices  32.4 us (33%)
  Pallas kernels  12.9 us (13%)
  local copies, waits for them, and re-layouts  7.61 us (8%)
  matrix products  7.5 us (8%)
  other arithmetic  2.01 us (2%)
    ppermute x12, starting transfers between devices, across(): return lax.ppermute(array, 'tile', pairs)  24 us
    ppermute x12, waiting for transfers between devices, across(): return lax.ppermute(array, 'tile', pairs)  18.5 us
    ppermute x13, waiting for transfers between devices, exchange(): lax.ppermute(array, axis, [(i, i ^ bit) for i in range(lax.axis_size(axis...  13.9 us
    pallas_call x7, Pallas kernels, call(): pl.pallas_call(kernel, out_shape=shapes, in_specs=[pl.BlockSpec(memory_sp...  12.9 us
    ppermute x13, starting transfers between devices, exchange(): lax.ppermute(array, axis, [(i, i ^ bit) for i in range(lax.axis_size(axis...  11 us
    dot_general x4, matrix products, mm(): jnp.einsum(spec, *arrays, precision=HIGH, preferred_element_type=jnp.floa...  7.5 us
    squeeze x3, local copies, waits for them, and re-layouts, take(): return lax.dynamic_index_in_dim(array, index, axis, keepdims=False)  5 us
    unnamed x27, local copies, waits for them, and re-layouts  2.61 us
  transfers between devices with their start and end apart: 25, of which 14 were waited for; matrix products, arithmetic and copies ran while one was open for 15% of the time, Pallas kernels for 10%

profile of v5, /device:TPU:0, one launch (start us, length us, event | category | flops | bytes accessed | tf_op | source)
XLA Modules:
  0.0 98.3 jit_solution(1887968758495125927)
XLA Ops:
  0.7 3.1 %collective-permute-start.1 = (f32[2,512,128]{2,1,0:T(8,128)}, f32[2,512,128]{2,1,0:T(8,128)}, u32[]{:S(2)}, u32[]{:S(2)}) collective-permute-start(f32[2,512,128]{2,1,0:T(8,128)} %param.9), channel_id=1, source_target_pairs={{0,1},{1,0},{2,3},{3,2},{4,5},{5,4},{6,7},{7,6},{8,9},{9,8},{10,11... | collective-permute-start | bytes 1572872 | tf_op jit(solution)/shard_map/ppermute | solution.py:242
  3.7 1.5 %collective-permute-start.2 = (f32[2,512,128]{2,1,0:T(8,128)}, f32[2,512,128]{2,1,0:T(8,128)}, u32[]{:S(2)}, u32[]{:S(2)}) collective-permute-start(f32[2,512,128]{2,1,0:T(8,128)} %param.9), channel_id=1, source_target_pairs={{1,2},{2,1},{5,6},{6,5},{9,10},{10,9},{13,14},{14,13},{17,18},{18,... | collective-permute-start | bytes 1572872 | tf_op jit(solution)/shard_map/ppermute | solution.py:242
  5.2 2.3 %dynamic-slice_bitcast_fusion = f32[2,4,256,128]{3,2,1,0:T(8,128)} fusion(f32[2,4,2,256,128]{4,3,2,1,0:T(8,128)} %bitcast.44, s32[]{:T(128)S(6)} %select_n.44), kind=kLoop, calls=%fused_computation.2 | loop fusion | bytes 2097156 | tf_op jit(solution)/shard_map/jit(dynamic_index_in_dim)/squeeze | solution.py:28
  7.5 1.6 %fusion.7 = f32[2,128,128]{2,1,0:T(8,128)S(1)} fusion(f32[2,512,128]{2,1,0:T(8,128)} %param.8, f32[512,128]{1,0:T(8,128)S(1)} %copy-done), kind=kOutput, calls=%fused_computation.13 | convolution fusion | flops 100663296 | bytes 917504 | tf_op jit(solution)/shard_map/kbq,bp->kqp/dot_general | solution.py:14
  9.1 3.7 %collective-permute-start.5 = (f32[2,128,128]{2,1,0:T(8,128)S(1)}, f32[2,128,128]{2,1,0:T(8,128)}, u32[]{:S(2)}, u32[]{:S(2)}) collective-permute-start(f32[2,128,128]{2,1,0:T(8,128)S(1)} %fusion.7), channel_id=1, source_target_pairs={{0,1},{1,0},{2,3},{3,2},{4,5},{5,4},{6,7},{7,6},{8,9},{9,8},{10,11... | collective-permute-start | bytes 393224 | tf_op jit(solution)/shard_map/ppermute | solution.py:242
  12.8 1.9 %dynamic-slice_bitcast_fusion.3 = (f32[2,256,128]{2,1,0:T(8,128)}, f32[2,256,128]{2,1,0:T(8,128)}) fusion(f32[2,2,256,128]{3,2,1,0:T(8,128)} %bitcast.50, s32[]{:T(128)S(6)} %select_n.53, s32[]{:T(128)S(6)} %select_n.44), kind=kLoop, calls=%fused_computation.16 | loop fusion | bytes 1048584 | tf_op jit(solution)/shard_map/jit(dynamic_index_in_dim)/squeeze | solution.py:28
  14.9 2.3 %fusion.2 = f32[2,128,128]{2,1,0:T(8,128)} fusion(f32[2,512,128]{2,1,0:T(8,128)} %param.9, f32[2,4,512,128]{3,2,1,0:T(8,128)S(1)} %bitcast.46, s32[]{:T(128)S(6)} %select_n.45), kind=kOutput, calls=%fused_computation.6 | convolution fusion | flops 100663296 | bytes 1179652 | tf_op jit(solution)/shard_map/kbr,kbq->krq/dot_general | solution.py:14
  20.5 5.7 %collective-permute-start.4 = (f32[2,512,128]{2,1,0:T(8,128)S(1)}, f32[2,512,128]{2,1,0:T(8,128)S(1)}, u32[]{:S(2)}, u32[]{:S(2)}) collective-permute-start(f32[2,512,128]{2,1,0:T(8,128)S(1)} %bitcast_select_fusion), channel_id=1, source_target_pairs={{0,1},{1,0},{2,3},{3,2},{4,5},{5,4},{6,7},{7,6},{8,9},{9,8},{10,11... | collective-permute-start | bytes 1572872 | tf_op jit(solution)/shard_map/ppermute | solution.py:242
  27.9 1.9 %collective-permute-start.17 = (f32[4,256,128]{2,1,0:T(8,128)S(1)}, f32[4,256,128]{2,1,0:T(8,128)}, u32[]{:S(2)}, u32[]{:S(2)}) collective-permute-start(f32[4,256,128]{2,1,0:T(8,128)S(1)} %pad_maximum_fusion.own), channel_id=1, source_target_pairs={{0,1},{1,0},{2,3},{3,2},{4,5},{5,4},{6,7},{7,6},{8,9},{9,8},{10,11... | collective-permute-start | bytes 1572872 | tf_op jit(solution)/shard_map/ppermute | solution.py:242
  29.8 1.4 %collective-permute-start.18 = (f32[4,256,128]{2,1,0:T(8,128)S(1)}, f32[4,256,128]{2,1,0:T(8,128)}, u32[]{:S(2)}, u32[]{:S(2)}) collective-permute-start(f32[4,256,128]{2,1,0:T(8,128)S(1)} %pad_maximum_fusion.own), channel_id=1, source_target_pairs={{1,2},{2,1},{5,6},{6,5},{9,10},{10,9},{13,14},{14,13},{17,18},{18,... | collective-permute-start | bytes 1572872 | tf_op jit(solution)/shard_map/ppermute | solution.py:242
  31.2 1.6 %convolution_add_fusion.1 = f32[2,128,128]{2,1,0:T(8,128)S(1)} fusion(f32[2,128,128]{2,1,0:T(8,128)S(1)} %copy-done.11, f32[2,512,128]{2,1,0:T(8,128)} %collective-permute-done.1, f32[2,4,512,128]{3,2,1,0:T(8,128)S(1)} %bitcast.49, s32[]{:T(128)S(6)} %select_n.46), kind=kOutput, calls=%fused_computation.1 | convolution fusion | flops 100696064 | bytes 1310724 | tf_op jit(solution)/shard_map/kbr,kbq->krq/dot_general | solution.py:14
  32.9 1.9 %convolution_add_fusion.part = f32[2,128,128]{2,1,0:T(8,128)S(1)} fusion(f32[2,128,128]{2,1,0:T(8,128)S(1)} %convolution_add_fusion.1, f32[2,512,128]{2,1,0:T(8,128)} %collective-permute-done.2, f32[2,4,512,128]{3,2,1,0:T(8,128)} %bitcast.45, s32[]{:T(128)S(6)} %select_n.48), kind=kOutput, calls=%fused_computation | convolution fusion | flops 100696064 | bytes 1310724 | tf_op jit(solution)/shard_map/kbr,kbq->krq/dot_general | solution.py:14
  34.8 4.2 %collective-permute-done.4.second = f32[2,512,128]{2,1,0:T(8,128)S(1)} collective-permute-done((f32[2,512,128]{2,1,0:T(8,128)S(1)}, f32[2,512,128]{2,1,0:T(8,128)S(1)}, u32[]{:S(2)}, u32[]{:S(2)}) %collective-permute-start.4) | collective-permute-done | bytes 524320 | tf_op jit(solution)/shard_map/ppermute | solution.py:242
  42.0 8.3 %collective-permute-done.17.near = f32[4,256,128]{2,1,0:T(8,128)} collective-permute-done((f32[4,256,128]{2,1,0:T(8,128)S(1)}, f32[4,256,128]{2,1,0:T(8,128)}, u32[]{:S(2)}, u32[]{:S(2)}) %collective-permute-start.17) | collective-permute-done | bytes 524320 | tf_op jit(solution)/shard_map/ppermute | solution.py:242
  50.4 1.5 %collective-permute-start.19 = (f32[4,256,128]{2,1,0:T(8,128)}, f32[4,256,128]{2,1,0:T(8,128)}, u32[]{:S(2)}, u32[]{:S(2)}) collective-permute-start(f32[4,256,128]{2,1,0:T(8,128)} %collective-permute-done.17.near), channel_id=1, source_target_pairs={{1,2},{2,1},{5,6},{6,5},{9,10},{10,9},{13,14},{14,13},{17,18},{18,... | collective-permute-start | bytes 1572872 | tf_op jit(solution)/shard_map/ppermute | solution.py:242
  57.0 1.5 %collective-permute-done.8.both_other = f32[4,128,128]{2,1,0:T(8,128)S(1)} collective-permute-done((f32[4,128,128]{2,1,0:T(8,128)S(1)}, f32[4,128,128]{2,1,0:T(8,128)S(1)}, u32[]{:S(2)}, u32[]{:S(2)}) %collective-permute-start.8) | collective-permute-done | bytes 262176 | tf_op jit(solution)/shard_map/ppermute | solution.py:24
  58.5 1.5 %shard_map.79 = (f32[256,128]{1,0:T(8,128)S(1)}, f32[256,128]{1,0:T(8,128)S(1)}, f32[256,128]{1,0:T(8,128)S(1)}, f32[256,128]{1,0:T(8,128)S(1)}) custom-call(f32[2,1,2048,128]{3,2,1,0:T(8,128)S(1)} %copy-done.1, f32[2,4,256,128]{3,2,1,0:T(8,128)S(1)} %collective-permute-done.left_other, f32[4,128,128]{2,1,0:T(8,128)S(1)} %shard_map.78.both, ...), custom_call_target="tpu_custom_call" | custom-call | tf_op jit(solution)/shard_map/pallas_call | solution.py:78
  59.9 2.5 %collective-permute-start.11 = (f32[256,128]{1,0:T(8,128)S(1)}, f32[256,128]{1,0:T(8,128)S(1)}, u32[]{:S(2)}, u32[]{:S(2)}) collective-permute-start(f32[256,128]{1,0:T(8,128)S(1)} %get-tuple-element.27), channel_id=1, source_target_pairs={{0,24},{4,28},{8,16},{12,20},{16,8},{20,12},{24,0},{28,4},{1,25},{... | collective-permute-start | bytes 393224 | tf_op jit(solution)/shard_map/ppermute | solution.py:24
  63.5 2.3 %collective-permute-done.20.outer = f32[4,256,128]{2,1,0:T(8,128)} collective-permute-done((f32[4,256,128]{2,1,0:T(8,128)}, f32[4,256,128]{2,1,0:T(8,128)}, u32[]{:S(2)}, u32[]{:S(2)}) %collective-permute-start.20) | collective-permute-done | bytes 524320 | tf_op jit(solution)/shard_map/ppermute | solution.py:242
  66.7 2.5 %collective-permute-done.10 = f32[256,128]{1,0:T(8,128)S(1)} collective-permute-done((f32[256,128]{1,0:T(8,128)S(1)}, f32[256,128]{1,0:T(8,128)S(1)}, u32[]{:S(2)}, u32[]{:S(2)}) %collective-permute-start.10) | collective-permute-done | bytes 131104 | tf_op jit(solution)/shard_map/ppermute | solution.py:24
  69.4 1.4 %collective-permute-start.21 = (f32[4,256,128]{2,1,0:T(8,128)}, f32[4,256,128]{2,1,0:T(8,128)S(1)}, u32[]{:S(2)}, u32[]{:S(2)}) collective-permute-start(f32[4,256,128]{2,1,0:T(8,128)} %collective-permute-done.19.inner_far), channel_id=1, source_target_pairs={{1,0},{2,3},{5,4},{6,7},{9,8},{10,11},{13,12},{14,15},{17,16},{18,... | collective-permute-start | bytes 1572872 | tf_op jit(solution)/shard_map/ppermute | solution.py:242
  70.8 1.6 %collective-permute-start.12 = (f32[256,128]{1,0:T(8,128)S(1)}, f32[256,128]{1,0:T(8,128)S(1)}, u32[]{:S(2)}, u32[]{:S(2)}) collective-permute-start(f32[256,128]{1,0:T(8,128)S(1)} %add_add_fusion.rest_0_.y_rows), channel_id=1, source_target_pairs={{0,8},{4,12},{8,0},{12,4},{16,24},{20,28},{24,16},{28,20},{1,9},{5... | collective-permute-start | bytes 393224 | tf_op jit(solution)/shard_map/ppermute | solution.py:24
  74.4 2.2 %collective-permute-done.12.rest_1_ = f32[256,128]{1,0:T(8,128)S(1)} collective-permute-done((f32[256,128]{1,0:T(8,128)S(1)}, f32[256,128]{1,0:T(8,128)S(1)}, u32[]{:S(2)}, u32[]{:S(2)}) %collective-permute-start.12) | collective-permute-done | bytes 131104 | tf_op jit(solution)/shard_map/ppermute | solution.py:24
  76.6 3.6 %collective-permute-done.13.rest_2_ = f32[256,128]{1,0:T(8,128)S(1)} collective-permute-done((f32[256,128]{1,0:T(8,128)S(1)}, f32[256,128]{1,0:T(8,128)S(1)}, u32[]{:S(2)}, u32[]{:S(2)}) %collective-permute-start.13) | collective-permute-done | bytes 131104 | tf_op jit(solution)/shard_map/ppermute | solution.py:24
  80.3 1.7 %shard_map.80.sent = f32[5,128,128]{2,1,0:T(8,128)S(1)} custom-call(f32[2,1,2048,128]{3,2,1,0:T(8,128)S(1)} %copy-done.1, f32[2,4,256,128]{3,2,1,0:T(8,128)S(1)} %collective-permute-done.left_other, f32[256,128]{1,0:T(8,128)S(1)} %add_add_fusion.rest_0_.y_rows, f32[256,128]{1,0:T(8,128)S(1)} %collective-permute-done.12.rest_1_, ...), custom_call_target="tpu_custom_call" | custom-call | tf_op jit(solution)/shard_map/pallas_call | solution.py:78
  82.1 1.6 %collective-permute-done.15.got = f32[5,128,128]{2,1,0:T(8,128)S(1)} collective-permute-done((f32[5,128,128]{2,1,0:T(8,128)S(1)}, f32[5,128,128]{2,1,0:T(8,128)S(1)}, u32[]{:S(2)}, u32[]{:S(2)}) %collective-permute-start.15) | collective-permute-done | bytes 327712 | tf_op jit(solution)/shard_map/ppermute | solution.py:24
  83.7 2.3 %collective-permute-done.21.last = f32[4,256,128]{2,1,0:T(8,128)S(1)} collective-permute-done((f32[4,256,128]{2,1,0:T(8,128)}, f32[4,256,128]{2,1,0:T(8,128)S(1)}, u32[]{:S(2)}, u32[]{:S(2)}) %collective-permute-start.21) | collective-permute-done | bytes 524320 | tf_op jit(solution)/shard_map/ppermute | solution.py:242
  86.0 2.1 %shard_map.82 = (f32[256,128]{1,0:T(8,128)S(1)}, f32[256,128]{1,0:T(8,128)S(1)}, f32[256,128]{1,0:T(8,128)S(1)}, f32[256,128]{1,0:T(8,128)S(1)}) custom-call(f32[5,128,128]{2,1,0:T(8,128)S(1)} %shard_map.80.sent, f32[5,128,128]{2,1,0:T(8,128)S(1)} %collective-permute-done.15.got, f32[4,128,128]{2,1,0:T(8,128)S(1)} %shard_map.78.both, ...), custom_call_target="tpu_custom_call" | custom-call | tf_op jit(solution)/shard_map/pallas_call | solution.py:78
  88.1 1.9 %collective-permute-start.22 = (f32[256,128]{1,0:T(8,128)S(1)}, f32[256,128]{1,0:T(8,128)S(1)}, u32[]{:S(2)}, u32[]{:S(2)}) collective-permute-start(f32[256,128]{1,0:T(8,128)S(1)} %get-tuple-element.36), channel_id=1, source_target_pairs={{0,8},{4,12},{8,0},{12,4},{16,24},{20,28},{24,16},{28,20},{1,9},{5... | collective-permute-start | bytes 393224 | tf_op jit(solution)/shard_map/ppermute | solution.py:24
  90.1 1.6 %collective-permute-start.24 = (f32[256,128]{1,0:T(8,128)S(1)}, f32[256,128]{1,0:T(8,128)S(1)}, u32[]{:S(2)}, u32[]{:S(2)}) collective-permute-start(f32[256,128]{1,0:T(8,128)S(1)} %get-tuple-element.38), channel_id=1, source_target_pairs={{0,24},{4,28},{8,16},{12,20},{16,8},{20,12},{24,0},{28,4},{1,25},{... | collective-permute-start | bytes 393224 | tf_op jit(solution)/shard_map/ppermute | solution.py:24
  91.7 4.4 %shard_map.81 = (f32[256,128]{1,0:T(8,128)}, f32[128,128]{1,0:T(8,128)S(1)}) custom-call(f32[5,128,128]{2,1,0:T(8,128)S(1)} %shard_map.80.sent, f32[5,128,128]{2,1,0:T(8,128)S(1)} %collective-permute-done.15.got, f32[256,128]{1,0:T(8,128)S(1)} %add_add_fusion.rest_0_.y_rows), custom_call_target="tpu_custom_call" | custom-call | flops 1000000000 | tf_op jit(solution)/shard_map/pallas_call | solution.py:78
  96.0 1.3 %collective-permute-done.23.c = f32[256,128]{1,0:T(8,128)S(1)} collective-permute-done((f32[256,128]{1,0:T(8,128)S(1)}, f32[256,128]{1,0:T(8,128)S(1)}, u32[]{:S(2)}, u32[]{:S(2)}) %collective-permute-start.23) | collective-permute-done | bytes 131104 | tf_op jit(solution)/shard_map/ppermute | solution.py:24
  (63 shorter events, 18.5 us)
Async XLA Ops:
  0.6 14.3 %copy-start.9 = (f32[2,1,2048,128]{3,2,1,0:T(8,128)S(1)}, f32[2,1,2048,128]{3,2,1,0:T(8,128)}, u32[]{:S(2)}) copy-start(f32[2,1,2048,128]{3,2,1,0:T(8,128)} %param.7) | copy-start | bytes 6291460
  0.7 19.1 %collective-permute-start.1 = (f32[2,512,128]{2,1,0:T(8,128)}, f32[2,512,128]{2,1,0:T(8,128)}, u32[]{:S(2)}, u32[]{:S(2)}) collective-permute-start(f32[2,512,128]{2,1,0:T(8,128)} %param.9), channel_id=1, source_target_pairs={{0,1},{1,0},{2,3},{3,2},{4,5},{5,4},{6,7},{7,6},{8,9},{9,8},{10,11... | collective-permute-start | bytes 1572872 | tf_op jit(solution)/shard_map/ppermute | solution.py:242
  3.7 16.7 %collective-permute-start.2 = (f32[2,512,128]{2,1,0:T(8,128)}, f32[2,512,128]{2,1,0:T(8,128)}, u32[]{:S(2)}, u32[]{:S(2)}) collective-permute-start(f32[2,512,128]{2,1,0:T(8,128)} %param.9), channel_id=1, source_target_pairs={{1,2},{2,1},{5,6},{6,5},{9,10},{10,9},{13,14},{14,13},{17,18},{18,... | collective-permute-start | bytes 1572872 | tf_op jit(solution)/shard_map/ppermute | solution.py:242
  7.5 49.4 %collective-permute-start = (f32[2,4,256,128]{3,2,1,0:T(8,128)}, f32[2,4,256,128]{3,2,1,0:T(8,128)S(1)}, u32[]{:S(2)}, u32[]{:S(2)}) collective-permute-start(f32[2,4,256,128]{3,2,1,0:T(8,128)} %dynamic-slice_bitcast_fusion), channel_id=1, source_target_pairs={{0,4},{4,0},{8,12},{12,8},{16,20},{20,16},{24,28},{28,24},{1,5},{5... | collective-permute-start | bytes 3145736 | tf_op jit(solution)/shard_map/ppermute | solution.py:24
  9.1 9.6 %collective-permute-start.5 = (f32[2,128,128]{2,1,0:T(8,128)S(1)}, f32[2,128,128]{2,1,0:T(8,128)}, u32[]{:S(2)}, u32[]{:S(2)}) collective-permute-start(f32[2,128,128]{2,1,0:T(8,128)S(1)} %fusion.7), channel_id=1, source_target_pairs={{0,1},{1,0},{2,3},{3,2},{4,5},{5,4},{6,7},{7,6},{8,9},{9,8},{10,11... | collective-permute-start | bytes 393224 | tf_op jit(solution)/shard_map/ppermute | solution.py:242
  14.7 12.2 %collective-permute-start.16 = (f32[2,256,128]{2,1,0:T(8,128)}, f32[2,256,128]{2,1,0:T(8,128)}, u32[]{:S(2)}, u32[]{:S(2)}) collective-permute-start(f32[2,256,128]{2,1,0:T(8,128)} %get-tuple-element.41), channel_id=1, source_target_pairs={{0,4},{4,0},{8,12},{12,8},{16,20},{20,16},{24,28},{28,24},{1,5},{5... | collective-permute-start | bytes 786440 | tf_op jit(solution)/shard_map/ppermute | solution.py:24
  18.1 13.2 %copy-start.11 = (f32[2,128,128]{2,1,0:T(8,128)S(1)}, f32[2,128,128]{2,1,0:T(8,128)}, u32[]{:S(2)}) copy-start(f32[2,128,128]{2,1,0:T(8,128)} %fusion.2) | copy-start | bytes 393220
  19.7 15.1 %copy-start.5 = (f32[2,128,128]{2,1,0:T(8,128)}, f32[2,128,128]{2,1,0:T(8,128)S(1)}, u32[]{:S(2)}) copy-start(f32[2,128,128]{2,1,0:T(8,128)S(1)} %add.58.probe_here) | copy-start | bytes 393220
  19.7 10.0 %collective-permute-start.6 = (f32[2,128,128]{2,1,0:T(8,128)S(1)}, f32[2,128,128]{2,1,0:T(8,128)S(1)}, u32[]{:S(2)}, u32[]{:S(2)}) collective-permute-start(f32[2,128,128]{2,1,0:T(8,128)S(1)} %add.58.probe_here), channel_id=1, source_target_pairs={{1,2},{2,1},{5,6},{6,5},{9,10},{10,9},{13,14},{14,13},{17,18},{18,... | collective-permute-start | bytes 393224 | tf_op jit(solution)/shard_map/ppermute | solution.py:242
  20.5 18.5 %copy-start.4 = (f32[2,512,128]{2,1,0:T(8,128)S(1)}, f32[2,512,128]{2,1,0:T(8,128)}, u32[]{:S(2)}) copy-start(f32[2,512,128]{2,1,0:T(8,128)} %dynamic-slice_bitcast_fusion.1.own_rows) | copy-start | bytes 1572868
  20.5 18.5 %collective-permute-start.4 = (f32[2,512,128]{2,1,0:T(8,128)S(1)}, f32[2,512,128]{2,1,0:T(8,128)S(1)}, u32[]{:S(2)}, u32[]{:S(2)}) collective-permute-start(f32[2,512,128]{2,1,0:T(8,128)S(1)} %bitcast_select_fusion), channel_id=1, source_target_pairs={{0,1},{1,0},{2,3},{3,2},{4,5},{5,4},{6,7},{7,6},{8,9},{9,8},{10,11... | collective-permute-start | bytes 1572872 | tf_op jit(solution)/shard_map/ppermute | solution.py:242
  26.2 8.7 %collective-permute-start.3 = (f32[2,512,128]{2,1,0:T(8,128)}, f32[2,512,128]{2,1,0:T(8,128)S(1)}, u32[]{:S(2)}, u32[]{:S(2)}) collective-permute-start(f32[2,512,128]{2,1,0:T(8,128)} %collective-permute-done.1), channel_id=1, source_target_pairs={{1,2},{2,1},{5,6},{6,5},{9,10},{10,9},{13,14},{14,13},{17,18},{18,... | collective-permute-start | bytes 1572872 | tf_op jit(solution)/shard_map/ppermute | solution.py:242
  27.9 25.2 %copy-start.12 = (s32[2,1]{0,1:T(1,128)S(1)}, s32[2,1]{0,1:T(1,128)}, u32[]{:S(2)}) copy-start(s32[2,1]{0,1:T(1,128)} %param.11) | copy-start | bytes 28
  27.9 22.5 %collective-permute-start.17 = (f32[4,256,128]{2,1,0:T(8,128)S(1)}, f32[4,256,128]{2,1,0:T(8,128)}, u32[]{:S(2)}, u32[]{:S(2)}) collective-permute-start(f32[4,256,128]{2,1,0:T(8,128)S(1)} %pad_maximum_fusion.own), channel_id=1, source_target_pairs={{0,1},{1,0},{2,3},{3,2},{4,5},{5,4},{6,7},{7,6},{8,9},{9,8},{10,11... | collective-permute-start | bytes 1572872 | tf_op jit(solution)/shard_map/ppermute | solution.py:242
  29.8 20.6 %collective-permute-start.18 = (f32[4,256,128]{2,1,0:T(8,128)S(1)}, f32[4,256,128]{2,1,0:T(8,128)}, u32[]{:S(2)}, u32[]{:S(2)}) collective-permute-start(f32[4,256,128]{2,1,0:T(8,128)S(1)} %pad_maximum_fusion.own), channel_id=1, source_target_pairs={{1,2},{2,1},{5,6},{6,5},{9,10},{10,9},{13,14},{14,13},{17,18},{18,... | collective-permute-start | bytes 1572872 | tf_op jit(solution)/shard_map/ppermute | solution.py:242
  32.9 25.6 %copy-start.1 = (f32[2,1,2048,128]{3,2,1,0:T(8,128)S(1)}, f32[2,1,2048,128]{3,2,1,0:T(8,128)}, u32[]{:S(2)}) copy-start(f32[2,1,2048,128]{3,2,1,0:T(8,128)} %left.3) | copy-start | bytes 6291460
  40.7 13.2 %collective-permute-start.7 = (f32[4,128,128]{2,1,0:T(8,128)}, f32[4,128,128]{2,1,0:T(8,128)}, u32[]{:S(2)}, u32[]{:S(2)}) collective-permute-start(f32[4,128,128]{2,1,0:T(8,128)} %get-tuple-element.23), channel_id=1, source_target_pairs={{1,0},{2,3},{5,4},{6,7},{9,8},{10,11},{13,12},{14,15},{17,16},{18,... | collective-permute-start | bytes 786440 | tf_op jit(solution)/shard_map/ppermute | solution.py:242
  50.4 13.1 %collective-permute-start.19 = (f32[4,256,128]{2,1,0:T(8,128)}, f32[4,256,128]{2,1,0:T(8,128)}, u32[]{:S(2)}, u32[]{:S(2)}) collective-permute-start(f32[4,256,128]{2,1,0:T(8,128)} %collective-permute-done.17.near), channel_id=1, source_target_pairs={{1,2},{2,1},{5,6},{6,5},{9,10},{10,9},{13,14},{14,13},{17,18},{18,... | collective-permute-start | bytes 1572872 | tf_op jit(solution)/shard_map/ppermute | solution.py:242
  51.8 14.0 %collective-permute-start.20 = (f32[4,256,128]{2,1,0:T(8,128)}, f32[4,256,128]{2,1,0:T(8,128)}, u32[]{:S(2)}, u32[]{:S(2)}) collective-permute-start(f32[4,256,128]{2,1,0:T(8,128)} %collective-permute-done.18.inner), channel_id=1, source_target_pairs={{1,0},{2,3},{5,4},{6,7},{9,8},{10,11},{13,12},{14,15},{17,16},{18,... | collective-permute-start | bytes 1572872 | tf_op jit(solution)/shard_map/ppermute | solution.py:242
  56.9 1.6 %collective-permute-start.8 = (f32[4,128,128]{2,1,0:T(8,128)S(1)}, f32[4,128,128]{2,1,0:T(8,128)S(1)}, u32[]{:S(2)}, u32[]{:S(2)}) collective-permute-start(f32[4,128,128]{2,1,0:T(8,128)S(1)} %shard_map.78.both), channel_id=1, source_target_pairs={{0,4},{4,0},{8,12},{12,8},{16,20},{20,16},{24,28},{28,24},{1,5},{5... | collective-permute-start | bytes 786440 | tf_op jit(solution)/shard_map/ppermute | solution.py:24
  59.9 6.8 %collective-permute-start.11 = (f32[256,128]{1,0:T(8,128)S(1)}, f32[256,128]{1,0:T(8,128)S(1)}, u32[]{:S(2)}, u32[]{:S(2)}) collective-permute-start(f32[256,128]{1,0:T(8,128)S(1)} %get-tuple-element.27), channel_id=1, source_target_pairs={{0,24},{4,28},{8,16},{12,20},{16,8},{20,12},{24,0},{28,4},{1,25},{... | collective-permute-start | bytes 393224 | tf_op jit(solution)/shard_map/ppermute | solution.py:24
  62.5 6.8 %collective-permute-start.10 = (f32[256,128]{1,0:T(8,128)S(1)}, f32[256,128]{1,0:T(8,128)S(1)}, u32[]{:S(2)}, u32[]{:S(2)}) collective-permute-start(f32[256,128]{1,0:T(8,128)S(1)} %get-tuple-element.26), channel_id=1, source_target_pairs={{0,16},{4,20},{8,24},{12,28},{16,0},{20,4},{24,8},{28,12},{1,17},{... | collective-permute-start | bytes 393224 | tf_op jit(solution)/shard_map/ppermute | solution.py:24
  63.0 6.4 %collective-permute-start.9 = (f32[256,128]{1,0:T(8,128)S(1)}, f32[256,128]{1,0:T(8,128)S(1)}, u32[]{:S(2)}, u32[]{:S(2)}) collective-permute-start(f32[256,128]{1,0:T(8,128)S(1)} %get-tuple-element.25), channel_id=1, source_target_pairs={{0,8},{4,12},{8,0},{12,4},{16,24},{20,28},{24,16},{28,20},{1,9},{5... | collective-permute-start | bytes 393224 | tf_op jit(solution)/shard_map/ppermute | solution.py:24
  69.4 16.6 %copy-start.3 = (f32[4,256,128]{2,1,0:T(8,128)S(1)}, f32[4,256,128]{2,1,0:T(8,128)}, u32[]{:S(2)}) copy-start(f32[4,256,128]{2,1,0:T(8,128)} %copy-done.2) | copy-start | bytes 1572868
  69.4 16.6 %collective-permute-start.21 = (f32[4,256,128]{2,1,0:T(8,128)}, f32[4,256,128]{2,1,0:T(8,128)S(1)}, u32[]{:S(2)}, u32[]{:S(2)}) collective-permute-start(f32[4,256,128]{2,1,0:T(8,128)} %collective-permute-done.19.inner_far), channel_id=1, source_target_pairs={{1,0},{2,3},{5,4},{6,7},{9,8},{10,11},{13,12},{14,15},{17,16},{18,... | collective-permute-start | bytes 1572872 | tf_op jit(solution)/shard_map/ppermute | solution.py:242
  70.8 5.8 %collective-permute-start.12 = (f32[256,128]{1,0:T(8,128)S(1)}, f32[256,128]{1,0:T(8,128)S(1)}, u32[]{:S(2)}, u32[]{:S(2)}) collective-permute-start(f32[256,128]{1,0:T(8,128)S(1)} %add_add_fusion.rest_0_.y_rows), channel_id=1, source_target_pairs={{0,8},{4,12},{8,0},{12,4},{16,24},{20,28},{24,16},{28,20},{1,9},{5... | collective-permute-start | bytes 393224 | tf_op jit(solution)/shard_map/ppermute | solution.py:24
  72.4 7.8 %collective-permute-start.13 = (f32[256,128]{1,0:T(8,128)S(1)}, f32[256,128]{1,0:T(8,128)S(1)}, u32[]{:S(2)}, u32[]{:S(2)}) collective-permute-start(f32[256,128]{1,0:T(8,128)S(1)} %add_add_fusion.rest_0_.y_rows), channel_id=1, source_target_pairs={{0,16},{4,20},{8,24},{12,28},{16,0},{20,4},{24,8},{28,12},{1,17},{... | collective-permute-start | bytes 393224 | tf_op jit(solution)/shard_map/ppermute | solution.py:24
  73.1 7.1 %collective-permute-start.14 = (f32[256,128]{1,0:T(8,128)S(1)}, f32[256,128]{1,0:T(8,128)S(1)}, u32[]{:S(2)}, u32[]{:S(2)}) collective-permute-start(f32[256,128]{1,0:T(8,128)S(1)} %add_add_fusion.rest_0_.y_rows), channel_id=1, source_target_pairs={{0,24},{4,28},{8,16},{12,20},{16,8},{20,12},{24,0},{28,4},{1,25},{... | collective-permute-start | bytes 393224 | tf_op jit(solution)/shard_map/ppermute | solution.py:24
  82.0 1.7 %collective-permute-start.15 = (f32[5,128,128]{2,1,0:T(8,128)S(1)}, f32[5,128,128]{2,1,0:T(8,128)S(1)}, u32[]{:S(2)}, u32[]{:S(2)}) collective-permute-start(f32[5,128,128]{2,1,0:T(8,128)S(1)} %shard_map.80.sent), channel_id=1, source_target_pairs={{0,4},{4,0},{8,12},{12,8},{16,20},{20,16},{24,28},{28,24},{1,5},{5... | collective-permute-start | bytes 983048 | tf_op jit(solution)/shard_map/ppermute | solution.py:24
  88.1 7.9 %collective-permute-start.22 = (f32[256,128]{1,0:T(8,128)S(1)}, f32[256,128]{1,0:T(8,128)S(1)}, u32[]{:S(2)}, u32[]{:S(2)}) collective-permute-start(f32[256,128]{1,0:T(8,128)S(1)} %get-tuple-element.36), channel_id=1, source_target_pairs={{0,8},{4,12},{8,0},{12,4},{16,24},{20,28},{24,16},{28,20},{1,9},{5... | collective-permute-start | bytes 393224 | tf_op jit(solution)/shard_map/ppermute | solution.py:24
  90.0 7.4 %collective-permute-start.23 = (f32[256,128]{1,0:T(8,128)S(1)}, f32[256,128]{1,0:T(8,128)S(1)}, u32[]{:S(2)}, u32[]{:S(2)}) collective-permute-start(f32[256,128]{1,0:T(8,128)S(1)} %get-tuple-element.37), channel_id=1, source_target_pairs={{0,16},{4,20},{8,24},{12,28},{16,0},{20,4},{24,8},{28,12},{1,17},{... | collective-permute-start | bytes 393224 | tf_op jit(solution)/shard_map/ppermute | solution.py:24
  90.1 7.3 %collective-permute-start.24 = (f32[256,128]{1,0:T(8,128)S(1)}, f32[256,128]{1,0:T(8,128)S(1)}, u32[]{:S(2)}, u32[]{:S(2)}) collective-permute-start(f32[256,128]{1,0:T(8,128)S(1)} %get-tuple-element.38), channel_id=1, source_target_pairs={{0,24},{4,28},{8,16},{12,20},{16,8},{20,12},{24,0},{28,4},{1,25},{... | collective-permute-start | bytes 393224 | tf_op jit(solution)/shard_map/ppermute | solution.py:24
  (6 other events, 30.4 us)

commit v6 on v5

--- a/solution.py
+++ b/solution.py
@@ -86,8 +86,7 @@
     )(*args)
 
 
-def core_kernel(planes, part, own_rows, first, second, probe_far, core, lent):
-    lent[pl.ds(2, 2)] = probe_far[...]
+def core_kernel(planes, part, own_rows, first, second, core, lent):
     plane = lax.axis_index("tile")
     is_end = jnp.logical_or(plane == 0, plane == planes - 1)
 
@@ -108,7 +107,7 @@
     for k in range(2):
         weight = pattern[k, 0].astype(jnp.float32)
         c = (core[k] + lent[k]) * weight
-        both[k] = dot3(c, probe_here[k] + probe_far[k] + lent[2 + k], NN)
+        both[k] = dot3(c, probe_here[k] + probe_far[k], NN)
         both[2 + k] = c
 
 
@@ -251,16 +250,20 @@
         return take(right_blocks, index, 1)
 
     inner_far = across(near, inner_pairs)
-    outer = across(jnp.where(is_end, block(planes - 1 - plane), inner), outer_pairs)
+    outer_rows = jnp.where(is_end, block(planes - 1 - plane), inner)
+    outer = across(outer_rows, outer_pairs)
     part = (
         mm("kbr,kbq->krq", block(plane), column_right)
         + mm("kbr,kbq->krq", block(plane ^ 1), near)
         + mm("kbr,kbq->krq", block(jnp.where(is_end, plane, planes - 1 - plane)), inner)
     )
-    _, probes_held = lax.optimization_barrier((near, probes))
-    probes_far = across(probes_held, inner_pairs)
-    far_rows = block(plane ^ 2)
-    core, lent = call(functools.partial(core_kernel, planes), [(2, rank, rank), (4, rank, rank)], [part, far_rows, inner_far, outer, probes_far])
+    _, probes_held = lax.optimization_barrier(((near, inner), probes))
+    probes_far = exchange(probes_held, "tile", 2)
+    core, lent = call(
+        functools.partial(core_kernel, planes),
+        [(2, rank, rank)] * 2,
+        [part, block(plane ^ 2), inner_far, outer],
+    )
     lent = across(lent, outward)
 
     left_split = target_left.reshape(2, chips, 2, row_count, rank)

time: 99 us -> 103 us (1.040)
  starting transfers between devices: 35 us -> 46.9 us
  waiting for transfers between devices: 32.4 us -> 22 us
  other arithmetic: 2.01 us -> 3.8 us
  Pallas kernels: 12.9 us -> 14.3 us
    ppermute x13 -> x14, starting transfers between devices: 11 us -> 26.3 us  [exchange(): lax.ppermute(array, axis, [(i, i ^ bit) for i in range(lax.axis_size(axis...]
    ppermute x12 -> x11, waiting for transfers between devices: 18.5 us -> 9.78 us  [across(): return lax.ppermute(array, 'tile', pairs)]
    ppermute x12 -> x11, starting transfers between devices: 24 us -> 20.7 us  [across(): return lax.ppermute(array, 'tile', pairs)]
    ppermute x13 -> x14, waiting for transfers between devices: 13.9 us -> 12.2 us  [exchange(): lax.ppermute(array, axis, [(i, i ^ bit) for i in range(lax.axis_size(axis...]
    pallas_call x7, Pallas kernels: 12.9 us -> 14.3 us  [call(): pl.pallas_call(kernel, out_shape=shapes, in_specs=[pl.BlockSpec(memory_sp...]
    unnamed x27 -> x17, local copies, waits for them, and re-layouts: 2.61 us -> 1.69 us
  transfers between devices with their start and end apart: 25 -> 25, of which waited for: 14 -> 10; matrix products, arithmetic and copies ran while one was open for 15% -> 16% of each run, Pallas kernels for 10% -> 11%
where the time goes in v6:
time: 103 us; the launch traced here: 102 us
  starting transfers between devices  46.9 us (46%)
  waiting for transfers between devices  22 us (21%)
  Pallas kernels  14.3 us (14%)
  matrix products  7.53 us (7%)
  local copies, waits for them, and re-layouts  6.64 us (6%)
  other arithmetic  3.8 us (4%)
    ppermute x14, starting transfers between devices, exchange(): lax.ppermute(array, axis, [(i, i ^ bit) for i in range(lax.axis_size(axis...  26.3 us
    ppermute x11, starting transfers between devices, across(): return lax.ppermute(array, 'tile', pairs)  20.7 us
    pallas_call x7, Pallas kernels, call(): pl.pallas_call(kernel, out_shape=shapes, in_specs=[pl.BlockSpec(memory_sp...  14.3 us
    ppermute x14, waiting for transfers between devices, exchange(): lax.ppermute(array, axis, [(i, i ^ bit) for i in range(lax.axis_size(axis...  12.2 us
    ppermute x11, waiting for transfers between devices, across(): return lax.ppermute(array, 'tile', pairs)  9.78 us
    dot_general x4, matrix products, mm(): jnp.einsum(spec, *arrays, precision=HIGH, preferred_element_type=jnp.floa...  7.53 us
    squeeze x3, local copies, waits for them, and re-layouts, take(): return lax.dynamic_index_in_dim(array, index, axis, keepdims=False)  4.95 us
  transfers between devices with their start and end apart: 25, of which 10 were waited for; matrix products, arithmetic and copies ran while one was open for 16% of the time, Pallas kernels for 11%

profile of v6, /device:TPU:0, one launch (start us, length us, event | category | flops | bytes accessed | tf_op | source)
XLA Modules:
  0.0 102.1 jit_solution(16248764163269298750)
XLA Ops:
  0.7 3.1 %collective-permute-start.1 = (f32[2,512,128]{2,1,0:T(8,128)}, f32[2,512,128]{2,1,0:T(8,128)}, u32[]{:S(2)}, u32[]{:S(2)}) collective-permute-start(f32[2,512,128]{2,1,0:T(8,128)} %param.9), channel_id=1, source_target_pairs={{0,1},{1,0},{2,3},{3,2},{4,5},{5,4},{6,7},{7,6},{8,9},{9,8},{10,11... | collective-permute-start | bytes 1572872 | tf_op jit(solution)/shard_map/ppermute | solution.py:241
  3.7 1.5 %collective-permute-start.2 = (f32[2,512,128]{2,1,0:T(8,128)}, f32[2,512,128]{2,1,0:T(8,128)}, u32[]{:S(2)}, u32[]{:S(2)}) collective-permute-start(f32[2,512,128]{2,1,0:T(8,128)} %param.9), channel_id=1, source_target_pairs={{1,2},{2,1},{5,6},{6,5},{9,10},{10,9},{13,14},{14,13},{17,18},{18,... | collective-permute-start | bytes 1572872 | tf_op jit(solution)/shard_map/ppermute | solution.py:241
  5.2 2.3 %dynamic-slice_bitcast_fusion = f32[2,4,256,128]{3,2,1,0:T(8,128)} fusion(f32[2,4,2,256,128]{4,3,2,1,0:T(8,128)} %bitcast.44, s32[]{:T(128)S(6)} %select_n.44), kind=kLoop, calls=%fused_computation.2 | loop fusion | bytes 2097156 | tf_op jit(solution)/shard_map/jit(dynamic_index_in_dim)/squeeze | solution.py:28
  7.5 1.9 %dynamic-slice_bitcast_fusion.3 = (f32[2,256,128]{2,1,0:T(8,128)}, f32[2,256,128]{2,1,0:T(8,128)}) fusion(f32[2,2,256,128]{3,2,1,0:T(8,128)} %bitcast.50, s32[]{:T(128)S(6)} %select_n.53, s32[]{:T(128)S(6)} %select_n.44), kind=kLoop, calls=%fused_computation.16 | loop fusion | bytes 1048584 | tf_op jit(solution)/shard_map/jit(dynamic_index_in_dim)/squeeze | solution.py:28
  9.9 1.6 %fusion.7 = f32[2,128,128]{2,1,0:T(8,128)S(1)} fusion(f32[2,512,128]{2,1,0:T(8,128)} %param.8, f32[512,128]{1,0:T(8,128)S(1)} %copy-done), kind=kOutput, calls=%fused_computation.13 | convolution fusion | flops 100663296 | bytes 917504 | tf_op jit(solution)/shard_map/kbq,bp->kqp/dot_general | solution.py:14
  11.5 3.7 %collective-permute-start.6 = (f32[2,128,128]{2,1,0:T(8,128)S(1)}, f32[2,128,128]{2,1,0:T(8,128)}, u32[]{:S(2)}, u32[]{:S(2)}) collective-permute-start(f32[2,128,128]{2,1,0:T(8,128)S(1)} %fusion.7), channel_id=1, source_target_pairs={{0,1},{1,0},{2,3},{3,2},{4,5},{5,4},{6,7},{7,6},{8,9},{9,8},{10,11... | collective-permute-start | bytes 393224 | tf_op jit(solution)/shard_map/ppermute | solution.py:241
  15.2 2.3 %fusion.2 = f32[2,128,128]{2,1,0:T(8,128)} fusion(f32[2,512,128]{2,1,0:T(8,128)} %param.9, f32[2,4,512,128]{3,2,1,0:T(8,128)S(1)} %bitcast.46, s32[]{:T(128)S(6)} %select_n.45), kind=kOutput, calls=%fused_computation.6 | convolution fusion | flops 100663296 | bytes 1179652 | tf_op jit(solution)/shard_map/kbr,kbq->krq/dot_general | solution.py:14
  17.5 1.9 %pad_maximum_fusion.own = f32[4,256,128]{2,1,0:T(8,128)} fusion(f32[2,256,128]{2,1,0:T(8,128)} %collective-permute-done.16, f32[2,256,128]{2,1,0:T(8,128)} %get-tuple-element.40), kind=kLoop, calls=%fused_computation.3 | loop fusion | flops 131072 | bytes 1048576 | tf_op jit(solution)/shard_map/concatenate | solution.py:272
  19.4 1.5 %collective-permute-start.18 = (f32[4,256,128]{2,1,0:T(8,128)}, f32[4,256,128]{2,1,0:T(8,128)}, u32[]{:S(2)}, u32[]{:S(2)}) collective-permute-start(f32[4,256,128]{2,1,0:T(8,128)} %pad_maximum_fusion.own), channel_id=1, source_target_pairs={{1,2},{2,1},{5,6},{6,5},{9,10},{10,9},{13,14},{14,13},{17,18},{18,... | collective-permute-start | bytes 1572872 | tf_op jit(solution)/shard_map/ppermute | solution.py:241
  21.7 4.1 %collective-permute-start.4 = (f32[2,512,128]{2,1,0:T(8,128)}, f32[2,512,128]{2,1,0:T(8,128)}, u32[]{:S(2)}, u32[]{:S(2)}) collective-permute-start(f32[2,512,128]{2,1,0:T(8,128)} %bitcast_select_fusion), channel_id=1, source_target_pairs={{0,1},{1,0},{2,3},{3,2},{4,5},{5,4},{6,7},{7,6},{8,9},{9,8},{10,11... | collective-permute-start | bytes 1572872 | tf_op jit(solution)/shard_map/ppermute | solution.py:241
  25.9 1.5 %collective-permute-start.3 = (f32[2,512,128]{2,1,0:T(8,128)}, f32[2,512,128]{2,1,0:T(8,128)}, u32[]{:S(2)}, u32[]{:S(2)}) collective-permute-start(f32[2,512,128]{2,1,0:T(8,128)} %collective-permute-done.1), channel_id=1, source_target_pairs={{1,2},{2,1},{5,6},{6,5},{9,10},{10,9},{13,14},{14,13},{17,18},{18,... | collective-permute-start | bytes 1572872 | tf_op jit(solution)/shard_map/ppermute | solution.py:241
  29.2 1.7 %convolution_add_fusion.1 = f32[2,128,128]{2,1,0:T(8,128)S(1)} fusion(f32[2,128,128]{2,1,0:T(8,128)} %fusion.2, f32[2,512,128]{2,1,0:T(8,128)} %collective-permute-done.1, f32[2,4,512,128]{3,2,1,0:T(8,128)S(1)} %bitcast.49, s32[]{:T(128)S(6)} %select_n.46), kind=kOutput, calls=%fused_computation.1 | convolution fusion | flops 100696064 | bytes 1310724 | tf_op jit(solution)/shard_map/kbr,kbq->krq/dot_general | solution.py:14
  30.9 1.9 %convolution_add_fusion.part = f32[2,128,128]{2,1,0:T(8,128)S(1)} fusion(f32[2,128,128]{2,1,0:T(8,128)S(1)} %convolution_add_fusion.1, f32[2,512,128]{2,1,0:T(8,128)} %collective-permute-done.2, f32[2,4,512,128]{3,2,1,0:T(8,128)} %bitcast.45, s32[]{:T(128)S(6)} %select_n.48), kind=kOutput, calls=%fused_computation | convolution fusion | flops 100696064 | bytes 1310724 | tf_op jit(solution)/shard_map/kbr,kbq->krq/dot_general | solution.py:14
  32.8 15.0 %collective-permute-start.7 = (f32[2,128,128]{2,1,0:T(8,128)S(1)}, f32[2,128,128]{2,1,0:T(8,128)}, u32[]{:S(2)}, u32[]{:S(2)}) collective-permute-start(f32[2,128,128]{2,1,0:T(8,128)S(1)} %add.58.probe_here), channel_id=1, source_target_pairs={{0,2},{1,3},{2,0},{3,1},{4,6},{5,7},{6,4},{7,5},{8,10},{9,11},{10,... | collective-permute-start | bytes 393224 | tf_op jit(solution)/shard_map/ppermute | solution.py:24
  47.8 2.2 %shard_map.77 = (f32[2,128,128]{2,1,0:T(8,128)S(1)}, f32[2,128,128]{2,1,0:T(8,128)}) custom-call(f32[2,128,128]{2,1,0:T(8,128)S(1)} %convolution_add_fusion.part, f32[2,512,128]{2,1,0:T(8,128)S(1)} %copy-done.2, f32[2,512,128]{2,1,0:T(8,128)} %collective-permute-done.3.first, f32[2,512,128]{2,1,0:T(8,128)} %collective-permute-done.4.second), custom_call_target="tpu_custom_call" | custom-call | tf_op jit(solution)/shard_map/pallas_call | solution.py:78
  52.0 1.5 %collective-permute-start.19 = (f32[4,256,128]{2,1,0:T(8,128)}, f32[4,256,128]{2,1,0:T(8,128)}, u32[]{:S(2)}, u32[]{:S(2)}) collective-permute-start(f32[4,256,128]{2,1,0:T(8,128)} %collective-permute-done.17.near), channel_id=1, source_target_pairs={{1,2},{2,1},{5,6},{6,5},{9,10},{10,9},{13,14},{14,13},{17,18},{18,... | collective-permute-start | bytes 1572872 | tf_op jit(solution)/shard_map/ppermute | solution.py:241
  54.9 3.0 %collective-permute-done.5.lent = f32[2,128,128]{2,1,0:T(8,128)} collective-permute-done((f32[2,128,128]{2,1,0:T(8,128)}, f32[2,128,128]{2,1,0:T(8,128)}, u32[]{:S(2)}, u32[]{:S(2)}) %collective-permute-start.5) | collective-permute-done | bytes 131104 | tf_op jit(solution)/shard_map/ppermute | solution.py:241
  60.0 1.5 %collective-permute-done.8.both_other = f32[4,128,128]{2,1,0:T(8,128)S(1)} collective-permute-done((f32[4,128,128]{2,1,0:T(8,128)S(1)}, f32[4,128,128]{2,1,0:T(8,128)S(1)}, u32[]{:S(2)}, u32[]{:S(2)}) %collective-permute-start.8) | collective-permute-done | bytes 262176 | tf_op jit(solution)/shard_map/ppermute | solution.py:24
  61.5 1.5 %shard_map.79 = (f32[256,128]{1,0:T(8,128)S(1)}, f32[256,128]{1,0:T(8,128)S(1)}, f32[256,128]{1,0:T(8,128)S(1)}, f32[256,128]{1,0:T(8,128)S(1)}) custom-call(f32[2,1,2048,128]{3,2,1,0:T(8,128)S(1)} %copy-done.1, f32[2,4,256,128]{3,2,1,0:T(8,128)S(1)} %collective-permute-done.left_other, f32[4,128,128]{2,1,0:T(8,128)S(1)} %shard_map.78.both, ...), custom_call_target="tpu_custom_call" | custom-call | tf_op jit(solution)/shard_map/pallas_call | solution.py:78
  63.0 2.5 %collective-permute-start.11 = (f32[256,128]{1,0:T(8,128)S(1)}, f32[256,128]{1,0:T(8,128)S(1)}, u32[]{:S(2)}, u32[]{:S(2)}) collective-permute-start(f32[256,128]{1,0:T(8,128)S(1)} %get-tuple-element.27), channel_id=1, source_target_pairs={{0,24},{4,28},{8,16},{12,20},{16,8},{20,12},{24,0},{28,4},{1,25},{... | collective-permute-start | bytes 393224 | tf_op jit(solution)/shard_map/ppermute | solution.py:24
  66.6 3.7 %collective-permute-done.20.outer = f32[4,256,128]{2,1,0:T(8,128)} collective-permute-done((f32[4,256,128]{2,1,0:T(8,128)}, f32[4,256,128]{2,1,0:T(8,128)}, u32[]{:S(2)}, u32[]{:S(2)}) %collective-permute-start.20) | collective-permute-done | bytes 524320 | tf_op jit(solution)/shard_map/ppermute | solution.py:241
  70.3 2.1 %collective-permute-done.10 = f32[256,128]{1,0:T(8,128)S(1)} collective-permute-done((f32[256,128]{1,0:T(8,128)S(1)}, f32[256,128]{1,0:T(8,128)S(1)}, u32[]{:S(2)}, u32[]{:S(2)}) %collective-permute-start.10) | collective-permute-done | bytes 131104 | tf_op jit(solution)/shard_map/ppermute | solution.py:24
  73.8 1.6 %collective-permute-start.12 = (f32[256,128]{1,0:T(8,128)S(1)}, f32[256,128]{1,0:T(8,128)S(1)}, u32[]{:S(2)}, u32[]{:S(2)}) collective-permute-start(f32[256,128]{1,0:T(8,128)S(1)} %add_add_fusion.rest_0_.y_rows), channel_id=1, source_target_pairs={{0,8},{4,12},{8,0},{12,4},{16,24},{20,28},{24,16},{28,20},{1,9},{5... | collective-permute-start | bytes 393224 | tf_op jit(solution)/shard_map/ppermute | solution.py:24
  77.3 2.2 %collective-permute-done.12.rest_1_ = f32[256,128]{1,0:T(8,128)S(1)} collective-permute-done((f32[256,128]{1,0:T(8,128)S(1)}, f32[256,128]{1,0:T(8,128)S(1)}, u32[]{:S(2)}, u32[]{:S(2)}) %collective-permute-start.12) | collective-permute-done | bytes 131104 | tf_op jit(solution)/shard_map/ppermute | solution.py:24
  79.5 3.7 %collective-permute-done.13.rest_2_ = f32[256,128]{1,0:T(8,128)S(1)} collective-permute-done((f32[256,128]{1,0:T(8,128)S(1)}, f32[256,128]{1,0:T(8,128)S(1)}, u32[]{:S(2)}, u32[]{:S(2)}) %collective-permute-start.13) | collective-permute-done | bytes 131104 | tf_op jit(solution)/shard_map/ppermute | solution.py:24
  83.2 1.7 %shard_map.80.sent = f32[5,128,128]{2,1,0:T(8,128)S(1)} custom-call(f32[2,1,2048,128]{3,2,1,0:T(8,128)S(1)} %copy-done.1, f32[2,4,256,128]{3,2,1,0:T(8,128)S(1)} %collective-permute-done.left_other, f32[256,128]{1,0:T(8,128)S(1)} %add_add_fusion.rest_0_.y_rows, f32[256,128]{1,0:T(8,128)S(1)} %collective-permute-done.12.rest_1_, ...), custom_call_target="tpu_custom_call" | custom-call | tf_op jit(solution)/shard_map/pallas_call | solution.py:78
  85.0 1.6 %collective-permute-done.15.got = f32[5,128,128]{2,1,0:T(8,128)S(1)} collective-permute-done((f32[5,128,128]{2,1,0:T(8,128)S(1)}, f32[5,128,128]{2,1,0:T(8,128)S(1)}, u32[]{:S(2)}, u32[]{:S(2)}) %collective-permute-start.15) | collective-permute-done | bytes 327712 | tf_op jit(solution)/shard_map/ppermute | solution.py:24
  86.6 3.1 %collective-permute-done.21.last = f32[4,256,128]{2,1,0:T(8,128)S(1)} collective-permute-done((f32[4,256,128]{2,1,0:T(8,128)}, f32[4,256,128]{2,1,0:T(8,128)S(1)}, u32[]{:S(2)}, u32[]{:S(2)}) %collective-permute-start.21) | collective-permute-done | bytes 524320 | tf_op jit(solution)/shard_map/ppermute | solution.py:241
  89.7 2.4 %shard_map.82 = (f32[256,128]{1,0:T(8,128)S(1)}, f32[256,128]{1,0:T(8,128)S(1)}, f32[256,128]{1,0:T(8,128)S(1)}, f32[256,128]{1,0:T(8,128)S(1)}) custom-call(f32[5,128,128]{2,1,0:T(8,128)S(1)} %shard_map.80.sent, f32[5,128,128]{2,1,0:T(8,128)S(1)} %collective-permute-done.15.got, f32[4,128,128]{2,1,0:T(8,128)S(1)} %shard_map.78.both, ...), custom_call_target="tpu_custom_call" | custom-call | tf_op jit(solution)/shard_map/pallas_call | solution.py:78
  92.2 1.6 %collective-permute-start.22 = (f32[256,128]{1,0:T(8,128)S(1)}, f32[256,128]{1,0:T(8,128)S(1)}, u32[]{:S(2)}, u32[]{:S(2)}) collective-permute-start(f32[256,128]{1,0:T(8,128)S(1)} %get-tuple-element.36), channel_id=1, source_target_pairs={{0,8},{4,12},{8,0},{12,4},{16,24},{20,28},{24,16},{28,20},{1,9},{5... | collective-permute-start | bytes 393224 | tf_op jit(solution)/shard_map/ppermute | solution.py:24
  93.8 1.9 %collective-permute-start.24 = (f32[256,128]{1,0:T(8,128)S(1)}, f32[256,128]{1,0:T(8,128)S(1)}, u32[]{:S(2)}, u32[]{:S(2)}) collective-permute-start(f32[256,128]{1,0:T(8,128)S(1)} %get-tuple-element.38), channel_id=1, source_target_pairs={{0,24},{4,28},{8,16},{12,20},{16,8},{20,12},{24,0},{28,4},{1,25},{... | collective-permute-start | bytes 393224 | tf_op jit(solution)/shard_map/ppermute | solution.py:24
  95.7 4.4 %shard_map.81 = (f32[256,128]{1,0:T(8,128)}, f32[128,128]{1,0:T(8,128)S(1)}) custom-call(f32[5,128,128]{2,1,0:T(8,128)S(1)} %shard_map.80.sent, f32[5,128,128]{2,1,0:T(8,128)S(1)} %collective-permute-done.15.got, f32[256,128]{1,0:T(8,128)S(1)} %add_add_fusion.rest_0_.y_rows), custom_call_target="tpu_custom_call" | custom-call | flops 1000000000 | tf_op jit(solution)/shard_map/pallas_call | solution.py:78
  (53 shorter events, 15.4 us)
Async XLA Ops:
  0.6 9.2 %copy-start = (f32[512,128]{1,0:T(8,128)S(1)}, f32[512,128]{1,0:T(8,128)}, u32[]{:S(2)}) copy-start(f32[512,128]{1,0:T(8,128)} %param.10) | copy-start | bytes 786436
  0.6 14.6 %copy-start.5 = (f32[2,1,2048,128]{3,2,1,0:T(8,128)S(1)}, f32[2,1,2048,128]{3,2,1,0:T(8,128)}, u32[]{:S(2)}) copy-start(f32[2,1,2048,128]{3,2,1,0:T(8,128)} %param.7) | copy-start | bytes 6291460
  0.7 18.7 %collective-permute-start.1 = (f32[2,512,128]{2,1,0:T(8,128)}, f32[2,512,128]{2,1,0:T(8,128)}, u32[]{:S(2)}, u32[]{:S(2)}) collective-permute-start(f32[2,512,128]{2,1,0:T(8,128)} %param.9), channel_id=1, source_target_pairs={{0,1},{1,0},{2,3},{3,2},{4,5},{5,4},{6,7},{7,6},{8,9},{9,8},{10,11... | collective-permute-start | bytes 1572872 | tf_op jit(solution)/shard_map/ppermute | solution.py:241
  3.7 17.1 %collective-permute-start.2 = (f32[2,512,128]{2,1,0:T(8,128)}, f32[2,512,128]{2,1,0:T(8,128)}, u32[]{:S(2)}, u32[]{:S(2)}) collective-permute-start(f32[2,512,128]{2,1,0:T(8,128)} %param.9), channel_id=1, source_target_pairs={{1,2},{2,1},{5,6},{6,5},{9,10},{10,9},{13,14},{14,13},{17,18},{18,... | collective-permute-start | bytes 1572872 | tf_op jit(solution)/shard_map/ppermute | solution.py:241
  7.5 52.5 %collective-permute-start = (f32[2,4,256,128]{3,2,1,0:T(8,128)}, f32[2,4,256,128]{3,2,1,0:T(8,128)S(1)}, u32[]{:S(2)}, u32[]{:S(2)}) collective-permute-start(f32[2,4,256,128]{3,2,1,0:T(8,128)} %dynamic-slice_bitcast_fusion), channel_id=1, source_target_pairs={{0,4},{4,0},{8,12},{12,8},{16,20},{20,16},{24,28},{28,24},{1,5},{5... | collective-permute-start | bytes 3145736 | tf_op jit(solution)/shard_map/ppermute | solution.py:24
  9.3 8.2 %collective-permute-start.16 = (f32[2,256,128]{2,1,0:T(8,128)}, f32[2,256,128]{2,1,0:T(8,128)}, u32[]{:S(2)}, u32[]{:S(2)}) collective-permute-start(f32[2,256,128]{2,1,0:T(8,128)} %get-tuple-element.41), channel_id=1, source_target_pairs={{0,4},{4,0},{8,12},{12,8},{16,20},{20,16},{24,28},{28,24},{1,5},{5... | collective-permute-start | bytes 786440 | tf_op jit(solution)/shard_map/ppermute | solution.py:24
  11.5 16.7 %copy-start.6 = (f32[2,128,128]{2,1,0:T(8,128)}, f32[2,128,128]{2,1,0:T(8,128)S(1)}, u32[]{:S(2)}) copy-start(f32[2,128,128]{2,1,0:T(8,128)S(1)} %fusion.7) | copy-start | bytes 393220
  11.5 14.4 %collective-permute-start.6 = (f32[2,128,128]{2,1,0:T(8,128)S(1)}, f32[2,128,128]{2,1,0:T(8,128)}, u32[]{:S(2)}, u32[]{:S(2)}) collective-permute-start(f32[2,128,128]{2,1,0:T(8,128)S(1)} %fusion.7), channel_id=1, source_target_pairs={{0,1},{1,0},{2,3},{3,2},{4,5},{5,4},{6,7},{7,6},{8,9},{9,8},{10,11... | collective-permute-start | bytes 393224 | tf_op jit(solution)/shard_map/ppermute | solution.py:241
  19.3 32.6 %collective-permute-start.17 = (f32[4,256,128]{2,1,0:T(8,128)}, f32[4,256,128]{2,1,0:T(8,128)}, u32[]{:S(2)}, u32[]{:S(2)}) collective-permute-start(f32[4,256,128]{2,1,0:T(8,128)} %pad_maximum_fusion.own), channel_id=1, source_target_pairs={{0,1},{1,0},{2,3},{3,2},{4,5},{5,4},{6,7},{7,6},{8,9},{9,8},{10,11... | collective-permute-start | bytes 1572872 | tf_op jit(solution)/shard_map/ppermute | solution.py:241
  19.4 32.6 %collective-permute-start.18 = (f32[4,256,128]{2,1,0:T(8,128)}, f32[4,256,128]{2,1,0:T(8,128)}, u32[]{:S(2)}, u32[]{:S(2)}) collective-permute-start(f32[4,256,128]{2,1,0:T(8,128)} %pad_maximum_fusion.own), channel_id=1, source_target_pairs={{1,2},{2,1},{5,6},{6,5},{9,10},{10,9},{13,14},{14,13},{17,18},{18,... | collective-permute-start | bytes 1572872 | tf_op jit(solution)/shard_map/ppermute | solution.py:241
  21.7 26.1 %collective-permute-start.4 = (f32[2,512,128]{2,1,0:T(8,128)}, f32[2,512,128]{2,1,0:T(8,128)}, u32[]{:S(2)}, u32[]{:S(2)}) collective-permute-start(f32[2,512,128]{2,1,0:T(8,128)} %bitcast_select_fusion), channel_id=1, source_target_pairs={{0,1},{1,0},{2,3},{3,2},{4,5},{5,4},{6,7},{7,6},{8,9},{9,8},{10,11... | collective-permute-start | bytes 1572872 | tf_op jit(solution)/shard_map/ppermute | solution.py:241
  25.9 7.0 %collective-permute-start.3 = (f32[2,512,128]{2,1,0:T(8,128)}, f32[2,512,128]{2,1,0:T(8,128)}, u32[]{:S(2)}, u32[]{:S(2)}) collective-permute-start(f32[2,512,128]{2,1,0:T(8,128)} %collective-permute-done.1), channel_id=1, source_target_pairs={{1,2},{2,1},{5,6},{6,5},{9,10},{10,9},{13,14},{14,13},{17,18},{18,... | collective-permute-start | bytes 1572872 | tf_op jit(solution)/shard_map/ppermute | solution.py:241
  28.1 19.7 %copy-start.2 = (f32[2,512,128]{2,1,0:T(8,128)S(1)}, f32[2,512,128]{2,1,0:T(8,128)}, u32[]{:S(2)}) copy-start(f32[2,512,128]{2,1,0:T(8,128)} %dynamic-slice_bitcast_fusion.1.own_rows) | copy-start | bytes 1572868
  29.2 25.6 %copy-start.7 = (s32[2,1]{0,1:T(1,128)S(1)}, s32[2,1]{0,1:T(1,128)}, u32[]{:S(2)}) copy-start(s32[2,1]{0,1:T(1,128)} %param.11) | copy-start | bytes 28
  30.9 30.7 %copy-start.1 = (f32[2,1,2048,128]{3,2,1,0:T(8,128)S(1)}, f32[2,1,2048,128]{3,2,1,0:T(8,128)}, u32[]{:S(2)}) copy-start(f32[2,1,2048,128]{3,2,1,0:T(8,128)} %left.3) | copy-start | bytes 6291460
  32.8 22.0 %collective-permute-start.7 = (f32[2,128,128]{2,1,0:T(8,128)S(1)}, f32[2,128,128]{2,1,0:T(8,128)}, u32[]{:S(2)}, u32[]{:S(2)}) collective-permute-start(f32[2,128,128]{2,1,0:T(8,128)S(1)} %add.58.probe_here), channel_id=1, source_target_pairs={{0,2},{1,3},{2,0},{3,1},{4,6},{5,7},{6,4},{7,5},{8,10},{9,11},{10,... | collective-permute-start | bytes 393224 | tf_op jit(solution)/shard_map/ppermute | solution.py:24
  50.7 7.2 %collective-permute-start.5 = (f32[2,128,128]{2,1,0:T(8,128)}, f32[2,128,128]{2,1,0:T(8,128)}, u32[]{:S(2)}, u32[]{:S(2)}) collective-permute-start(f32[2,128,128]{2,1,0:T(8,128)} %get-tuple-element.22), channel_id=1, source_target_pairs={{1,0},{2,3},{5,4},{6,7},{9,8},{10,11},{13,12},{14,15},{17,16},{18,... | collective-permute-start | bytes 393224 | tf_op jit(solution)/shard_map/ppermute | solution.py:241
  52.0 14.6 %collective-permute-start.19 = (f32[4,256,128]{2,1,0:T(8,128)}, f32[4,256,128]{2,1,0:T(8,128)}, u32[]{:S(2)}, u32[]{:S(2)}) collective-permute-start(f32[4,256,128]{2,1,0:T(8,128)} %collective-permute-done.17.near), channel_id=1, source_target_pairs={{1,2},{2,1},{5,6},{6,5},{9,10},{10,9},{13,14},{14,13},{17,18},{18,... | collective-permute-start | bytes 1572872 | tf_op jit(solution)/shard_map/ppermute | solution.py:241
  53.5 16.8 %collective-permute-start.20 = (f32[4,256,128]{2,1,0:T(8,128)}, f32[4,256,128]{2,1,0:T(8,128)}, u32[]{:S(2)}, u32[]{:S(2)}) collective-permute-start(f32[4,256,128]{2,1,0:T(8,128)} %collective-permute-done.18.inner), channel_id=1, source_target_pairs={{1,0},{2,3},{5,4},{6,7},{9,8},{10,11},{13,12},{14,15},{17,16},{18,... | collective-permute-start | bytes 1572872 | tf_op jit(solution)/shard_map/ppermute | solution.py:241
  57.9 0.9 copy-start.4
  59.9 1.6 %collective-permute-start.8 = (f32[4,128,128]{2,1,0:T(8,128)S(1)}, f32[4,128,128]{2,1,0:T(8,128)S(1)}, u32[]{:S(2)}, u32[]{:S(2)}) collective-permute-start(f32[4,128,128]{2,1,0:T(8,128)S(1)} %shard_map.78.both), channel_id=1, source_target_pairs={{0,4},{4,0},{8,12},{12,8},{16,20},{20,16},{24,28},{28,24},{1,5},{5... | collective-permute-start | bytes 786440 | tf_op jit(solution)/shard_map/ppermute | solution.py:24
  63.0 7.2 %collective-permute-start.11 = (f32[256,128]{1,0:T(8,128)S(1)}, f32[256,128]{1,0:T(8,128)S(1)}, u32[]{:S(2)}, u32[]{:S(2)}) collective-permute-start(f32[256,128]{1,0:T(8,128)S(1)} %get-tuple-element.27), channel_id=1, source_target_pairs={{0,24},{4,28},{8,16},{12,20},{16,8},{20,12},{24,0},{28,4},{1,25},{... | collective-permute-start | bytes 393224 | tf_op jit(solution)/shard_map/ppermute | solution.py:24
  65.5 6.8 %collective-permute-start.10 = (f32[256,128]{1,0:T(8,128)S(1)}, f32[256,128]{1,0:T(8,128)S(1)}, u32[]{:S(2)}, u32[]{:S(2)}) collective-permute-start(f32[256,128]{1,0:T(8,128)S(1)} %get-tuple-element.26), channel_id=1, source_target_pairs={{0,16},{4,20},{8,24},{12,28},{16,0},{20,4},{24,8},{28,12},{1,17},{... | collective-permute-start | bytes 393224 | tf_op jit(solution)/shard_map/ppermute | solution.py:24
  66.0 6.4 %collective-permute-start.9 = (f32[256,128]{1,0:T(8,128)S(1)}, f32[256,128]{1,0:T(8,128)S(1)}, u32[]{:S(2)}, u32[]{:S(2)}) collective-permute-start(f32[256,128]{1,0:T(8,128)S(1)} %get-tuple-element.25), channel_id=1, source_target_pairs={{0,8},{4,12},{8,0},{12,4},{16,24},{20,28},{24,16},{28,20},{1,9},{5... | collective-permute-start | bytes 393224 | tf_op jit(solution)/shard_map/ppermute | solution.py:24
  72.5 17.3 %collective-permute-start.21 = (f32[4,256,128]{2,1,0:T(8,128)}, f32[4,256,128]{2,1,0:T(8,128)S(1)}, u32[]{:S(2)}, u32[]{:S(2)}) collective-permute-start(f32[4,256,128]{2,1,0:T(8,128)} %collective-permute-done.19.inner_far), channel_id=1, source_target_pairs={{1,0},{2,3},{5,4},{6,7},{9,8},{10,11},{13,12},{14,15},{17,16},{18,... | collective-permute-start | bytes 1572872 | tf_op jit(solution)/shard_map/ppermute | solution.py:241
  73.8 5.8 %collective-permute-start.12 = (f32[256,128]{1,0:T(8,128)S(1)}, f32[256,128]{1,0:T(8,128)S(1)}, u32[]{:S(2)}, u32[]{:S(2)}) collective-permute-start(f32[256,128]{1,0:T(8,128)S(1)} %add_add_fusion.rest_0_.y_rows), channel_id=1, source_target_pairs={{0,8},{4,12},{8,0},{12,4},{16,24},{20,28},{24,16},{28,20},{1,9},{5... | collective-permute-start | bytes 393224 | tf_op jit(solution)/shard_map/ppermute | solution.py:24
  75.3 7.8 %collective-permute-start.13 = (f32[256,128]{1,0:T(8,128)S(1)}, f32[256,128]{1,0:T(8,128)S(1)}, u32[]{:S(2)}, u32[]{:S(2)}) collective-permute-start(f32[256,128]{1,0:T(8,128)S(1)} %add_add_fusion.rest_0_.y_rows), channel_id=1, source_target_pairs={{0,16},{4,20},{8,24},{12,28},{16,0},{20,4},{24,8},{28,12},{1,17},{... | collective-permute-start | bytes 393224 | tf_op jit(solution)/shard_map/ppermute | solution.py:24
  76.1 7.1 %collective-permute-start.14 = (f32[256,128]{1,0:T(8,128)S(1)}, f32[256,128]{1,0:T(8,128)S(1)}, u32[]{:S(2)}, u32[]{:S(2)}) collective-permute-start(f32[256,128]{1,0:T(8,128)S(1)} %add_add_fusion.rest_0_.y_rows), channel_id=1, source_target_pairs={{0,24},{4,28},{8,16},{12,20},{16,8},{20,12},{24,0},{28,4},{1,25},{... | collective-permute-start | bytes 393224 | tf_op jit(solution)/shard_map/ppermute | solution.py:24
  84.9 1.7 %collective-permute-start.15 = (f32[5,128,128]{2,1,0:T(8,128)S(1)}, f32[5,128,128]{2,1,0:T(8,128)S(1)}, u32[]{:S(2)}, u32[]{:S(2)}) collective-permute-start(f32[5,128,128]{2,1,0:T(8,128)S(1)} %shard_map.80.sent), channel_id=1, source_target_pairs={{0,4},{4,0},{8,12},{12,8},{16,20},{20,16},{24,28},{28,24},{1,5},{5... | collective-permute-start | bytes 983048 | tf_op jit(solution)/shard_map/ppermute | solution.py:24
  92.2 7.9 %collective-permute-start.22 = (f32[256,128]{1,0:T(8,128)S(1)}, f32[256,128]{1,0:T(8,128)S(1)}, u32[]{:S(2)}, u32[]{:S(2)}) collective-permute-start(f32[256,128]{1,0:T(8,128)S(1)} %get-tuple-element.36), channel_id=1, source_target_pairs={{0,8},{4,12},{8,0},{12,4},{16,24},{20,28},{24,16},{28,20},{1,9},{5... | collective-permute-start | bytes 393224 | tf_op jit(solution)/shard_map/ppermute | solution.py:24
  93.7 7.4 %collective-permute-start.23 = (f32[256,128]{1,0:T(8,128)S(1)}, f32[256,128]{1,0:T(8,128)S(1)}, u32[]{:S(2)}, u32[]{:S(2)}) collective-permute-start(f32[256,128]{1,0:T(8,128)S(1)} %get-tuple-element.37), channel_id=1, source_target_pairs={{0,16},{4,20},{8,24},{12,28},{16,0},{20,4},{24,8},{28,12},{1,17},{... | collective-permute-start | bytes 393224 | tf_op jit(solution)/shard_map/ppermute | solution.py:24
  93.8 7.3 %collective-permute-start.24 = (f32[256,128]{1,0:T(8,128)S(1)}, f32[256,128]{1,0:T(8,128)S(1)}, u32[]{:S(2)}, u32[]{:S(2)}) collective-permute-start(f32[256,128]{1,0:T(8,128)S(1)} %get-tuple-element.38), channel_id=1, source_target_pairs={{0,24},{4,28},{8,16},{12,20},{16,8},{20,12},{24,0},{28,4},{1,25},{... | collective-permute-start | bytes 393224 | tf_op jit(solution)/shard_map/ppermute | solution.py:24
  (1 other events, 0.7 us)

commit v7 on v5

--- a/solution.py
+++ b/solution.py
@@ -282,8 +282,7 @@
     for bit in range(1, chips):
         y_rows = y_rows + exchange(y_parts[bit], "step", 2 * bit)
     y_all = [y_rows] + [exchange(y_rows, "step", 2 * bit) for bit in range(1, chips)]
-    _, col_last = lax.optimization_barrier((y_rows, col_inner_far))
-    col_last = across(col_last, outward)
+    col_last = across(col_inner_far, outward)
     (sent,) = call(z_kernel, [(5, rank, rank)], [target_left, left_other, *y_all], "aa" + "v" * chips, rows_scratch)
     got = exchange(sent, "step", 1)
     w_parts = call(

time: 99 us -> 95 us (0.960)
  waiting for transfers between devices: 32.4 us -> 28.5 us
    ppermute x12, waiting for transfers between devices: 18.5 us -> 16.2 us  [across(): return lax.ppermute(array, 'tile', pairs)]
    ppermute x13, waiting for transfers between devices: 13.9 us -> 12.3 us  [exchange(): lax.ppermute(array, axis, [(i, i ^ bit) for i in range(lax.axis_size(axis...]
  transfers between devices with their start and end apart: 25 -> 25, of which waited for: 14 -> 12; matrix products, arithmetic and copies ran while one was open for 15% -> 15% of each run, Pallas kernels for 10% -> 10%
where the time goes in v7:
time: 95 us; the launch traced here: 94.3 us
  starting transfers between devices  34.9 us (37%)
  waiting for transfers between devices  28.5 us (30%)
  Pallas kernels  12.8 us (13%)
  local copies, waits for them, and re-layouts  7.61 us (8%)
  matrix products  7.5 us (8%)
  other arithmetic  2.01 us (2%)
    ppermute x12, starting transfers between devices, across(): return lax.ppermute(array, 'tile', pairs)  23.9 us
    ppermute x12, waiting for transfers between devices, across(): return lax.ppermute(array, 'tile', pairs)  16.2 us
    pallas_call x7, Pallas kernels, call(): pl.pallas_call(kernel, out_shape=shapes, in_specs=[pl.BlockSpec(memory_sp...  12.8 us
    ppermute x13, waiting for transfers between devices, exchange(): lax.ppermute(array, axis, [(i, i ^ bit) for i in range(lax.axis_size(axis...  12.3 us
    ppermute x13, starting transfers between devices, exchange(): lax.ppermute(array, axis, [(i, i ^ bit) for i in range(lax.axis_size(axis...  11 us
    dot_general x4, matrix products, mm(): jnp.einsum(spec, *arrays, precision=HIGH, preferred_element_type=jnp.floa...  7.5 us
    squeeze x3, local copies, waits for them, and re-layouts, take(): return lax.dynamic_index_in_dim(array, index, axis, keepdims=False)  5 us
    unnamed x27, local copies, waits for them, and re-layouts  2.61 us
  transfers between devices with their start and end apart: 25, of which 12 were waited for; matrix products, arithmetic and copies ran while one was open for 15% of the time, Pallas kernels for 10%

profile of v7, /device:TPU:0, one launch (start us, length us, event | category | flops | bytes accessed | tf_op | source)
XLA Modules:
  0.0 94.3 jit_solution(13128273902287483642)
XLA Ops:
  0.7 3.1 %collective-permute-start.1 = (f32[2,512,128]{2,1,0:T(8,128)}, f32[2,512,128]{2,1,0:T(8,128)}, u32[]{:S(2)}, u32[]{:S(2)}) collective-permute-start(f32[2,512,128]{2,1,0:T(8,128)} %param.9), channel_id=1, source_target_pairs={{0,1},{1,0},{2,3},{3,2},{4,5},{5,4},{6,7},{7,6},{8,9},{9,8},{10,11... | collective-permute-start | bytes 1572872 | tf_op jit(solution)/shard_map/ppermute | solution.py:242
  3.7 1.5 %collective-permute-start.2 = (f32[2,512,128]{2,1,0:T(8,128)}, f32[2,512,128]{2,1,0:T(8,128)}, u32[]{:S(2)}, u32[]{:S(2)}) collective-permute-start(f32[2,512,128]{2,1,0:T(8,128)} %param.9), channel_id=1, source_target_pairs={{1,2},{2,1},{5,6},{6,5},{9,10},{10,9},{13,14},{14,13},{17,18},{18,... | collective-permute-start | bytes 1572872 | tf_op jit(solution)/shard_map/ppermute | solution.py:242
  5.2 2.3 %dynamic-slice_bitcast_fusion = f32[2,4,256,128]{3,2,1,0:T(8,128)} fusion(f32[2,4,2,256,128]{4,3,2,1,0:T(8,128)} %bitcast.44, s32[]{:T(128)S(6)} %select_n.44), kind=kLoop, calls=%fused_computation.2 | loop fusion | bytes 2097156 | tf_op jit(solution)/shard_map/jit(dynamic_index_in_dim)/squeeze | solution.py:28
  7.5 1.6 %fusion.7 = f32[2,128,128]{2,1,0:T(8,128)S(1)} fusion(f32[2,512,128]{2,1,0:T(8,128)} %param.8, f32[512,128]{1,0:T(8,128)S(1)} %copy-done), kind=kOutput, calls=%fused_computation.13 | convolution fusion | flops 100663296 | bytes 917504 | tf_op jit(solution)/shard_map/kbq,bp->kqp/dot_general | solution.py:14
  9.1 3.7 %collective-permute-start.5 = (f32[2,128,128]{2,1,0:T(8,128)S(1)}, f32[2,128,128]{2,1,0:T(8,128)}, u32[]{:S(2)}, u32[]{:S(2)}) collective-permute-start(f32[2,128,128]{2,1,0:T(8,128)S(1)} %fusion.7), channel_id=1, source_target_pairs={{0,1},{1,0},{2,3},{3,2},{4,5},{5,4},{6,7},{7,6},{8,9},{9,8},{10,11... | collective-permute-start | bytes 393224 | tf_op jit(solution)/shard_map/ppermute | solution.py:242
  12.8 1.9 %dynamic-slice_bitcast_fusion.3 = (f32[2,256,128]{2,1,0:T(8,128)}, f32[2,256,128]{2,1,0:T(8,128)}) fusion(f32[2,2,256,128]{3,2,1,0:T(8,128)} %bitcast.50, s32[]{:T(128)S(6)} %select_n.53, s32[]{:T(128)S(6)} %select_n.44), kind=kLoop, calls=%fused_computation.16 | loop fusion | bytes 1048584 | tf_op jit(solution)/shard_map/jit(dynamic_index_in_dim)/squeeze | solution.py:28
  14.9 2.3 %fusion.2 = f32[2,128,128]{2,1,0:T(8,128)} fusion(f32[2,512,128]{2,1,0:T(8,128)} %param.9, f32[2,4,512,128]{3,2,1,0:T(8,128)S(1)} %bitcast.46, s32[]{:T(128)S(6)} %select_n.45), kind=kOutput, calls=%fused_computation.6 | convolution fusion | flops 100663296 | bytes 1179652 | tf_op jit(solution)/shard_map/kbr,kbq->krq/dot_general | solution.py:14
  20.5 5.7 %collective-permute-start.4 = (f32[2,512,128]{2,1,0:T(8,128)S(1)}, f32[2,512,128]{2,1,0:T(8,128)S(1)}, u32[]{:S(2)}, u32[]{:S(2)}) collective-permute-start(f32[2,512,128]{2,1,0:T(8,128)S(1)} %bitcast_select_fusion), channel_id=1, source_target_pairs={{0,1},{1,0},{2,3},{3,2},{4,5},{5,4},{6,7},{7,6},{8,9},{9,8},{10,11... | collective-permute-start | bytes 1572872 | tf_op jit(solution)/shard_map/ppermute | solution.py:242
  27.9 1.9 %collective-permute-start.17 = (f32[4,256,128]{2,1,0:T(8,128)S(1)}, f32[4,256,128]{2,1,0:T(8,128)}, u32[]{:S(2)}, u32[]{:S(2)}) collective-permute-start(f32[4,256,128]{2,1,0:T(8,128)S(1)} %pad_maximum_fusion.own), channel_id=1, source_target_pairs={{0,1},{1,0},{2,3},{3,2},{4,5},{5,4},{6,7},{7,6},{8,9},{9,8},{10,11... | collective-permute-start | bytes 1572872 | tf_op jit(solution)/shard_map/ppermute | solution.py:242
  29.8 1.4 %collective-permute-start.18 = (f32[4,256,128]{2,1,0:T(8,128)S(1)}, f32[4,256,128]{2,1,0:T(8,128)}, u32[]{:S(2)}, u32[]{:S(2)}) collective-permute-start(f32[4,256,128]{2,1,0:T(8,128)S(1)} %pad_maximum_fusion.own), channel_id=1, source_target_pairs={{1,2},{2,1},{5,6},{6,5},{9,10},{10,9},{13,14},{14,13},{17,18},{18,... | collective-permute-start | bytes 1572872 | tf_op jit(solution)/shard_map/ppermute | solution.py:242
  31.2 1.6 %convolution_add_fusion.1 = f32[2,128,128]{2,1,0:T(8,128)S(1)} fusion(f32[2,128,128]{2,1,0:T(8,128)S(1)} %copy-done.11, f32[2,512,128]{2,1,0:T(8,128)} %collective-permute-done.1, f32[2,4,512,128]{3,2,1,0:T(8,128)S(1)} %bitcast.49, s32[]{:T(128)S(6)} %select_n.46), kind=kOutput, calls=%fused_computation.1 | convolution fusion | flops 100696064 | bytes 1310724 | tf_op jit(solution)/shard_map/kbr,kbq->krq/dot_general | solution.py:14
  32.9 1.9 %convolution_add_fusion.part = f32[2,128,128]{2,1,0:T(8,128)S(1)} fusion(f32[2,128,128]{2,1,0:T(8,128)S(1)} %convolution_add_fusion.1, f32[2,512,128]{2,1,0:T(8,128)} %collective-permute-done.2, f32[2,4,512,128]{3,2,1,0:T(8,128)} %bitcast.45, s32[]{:T(128)S(6)} %select_n.48), kind=kOutput, calls=%fused_computation | convolution fusion | flops 100696064 | bytes 1310724 | tf_op jit(solution)/shard_map/kbr,kbq->krq/dot_general | solution.py:14
  34.8 4.2 %collective-permute-done.4.second = f32[2,512,128]{2,1,0:T(8,128)S(1)} collective-permute-done((f32[2,512,128]{2,1,0:T(8,128)S(1)}, f32[2,512,128]{2,1,0:T(8,128)S(1)}, u32[]{:S(2)}, u32[]{:S(2)}) %collective-permute-start.4) | collective-permute-done | bytes 524320 | tf_op jit(solution)/shard_map/ppermute | solution.py:242
  40.7 1.3 %collective-permute-start.7 = (f32[4,128,128]{2,1,0:T(8,128)}, f32[4,128,128]{2,1,0:T(8,128)}, u32[]{:S(2)}, u32[]{:S(2)}) collective-permute-start(f32[4,128,128]{2,1,0:T(8,128)} %get-tuple-element.22), channel_id=1, source_target_pairs={{1,0},{2,3},{5,4},{6,7},{9,8},{10,11},{13,12},{14,15},{17,16},{18,... | collective-permute-start | bytes 786440 | tf_op jit(solution)/shard_map/ppermute | solution.py:242
  42.0 8.3 %collective-permute-done.17.near = f32[4,256,128]{2,1,0:T(8,128)} collective-permute-done((f32[4,256,128]{2,1,0:T(8,128)S(1)}, f32[4,256,128]{2,1,0:T(8,128)}, u32[]{:S(2)}, u32[]{:S(2)}) %collective-permute-start.17) | collective-permute-done | bytes 524320 | tf_op jit(solution)/shard_map/ppermute | solution.py:242
  50.4 1.5 %collective-permute-start.19 = (f32[4,256,128]{2,1,0:T(8,128)}, f32[4,256,128]{2,1,0:T(8,128)}, u32[]{:S(2)}, u32[]{:S(2)}) collective-permute-start(f32[4,256,128]{2,1,0:T(8,128)} %collective-permute-done.17.near), channel_id=1, source_target_pairs={{1,2},{2,1},{5,6},{6,5},{9,10},{10,9},{13,14},{14,13},{17,18},{18,... | collective-permute-start | bytes 1572872 | tf_op jit(solution)/shard_map/ppermute | solution.py:242
  51.8 1.3 %collective-permute-start.20 = (f32[4,256,128]{2,1,0:T(8,128)}, f32[4,256,128]{2,1,0:T(8,128)}, u32[]{:S(2)}, u32[]{:S(2)}) collective-permute-start(f32[4,256,128]{2,1,0:T(8,128)} %collective-permute-done.18.inner), channel_id=1, source_target_pairs={{1,0},{2,3},{5,4},{6,7},{9,8},{10,11},{13,12},{14,15},{17,16},{18,... | collective-permute-start | bytes 1572872 | tf_op jit(solution)/shard_map/ppermute | solution.py:242
  57.0 1.5 %collective-permute-done.8.both_other = f32[4,128,128]{2,1,0:T(8,128)S(1)} collective-permute-done((f32[4,128,128]{2,1,0:T(8,128)S(1)}, f32[4,128,128]{2,1,0:T(8,128)S(1)}, u32[]{:S(2)}, u32[]{:S(2)}) %collective-permute-start.8) | collective-permute-done | bytes 262176 | tf_op jit(solution)/shard_map/ppermute | solution.py:24
  58.5 1.5 %shard_map.79 = (f32[256,128]{1,0:T(8,128)S(1)}, f32[256,128]{1,0:T(8,128)S(1)}, f32[256,128]{1,0:T(8,128)S(1)}, f32[256,128]{1,0:T(8,128)S(1)}) custom-call(f32[2,1,2048,128]{3,2,1,0:T(8,128)S(1)} %copy-done.1, f32[2,4,256,128]{3,2,1,0:T(8,128)S(1)} %collective-permute-done.left_other, f32[4,128,128]{2,1,0:T(8,128)S(1)} %shard_map.78.both, ...), custom_call_target="tpu_custom_call" | custom-call | tf_op jit(solution)/shard_map/pallas_call | solution.py:78
  59.9 2.5 %collective-permute-start.11 = (f32[256,128]{1,0:T(8,128)S(1)}, f32[256,128]{1,0:T(8,128)S(1)}, u32[]{:S(2)}, u32[]{:S(2)}) collective-permute-start(f32[256,128]{1,0:T(8,128)S(1)} %get-tuple-element.26), channel_id=1, source_target_pairs={{0,24},{4,28},{8,16},{12,20},{16,8},{20,12},{24,0},{28,4},{1,25},{... | collective-permute-start | bytes 393224 | tf_op jit(solution)/shard_map/ppermute | solution.py:24
  63.5 2.3 %collective-permute-done.20.outer = f32[4,256,128]{2,1,0:T(8,128)} collective-permute-done((f32[4,256,128]{2,1,0:T(8,128)}, f32[4,256,128]{2,1,0:T(8,128)}, u32[]{:S(2)}, u32[]{:S(2)}) %collective-permute-start.20) | collective-permute-done | bytes 524320 | tf_op jit(solution)/shard_map/ppermute | solution.py:242
  65.8 1.3 %collective-permute-start.21 = (f32[4,256,128]{2,1,0:T(8,128)}, f32[4,256,128]{2,1,0:T(8,128)S(1)}, u32[]{:S(2)}, u32[]{:S(2)}) collective-permute-start(f32[4,256,128]{2,1,0:T(8,128)} %collective-permute-done.19.inner_far), channel_id=1, source_target_pairs={{1,0},{2,3},{5,4},{6,7},{9,8},{10,11},{13,12},{14,15},{17,16},{18,... | collective-permute-start | bytes 1572872 | tf_op jit(solution)/shard_map/ppermute | solution.py:242
  67.1 2.2 %collective-permute-done.10 = f32[256,128]{1,0:T(8,128)S(1)} collective-permute-done((f32[256,128]{1,0:T(8,128)S(1)}, f32[256,128]{1,0:T(8,128)S(1)}, u32[]{:S(2)}, u32[]{:S(2)}) %collective-permute-start.10) | collective-permute-done | bytes 131104 | tf_op jit(solution)/shard_map/ppermute | solution.py:24
  69.4 1.6 %collective-permute-start.12 = (f32[256,128]{1,0:T(8,128)S(1)}, f32[256,128]{1,0:T(8,128)S(1)}, u32[]{:S(2)}, u32[]{:S(2)}) collective-permute-start(f32[256,128]{1,0:T(8,128)S(1)} %add_add_fusion.rest_0_.y_rows), channel_id=1, source_target_pairs={{0,8},{4,12},{8,0},{12,4},{16,24},{20,28},{24,16},{28,20},{1,9},{5... | collective-permute-start | bytes 393224 | tf_op jit(solution)/shard_map/ppermute | solution.py:24
  71.7 1.3 %collective-permute-start.14 = (f32[256,128]{1,0:T(8,128)S(1)}, f32[256,128]{1,0:T(8,128)S(1)}, u32[]{:S(2)}, u32[]{:S(2)}) collective-permute-start(f32[256,128]{1,0:T(8,128)S(1)} %add_add_fusion.rest_0_.y_rows), channel_id=1, source_target_pairs={{0,24},{4,28},{8,16},{12,20},{16,8},{20,12},{24,0},{28,4},{1,25},{... | collective-permute-start | bytes 393224 | tf_op jit(solution)/shard_map/ppermute | solution.py:24
  72.9 2.2 %collective-permute-done.12.rest_1_ = f32[256,128]{1,0:T(8,128)S(1)} collective-permute-done((f32[256,128]{1,0:T(8,128)S(1)}, f32[256,128]{1,0:T(8,128)S(1)}, u32[]{:S(2)}, u32[]{:S(2)}) %collective-permute-start.12) | collective-permute-done | bytes 131104 | tf_op jit(solution)/shard_map/ppermute | solution.py:24
  75.2 3.6 %collective-permute-done.13.rest_2_ = f32[256,128]{1,0:T(8,128)S(1)} collective-permute-done((f32[256,128]{1,0:T(8,128)S(1)}, f32[256,128]{1,0:T(8,128)S(1)}, u32[]{:S(2)}, u32[]{:S(2)}) %collective-permute-start.13) | collective-permute-done | bytes 131104 | tf_op jit(solution)/shard_map/ppermute | solution.py:24
  78.8 1.7 %shard_map.80.sent = f32[5,128,128]{2,1,0:T(8,128)S(1)} custom-call(f32[2,1,2048,128]{3,2,1,0:T(8,128)S(1)} %copy-done.1, f32[2,4,256,128]{3,2,1,0:T(8,128)S(1)} %collective-permute-done.left_other, f32[256,128]{1,0:T(8,128)S(1)} %add_add_fusion.rest_0_.y_rows, f32[256,128]{1,0:T(8,128)S(1)} %collective-permute-done.12.rest_1_, ...), custom_call_target="tpu_custom_call" | custom-call | tf_op jit(solution)/shard_map/pallas_call | solution.py:78
  80.7 1.6 %collective-permute-done.15.got = f32[5,128,128]{2,1,0:T(8,128)S(1)} collective-permute-done((f32[5,128,128]{2,1,0:T(8,128)S(1)}, f32[5,128,128]{2,1,0:T(8,128)S(1)}, u32[]{:S(2)}, u32[]{:S(2)}) %collective-permute-start.15) | collective-permute-done | bytes 327712 | tf_op jit(solution)/shard_map/ppermute | solution.py:24
  82.3 2.1 %shard_map.82 = (f32[256,128]{1,0:T(8,128)S(1)}, f32[256,128]{1,0:T(8,128)S(1)}, f32[256,128]{1,0:T(8,128)S(1)}, f32[256,128]{1,0:T(8,128)S(1)}) custom-call(f32[5,128,128]{2,1,0:T(8,128)S(1)} %shard_map.80.sent, f32[5,128,128]{2,1,0:T(8,128)S(1)} %collective-permute-done.15.got, f32[4,128,128]{2,1,0:T(8,128)S(1)} %shard_map.78.both, ...), custom_call_target="tpu_custom_call" | custom-call | tf_op jit(solution)/shard_map/pallas_call | solution.py:78
  86.5 1.4 %collective-permute-start.24 = (f32[256,128]{1,0:T(8,128)S(1)}, f32[256,128]{1,0:T(8,128)S(1)}, u32[]{:S(2)}, u32[]{:S(2)}) collective-permute-start(f32[256,128]{1,0:T(8,128)S(1)} %get-tuple-element.36), channel_id=1, source_target_pairs={{0,24},{4,28},{8,16},{12,20},{16,8},{20,12},{24,0},{28,4},{1,25},{... | collective-permute-start | bytes 393224 | tf_op jit(solution)/shard_map/ppermute | solution.py:24
  87.9 4.4 %shard_map.81 = (f32[256,128]{1,0:T(8,128)}, f32[128,128]{1,0:T(8,128)S(1)}) custom-call(f32[5,128,128]{2,1,0:T(8,128)S(1)} %shard_map.80.sent, f32[5,128,128]{2,1,0:T(8,128)S(1)} %collective-permute-done.15.got, f32[256,128]{1,0:T(8,128)S(1)} %add_add_fusion.rest_0_.y_rows), custom_call_target="tpu_custom_call" | custom-call | flops 1000000000 | tf_op jit(solution)/shard_map/pallas_call | solution.py:78
  (63 shorter events, 16.8 us)
Async XLA Ops:
  0.6 14.3 %copy-start.9 = (f32[2,1,2048,128]{3,2,1,0:T(8,128)S(1)}, f32[2,1,2048,128]{3,2,1,0:T(8,128)}, u32[]{:S(2)}) copy-start(f32[2,1,2048,128]{3,2,1,0:T(8,128)} %param.7) | copy-start | bytes 6291460
  0.7 19.1 %collective-permute-start.1 = (f32[2,512,128]{2,1,0:T(8,128)}, f32[2,512,128]{2,1,0:T(8,128)}, u32[]{:S(2)}, u32[]{:S(2)}) collective-permute-start(f32[2,512,128]{2,1,0:T(8,128)} %param.9), channel_id=1, source_target_pairs={{0,1},{1,0},{2,3},{3,2},{4,5},{5,4},{6,7},{7,6},{8,9},{9,8},{10,11... | collective-permute-start | bytes 1572872 | tf_op jit(solution)/shard_map/ppermute | solution.py:242
  3.7 16.7 %collective-permute-start.2 = (f32[2,512,128]{2,1,0:T(8,128)}, f32[2,512,128]{2,1,0:T(8,128)}, u32[]{:S(2)}, u32[]{:S(2)}) collective-permute-start(f32[2,512,128]{2,1,0:T(8,128)} %param.9), channel_id=1, source_target_pairs={{1,2},{2,1},{5,6},{6,5},{9,10},{10,9},{13,14},{14,13},{17,18},{18,... | collective-permute-start | bytes 1572872 | tf_op jit(solution)/shard_map/ppermute | solution.py:242
  7.5 49.4 %collective-permute-start = (f32[2,4,256,128]{3,2,1,0:T(8,128)}, f32[2,4,256,128]{3,2,1,0:T(8,128)S(1)}, u32[]{:S(2)}, u32[]{:S(2)}) collective-permute-start(f32[2,4,256,128]{3,2,1,0:T(8,128)} %dynamic-slice_bitcast_fusion), channel_id=1, source_target_pairs={{0,4},{4,0},{8,12},{12,8},{16,20},{20,16},{24,28},{28,24},{1,5},{5... | collective-permute-start | bytes 3145736 | tf_op jit(solution)/shard_map/ppermute | solution.py:24
  9.1 9.6 %collective-permute-start.5 = (f32[2,128,128]{2,1,0:T(8,128)S(1)}, f32[2,128,128]{2,1,0:T(8,128)}, u32[]{:S(2)}, u32[]{:S(2)}) collective-permute-start(f32[2,128,128]{2,1,0:T(8,128)S(1)} %fusion.7), channel_id=1, source_target_pairs={{0,1},{1,0},{2,3},{3,2},{4,5},{5,4},{6,7},{7,6},{8,9},{9,8},{10,11... | collective-permute-start | bytes 393224 | tf_op jit(solution)/shard_map/ppermute | solution.py:242
  14.7 12.2 %collective-permute-start.16 = (f32[2,256,128]{2,1,0:T(8,128)}, f32[2,256,128]{2,1,0:T(8,128)}, u32[]{:S(2)}, u32[]{:S(2)}) collective-permute-start(f32[2,256,128]{2,1,0:T(8,128)} %get-tuple-element.39), channel_id=1, source_target_pairs={{0,4},{4,0},{8,12},{12,8},{16,20},{20,16},{24,28},{28,24},{1,5},{5... | collective-permute-start | bytes 786440 | tf_op jit(solution)/shard_map/ppermute | solution.py:24
  18.1 13.2 %copy-start.11 = (f32[2,128,128]{2,1,0:T(8,128)S(1)}, f32[2,128,128]{2,1,0:T(8,128)}, u32[]{:S(2)}) copy-start(f32[2,128,128]{2,1,0:T(8,128)} %fusion.2) | copy-start | bytes 393220
  19.7 15.1 %copy-start.5 = (f32[2,128,128]{2,1,0:T(8,128)}, f32[2,128,128]{2,1,0:T(8,128)S(1)}, u32[]{:S(2)}) copy-start(f32[2,128,128]{2,1,0:T(8,128)S(1)} %add.58.probe_here) | copy-start | bytes 393220
  19.7 10.0 %collective-permute-start.6 = (f32[2,128,128]{2,1,0:T(8,128)S(1)}, f32[2,128,128]{2,1,0:T(8,128)S(1)}, u32[]{:S(2)}, u32[]{:S(2)}) collective-permute-start(f32[2,128,128]{2,1,0:T(8,128)S(1)} %add.58.probe_here), channel_id=1, source_target_pairs={{1,2},{2,1},{5,6},{6,5},{9,10},{10,9},{13,14},{14,13},{17,18},{18,... | collective-permute-start | bytes 393224 | tf_op jit(solution)/shard_map/ppermute | solution.py:242
  20.5 18.5 %copy-start.4 = (f32[2,512,128]{2,1,0:T(8,128)S(1)}, f32[2,512,128]{2,1,0:T(8,128)}, u32[]{:S(2)}) copy-start(f32[2,512,128]{2,1,0:T(8,128)} %dynamic-slice_bitcast_fusion.1.own_rows) | copy-start | bytes 1572868
  20.5 18.5 %collective-permute-start.4 = (f32[2,512,128]{2,1,0:T(8,128)S(1)}, f32[2,512,128]{2,1,0:T(8,128)S(1)}, u32[]{:S(2)}, u32[]{:S(2)}) collective-permute-start(f32[2,512,128]{2,1,0:T(8,128)S(1)} %bitcast_select_fusion), channel_id=1, source_target_pairs={{0,1},{1,0},{2,3},{3,2},{4,5},{5,4},{6,7},{7,6},{8,9},{9,8},{10,11... | collective-permute-start | bytes 1572872 | tf_op jit(solution)/shard_map/ppermute | solution.py:242
  26.2 8.7 %collective-permute-start.3 = (f32[2,512,128]{2,1,0:T(8,128)}, f32[2,512,128]{2,1,0:T(8,128)S(1)}, u32[]{:S(2)}, u32[]{:S(2)}) collective-permute-start(f32[2,512,128]{2,1,0:T(8,128)} %collective-permute-done.1), channel_id=1, source_target_pairs={{1,2},{2,1},{5,6},{6,5},{9,10},{10,9},{13,14},{14,13},{17,18},{18,... | collective-permute-start | bytes 1572872 | tf_op jit(solution)/shard_map/ppermute | solution.py:242
  27.9 25.2 %copy-start.12 = (s32[2,1]{0,1:T(1,128)S(1)}, s32[2,1]{0,1:T(1,128)}, u32[]{:S(2)}) copy-start(s32[2,1]{0,1:T(1,128)} %param.11) | copy-start | bytes 28
  27.9 22.5 %collective-permute-start.17 = (f32[4,256,128]{2,1,0:T(8,128)S(1)}, f32[4,256,128]{2,1,0:T(8,128)}, u32[]{:S(2)}, u32[]{:S(2)}) collective-permute-start(f32[4,256,128]{2,1,0:T(8,128)S(1)} %pad_maximum_fusion.own), channel_id=1, source_target_pairs={{0,1},{1,0},{2,3},{3,2},{4,5},{5,4},{6,7},{7,6},{8,9},{9,8},{10,11... | collective-permute-start | bytes 1572872 | tf_op jit(solution)/shard_map/ppermute | solution.py:242
  29.8 20.6 %collective-permute-start.18 = (f32[4,256,128]{2,1,0:T(8,128)S(1)}, f32[4,256,128]{2,1,0:T(8,128)}, u32[]{:S(2)}, u32[]{:S(2)}) collective-permute-start(f32[4,256,128]{2,1,0:T(8,128)S(1)} %pad_maximum_fusion.own), channel_id=1, source_target_pairs={{1,2},{2,1},{5,6},{6,5},{9,10},{10,9},{13,14},{14,13},{17,18},{18,... | collective-permute-start | bytes 1572872 | tf_op jit(solution)/shard_map/ppermute | solution.py:242
  32.9 25.6 %copy-start.1 = (f32[2,1,2048,128]{3,2,1,0:T(8,128)S(1)}, f32[2,1,2048,128]{3,2,1,0:T(8,128)}, u32[]{:S(2)}) copy-start(f32[2,1,2048,128]{3,2,1,0:T(8,128)} %left.3) | copy-start | bytes 6291460
  40.7 13.2 %collective-permute-start.7 = (f32[4,128,128]{2,1,0:T(8,128)}, f32[4,128,128]{2,1,0:T(8,128)}, u32[]{:S(2)}, u32[]{:S(2)}) collective-permute-start(f32[4,128,128]{2,1,0:T(8,128)} %get-tuple-element.22), channel_id=1, source_target_pairs={{1,0},{2,3},{5,4},{6,7},{9,8},{10,11},{13,12},{14,15},{17,16},{18,... | collective-permute-start | bytes 786440 | tf_op jit(solution)/shard_map/ppermute | solution.py:242
  50.4 13.1 %collective-permute-start.19 = (f32[4,256,128]{2,1,0:T(8,128)}, f32[4,256,128]{2,1,0:T(8,128)}, u32[]{:S(2)}, u32[]{:S(2)}) collective-permute-start(f32[4,256,128]{2,1,0:T(8,128)} %collective-permute-done.17.near), channel_id=1, source_target_pairs={{1,2},{2,1},{5,6},{6,5},{9,10},{10,9},{13,14},{14,13},{17,18},{18,... | collective-permute-start | bytes 1572872 | tf_op jit(solution)/shard_map/ppermute | solution.py:242
  51.8 14.0 %collective-permute-start.20 = (f32[4,256,128]{2,1,0:T(8,128)}, f32[4,256,128]{2,1,0:T(8,128)}, u32[]{:S(2)}, u32[]{:S(2)}) collective-permute-start(f32[4,256,128]{2,1,0:T(8,128)} %collective-permute-done.18.inner), channel_id=1, source_target_pairs={{1,0},{2,3},{5,4},{6,7},{9,8},{10,11},{13,12},{14,15},{17,16},{18,... | collective-permute-start | bytes 1572872 | tf_op jit(solution)/shard_map/ppermute | solution.py:242
  56.9 1.6 %collective-permute-start.8 = (f32[4,128,128]{2,1,0:T(8,128)S(1)}, f32[4,128,128]{2,1,0:T(8,128)S(1)}, u32[]{:S(2)}, u32[]{:S(2)}) collective-permute-start(f32[4,128,128]{2,1,0:T(8,128)S(1)} %shard_map.78.both), channel_id=1, source_target_pairs={{0,4},{4,0},{8,12},{12,8},{16,20},{20,16},{24,28},{28,24},{1,5},{5... | collective-permute-start | bytes 786440 | tf_op jit(solution)/shard_map/ppermute | solution.py:24
  59.9 7.1 %collective-permute-start.11 = (f32[256,128]{1,0:T(8,128)S(1)}, f32[256,128]{1,0:T(8,128)S(1)}, u32[]{:S(2)}, u32[]{:S(2)}) collective-permute-start(f32[256,128]{1,0:T(8,128)S(1)} %get-tuple-element.26), channel_id=1, source_target_pairs={{0,24},{4,28},{8,16},{12,20},{16,8},{20,12},{24,0},{28,4},{1,25},{... | collective-permute-start | bytes 393224 | tf_op jit(solution)/shard_map/ppermute | solution.py:24
  62.5 6.8 %collective-permute-start.10 = (f32[256,128]{1,0:T(8,128)S(1)}, f32[256,128]{1,0:T(8,128)S(1)}, u32[]{:S(2)}, u32[]{:S(2)}) collective-permute-start(f32[256,128]{1,0:T(8,128)S(1)} %get-tuple-element.25), channel_id=1, source_target_pairs={{0,16},{4,20},{8,24},{12,28},{16,0},{20,4},{24,8},{28,12},{1,17},{... | collective-permute-start | bytes 393224 | tf_op jit(solution)/shard_map/ppermute | solution.py:24
  63.0 6.4 %collective-permute-start.9 = (f32[256,128]{1,0:T(8,128)S(1)}, f32[256,128]{1,0:T(8,128)S(1)}, u32[]{:S(2)}, u32[]{:S(2)}) collective-permute-start(f32[256,128]{1,0:T(8,128)S(1)} %get-tuple-element.24), channel_id=1, source_target_pairs={{0,8},{4,12},{8,0},{12,4},{16,24},{20,28},{24,16},{28,20},{1,9},{5... | collective-permute-start | bytes 393224 | tf_op jit(solution)/shard_map/ppermute | solution.py:24
  65.8 14.9 %collective-permute-start.21 = (f32[4,256,128]{2,1,0:T(8,128)}, f32[4,256,128]{2,1,0:T(8,128)S(1)}, u32[]{:S(2)}, u32[]{:S(2)}) collective-permute-start(f32[4,256,128]{2,1,0:T(8,128)} %collective-permute-done.19.inner_far), channel_id=1, source_target_pairs={{1,0},{2,3},{5,4},{6,7},{9,8},{10,11},{13,12},{14,15},{17,16},{18,... | collective-permute-start | bytes 1572872 | tf_op jit(solution)/shard_map/ppermute | solution.py:242
  69.4 12.9 %copy-start.3 = (f32[4,256,128]{2,1,0:T(8,128)S(1)}, f32[4,256,128]{2,1,0:T(8,128)}, u32[]{:S(2)}) copy-start(f32[4,256,128]{2,1,0:T(8,128)} %copy-done.2) | copy-start | bytes 1572868
  69.4 5.8 %collective-permute-start.12 = (f32[256,128]{1,0:T(8,128)S(1)}, f32[256,128]{1,0:T(8,128)S(1)}, u32[]{:S(2)}, u32[]{:S(2)}) collective-permute-start(f32[256,128]{1,0:T(8,128)S(1)} %add_add_fusion.rest_0_.y_rows), channel_id=1, source_target_pairs={{0,8},{4,12},{8,0},{12,4},{16,24},{20,28},{24,16},{28,20},{1,9},{5... | collective-permute-start | bytes 393224 | tf_op jit(solution)/shard_map/ppermute | solution.py:24
  71.0 7.8 %collective-permute-start.13 = (f32[256,128]{1,0:T(8,128)S(1)}, f32[256,128]{1,0:T(8,128)S(1)}, u32[]{:S(2)}, u32[]{:S(2)}) collective-permute-start(f32[256,128]{1,0:T(8,128)S(1)} %add_add_fusion.rest_0_.y_rows), channel_id=1, source_target_pairs={{0,16},{4,20},{8,24},{12,28},{16,0},{20,4},{24,8},{28,12},{1,17},{... | collective-permute-start | bytes 393224 | tf_op jit(solution)/shard_map/ppermute | solution.py:24
  71.7 7.1 %collective-permute-start.14 = (f32[256,128]{1,0:T(8,128)S(1)}, f32[256,128]{1,0:T(8,128)S(1)}, u32[]{:S(2)}, u32[]{:S(2)}) collective-permute-start(f32[256,128]{1,0:T(8,128)S(1)} %add_add_fusion.rest_0_.y_rows), channel_id=1, source_target_pairs={{0,24},{4,28},{8,16},{12,20},{16,8},{20,12},{24,0},{28,4},{1,25},{... | collective-permute-start | bytes 393224 | tf_op jit(solution)/shard_map/ppermute | solution.py:24
  80.6 1.7 %collective-permute-start.15 = (f32[5,128,128]{2,1,0:T(8,128)S(1)}, f32[5,128,128]{2,1,0:T(8,128)S(1)}, u32[]{:S(2)}, u32[]{:S(2)}) collective-permute-start(f32[5,128,128]{2,1,0:T(8,128)S(1)} %shard_map.80.sent), channel_id=1, source_target_pairs={{0,4},{4,0},{8,12},{12,8},{16,20},{20,16},{24,28},{28,24},{1,5},{5... | collective-permute-start | bytes 983048 | tf_op jit(solution)/shard_map/ppermute | solution.py:24
  84.4 7.9 %collective-permute-start.22 = (f32[256,128]{1,0:T(8,128)S(1)}, f32[256,128]{1,0:T(8,128)S(1)}, u32[]{:S(2)}, u32[]{:S(2)}) collective-permute-start(f32[256,128]{1,0:T(8,128)S(1)} %get-tuple-element.34), channel_id=1, source_target_pairs={{0,8},{4,12},{8,0},{12,4},{16,24},{20,28},{24,16},{28,20},{1,9},{5... | collective-permute-start | bytes 393224 | tf_op jit(solution)/shard_map/ppermute | solution.py:24
  85.3 8.1 %collective-permute-start.23 = (f32[256,128]{1,0:T(8,128)S(1)}, f32[256,128]{1,0:T(8,128)S(1)}, u32[]{:S(2)}, u32[]{:S(2)}) collective-permute-start(f32[256,128]{1,0:T(8,128)S(1)} %get-tuple-element.35), channel_id=1, source_target_pairs={{0,16},{4,20},{8,24},{12,28},{16,0},{20,4},{24,8},{28,12},{1,17},{... | collective-permute-start | bytes 393224 | tf_op jit(solution)/shard_map/ppermute | solution.py:24
  86.5 6.9 %collective-permute-start.24 = (f32[256,128]{1,0:T(8,128)S(1)}, f32[256,128]{1,0:T(8,128)S(1)}, u32[]{:S(2)}, u32[]{:S(2)}) collective-permute-start(f32[256,128]{1,0:T(8,128)S(1)} %get-tuple-element.36), channel_id=1, source_target_pairs={{0,24},{4,28},{8,16},{12,20},{16,8},{20,12},{24,0},{28,4},{1,25},{... | collective-permute-start | bytes 393224 | tf_op jit(solution)/shard_map/ppermute | solution.py:24
  (6 other events, 30.4 us)

commit v8 on v6

--- a/solution.py
+++ b/solution.py
@@ -86,21 +86,36 @@
     )(*args)
 
 
-def core_kernel(planes, part, own_rows, first, second, core, lent):
+def lent_kernel(planes, first, second, lent):
     plane = lax.axis_index("tile")
     is_end = jnp.logical_or(plane == 0, plane == planes - 1)
 
     @pl.when(is_end)
     def _():
         for k in range(2):
-            core[k] = part[k] + dot3(own_rows[k], second[k], TN)
-            lent[k] = jnp.zeros_like(core[k])
+            lent[k] = jnp.zeros(lent.shape[1:], jnp.float32)
 
     @pl.when(jnp.logical_not(is_end))
     def _():
         for k in range(2):
-            core[k] = part[k] + dot3(own_rows[k], first[k], TN)
             lent[k] = dot3(second[k], first[k], TN)
+
+
+def core_kernel(planes, part, right, first, second, core):
+    plane = lax.axis_index("tile")
+    rows = first.shape[1]
+    far = pl.ds(pl.multiple_of(jnp.bitwise_xor(plane, 2) * rows, rows), rows)
+    is_end = jnp.logical_or(plane == 0, plane == planes - 1)
+
+    @pl.when(is_end)
+    def _():
+        for k in range(2):
+            core[k] = part[k] + dot3(right[k, 0, far, :], second[k], TN)
+
+    @pl.when(jnp.logical_not(is_end))
+    def _():
+        for k in range(2):
+            core[k] = part[k] + dot3(right[k, 0, far, :], first[k], TN)
 
 
 def reduced_kernel(core, lent, probe_here, probe_far, pattern, both):
@@ -244,6 +259,7 @@
     inner = across(column_right, inner_pairs)
     probes = mm("kbq,bp->kqp", column_left, sketch)
     probes = probes + across(probes, outer_pairs)
+    near, inner = lax.optimization_barrier((near, inner))
     right_blocks = target_right.reshape(2, planes, -1, rank)
 
     def block(index):
@@ -259,25 +275,22 @@
     )
     _, probes_held = lax.optimization_barrier(((near, inner), probes))
     probes_far = exchange(probes_held, "tile", 2)
-    core, lent = call(
-        functools.partial(core_kernel, planes),
-        [(2, rank, rank)] * 2,
-        [part, block(plane ^ 2), inner_far, outer],
-    )
+    (lent,) = call(functools.partial(lent_kernel, planes), [(2, rank, rank)], [inner_far, outer])
+    (core,) = call(functools.partial(core_kernel, planes), [(2, rank, rank)], [part, target_right, inner_far, outer])
     lent = across(lent, outward)
 
     left_split = target_left.reshape(2, chips, 2, row_count, rank)
     left_other = exchange(take(left_split, 1 - core_bit, 2), "step", 1)
     col_split = column_left.reshape(2, 2, row_count, rank)
     col_half = jnp.concatenate([take(col_split, core_bit, 1), exchange(take(col_split, 1 - core_bit, 1), "step", 1)])
-    _, col_held = lax.optimization_barrier((near, col_half))
+    _, col_held = lax.optimization_barrier((part, col_half))
     col_near = across(col_held, outer_pairs)
     col_inner = across(col_held, inner_pairs)
-    col_near, col_inner = lax.optimization_barrier((col_near, col_inner))
-    col_inner_far = across(col_near, inner_pairs)
-    col_outer = across(col_inner, outward)
+    (both,) = call(reduced_kernel, [(4, rank, rank)], [core, lent, probes, probes_far, pattern], "vvvvs")
+    _, near_held, inner_held = lax.optimization_barrier((both, col_near, col_inner))
+    col_inner_far = across(near_held, inner_pairs)
+    col_outer = across(inner_held, outward)
     col_inner_far, col_outer = lax.optimization_barrier((col_inner_far, col_outer))
-    (both,) = call(reduced_kernel, [(4, rank, rank)], [core, lent, probes, probes_far, pattern], "vvvvs")
     both_other = exchange(both, "step", 1)
     rows_scratch = [pltpu.VMEM((chips, 4, row_count, rank), jnp.float32), pltpu.SemaphoreType.DMA((2 * chips,))]
     y_parts = call(y_kernel, [(row_count, rank)] * chips, [target_left, left_other, both, both_other], "aavv", rows_scratch)
@@ -285,8 +298,7 @@
     for bit in range(1, chips):
         y_rows = y_rows + exchange(y_parts[bit], "step", 2 * bit)
     y_all = [y_rows] + [exchange(y_rows, "step", 2 * bit) for bit in range(1, chips)]
-    _, col_last = lax.optimization_barrier((y_rows, col_inner_far))
-    col_last = across(col_last, outward)
+    col_last = across(col_inner_far, outward)
     (sent,) = call(z_kernel, [(5, rank, rank)], [target_left, left_other, *y_all], "aa" + "v" * chips, rows_scratch)
     got = exchange(sent, "step", 1)
     w_parts = call(

time: 103 us -> 94.5 us (0.917)
  starting transfers between devices: 46.9 us -> 39.2 us
  local copies, waits for them, and re-layouts: 6.64 us -> 8.18 us
  Pallas kernels: 14.3 us -> 13.2 us
    ppermute x14, starting transfers between devices: 26.3 us -> 18.2 us  [exchange(): lax.ppermute(array, axis, [(i, i ^ bit) for i in range(lax.axis_size(axis...]
    ppermute x14, waiting for transfers between devices: 12.2 us -> 17 us  [exchange(): lax.ppermute(array, axis, [(i, i ^ bit) for i in range(lax.axis_size(axis...]
    ppermute x11, waiting for transfers between devices: 9.78 us -> 5.25 us  [across(): return lax.ppermute(array, 'tile', pairs)]
    unnamed x17 -> x21, local copies, waits for them, and re-layouts: 1.69 us -> 4.06 us
    pallas_call x7 -> x8, Pallas kernels: 14.3 us -> 13.2 us  [call(): pl.pallas_call(kernel, out_shape=shapes, in_specs=[pl.BlockSpec(memory_sp...]
    squeeze x3 -> x2, local copies, waits for them, and re-layouts: 4.95 us -> 4.13 us  [take(): return lax.dynamic_index_in_dim(array, index, axis, keepdims=False)]
  transfers between devices with their start and end apart: 25 -> 25, of which waited for: 10 -> 10; matrix products, arithmetic and copies ran while one was open for 16% -> 15% of each run, Pallas kernels for 11% -> 10%
where the time goes in v8:
time: 94.5 us; the launch traced here: 93.8 us
  starting transfers between devices  39.2 us (41%)
  waiting for transfers between devices  22.2 us (23%)
  Pallas kernels  13.2 us (14%)
  local copies, waits for them, and re-layouts  8.18 us (9%)
  matrix products  7.19 us (8%)
  other arithmetic  2.96 us (3%)
    ppermute x11, starting transfers between devices, across(): return lax.ppermute(array, 'tile', pairs)  21 us
    ppermute x14, starting transfers between devices, exchange(): lax.ppermute(array, axis, [(i, i ^ bit) for i in range(lax.axis_size(axis...  18.2 us
    ppermute x14, waiting for transfers between devices, exchange(): lax.ppermute(array, axis, [(i, i ^ bit) for i in range(lax.axis_size(axis...  17 us
    pallas_call x8, Pallas kernels, call(): pl.pallas_call(kernel, out_shape=shapes, in_specs=[pl.BlockSpec(memory_sp...  13.2 us
    dot_general x4, matrix products, mm(): jnp.einsum(spec, *arrays, precision=HIGH, preferred_element_type=jnp.floa...  7.19 us
    ppermute x11, waiting for transfers between devices, across(): return lax.ppermute(array, 'tile', pairs)  5.25 us
    squeeze x2, local copies, waits for them, and re-layouts, take(): return lax.dynamic_index_in_dim(array, index, axis, keepdims=False)  4.13 us
    unnamed x21, local copies, waits for them, and re-layouts  4.06 us
  transfers between devices with their start and end apart: 25, of which 10 were waited for; matrix products, arithmetic and copies ran while one was open for 15% of the time, Pallas kernels for 10%

profile of v8, /device:TPU:0, one launch (start us, length us, event | category | flops | bytes accessed | tf_op | source)
XLA Modules:
  0.0 93.8 jit_solution(1825597508154303395)
XLA Ops:
  0.7 3.1 %collective-permute-start.1 = (f32[2,512,128]{2,1,0:T(8,128)}, f32[2,512,128]{2,1,0:T(8,128)}, u32[]{:S(2)}, u32[]{:S(2)}) collective-permute-start(f32[2,512,128]{2,1,0:T(8,128)} %param.9), channel_id=1, source_target_pairs={{0,1},{1,0},{2,3},{3,2},{4,5},{5,4},{6,7},{7,6},{8,9},{9,8},{10,11... | collective-permute-start | bytes 1572872 | tf_op jit(solution)/shard_map/ppermute | solution.py:256
  3.7 1.5 %collective-permute-start.2 = (f32[2,512,128]{2,1,0:T(8,128)}, f32[2,512,128]{2,1,0:T(8,128)}, u32[]{:S(2)}, u32[]{:S(2)}) collective-permute-start(f32[2,512,128]{2,1,0:T(8,128)} %param.9), channel_id=1, source_target_pairs={{1,2},{2,1},{5,6},{6,5},{9,10},{10,9},{13,14},{14,13},{17,18},{18,... | collective-permute-start | bytes 1572872 | tf_op jit(solution)/shard_map/ppermute | solution.py:256
  5.2 2.3 %dynamic-slice_bitcast_fusion = f32[2,4,256,128]{3,2,1,0:T(8,128)} fusion(f32[2,4,2,256,128]{4,3,2,1,0:T(8,128)} %bitcast.40, s32[]{:T(128)S(6)} %select_n.41), kind=kLoop, calls=%fused_computation.2 | loop fusion | bytes 2097156 | tf_op jit(solution)/shard_map/jit(dynamic_index_in_dim)/squeeze | solution.py:28
  7.5 1.9 %dynamic-slice_bitcast_fusion.2 = (f32[2,256,128]{2,1,0:T(8,128)}, f32[2,256,128]{2,1,0:T(8,128)}) fusion(f32[2,2,256,128]{3,2,1,0:T(8,128)} %bitcast.45, s32[]{:T(128)S(6)} %select_n.49, s32[]{:T(128)S(6)} %select_n.41), kind=kLoop, calls=%fused_computation.15 | loop fusion | bytes 1048584 | tf_op jit(solution)/shard_map/jit(dynamic_index_in_dim)/squeeze | solution.py:28
  9.9 1.6 %fusion.7 = f32[2,128,128]{2,1,0:T(8,128)S(1)} fusion(f32[2,512,128]{2,1,0:T(8,128)} %param.8, f32[512,128]{1,0:T(8,128)S(1)} %copy-done), kind=kOutput, calls=%fused_computation.12 | convolution fusion | flops 100663296 | bytes 917504 | tf_op jit(solution)/shard_map/kbq,bp->kqp/dot_general | solution.py:14
  11.5 3.7 %collective-permute-start.6 = (f32[2,128,128]{2,1,0:T(8,128)S(1)}, f32[2,128,128]{2,1,0:T(8,128)}, u32[]{:S(2)}, u32[]{:S(2)}) collective-permute-start(f32[2,128,128]{2,1,0:T(8,128)S(1)} %fusion.7), channel_id=1, source_target_pairs={{0,1},{1,0},{2,3},{3,2},{4,5},{5,4},{6,7},{7,6},{8,9},{9,8},{10,11... | collective-permute-start | bytes 393224 | tf_op jit(solution)/shard_map/ppermute | solution.py:256
  15.2 1.6 %fusion.2 = f32[2,128,128]{2,1,0:T(8,128)S(1)} fusion(f32[2,512,128]{2,1,0:T(8,128)} %param.9, f32[2,4,512,128]{3,2,1,0:T(8,128)S(1)} %bitcast.41, s32[]{:T(128)S(6)} %select_n.42), kind=kOutput, calls=%fused_computation.6 | convolution fusion | flops 100663296 | bytes 1179652 | tf_op jit(solution)/shard_map/kbr,kbq->krq/dot_general | solution.py:14
  16.8 1.9 %pad_maximum_fusion.own = f32[4,256,128]{2,1,0:T(8,128)} fusion(f32[2,256,128]{2,1,0:T(8,128)} %collective-permute-done.16, f32[2,256,128]{2,1,0:T(8,128)} %get-tuple-element.38), kind=kLoop, calls=%fused_computation.3 | loop fusion | flops 131072 | bytes 1048576 | tf_op jit(solution)/shard_map/concatenate | solution.py:285
  19.5 6.1 %collective-permute-start.4 = (f32[2,512,128]{2,1,0:T(8,128)S(1)}, f32[2,512,128]{2,1,0:T(8,128)S(1)}, u32[]{:S(2)}, u32[]{:S(2)}) collective-permute-start(f32[2,512,128]{2,1,0:T(8,128)S(1)} %bitcast_select_fusion), channel_id=1, source_target_pairs={{0,1},{1,0},{2,3},{3,2},{4,5},{5,4},{6,7},{7,6},{8,9},{9,8},{10,11... | collective-permute-start | bytes 1572872 | tf_op jit(solution)/shard_map/ppermute | solution.py:256
  25.6 1.6 %convolution_add_fusion.1 = f32[2,128,128]{2,1,0:T(8,128)S(1)} fusion(f32[2,128,128]{2,1,0:T(8,128)S(1)} %fusion.2, f32[2,512,128]{2,1,0:T(8,128)} %collective-permute-done.1, f32[2,4,512,128]{3,2,1,0:T(8,128)S(1)} %bitcast.43, s32[]{:T(128)S(6)} %select_n.43), kind=kOutput, calls=%fused_computation.1 | convolution fusion | flops 100696064 | bytes 1310724 | tf_op jit(solution)/shard_map/kbr,kbq->krq/dot_general | solution.py:14
  27.2 2.3 %convolution_add_fusion.part = f32[2,128,128]{2,1,0:T(8,128)} fusion(f32[2,128,128]{2,1,0:T(8,128)S(1)} %convolution_add_fusion.1, f32[2,512,128]{2,1,0:T(8,128)} %collective-permute-done.2, f32[2,4,512,128]{3,2,1,0:T(8,128)S(1)} %bitcast.44, s32[]{:T(128)S(6)} %select_n.45), kind=kOutput, calls=%fused_computation | convolution fusion | flops 100696064 | bytes 1310724 | tf_op jit(solution)/shard_map/kbr,kbq->krq/dot_general | solution.py:14
  29.5 1.4 %collective-permute-start.18 = (f32[4,256,128]{2,1,0:T(8,128)}, f32[4,256,128]{2,1,0:T(8,128)}, u32[]{:S(2)}, u32[]{:S(2)}) collective-permute-start(f32[4,256,128]{2,1,0:T(8,128)} %pad_maximum_fusion.own), channel_id=1, source_target_pairs={{1,2},{2,1},{5,6},{6,5},{9,10},{10,9},{13,14},{14,13},{17,18},{18,... | collective-permute-start | bytes 1572872 | tf_op jit(solution)/shard_map/ppermute | solution.py:256
  32.0 6.9 %collective-permute-start.7 = (f32[2,128,128]{2,1,0:T(8,128)S(1)}, f32[2,128,128]{2,1,0:T(8,128)}, u32[]{:S(2)}, u32[]{:S(2)}) collective-permute-start(f32[2,128,128]{2,1,0:T(8,128)S(1)} %add.54.probe_here), channel_id=1, source_target_pairs={{0,2},{1,3},{2,0},{3,1},{4,6},{5,7},{6,4},{7,5},{8,10},{9,11},{10,... | collective-permute-start | bytes 393224 | tf_op jit(solution)/shard_map/ppermute | solution.py:24
  40.5 1.3 %collective-permute-start.5 = (f32[2,128,128]{2,1,0:T(8,128)}, f32[2,128,128]{2,1,0:T(8,128)}, u32[]{:S(2)}, u32[]{:S(2)}) collective-permute-start(f32[2,128,128]{2,1,0:T(8,128)} %shard_map.78), channel_id=1, source_target_pairs={{1,0},{2,3},{5,4},{6,7},{9,8},{10,11},{13,12},{14,15},{17,16},{18,... | collective-permute-start | bytes 393224 | tf_op jit(solution)/shard_map/ppermute | solution.py:256
  41.9 1.0 %copy-done.4 = f32[2,512,128]{2,1,0:T(8,128)S(1)} copy-done((f32[2,512,128]{2,1,0:T(8,128)S(1)}, f32[2,512,128]{2,1,0:T(8,128)}, u32[]{:S(2)}) %copy-start.4) | copy-done | bytes 524312
  45.3 6.9 %collective-permute-done.7.probe_far = f32[2,128,128]{2,1,0:T(8,128)} collective-permute-done((f32[2,128,128]{2,1,0:T(8,128)S(1)}, f32[2,128,128]{2,1,0:T(8,128)}, u32[]{:S(2)}, u32[]{:S(2)}) %collective-permute-start.7) | collective-permute-done | bytes 131104 | tf_op jit(solution)/shard_map/ppermute | solution.py:24
  53.0 1.2 %shard_map.79.both = f32[4,128,128]{2,1,0:T(8,128)S(1)} custom-call(f32[2,128,128]{2,1,0:T(8,128)S(1)} %shard_map.77.core, f32[2,128,128]{2,1,0:T(8,128)} %collective-permute-done.5.lent, f32[2,128,128]{2,1,0:T(8,128)S(1)} %add.54.probe_here, f32[2,128,128]{2,1,0:T(8,128)} %collective-permute-done.7.probe_far, s32[2,1]{1,0:T(2,128)S(1)} %copy.14.pattern), custom_call_target="tpu_custom_call" | custom-call | tf_op jit(solution)/shard_map/pallas_call | solution.py:78
  54.9 1.3 %collective-permute-start.20 = (f32[4,256,128]{2,1,0:T(8,128)}, f32[4,256,128]{2,1,0:T(8,128)S(1)}, u32[]{:S(2)}, u32[]{:S(2)}) collective-permute-start(f32[4,256,128]{2,1,0:T(8,128)} %collective-permute-done.18.inner), channel_id=1, source_target_pairs={{1,0},{2,3},{5,4},{6,7},{9,8},{10,11},{13,12},{14,15},{17,16},{18,... | collective-permute-start | bytes 1572872 | tf_op jit(solution)/shard_map/ppermute | solution.py:256
  56.3 1.5 %collective-permute-done.8.both_other = f32[4,128,128]{2,1,0:T(8,128)S(1)} collective-permute-done((f32[4,128,128]{2,1,0:T(8,128)S(1)}, f32[4,128,128]{2,1,0:T(8,128)S(1)}, u32[]{:S(2)}, u32[]{:S(2)}) %collective-permute-start.8) | collective-permute-done | bytes 262176 | tf_op jit(solution)/shard_map/ppermute | solution.py:24
  57.8 1.5 %shard_map.80 = (f32[256,128]{1,0:T(8,128)S(1)}, f32[256,128]{1,0:T(8,128)S(1)}, f32[256,128]{1,0:T(8,128)S(1)}, f32[256,128]{1,0:T(8,128)S(1)}) custom-call(f32[2,1,2048,128]{3,2,1,0:T(8,128)S(1)} %copy-done.1, f32[2,4,256,128]{3,2,1,0:T(8,128)S(1)} %collective-permute-done.left_other, f32[4,128,128]{2,1,0:T(8,128)S(1)} %shard_map.79.both, ...), custom_call_target="tpu_custom_call" | custom-call | tf_op jit(solution)/shard_map/pallas_call | solution.py:78
  59.3 2.5 %collective-permute-start.11 = (f32[256,128]{1,0:T(8,128)S(1)}, f32[256,128]{1,0:T(8,128)S(1)}, u32[]{:S(2)}, u32[]{:S(2)}) collective-permute-start(f32[256,128]{1,0:T(8,128)S(1)} %get-tuple-element.26), channel_id=1, source_target_pairs={{0,24},{4,28},{8,16},{12,20},{16,8},{20,12},{24,0},{28,4},{1,25},{... | collective-permute-start | bytes 393224 | tf_op jit(solution)/shard_map/ppermute | solution.py:24
  62.8 4.4 %collective-permute-done.20.outer = f32[4,256,128]{2,1,0:T(8,128)S(1)} collective-permute-done((f32[4,256,128]{2,1,0:T(8,128)}, f32[4,256,128]{2,1,0:T(8,128)S(1)}, u32[]{:S(2)}, u32[]{:S(2)}) %collective-permute-start.20) | collective-permute-done | bytes 524320 | tf_op jit(solution)/shard_map/ppermute | solution.py:256
  67.2 1.3 %collective-permute-start.21 = (f32[4,256,128]{2,1,0:T(8,128)S(1)}, f32[4,256,128]{2,1,0:T(8,128)S(1)}, u32[]{:S(2)}, u32[]{:S(2)}) collective-permute-start(f32[4,256,128]{2,1,0:T(8,128)S(1)} %collective-permute-done.19.inner_far), channel_id=1, source_target_pairs={{1,0},{2,3},{5,4},{6,7},{9,8},{10,11},{13,12},{14,15},{17,16},{18,... | collective-permute-start | bytes 1572872 | tf_op jit(solution)/shard_map/ppermute | solution.py:256
  68.7 1.6 %collective-permute-start.12 = (f32[256,128]{1,0:T(8,128)S(1)}, f32[256,128]{1,0:T(8,128)S(1)}, u32[]{:S(2)}, u32[]{:S(2)}) collective-permute-start(f32[256,128]{1,0:T(8,128)S(1)} %add_add_fusion.rest_0_.y_rows), channel_id=1, source_target_pairs={{0,8},{4,12},{8,0},{12,4},{16,24},{20,28},{24,16},{28,20},{1,9},{5... | collective-permute-start | bytes 393224 | tf_op jit(solution)/shard_map/ppermute | solution.py:24
  70.3 1.4 %collective-permute-start.13 = (f32[256,128]{1,0:T(8,128)S(1)}, f32[256,128]{1,0:T(8,128)S(1)}, u32[]{:S(2)}, u32[]{:S(2)}) collective-permute-start(f32[256,128]{1,0:T(8,128)S(1)} %add_add_fusion.rest_0_.y_rows), channel_id=1, source_target_pairs={{0,16},{4,20},{8,24},{12,28},{16,0},{20,4},{24,8},{28,12},{1,17},{... | collective-permute-start | bytes 393224 | tf_op jit(solution)/shard_map/ppermute | solution.py:24
  72.3 2.2 %collective-permute-done.12.rest_1_ = f32[256,128]{1,0:T(8,128)S(1)} collective-permute-done((f32[256,128]{1,0:T(8,128)S(1)}, f32[256,128]{1,0:T(8,128)S(1)}, u32[]{:S(2)}, u32[]{:S(2)}) %collective-permute-start.12) | collective-permute-done | bytes 131104 | tf_op jit(solution)/shard_map/ppermute | solution.py:24
  74.5 3.6 %collective-permute-done.13.rest_2_ = f32[256,128]{1,0:T(8,128)S(1)} collective-permute-done((f32[256,128]{1,0:T(8,128)S(1)}, f32[256,128]{1,0:T(8,128)S(1)}, u32[]{:S(2)}, u32[]{:S(2)}) %collective-permute-start.13) | collective-permute-done | bytes 131104 | tf_op jit(solution)/shard_map/ppermute | solution.py:24
  78.1 1.7 %shard_map.81.sent = f32[5,128,128]{2,1,0:T(8,128)S(1)} custom-call(f32[2,1,2048,128]{3,2,1,0:T(8,128)S(1)} %copy-done.1, f32[2,4,256,128]{3,2,1,0:T(8,128)S(1)} %collective-permute-done.left_other, f32[256,128]{1,0:T(8,128)S(1)} %add_add_fusion.rest_0_.y_rows, f32[256,128]{1,0:T(8,128)S(1)} %collective-permute-done.12.rest_1_, ...), custom_call_target="tpu_custom_call" | custom-call | tf_op jit(solution)/shard_map/pallas_call | solution.py:78
  80.0 1.6 %collective-permute-done.15.got = f32[5,128,128]{2,1,0:T(8,128)S(1)} collective-permute-done((f32[5,128,128]{2,1,0:T(8,128)S(1)}, f32[5,128,128]{2,1,0:T(8,128)S(1)}, u32[]{:S(2)}, u32[]{:S(2)}) %collective-permute-start.15) | collective-permute-done | bytes 327712 | tf_op jit(solution)/shard_map/ppermute | solution.py:24
  81.6 2.4 %shard_map.83 = (f32[256,128]{1,0:T(8,128)S(1)}, f32[256,128]{1,0:T(8,128)S(1)}, f32[256,128]{1,0:T(8,128)S(1)}, f32[256,128]{1,0:T(8,128)S(1)}) custom-call(f32[5,128,128]{2,1,0:T(8,128)S(1)} %shard_map.81.sent, f32[5,128,128]{2,1,0:T(8,128)S(1)} %collective-permute-done.15.got, f32[4,128,128]{2,1,0:T(8,128)S(1)} %shard_map.79.both, ...), custom_call_target="tpu_custom_call" | custom-call | tf_op jit(solution)/shard_map/pallas_call | solution.py:78
  85.7 1.9 %collective-permute-start.24 = (f32[256,128]{1,0:T(8,128)S(1)}, f32[256,128]{1,0:T(8,128)S(1)}, u32[]{:S(2)}, u32[]{:S(2)}) collective-permute-start(f32[256,128]{1,0:T(8,128)S(1)} %get-tuple-element.36), channel_id=1, source_target_pairs={{0,24},{4,28},{8,16},{12,20},{16,8},{20,12},{24,0},{28,4},{1,25},{... | collective-permute-start | bytes 393224 | tf_op jit(solution)/shard_map/ppermute | solution.py:24
  87.6 4.4 %shard_map.82 = (f32[256,128]{1,0:T(8,128)}, f32[128,128]{1,0:T(8,128)S(1)}) custom-call(f32[5,128,128]{2,1,0:T(8,128)S(1)} %shard_map.81.sent, f32[5,128,128]{2,1,0:T(8,128)S(1)} %collective-permute-done.15.got, f32[256,128]{1,0:T(8,128)S(1)} %add_add_fusion.rest_0_.y_rows), custom_call_target="tpu_custom_call" | custom-call | flops 1000000000 | tf_op jit(solution)/shard_map/pallas_call | solution.py:78
  (57 shorter events, 13.5 us)
Async XLA Ops:
  0.6 9.2 %copy-start = (f32[512,128]{1,0:T(8,128)S(1)}, f32[512,128]{1,0:T(8,128)}, u32[]{:S(2)}) copy-start(f32[512,128]{1,0:T(8,128)} %param.10) | copy-start | bytes 786436
  0.6 14.5 %copy-start.2 = (f32[2,1,2048,128]{3,2,1,0:T(8,128)S(1)}, f32[2,1,2048,128]{3,2,1,0:T(8,128)}, u32[]{:S(2)}) copy-start(f32[2,1,2048,128]{3,2,1,0:T(8,128)} %right.1) | copy-start | bytes 6291460
  0.7 18.1 %collective-permute-start.1 = (f32[2,512,128]{2,1,0:T(8,128)}, f32[2,512,128]{2,1,0:T(8,128)}, u32[]{:S(2)}, u32[]{:S(2)}) collective-permute-start(f32[2,512,128]{2,1,0:T(8,128)} %param.9), channel_id=1, source_target_pairs={{0,1},{1,0},{2,3},{3,2},{4,5},{5,4},{6,7},{7,6},{8,9},{9,8},{10,11... | collective-permute-start | bytes 1572872 | tf_op jit(solution)/shard_map/ppermute | solution.py:256
  3.7 15.0 %collective-permute-start.2 = (f32[2,512,128]{2,1,0:T(8,128)}, f32[2,512,128]{2,1,0:T(8,128)}, u32[]{:S(2)}, u32[]{:S(2)}) collective-permute-start(f32[2,512,128]{2,1,0:T(8,128)} %param.9), channel_id=1, source_target_pairs={{1,2},{2,1},{5,6},{6,5},{9,10},{10,9},{13,14},{14,13},{17,18},{18,... | collective-permute-start | bytes 1572872 | tf_op jit(solution)/shard_map/ppermute | solution.py:256
  7.5 48.8 %collective-permute-start = (f32[2,4,256,128]{3,2,1,0:T(8,128)}, f32[2,4,256,128]{3,2,1,0:T(8,128)S(1)}, u32[]{:S(2)}, u32[]{:S(2)}) collective-permute-start(f32[2,4,256,128]{3,2,1,0:T(8,128)} %dynamic-slice_bitcast_fusion), channel_id=1, source_target_pairs={{0,4},{4,0},{8,12},{12,8},{16,20},{20,16},{24,28},{28,24},{1,5},{5... | collective-permute-start | bytes 3145736 | tf_op jit(solution)/shard_map/ppermute | solution.py:24
  9.3 7.5 %collective-permute-start.16 = (f32[2,256,128]{2,1,0:T(8,128)}, f32[2,256,128]{2,1,0:T(8,128)}, u32[]{:S(2)}, u32[]{:S(2)}) collective-permute-start(f32[2,256,128]{2,1,0:T(8,128)} %get-tuple-element.39), channel_id=1, source_target_pairs={{0,4},{4,0},{8,12},{12,8},{16,20},{20,16},{24,28},{28,24},{1,5},{5... | collective-permute-start | bytes 786440 | tf_op jit(solution)/shard_map/ppermute | solution.py:24
  11.5 15.7 %copy-start.8 = (f32[2,128,128]{2,1,0:T(8,128)}, f32[2,128,128]{2,1,0:T(8,128)S(1)}, u32[]{:S(2)}) copy-start(f32[2,128,128]{2,1,0:T(8,128)S(1)} %fusion.7) | copy-start | bytes 393220
  11.5 18.0 %collective-permute-start.6 = (f32[2,128,128]{2,1,0:T(8,128)S(1)}, f32[2,128,128]{2,1,0:T(8,128)}, u32[]{:S(2)}, u32[]{:S(2)}) collective-permute-start(f32[2,128,128]{2,1,0:T(8,128)S(1)} %fusion.7), channel_id=1, source_target_pairs={{0,1},{1,0},{2,3},{3,2},{4,5},{5,4},{6,7},{7,6},{8,9},{9,8},{10,11... | collective-permute-start | bytes 393224 | tf_op jit(solution)/shard_map/ppermute | solution.py:256
  18.7 13.3 %collective-permute-start.3 = (f32[2,512,128]{2,1,0:T(8,128)}, f32[2,512,128]{2,1,0:T(8,128)S(1)}, u32[]{:S(2)}, u32[]{:S(2)}) collective-permute-start(f32[2,512,128]{2,1,0:T(8,128)} %collective-permute-done.1), channel_id=1, source_target_pairs={{1,2},{2,1},{5,6},{6,5},{9,10},{10,9},{13,14},{14,13},{17,18},{18,... | collective-permute-start | bytes 1572872 | tf_op jit(solution)/shard_map/ppermute | solution.py:256
  19.5 22.3 %copy-start.9 = (s32[2,1]{0,1:T(1,128)S(1)}, s32[2,1]{0,1:T(1,128)}, u32[]{:S(2)}) copy-start(s32[2,1]{0,1:T(1,128)} %param.11) | copy-start | bytes 28
  19.5 19.4 %collective-permute-start.4 = (f32[2,512,128]{2,1,0:T(8,128)S(1)}, f32[2,512,128]{2,1,0:T(8,128)S(1)}, u32[]{:S(2)}, u32[]{:S(2)}) collective-permute-start(f32[2,512,128]{2,1,0:T(8,128)S(1)} %bitcast_select_fusion), channel_id=1, source_target_pairs={{0,1},{1,0},{2,3},{3,2},{4,5},{5,4},{6,7},{7,6},{8,9},{9,8},{10,11... | collective-permute-start | bytes 1572872 | tf_op jit(solution)/shard_map/ppermute | solution.py:256
  29.5 24.7 %collective-permute-start.17 = (f32[4,256,128]{2,1,0:T(8,128)}, f32[4,256,128]{2,1,0:T(8,128)}, u32[]{:S(2)}, u32[]{:S(2)}) collective-permute-start(f32[4,256,128]{2,1,0:T(8,128)} %pad_maximum_fusion.own), channel_id=1, source_target_pairs={{0,1},{1,0},{2,3},{3,2},{4,5},{5,4},{6,7},{7,6},{8,9},{9,8},{10,11... | collective-permute-start | bytes 1572872 | tf_op jit(solution)/shard_map/ppermute | solution.py:256
  29.5 24.6 %collective-permute-start.18 = (f32[4,256,128]{2,1,0:T(8,128)}, f32[4,256,128]{2,1,0:T(8,128)}, u32[]{:S(2)}, u32[]{:S(2)}) collective-permute-start(f32[4,256,128]{2,1,0:T(8,128)} %pad_maximum_fusion.own), channel_id=1, source_target_pairs={{1,2},{2,1},{5,6},{6,5},{9,10},{10,9},{13,14},{14,13},{17,18},{18,... | collective-permute-start | bytes 1572872 | tf_op jit(solution)/shard_map/ppermute | solution.py:256
  32.0 20.1 %collective-permute-start.7 = (f32[2,128,128]{2,1,0:T(8,128)S(1)}, f32[2,128,128]{2,1,0:T(8,128)}, u32[]{:S(2)}, u32[]{:S(2)}) collective-permute-start(f32[2,128,128]{2,1,0:T(8,128)S(1)} %add.54.probe_here), channel_id=1, source_target_pairs={{0,2},{1,3},{2,0},{3,1},{4,6},{5,7},{6,4},{7,5},{8,10},{9,11},{10,... | collective-permute-start | bytes 393224 | tf_op jit(solution)/shard_map/ppermute | solution.py:24
  40.5 12.5 %collective-permute-start.5 = (f32[2,128,128]{2,1,0:T(8,128)}, f32[2,128,128]{2,1,0:T(8,128)}, u32[]{:S(2)}, u32[]{:S(2)}) collective-permute-start(f32[2,128,128]{2,1,0:T(8,128)} %shard_map.78), channel_id=1, source_target_pairs={{1,0},{2,3},{5,4},{6,7},{9,8},{10,11},{13,12},{14,15},{17,16},{18,... | collective-permute-start | bytes 393224 | tf_op jit(solution)/shard_map/ppermute | solution.py:256
  41.9 1.0 %copy-start.4 = (f32[2,512,128]{2,1,0:T(8,128)S(1)}, f32[2,512,128]{2,1,0:T(8,128)}, u32[]{:S(2)}) copy-start(f32[2,512,128]{2,1,0:T(8,128)} %copy-done.3) | copy-start | bytes 1572868
  43.0 1.0 %copy-start.6 = (f32[2,512,128]{2,1,0:T(8,128)S(1)}, f32[2,512,128]{2,1,0:T(8,128)}, u32[]{:S(2)}) copy-start(f32[2,512,128]{2,1,0:T(8,128)} %copy-done.5) | copy-start | bytes 1572868
  44.9 12.9 %copy-start.1 = (f32[2,1,2048,128]{3,2,1,0:T(8,128)S(1)}, f32[2,1,2048,128]{3,2,1,0:T(8,128)}, u32[]{:S(2)}) copy-start(f32[2,1,2048,128]{3,2,1,0:T(8,128)} %left.3) | copy-start | bytes 6291460
  54.2 8.6 %collective-permute-start.19 = (f32[4,256,128]{2,1,0:T(8,128)}, f32[4,256,128]{2,1,0:T(8,128)S(1)}, u32[]{:S(2)}, u32[]{:S(2)}) collective-permute-start(f32[4,256,128]{2,1,0:T(8,128)} %collective-permute-done.17.near), channel_id=1, source_target_pairs={{1,2},{2,1},{5,6},{6,5},{9,10},{10,9},{13,14},{14,13},{17,18},{18,... | collective-permute-start | bytes 1572872 | tf_op jit(solution)/shard_map/ppermute | solution.py:256
  54.9 12.3 %collective-permute-start.20 = (f32[4,256,128]{2,1,0:T(8,128)}, f32[4,256,128]{2,1,0:T(8,128)S(1)}, u32[]{:S(2)}, u32[]{:S(2)}) collective-permute-start(f32[4,256,128]{2,1,0:T(8,128)} %collective-permute-done.18.inner), channel_id=1, source_target_pairs={{1,0},{2,3},{5,4},{6,7},{9,8},{10,11},{13,12},{14,15},{17,16},{18,... | collective-permute-start | bytes 1572872 | tf_op jit(solution)/shard_map/ppermute | solution.py:256
  56.2 1.6 %collective-permute-start.8 = (f32[4,128,128]{2,1,0:T(8,128)S(1)}, f32[4,128,128]{2,1,0:T(8,128)S(1)}, u32[]{:S(2)}, u32[]{:S(2)}) collective-permute-start(f32[4,128,128]{2,1,0:T(8,128)S(1)} %shard_map.79.both), channel_id=1, source_target_pairs={{0,4},{4,0},{8,12},{12,8},{16,20},{20,16},{24,28},{28,24},{1,5},{5... | collective-permute-start | bytes 786440 | tf_op jit(solution)/shard_map/ppermute | solution.py:24
  59.3 9.2 %collective-permute-start.11 = (f32[256,128]{1,0:T(8,128)S(1)}, f32[256,128]{1,0:T(8,128)S(1)}, u32[]{:S(2)}, u32[]{:S(2)}) collective-permute-start(f32[256,128]{1,0:T(8,128)S(1)} %get-tuple-element.26), channel_id=1, source_target_pairs={{0,24},{4,28},{8,16},{12,20},{16,8},{20,12},{24,0},{28,4},{1,25},{... | collective-permute-start | bytes 393224 | tf_op jit(solution)/shard_map/ppermute | solution.py:24
  61.8 6.8 %collective-permute-start.10 = (f32[256,128]{1,0:T(8,128)S(1)}, f32[256,128]{1,0:T(8,128)S(1)}, u32[]{:S(2)}, u32[]{:S(2)}) collective-permute-start(f32[256,128]{1,0:T(8,128)S(1)} %get-tuple-element.25), channel_id=1, source_target_pairs={{0,16},{4,20},{8,24},{12,28},{16,0},{20,4},{24,8},{28,12},{1,17},{... | collective-permute-start | bytes 393224 | tf_op jit(solution)/shard_map/ppermute | solution.py:24
  62.3 6.4 %collective-permute-start.9 = (f32[256,128]{1,0:T(8,128)S(1)}, f32[256,128]{1,0:T(8,128)S(1)}, u32[]{:S(2)}, u32[]{:S(2)}) collective-permute-start(f32[256,128]{1,0:T(8,128)S(1)} %get-tuple-element.24), channel_id=1, source_target_pairs={{0,8},{4,12},{8,0},{12,4},{16,24},{20,28},{24,16},{28,20},{1,9},{5... | collective-permute-start | bytes 393224 | tf_op jit(solution)/shard_map/ppermute | solution.py:24
  67.2 14.4 %collective-permute-start.21 = (f32[4,256,128]{2,1,0:T(8,128)S(1)}, f32[4,256,128]{2,1,0:T(8,128)S(1)}, u32[]{:S(2)}, u32[]{:S(2)}) collective-permute-start(f32[4,256,128]{2,1,0:T(8,128)S(1)} %collective-permute-done.19.inner_far), channel_id=1, source_target_pairs={{1,0},{2,3},{5,4},{6,7},{9,8},{10,11},{13,12},{14,15},{17,16},{18,... | collective-permute-start | bytes 1572872 | tf_op jit(solution)/shard_map/ppermute | solution.py:256
  68.7 5.8 %collective-permute-start.12 = (f32[256,128]{1,0:T(8,128)S(1)}, f32[256,128]{1,0:T(8,128)S(1)}, u32[]{:S(2)}, u32[]{:S(2)}) collective-permute-start(f32[256,128]{1,0:T(8,128)S(1)} %add_add_fusion.rest_0_.y_rows), channel_id=1, source_target_pairs={{0,8},{4,12},{8,0},{12,4},{16,24},{20,28},{24,16},{28,20},{1,9},{5... | collective-permute-start | bytes 393224 | tf_op jit(solution)/shard_map/ppermute | solution.py:24
  70.3 7.8 %collective-permute-start.13 = (f32[256,128]{1,0:T(8,128)S(1)}, f32[256,128]{1,0:T(8,128)S(1)}, u32[]{:S(2)}, u32[]{:S(2)}) collective-permute-start(f32[256,128]{1,0:T(8,128)S(1)} %add_add_fusion.rest_0_.y_rows), channel_id=1, source_target_pairs={{0,16},{4,20},{8,24},{12,28},{16,0},{20,4},{24,8},{28,12},{1,17},{... | collective-permute-start | bytes 393224 | tf_op jit(solution)/shard_map/ppermute | solution.py:24
  71.6 6.5 %collective-permute-start.14 = (f32[256,128]{1,0:T(8,128)S(1)}, f32[256,128]{1,0:T(8,128)S(1)}, u32[]{:S(2)}, u32[]{:S(2)}) collective-permute-start(f32[256,128]{1,0:T(8,128)S(1)} %add_add_fusion.rest_0_.y_rows), channel_id=1, source_target_pairs={{0,24},{4,28},{8,16},{12,20},{16,8},{20,12},{24,0},{28,4},{1,25},{... | collective-permute-start | bytes 393224 | tf_op jit(solution)/shard_map/ppermute | solution.py:24
  79.9 1.7 %collective-permute-start.15 = (f32[5,128,128]{2,1,0:T(8,128)S(1)}, f32[5,128,128]{2,1,0:T(8,128)S(1)}, u32[]{:S(2)}, u32[]{:S(2)}) collective-permute-start(f32[5,128,128]{2,1,0:T(8,128)S(1)} %shard_map.81.sent), channel_id=1, source_target_pairs={{0,4},{4,0},{8,12},{12,8},{16,20},{20,16},{24,28},{28,24},{1,5},{5... | collective-permute-start | bytes 983048 | tf_op jit(solution)/shard_map/ppermute | solution.py:24
  84.0 7.9 %collective-permute-start.22 = (f32[256,128]{1,0:T(8,128)S(1)}, f32[256,128]{1,0:T(8,128)S(1)}, u32[]{:S(2)}, u32[]{:S(2)}) collective-permute-start(f32[256,128]{1,0:T(8,128)S(1)} %get-tuple-element.34), channel_id=1, source_target_pairs={{0,8},{4,12},{8,0},{12,4},{16,24},{20,28},{24,16},{28,20},{1,9},{5... | collective-permute-start | bytes 393224 | tf_op jit(solution)/shard_map/ppermute | solution.py:24
  84.8 8.1 %collective-permute-start.23 = (f32[256,128]{1,0:T(8,128)S(1)}, f32[256,128]{1,0:T(8,128)S(1)}, u32[]{:S(2)}, u32[]{:S(2)}) collective-permute-start(f32[256,128]{1,0:T(8,128)S(1)} %get-tuple-element.35), channel_id=1, source_target_pairs={{0,16},{4,20},{8,24},{12,28},{16,0},{20,4},{24,8},{28,12},{1,17},{... | collective-permute-start | bytes 393224 | tf_op jit(solution)/shard_map/ppermute | solution.py:24
  85.7 7.2 %collective-permute-start.24 = (f32[256,128]{1,0:T(8,128)S(1)}, f32[256,128]{1,0:T(8,128)S(1)}, u32[]{:S(2)}, u32[]{:S(2)}) collective-permute-start(f32[256,128]{1,0:T(8,128)S(1)} %get-tuple-element.36), channel_id=1, source_target_pairs={{0,24},{4,28},{8,16},{12,20},{16,8},{20,12},{24,0},{28,4},{1,25},{... | collective-permute-start | bytes 393224 | tf_op jit(solution)/shard_map/ppermute | solution.py:24
  (3 other events, 2.6 us)

commit v9 on v8

--- a/solution.py
+++ b/solution.py
@@ -155,20 +155,33 @@
 
 
 def z_kernel(left, left_other, *rest):
-    *ys, out, held, sems = rest
-    chips, rows = len(ys), ys[0].shape[0]
+    *ys, before, out, held, sems = rest
+    rows = ys[0].shape[0]
     rank = out.shape[-1]
-    copies = start_rows(left, left_other, held, sems, chips, rows)
-    total = jnp.zeros((rank, 5 * rank), jnp.float32)
-    dot = functools.partial(lax.dot_general, dimension_numbers=TN, preferred_element_type=jnp.float32)
-    for i, y in enumerate(ys):
-        y_here = y[...]
+    copies = start_rows(left, left_other, held, sems, len(ys) + 1, rows)
+    total = jnp.concatenate([before[k] for k in range(5)], 1)
+    for i, y in enumerate(ys, 1):
         for copy in copies[i]:
             copy.wait()
-        beside = jnp.concatenate([held[i, 2], held[i, 3], held[i, 0], held[i, 1], y_here], 1)
-        b_high, b_low = split(beside)
-        a_high, a_low = split(y_here)
-        total += dot(a_high, b_high) + dot(a_high, b_low) + dot(a_low, b_high)
+        total += block_products(y[...], held, i)
+    for copy in copies[0]:
+        copy.wait()
+    for k in range(5):
+        out[k] = total[:, k * rank:(k + 1) * rank]
+
+
+def block_products(y_here, held, i):
+    dot = functools.partial(lax.dot_general, dimension_numbers=TN, preferred_element_type=jnp.float32)
+    b_high, b_low = split(jnp.concatenate([held[i, 2], held[i, 3], held[i, 0], held[i, 1], y_here], 1))
+    a_high, a_low = split(y_here)
+    return dot(a_high, b_high) + dot(a_high, b_low) + dot(a_low, b_high)
+
+
+def z_own_kernel(left, left_other, y, out, held, sems):
+    rank = out.shape[-1]
+    for copy in start_rows(left, left_other, held, sems, 1, y.shape[0])[0]:
+        copy.wait()
+    total = block_products(y[...], held, 0)
     for k in range(5):
         out[k] = total[:, k * rank:(k + 1) * rank]
 
@@ -295,11 +308,12 @@
     rows_scratch = [pltpu.VMEM((chips, 4, row_count, rank), jnp.float32), pltpu.SemaphoreType.DMA((2 * chips,))]
     y_parts = call(y_kernel, [(row_count, rank)] * chips, [target_left, left_other, both, both_other], "aavv", rows_scratch)
     y_rows = y_parts[0]
-    for bit in range(1, chips):
+    for bit in range(chips - 1, 0, -1):
         y_rows = y_rows + exchange(y_parts[bit], "step", 2 * bit)
     y_all = [y_rows] + [exchange(y_rows, "step", 2 * bit) for bit in range(1, chips)]
     col_last = across(col_inner_far, outward)
-    (sent,) = call(z_kernel, [(5, rank, rank)], [target_left, left_other, *y_all], "aa" + "v" * chips, rows_scratch)
+    (own_sent,) = call(z_own_kernel, [(5, rank, rank)], [target_left, left_other, y_rows], "aav", rows_scratch)
+    (sent,) = call(z_kernel, [(5, rank, rank)], [target_left, left_other, *y_all[1:], own_sent], "aa" + "v" * chips, rows_scratch)
     got = exchange(sent, "step", 1)
     w_parts = call(
         functools.partial(w_kernel, planes),

time: 94.5 us -> 94 us (level)
    pallas_call x8 -> x9, Pallas kernels: 13.2 us -> 13.3 us  [call(): pl.pallas_call(kernel, out_shape=shapes, in_specs=[pl.BlockSpec(memory_sp...]
  transfers between devices with their start and end apart: 25 -> 25, of which waited for: 10 -> 10; matrix products, arithmetic and copies ran while one was open for 15% -> 15% of each run, Pallas kernels for 10% -> 11%
where the time goes in v9:
time: 94 us; the launch traced here: 93.3 us
  starting transfers between devices  39.2 us (42%)
  waiting for transfers between devices  21.6 us (23%)
  Pallas kernels  13.3 us (14%)
  local copies, waits for them, and re-layouts  8.18 us (9%)
  matrix products  7.19 us (8%)
  other arithmetic  2.96 us (3%)
    ppermute x11, starting transfers between devices, across(): return lax.ppermute(array, 'tile', pairs)  21 us
    ppermute x14, starting transfers between devices, exchange(): lax.ppermute(array, axis, [(i, i ^ bit) for i in range(lax.axis_size(axis...  18.2 us
    ppermute x14, waiting for transfers between devices, exchange(): lax.ppermute(array, axis, [(i, i ^ bit) for i in range(lax.axis_size(axis...  16.3 us
    pallas_call x9, Pallas kernels, call(): pl.pallas_call(kernel, out_shape=shapes, in_specs=[pl.BlockSpec(memory_sp...  13.3 us
    dot_general x4, matrix products, mm(): jnp.einsum(spec, *arrays, precision=HIGH, preferred_element_type=jnp.floa...  7.19 us
    ppermute x11, waiting for transfers between devices, across(): return lax.ppermute(array, 'tile', pairs)  5.25 us
    squeeze x2, local copies, waits for them, and re-layouts, take(): return lax.dynamic_index_in_dim(array, index, axis, keepdims=False)  4.13 us
    unnamed x21, local copies, waits for them, and re-layouts  4.06 us
  transfers between devices with their start and end apart: 25, of which 10 were waited for; matrix products, arithmetic and copies ran while one was open for 15% of the time, Pallas kernels for 11%

profile of v9, /device:TPU:0, one launch (start us, length us, event | category | flops | bytes accessed | tf_op | source)
XLA Modules:
  0.0 93.3 jit_solution(10479350864911866008)
XLA Ops:
  0.7 3.1 %collective-permute-start.1 = (f32[2,512,128]{2,1,0:T(8,128)}, f32[2,512,128]{2,1,0:T(8,128)}, u32[]{:S(2)}, u32[]{:S(2)}) collective-permute-start(f32[2,512,128]{2,1,0:T(8,128)} %param.9), channel_id=1, source_target_pairs={{0,1},{1,0},{2,3},{3,2},{4,5},{5,4},{6,7},{7,6},{8,9},{9,8},{10,11... | collective-permute-start | bytes 1572872 | tf_op jit(solution)/shard_map/ppermute | solution.py:269
  3.7 1.5 %collective-permute-start.2 = (f32[2,512,128]{2,1,0:T(8,128)}, f32[2,512,128]{2,1,0:T(8,128)}, u32[]{:S(2)}, u32[]{:S(2)}) collective-permute-start(f32[2,512,128]{2,1,0:T(8,128)} %param.9), channel_id=1, source_target_pairs={{1,2},{2,1},{5,6},{6,5},{9,10},{10,9},{13,14},{14,13},{17,18},{18,... | collective-permute-start | bytes 1572872 | tf_op jit(solution)/shard_map/ppermute | solution.py:269
  5.2 2.3 %dynamic-slice_bitcast_fusion = f32[2,4,256,128]{3,2,1,0:T(8,128)} fusion(f32[2,4,2,256,128]{4,3,2,1,0:T(8,128)} %bitcast.40, s32[]{:T(128)S(6)} %select_n.41), kind=kLoop, calls=%fused_computation.2 | loop fusion | bytes 2097156 | tf_op jit(solution)/shard_map/jit(dynamic_index_in_dim)/squeeze | solution.py:28
  7.5 1.9 %dynamic-slice_bitcast_fusion.2 = (f32[2,256,128]{2,1,0:T(8,128)}, f32[2,256,128]{2,1,0:T(8,128)}) fusion(f32[2,2,256,128]{3,2,1,0:T(8,128)} %bitcast.45, s32[]{:T(128)S(6)} %select_n.49, s32[]{:T(128)S(6)} %select_n.41), kind=kLoop, calls=%fused_computation.15 | loop fusion | bytes 1048584 | tf_op jit(solution)/shard_map/jit(dynamic_index_in_dim)/squeeze | solution.py:28
  9.9 1.6 %fusion.7 = f32[2,128,128]{2,1,0:T(8,128)S(1)} fusion(f32[2,512,128]{2,1,0:T(8,128)} %param.8, f32[512,128]{1,0:T(8,128)S(1)} %copy-done), kind=kOutput, calls=%fused_computation.12 | convolution fusion | flops 100663296 | bytes 917504 | tf_op jit(solution)/shard_map/kbq,bp->kqp/dot_general | solution.py:14
  11.5 3.7 %collective-permute-start.6 = (f32[2,128,128]{2,1,0:T(8,128)S(1)}, f32[2,128,128]{2,1,0:T(8,128)}, u32[]{:S(2)}, u32[]{:S(2)}) collective-permute-start(f32[2,128,128]{2,1,0:T(8,128)S(1)} %fusion.7), channel_id=1, source_target_pairs={{0,1},{1,0},{2,3},{3,2},{4,5},{5,4},{6,7},{7,6},{8,9},{9,8},{10,11... | collective-permute-start | bytes 393224 | tf_op jit(solution)/shard_map/ppermute | solution.py:269
  15.2 1.6 %fusion.2 = f32[2,128,128]{2,1,0:T(8,128)S(1)} fusion(f32[2,512,128]{2,1,0:T(8,128)} %param.9, f32[2,4,512,128]{3,2,1,0:T(8,128)S(1)} %bitcast.41, s32[]{:T(128)S(6)} %select_n.42), kind=kOutput, calls=%fused_computation.6 | convolution fusion | flops 100663296 | bytes 1179652 | tf_op jit(solution)/shard_map/kbr,kbq->krq/dot_general | solution.py:14
  16.8 1.9 %pad_maximum_fusion.own = f32[4,256,128]{2,1,0:T(8,128)} fusion(f32[2,256,128]{2,1,0:T(8,128)} %collective-permute-done.16, f32[2,256,128]{2,1,0:T(8,128)} %get-tuple-element.38), kind=kLoop, calls=%fused_computation.3 | loop fusion | flops 131072 | bytes 1048576 | tf_op jit(solution)/shard_map/concatenate | solution.py:298
  19.5 6.1 %collective-permute-start.4 = (f32[2,512,128]{2,1,0:T(8,128)S(1)}, f32[2,512,128]{2,1,0:T(8,128)S(1)}, u32[]{:S(2)}, u32[]{:S(2)}) collective-permute-start(f32[2,512,128]{2,1,0:T(8,128)S(1)} %bitcast_select_fusion), channel_id=1, source_target_pairs={{0,1},{1,0},{2,3},{3,2},{4,5},{5,4},{6,7},{7,6},{8,9},{9,8},{10,11... | collective-permute-start | bytes 1572872 | tf_op jit(solution)/shard_map/ppermute | solution.py:269
  25.6 1.6 %convolution_add_fusion.1 = f32[2,128,128]{2,1,0:T(8,128)S(1)} fusion(f32[2,128,128]{2,1,0:T(8,128)S(1)} %fusion.2, f32[2,512,128]{2,1,0:T(8,128)} %collective-permute-done.1, f32[2,4,512,128]{3,2,1,0:T(8,128)S(1)} %bitcast.43, s32[]{:T(128)S(6)} %select_n.43), kind=kOutput, calls=%fused_computation.1 | convolution fusion | flops 100696064 | bytes 1310724 | tf_op jit(solution)/shard_map/kbr,kbq->krq/dot_general | solution.py:14
  27.2 2.3 %convolution_add_fusion.part = f32[2,128,128]{2,1,0:T(8,128)} fusion(f32[2,128,128]{2,1,0:T(8,128)S(1)} %convolution_add_fusion.1, f32[2,512,128]{2,1,0:T(8,128)} %collective-permute-done.2, f32[2,4,512,128]{3,2,1,0:T(8,128)S(1)} %bitcast.44, s32[]{:T(128)S(6)} %select_n.45), kind=kOutput, calls=%fused_computation | convolution fusion | flops 100696064 | bytes 1310724 | tf_op jit(solution)/shard_map/kbr,kbq->krq/dot_general | solution.py:14
  29.5 1.4 %collective-permute-start.18 = (f32[4,256,128]{2,1,0:T(8,128)}, f32[4,256,128]{2,1,0:T(8,128)}, u32[]{:S(2)}, u32[]{:S(2)}) collective-permute-start(f32[4,256,128]{2,1,0:T(8,128)} %pad_maximum_fusion.own), channel_id=1, source_target_pairs={{1,2},{2,1},{5,6},{6,5},{9,10},{10,9},{13,14},{14,13},{17,18},{18,... | collective-permute-start | bytes 1572872 | tf_op jit(solution)/shard_map/ppermute | solution.py:269
  32.0 6.9 %collective-permute-start.7 = (f32[2,128,128]{2,1,0:T(8,128)S(1)}, f32[2,128,128]{2,1,0:T(8,128)}, u32[]{:S(2)}, u32[]{:S(2)}) collective-permute-start(f32[2,128,128]{2,1,0:T(8,128)S(1)} %add.54.probe_here), channel_id=1, source_target_pairs={{0,2},{1,3},{2,0},{3,1},{4,6},{5,7},{6,4},{7,5},{8,10},{9,11},{10,... | collective-permute-start | bytes 393224 | tf_op jit(solution)/shard_map/ppermute | solution.py:24
  40.5 1.3 %collective-permute-start.5 = (f32[2,128,128]{2,1,0:T(8,128)}, f32[2,128,128]{2,1,0:T(8,128)}, u32[]{:S(2)}, u32[]{:S(2)}) collective-permute-start(f32[2,128,128]{2,1,0:T(8,128)} %shard_map.78), channel_id=1, source_target_pairs={{1,0},{2,3},{5,4},{6,7},{9,8},{10,11},{13,12},{14,15},{17,16},{18,... | collective-permute-start | bytes 393224 | tf_op jit(solution)/shard_map/ppermute | solution.py:269
  45.3 6.9 %collective-permute-done.7.probe_far = f32[2,128,128]{2,1,0:T(8,128)} collective-permute-done((f32[2,128,128]{2,1,0:T(8,128)S(1)}, f32[2,128,128]{2,1,0:T(8,128)}, u32[]{:S(2)}, u32[]{:S(2)}) %collective-permute-start.7) | collective-permute-done | bytes 131104 | tf_op jit(solution)/shard_map/ppermute | solution.py:24
  54.9 1.3 %collective-permute-start.20 = (f32[4,256,128]{2,1,0:T(8,128)}, f32[4,256,128]{2,1,0:T(8,128)S(1)}, u32[]{:S(2)}, u32[]{:S(2)}) collective-permute-start(f32[4,256,128]{2,1,0:T(8,128)} %collective-permute-done.18.inner), channel_id=1, source_target_pairs={{1,0},{2,3},{5,4},{6,7},{9,8},{10,11},{13,12},{14,15},{17,16},{18,... | collective-permute-start | bytes 1572872 | tf_op jit(solution)/shard_map/ppermute | solution.py:269
  56.3 1.5 %collective-permute-done.8.both_other = f32[4,128,128]{2,1,0:T(8,128)S(1)} collective-permute-done((f32[4,128,128]{2,1,0:T(8,128)S(1)}, f32[4,128,128]{2,1,0:T(8,128)S(1)}, u32[]{:S(2)}, u32[]{:S(2)}) %collective-permute-start.8) | collective-permute-done | bytes 262176 | tf_op jit(solution)/shard_map/ppermute | solution.py:24
  57.8 1.5 %shard_map.80 = (f32[256,128]{1,0:T(8,128)S(1)}, f32[256,128]{1,0:T(8,128)S(1)}, f32[256,128]{1,0:T(8,128)S(1)}, f32[256,128]{1,0:T(8,128)S(1)}) custom-call(f32[2,1,2048,128]{3,2,1,0:T(8,128)S(1)} %copy-done.1, f32[2,4,256,128]{3,2,1,0:T(8,128)S(1)} %collective-permute-done.left_other, f32[4,128,128]{2,1,0:T(8,128)S(1)} %shard_map.79.both, ...), custom_call_target="tpu_custom_call" | custom-call | tf_op jit(solution)/shard_map/pallas_call | solution.py:78
  59.3 1.6 %collective-permute-start.11 = (f32[256,128]{1,0:T(8,128)S(1)}, f32[256,128]{1,0:T(8,128)S(1)}, u32[]{:S(2)}, u32[]{:S(2)}) collective-permute-start(f32[256,128]{1,0:T(8,128)S(1)} %get-tuple-element.26), channel_id=1, source_target_pairs={{0,8},{4,12},{8,0},{12,4},{16,24},{20,28},{24,16},{28,20},{1,9},{5... | collective-permute-start | bytes 393224 | tf_op jit(solution)/shard_map/ppermute | solution.py:24
  60.8 1.5 %collective-permute-start.10 = (f32[256,128]{1,0:T(8,128)S(1)}, f32[256,128]{1,0:T(8,128)S(1)}, u32[]{:S(2)}, u32[]{:S(2)}) collective-permute-start(f32[256,128]{1,0:T(8,128)S(1)} %get-tuple-element.25), channel_id=1, source_target_pairs={{0,16},{4,20},{8,24},{12,28},{16,0},{20,4},{24,8},{28,12},{1,17},{... | collective-permute-start | bytes 393224 | tf_op jit(solution)/shard_map/ppermute | solution.py:24
  62.8 4.4 %collective-permute-done.20.outer = f32[4,256,128]{2,1,0:T(8,128)S(1)} collective-permute-done((f32[4,256,128]{2,1,0:T(8,128)}, f32[4,256,128]{2,1,0:T(8,128)S(1)}, u32[]{:S(2)}, u32[]{:S(2)}) %collective-permute-start.20) | collective-permute-done | bytes 524320 | tf_op jit(solution)/shard_map/ppermute | solution.py:269
  67.2 1.3 %collective-permute-start.21 = (f32[4,256,128]{2,1,0:T(8,128)S(1)}, f32[4,256,128]{2,1,0:T(8,128)S(1)}, u32[]{:S(2)}, u32[]{:S(2)}) collective-permute-start(f32[4,256,128]{2,1,0:T(8,128)S(1)} %collective-permute-done.19.inner_far), channel_id=1, source_target_pairs={{1,0},{2,3},{5,4},{6,7},{9,8},{10,11},{13,12},{14,15},{17,16},{18,... | collective-permute-start | bytes 1572872 | tf_op jit(solution)/shard_map/ppermute | solution.py:269
  68.9 1.3 %collective-permute-start.12 = (f32[256,128]{1,0:T(8,128)S(1)}, f32[256,128]{1,0:T(8,128)S(1)}, u32[]{:S(2)}, u32[]{:S(2)}) collective-permute-start(f32[256,128]{1,0:T(8,128)S(1)} %add_add_fusion.y.y_rows), channel_id=1, source_target_pairs={{0,8},{4,12},{8,0},{12,4},{16,24},{20,28},{24,16},{28,20},{1,9},{5... | collective-permute-start | bytes 393224 | tf_op jit(solution)/shard_map/ppermute | solution.py:24
  70.2 1.4 %collective-permute-start.13 = (f32[256,128]{1,0:T(8,128)S(1)}, f32[256,128]{1,0:T(8,128)S(1)}, u32[]{:S(2)}, u32[]{:S(2)}) collective-permute-start(f32[256,128]{1,0:T(8,128)S(1)} %add_add_fusion.y.y_rows), channel_id=1, source_target_pairs={{0,16},{4,20},{8,24},{12,28},{16,0},{20,4},{24,8},{28,12},{1,17},{... | collective-permute-start | bytes 393224 | tf_op jit(solution)/shard_map/ppermute | solution.py:24
  73.0 2.0 %collective-permute-done.12.rest_0_ = f32[256,128]{1,0:T(8,128)S(1)} collective-permute-done((f32[256,128]{1,0:T(8,128)S(1)}, f32[256,128]{1,0:T(8,128)S(1)}, u32[]{:S(2)}, u32[]{:S(2)}) %collective-permute-start.12) | collective-permute-done | bytes 131104 | tf_op jit(solution)/shard_map/ppermute | solution.py:24
  75.0 1.6 %collective-permute-done.13.rest_1_ = f32[256,128]{1,0:T(8,128)S(1)} collective-permute-done((f32[256,128]{1,0:T(8,128)S(1)}, f32[256,128]{1,0:T(8,128)S(1)}, u32[]{:S(2)}, u32[]{:S(2)}) %collective-permute-start.13) | collective-permute-done | bytes 131104 | tf_op jit(solution)/shard_map/ppermute | solution.py:24
  77.5 1.4 %shard_map.82.sent = f32[5,128,128]{2,1,0:T(8,128)S(1)} custom-call(f32[2,1,2048,128]{3,2,1,0:T(8,128)S(1)} %copy-done.1, f32[2,4,256,128]{3,2,1,0:T(8,128)S(1)} %collective-permute-done.left_other, f32[256,128]{1,0:T(8,128)S(1)} %collective-permute-done.12.rest_0_, f32[256,128]{1,0:T(8,128)S(1)} %collective-permute-done.13.rest_1_, ...), custom_call_target="tpu_custom_call" | custom-call | tf_op jit(solution)/shard_map/pallas_call | solution.py:78
  79.0 1.6 %collective-permute-done.15.got = f32[5,128,128]{2,1,0:T(8,128)S(1)} collective-permute-done((f32[5,128,128]{2,1,0:T(8,128)S(1)}, f32[5,128,128]{2,1,0:T(8,128)S(1)}, u32[]{:S(2)}, u32[]{:S(2)}) %collective-permute-start.15) | collective-permute-done | bytes 327712 | tf_op jit(solution)/shard_map/ppermute | solution.py:24
  80.6 2.4 %shard_map.84 = (f32[256,128]{1,0:T(8,128)S(1)}, f32[256,128]{1,0:T(8,128)S(1)}, f32[256,128]{1,0:T(8,128)S(1)}, f32[256,128]{1,0:T(8,128)S(1)}) custom-call(f32[5,128,128]{2,1,0:T(8,128)S(1)} %shard_map.82.sent, f32[5,128,128]{2,1,0:T(8,128)S(1)} %collective-permute-done.15.got, f32[4,128,128]{2,1,0:T(8,128)S(1)} %shard_map.79.both, ...), custom_call_target="tpu_custom_call" | custom-call | tf_op jit(solution)/shard_map/pallas_call | solution.py:78
  84.7 1.8 %collective-permute-start.24 = (f32[256,128]{1,0:T(8,128)S(1)}, f32[256,128]{1,0:T(8,128)S(1)}, u32[]{:S(2)}, u32[]{:S(2)}) collective-permute-start(f32[256,128]{1,0:T(8,128)S(1)} %get-tuple-element.36), channel_id=1, source_target_pairs={{0,24},{4,28},{8,16},{12,20},{16,8},{20,12},{24,0},{28,4},{1,25},{... | collective-permute-start | bytes 393224 | tf_op jit(solution)/shard_map/ppermute | solution.py:24
  86.6 4.4 %shard_map.83 = (f32[256,128]{1,0:T(8,128)}, f32[128,128]{1,0:T(8,128)S(1)}) custom-call(f32[5,128,128]{2,1,0:T(8,128)S(1)} %shard_map.82.sent, f32[5,128,128]{2,1,0:T(8,128)S(1)} %collective-permute-done.15.got, f32[256,128]{1,0:T(8,128)S(1)} %add_add_fusion.y.y_rows), custom_call_target="tpu_custom_call" | custom-call | flops 1000000000 | tf_op jit(solution)/shard_map/pallas_call | solution.py:78
  90.9 1.4 %collective-permute-done.23.c = f32[256,128]{1,0:T(8,128)S(1)} collective-permute-done((f32[256,128]{1,0:T(8,128)S(1)}, f32[256,128]{1,0:T(8,128)S(1)}, u32[]{:S(2)}, u32[]{:S(2)}) %collective-permute-start.23) | collective-permute-done | bytes 131104 | tf_op jit(solution)/shard_map/ppermute | solution.py:24
  (58 shorter events, 16.1 us)
Async XLA Ops:
  0.6 9.2 %copy-start = (f32[512,128]{1,0:T(8,128)S(1)}, f32[512,128]{1,0:T(8,128)}, u32[]{:S(2)}) copy-start(f32[512,128]{1,0:T(8,128)} %param.10) | copy-start | bytes 786436
  0.6 14.5 %copy-start.2 = (f32[2,1,2048,128]{3,2,1,0:T(8,128)S(1)}, f32[2,1,2048,128]{3,2,1,0:T(8,128)}, u32[]{:S(2)}) copy-start(f32[2,1,2048,128]{3,2,1,0:T(8,128)} %right.1) | copy-start | bytes 6291460
  0.7 18.1 %collective-permute-start.1 = (f32[2,512,128]{2,1,0:T(8,128)}, f32[2,512,128]{2,1,0:T(8,128)}, u32[]{:S(2)}, u32[]{:S(2)}) collective-permute-start(f32[2,512,128]{2,1,0:T(8,128)} %param.9), channel_id=1, source_target_pairs={{0,1},{1,0},{2,3},{3,2},{4,5},{5,4},{6,7},{7,6},{8,9},{9,8},{10,11... | collective-permute-start | bytes 1572872 | tf_op jit(solution)/shard_map/ppermute | solution.py:269
  3.7 15.0 %collective-permute-start.2 = (f32[2,512,128]{2,1,0:T(8,128)}, f32[2,512,128]{2,1,0:T(8,128)}, u32[]{:S(2)}, u32[]{:S(2)}) collective-permute-start(f32[2,512,128]{2,1,0:T(8,128)} %param.9), channel_id=1, source_target_pairs={{1,2},{2,1},{5,6},{6,5},{9,10},{10,9},{13,14},{14,13},{17,18},{18,... | collective-permute-start | bytes 1572872 | tf_op jit(solution)/shard_map/ppermute | solution.py:269
  7.5 48.8 %collective-permute-start = (f32[2,4,256,128]{3,2,1,0:T(8,128)}, f32[2,4,256,128]{3,2,1,0:T(8,128)S(1)}, u32[]{:S(2)}, u32[]{:S(2)}) collective-permute-start(f32[2,4,256,128]{3,2,1,0:T(8,128)} %dynamic-slice_bitcast_fusion), channel_id=1, source_target_pairs={{0,4},{4,0},{8,12},{12,8},{16,20},{20,16},{24,28},{28,24},{1,5},{5... | collective-permute-start | bytes 3145736 | tf_op jit(solution)/shard_map/ppermute | solution.py:24
  9.3 7.5 %collective-permute-start.16 = (f32[2,256,128]{2,1,0:T(8,128)}, f32[2,256,128]{2,1,0:T(8,128)}, u32[]{:S(2)}, u32[]{:S(2)}) collective-permute-start(f32[2,256,128]{2,1,0:T(8,128)} %get-tuple-element.39), channel_id=1, source_target_pairs={{0,4},{4,0},{8,12},{12,8},{16,20},{20,16},{24,28},{28,24},{1,5},{5... | collective-permute-start | bytes 786440 | tf_op jit(solution)/shard_map/ppermute | solution.py:24
  11.5 15.7 %copy-start.8 = (f32[2,128,128]{2,1,0:T(8,128)}, f32[2,128,128]{2,1,0:T(8,128)S(1)}, u32[]{:S(2)}) copy-start(f32[2,128,128]{2,1,0:T(8,128)S(1)} %fusion.7) | copy-start | bytes 393220
  11.5 18.0 %collective-permute-start.6 = (f32[2,128,128]{2,1,0:T(8,128)S(1)}, f32[2,128,128]{2,1,0:T(8,128)}, u32[]{:S(2)}, u32[]{:S(2)}) collective-permute-start(f32[2,128,128]{2,1,0:T(8,128)S(1)} %fusion.7), channel_id=1, source_target_pairs={{0,1},{1,0},{2,3},{3,2},{4,5},{5,4},{6,7},{7,6},{8,9},{9,8},{10,11... | collective-permute-start | bytes 393224 | tf_op jit(solution)/shard_map/ppermute | solution.py:269
  18.7 13.3 %collective-permute-start.3 = (f32[2,512,128]{2,1,0:T(8,128)}, f32[2,512,128]{2,1,0:T(8,128)S(1)}, u32[]{:S(2)}, u32[]{:S(2)}) collective-permute-start(f32[2,512,128]{2,1,0:T(8,128)} %collective-permute-done.1), channel_id=1, source_target_pairs={{1,2},{2,1},{5,6},{6,5},{9,10},{10,9},{13,14},{14,13},{17,18},{18,... | collective-permute-start | bytes 1572872 | tf_op jit(solution)/shard_map/ppermute | solution.py:269
  19.5 22.3 %copy-start.9 = (s32[2,1]{0,1:T(1,128)S(1)}, s32[2,1]{0,1:T(1,128)}, u32[]{:S(2)}) copy-start(s32[2,1]{0,1:T(1,128)} %param.11) | copy-start | bytes 28
  19.5 19.4 %collective-permute-start.4 = (f32[2,512,128]{2,1,0:T(8,128)S(1)}, f32[2,512,128]{2,1,0:T(8,128)S(1)}, u32[]{:S(2)}, u32[]{:S(2)}) collective-permute-start(f32[2,512,128]{2,1,0:T(8,128)S(1)} %bitcast_select_fusion), channel_id=1, source_target_pairs={{0,1},{1,0},{2,3},{3,2},{4,5},{5,4},{6,7},{7,6},{8,9},{9,8},{10,11... | collective-permute-start | bytes 1572872 | tf_op jit(solution)/shard_map/ppermute | solution.py:269
  29.5 24.7 %collective-permute-start.17 = (f32[4,256,128]{2,1,0:T(8,128)}, f32[4,256,128]{2,1,0:T(8,128)}, u32[]{:S(2)}, u32[]{:S(2)}) collective-permute-start(f32[4,256,128]{2,1,0:T(8,128)} %pad_maximum_fusion.own), channel_id=1, source_target_pairs={{0,1},{1,0},{2,3},{3,2},{4,5},{5,4},{6,7},{7,6},{8,9},{9,8},{10,11... | collective-permute-start | bytes 1572872 | tf_op jit(solution)/shard_map/ppermute | solution.py:269
  29.5 24.6 %collective-permute-start.18 = (f32[4,256,128]{2,1,0:T(8,128)}, f32[4,256,128]{2,1,0:T(8,128)}, u32[]{:S(2)}, u32[]{:S(2)}) collective-permute-start(f32[4,256,128]{2,1,0:T(8,128)} %pad_maximum_fusion.own), channel_id=1, source_target_pairs={{1,2},{2,1},{5,6},{6,5},{9,10},{10,9},{13,14},{14,13},{17,18},{18,... | collective-permute-start | bytes 1572872 | tf_op jit(solution)/shard_map/ppermute | solution.py:269
  32.0 20.1 %collective-permute-start.7 = (f32[2,128,128]{2,1,0:T(8,128)S(1)}, f32[2,128,128]{2,1,0:T(8,128)}, u32[]{:S(2)}, u32[]{:S(2)}) collective-permute-start(f32[2,128,128]{2,1,0:T(8,128)S(1)} %add.54.probe_here), channel_id=1, source_target_pairs={{0,2},{1,3},{2,0},{3,1},{4,6},{5,7},{6,4},{7,5},{8,10},{9,11},{10,... | collective-permute-start | bytes 393224 | tf_op jit(solution)/shard_map/ppermute | solution.py:24
  40.5 12.5 %collective-permute-start.5 = (f32[2,128,128]{2,1,0:T(8,128)}, f32[2,128,128]{2,1,0:T(8,128)}, u32[]{:S(2)}, u32[]{:S(2)}) collective-permute-start(f32[2,128,128]{2,1,0:T(8,128)} %shard_map.78), channel_id=1, source_target_pairs={{1,0},{2,3},{5,4},{6,7},{9,8},{10,11},{13,12},{14,15},{17,16},{18,... | collective-permute-start | bytes 393224 | tf_op jit(solution)/shard_map/ppermute | solution.py:269
  41.9 1.0 %copy-start.4 = (f32[2,512,128]{2,1,0:T(8,128)S(1)}, f32[2,512,128]{2,1,0:T(8,128)}, u32[]{:S(2)}) copy-start(f32[2,512,128]{2,1,0:T(8,128)} %copy-done.3) | copy-start | bytes 1572868
  43.0 1.0 %copy-start.6 = (f32[2,512,128]{2,1,0:T(8,128)S(1)}, f32[2,512,128]{2,1,0:T(8,128)}, u32[]{:S(2)}) copy-start(f32[2,512,128]{2,1,0:T(8,128)} %copy-done.5) | copy-start | bytes 1572868
  44.9 12.9 %copy-start.1 = (f32[2,1,2048,128]{3,2,1,0:T(8,128)S(1)}, f32[2,1,2048,128]{3,2,1,0:T(8,128)}, u32[]{:S(2)}) copy-start(f32[2,1,2048,128]{3,2,1,0:T(8,128)} %left.5) | copy-start | bytes 6291460
  54.2 8.6 %collective-permute-start.19 = (f32[4,256,128]{2,1,0:T(8,128)}, f32[4,256,128]{2,1,0:T(8,128)S(1)}, u32[]{:S(2)}, u32[]{:S(2)}) collective-permute-start(f32[4,256,128]{2,1,0:T(8,128)} %collective-permute-done.17.near), channel_id=1, source_target_pairs={{1,2},{2,1},{5,6},{6,5},{9,10},{10,9},{13,14},{14,13},{17,18},{18,... | collective-permute-start | bytes 1572872 | tf_op jit(solution)/shard_map/ppermute | solution.py:269
  54.9 12.3 %collective-permute-start.20 = (f32[4,256,128]{2,1,0:T(8,128)}, f32[4,256,128]{2,1,0:T(8,128)S(1)}, u32[]{:S(2)}, u32[]{:S(2)}) collective-permute-start(f32[4,256,128]{2,1,0:T(8,128)} %collective-permute-done.18.inner), channel_id=1, source_target_pairs={{1,0},{2,3},{5,4},{6,7},{9,8},{10,11},{13,12},{14,15},{17,16},{18,... | collective-permute-start | bytes 1572872 | tf_op jit(solution)/shard_map/ppermute | solution.py:269
  56.2 1.6 %collective-permute-start.8 = (f32[4,128,128]{2,1,0:T(8,128)S(1)}, f32[4,128,128]{2,1,0:T(8,128)S(1)}, u32[]{:S(2)}, u32[]{:S(2)}) collective-permute-start(f32[4,128,128]{2,1,0:T(8,128)S(1)} %shard_map.79.both), channel_id=1, source_target_pairs={{0,4},{4,0},{8,12},{12,8},{16,20},{20,16},{24,28},{28,24},{1,5},{5... | collective-permute-start | bytes 786440 | tf_op jit(solution)/shard_map/ppermute | solution.py:24
  59.3 9.2 %collective-permute-start.11 = (f32[256,128]{1,0:T(8,128)S(1)}, f32[256,128]{1,0:T(8,128)S(1)}, u32[]{:S(2)}, u32[]{:S(2)}) collective-permute-start(f32[256,128]{1,0:T(8,128)S(1)} %get-tuple-element.26), channel_id=1, source_target_pairs={{0,8},{4,12},{8,0},{12,4},{16,24},{20,28},{24,16},{28,20},{1,9},{5... | collective-permute-start | bytes 393224 | tf_op jit(solution)/shard_map/ppermute | solution.py:24
  60.8 8.1 %collective-permute-start.10 = (f32[256,128]{1,0:T(8,128)S(1)}, f32[256,128]{1,0:T(8,128)S(1)}, u32[]{:S(2)}, u32[]{:S(2)}) collective-permute-start(f32[256,128]{1,0:T(8,128)S(1)} %get-tuple-element.25), channel_id=1, source_target_pairs={{0,16},{4,20},{8,24},{12,28},{16,0},{20,4},{24,8},{28,12},{1,17},{... | collective-permute-start | bytes 393224 | tf_op jit(solution)/shard_map/ppermute | solution.py:24
  62.3 6.6 %collective-permute-start.9 = (f32[256,128]{1,0:T(8,128)S(1)}, f32[256,128]{1,0:T(8,128)S(1)}, u32[]{:S(2)}, u32[]{:S(2)}) collective-permute-start(f32[256,128]{1,0:T(8,128)S(1)} %get-tuple-element.24), channel_id=1, source_target_pairs={{0,24},{4,28},{8,16},{12,20},{16,8},{20,12},{24,0},{28,4},{1,25},{... | collective-permute-start | bytes 393224 | tf_op jit(solution)/shard_map/ppermute | solution.py:24
  67.2 13.4 %collective-permute-start.21 = (f32[4,256,128]{2,1,0:T(8,128)S(1)}, f32[4,256,128]{2,1,0:T(8,128)S(1)}, u32[]{:S(2)}, u32[]{:S(2)}) collective-permute-start(f32[4,256,128]{2,1,0:T(8,128)S(1)} %collective-permute-done.19.inner_far), channel_id=1, source_target_pairs={{1,0},{2,3},{5,4},{6,7},{9,8},{10,11},{13,12},{14,15},{17,16},{18,... | collective-permute-start | bytes 1572872 | tf_op jit(solution)/shard_map/ppermute | solution.py:269
  68.9 6.0 %collective-permute-start.12 = (f32[256,128]{1,0:T(8,128)S(1)}, f32[256,128]{1,0:T(8,128)S(1)}, u32[]{:S(2)}, u32[]{:S(2)}) collective-permute-start(f32[256,128]{1,0:T(8,128)S(1)} %add_add_fusion.y.y_rows), channel_id=1, source_target_pairs={{0,8},{4,12},{8,0},{12,4},{16,24},{20,28},{24,16},{28,20},{1,9},{5... | collective-permute-start | bytes 393224 | tf_op jit(solution)/shard_map/ppermute | solution.py:24
  70.2 6.3 %collective-permute-start.13 = (f32[256,128]{1,0:T(8,128)S(1)}, f32[256,128]{1,0:T(8,128)S(1)}, u32[]{:S(2)}, u32[]{:S(2)}) collective-permute-start(f32[256,128]{1,0:T(8,128)S(1)} %add_add_fusion.y.y_rows), channel_id=1, source_target_pairs={{0,16},{4,20},{8,24},{12,28},{16,0},{20,4},{24,8},{28,12},{1,17},{... | collective-permute-start | bytes 393224 | tf_op jit(solution)/shard_map/ppermute | solution.py:24
  71.6 5.9 %collective-permute-start.14 = (f32[256,128]{1,0:T(8,128)S(1)}, f32[256,128]{1,0:T(8,128)S(1)}, u32[]{:S(2)}, u32[]{:S(2)}) collective-permute-start(f32[256,128]{1,0:T(8,128)S(1)} %add_add_fusion.y.y_rows), channel_id=1, source_target_pairs={{0,24},{4,28},{8,16},{12,20},{16,8},{20,12},{24,0},{28,4},{1,25},{... | collective-permute-start | bytes 393224 | tf_op jit(solution)/shard_map/ppermute | solution.py:24
  78.9 1.7 %collective-permute-start.15 = (f32[5,128,128]{2,1,0:T(8,128)S(1)}, f32[5,128,128]{2,1,0:T(8,128)S(1)}, u32[]{:S(2)}, u32[]{:S(2)}) collective-permute-start(f32[5,128,128]{2,1,0:T(8,128)S(1)} %shard_map.82.sent), channel_id=1, source_target_pairs={{0,4},{4,0},{8,12},{12,8},{16,20},{20,16},{24,28},{28,24},{1,5},{5... | collective-permute-start | bytes 983048 | tf_op jit(solution)/shard_map/ppermute | solution.py:24
  83.0 7.9 %collective-permute-start.22 = (f32[256,128]{1,0:T(8,128)S(1)}, f32[256,128]{1,0:T(8,128)S(1)}, u32[]{:S(2)}, u32[]{:S(2)}) collective-permute-start(f32[256,128]{1,0:T(8,128)S(1)} %get-tuple-element.34), channel_id=1, source_target_pairs={{0,8},{4,12},{8,0},{12,4},{16,24},{20,28},{24,16},{28,20},{1,9},{5... | collective-permute-start | bytes 393224 | tf_op jit(solution)/shard_map/ppermute | solution.py:24
  84.3 8.1 %collective-permute-start.23 = (f32[256,128]{1,0:T(8,128)S(1)}, f32[256,128]{1,0:T(8,128)S(1)}, u32[]{:S(2)}, u32[]{:S(2)}) collective-permute-start(f32[256,128]{1,0:T(8,128)S(1)} %get-tuple-element.35), channel_id=1, source_target_pairs={{0,16},{4,20},{8,24},{12,28},{16,0},{20,4},{24,8},{28,12},{1,17},{... | collective-permute-start | bytes 393224 | tf_op jit(solution)/shard_map/ppermute | solution.py:24
  84.7 7.6 %collective-permute-start.24 = (f32[256,128]{1,0:T(8,128)S(1)}, f32[256,128]{1,0:T(8,128)S(1)}, u32[]{:S(2)}, u32[]{:S(2)}) collective-permute-start(f32[256,128]{1,0:T(8,128)S(1)} %get-tuple-element.36), channel_id=1, source_target_pairs={{0,24},{4,28},{8,16},{12,20},{16,8},{20,12},{24,0},{28,4},{1,25},{... | collective-permute-start | bytes 393224 | tf_op jit(solution)/shard_map/ppermute | solution.py:24
  (3 other events, 2.6 us)

commit v10 on v9

--- a/solution.py
+++ b/solution.py
@@ -132,26 +132,39 @@
     copies = []
     for i in range(chips):
         block = jnp.bitwise_xor(chip, i)
-        mine = left.at[:, 0, pl.ds(pl.multiple_of((block * 2 + bit) * rows, rows), rows), :]
-        copies.append((
-            pltpu.make_async_copy(mine, held.at[i, pl.ds(0, 2)], sems.at[2 * i]),
-            pltpu.make_async_copy(left_other.at[:, block], held.at[i, pl.ds(2, 2)], sems.at[2 * i + 1]),
-        ))
+        pair = [None, None]
+        if left is not None:
+            mine = left.at[:, 0, pl.ds(pl.multiple_of((block * 2 + bit) * rows, rows), rows), :]
+            pair[0] = pltpu.make_async_copy(mine, held.at[i, pl.ds(0, 2)], sems.at[2 * i])
+        if left_other is not None:
+            pair[1] = pltpu.make_async_copy(left_other.at[:, block], held.at[i, pl.ds(2, 2)], sems.at[2 * i + 1])
+        copies.append(pair)
     for pair in copies:
         for copy in pair:
-            copy.start()
+            if copy is not None:
+                copy.start()
     return copies
 
 
-def y_kernel(left, left_other, both, both_other, *rest):
+def y_own_kernel(left, both, *rest):
     *outs, held, sems = rest
     chips, rows = len(outs), outs[0].shape[0]
-    copies = start_rows(left, left_other, held, sems, chips, rows)
-    reduced = jnp.concatenate([both[0], both[1], both_other[0], both_other[1]], 0)
+    copies = [pair[0] for pair in start_rows(left, None, held, sems, chips, rows)]
+    reduced = jnp.concatenate([both[0], both[1]], 0)
     for i, out in enumerate(outs):
-        for copy in copies[i]:
-            copy.wait()
-        out[...] = dot3(jnp.concatenate([held[i, k] for k in range(4)], 1), reduced, NN)
+        copies[i].wait()
+        out[...] = dot3(jnp.concatenate([held[i, 0], held[i, 1]], 1), reduced, NN)
+
+
+def y_kernel(left_other, both_other, *rest):
+    *blocks, held, sems = rest
+    chips = len(blocks) // 2
+    rows = blocks[0].shape[0]
+    copies = [pair[1] for pair in start_rows(None, left_other, held, sems, chips, rows)]
+    reduced = jnp.concatenate([both_other[0], both_other[1]], 0)
+    for i in range(chips):
+        copies[i].wait()
+        blocks[chips + i][...] = blocks[i][...] + dot3(jnp.concatenate([held[i, 2], held[i, 3]], 1), reduced, NN)
 
 
 def z_kernel(left, left_other, *rest):
@@ -306,7 +319,8 @@
     col_inner_far, col_outer = lax.optimization_barrier((col_inner_far, col_outer))
     both_other = exchange(both, "step", 1)
     rows_scratch = [pltpu.VMEM((chips, 4, row_count, rank), jnp.float32), pltpu.SemaphoreType.DMA((2 * chips,))]
-    y_parts = call(y_kernel, [(row_count, rank)] * chips, [target_left, left_other, both, both_other], "aavv", rows_scratch)
+    y_own = call(y_own_kernel, [(row_count, rank)] * chips, [target_left, both], "av", rows_scratch)
+    y_parts = call(y_kernel, [(row_count, rank)] * chips, [left_other, both_other, *y_own], "av" + "v" * chips, rows_scratch)
     y_rows = y_parts[0]
     for bit in range(chips - 1, 0, -1):
         y_rows = y_rows + exchange(y_parts[bit], "step", 2 * bit)

time: 94 us -> 93.6 us (level)
  waiting for transfers between devices: 21.6 us -> 20.5 us
    ppermute x14, waiting for transfers between devices: 16.3 us -> 14.8 us  [exchange(): lax.ppermute(array, axis, [(i, i ^ bit) for i in range(lax.axis_size(axis...]
    pallas_call x9 -> x10, Pallas kernels: 13.3 us -> 14 us  [call(): pl.pallas_call(kernel, out_shape=shapes, in_specs=[pl.BlockSpec(memory_sp...]
  transfers between devices with their start and end apart: 25 -> 25, of which waited for: 10 -> 9; matrix products, arithmetic and copies ran while one was open for 15% -> 15% of each run, Pallas kernels for 11% -> 11%
where the time goes in v10:
time: 93.6 us; the launch traced here: 92.9 us
  starting transfers between devices  39.2 us (42%)
  waiting for transfers between devices  20.5 us (22%)
  Pallas kernels  14 us (15%)
  local copies, waits for them, and re-layouts  8.18 us (9%)
  matrix products  7.19 us (8%)
  other arithmetic  2.95 us (3%)
    ppermute x11, starting transfers between devices, across(): return lax.ppermute(array, 'tile', pairs)  21 us
    ppermute x14, starting transfers between devices, exchange(): lax.ppermute(array, axis, [(i, i ^ bit) for i in range(lax.axis_size(axis...  18.2 us
    ppermute x14, waiting for transfers between devices, exchange(): lax.ppermute(array, axis, [(i, i ^ bit) for i in range(lax.axis_size(axis...  14.8 us
    pallas_call x10, Pallas kernels, call(): pl.pallas_call(kernel, out_shape=shapes, in_specs=[pl.BlockSpec(memory_sp...  14 us
    dot_general x4, matrix products, mm(): jnp.einsum(spec, *arrays, precision=HIGH, preferred_element_type=jnp.floa...  7.19 us
    ppermute x11, waiting for transfers between devices, across(): return lax.ppermute(array, 'tile', pairs)  5.64 us
    squeeze x2, local copies, waits for them, and re-layouts, take(): return lax.dynamic_index_in_dim(array, index, axis, keepdims=False)  4.14 us
    unnamed x21, local copies, waits for them, and re-layouts  4.04 us
  transfers between devices with their start and end apart: 25, of which 9 were waited for; matrix products, arithmetic and copies ran while one was open for 15% of the time, Pallas kernels for 11%

profile of v10, /device:TPU:0, one launch (start us, length us, event | category | flops | bytes accessed | tf_op | source)
XLA Modules:
  0.0 92.9 jit_solution(10590619416017835240)
XLA Ops:
  0.7 3.1 %collective-permute-start.1 = (f32[2,512,128]{2,1,0:T(8,128)}, f32[2,512,128]{2,1,0:T(8,128)}, u32[]{:S(2)}, u32[]{:S(2)}) collective-permute-start(f32[2,512,128]{2,1,0:T(8,128)} %param.9), channel_id=1, source_target_pairs={{0,1},{1,0},{2,3},{3,2},{4,5},{5,4},{6,7},{7,6},{8,9},{9,8},{10,11... | collective-permute-start | bytes 1572872 | tf_op jit(solution)/shard_map/ppermute | solution.py:282
  3.7 1.5 %collective-permute-start.2 = (f32[2,512,128]{2,1,0:T(8,128)}, f32[2,512,128]{2,1,0:T(8,128)}, u32[]{:S(2)}, u32[]{:S(2)}) collective-permute-start(f32[2,512,128]{2,1,0:T(8,128)} %param.9), channel_id=1, source_target_pairs={{1,2},{2,1},{5,6},{6,5},{9,10},{10,9},{13,14},{14,13},{17,18},{18,... | collective-permute-start | bytes 1572872 | tf_op jit(solution)/shard_map/ppermute | solution.py:282
  5.2 2.3 %dynamic-slice_bitcast_fusion = f32[2,4,256,128]{3,2,1,0:T(8,128)} fusion(f32[2,4,2,256,128]{4,3,2,1,0:T(8,128)} %bitcast.40, s32[]{:T(128)S(6)} %select_n.41), kind=kLoop, calls=%fused_computation.2 | loop fusion | bytes 2097156 | tf_op jit(solution)/shard_map/jit(dynamic_index_in_dim)/squeeze | solution.py:28
  7.5 1.9 %dynamic-slice_bitcast_fusion.2 = (f32[2,256,128]{2,1,0:T(8,128)}, f32[2,256,128]{2,1,0:T(8,128)}) fusion(f32[2,2,256,128]{3,2,1,0:T(8,128)} %bitcast.45, s32[]{:T(128)S(6)} %select_n.49, s32[]{:T(128)S(6)} %select_n.41), kind=kLoop, calls=%fused_computation.15 | loop fusion | bytes 1048584 | tf_op jit(solution)/shard_map/jit(dynamic_index_in_dim)/squeeze | solution.py:28
  9.9 1.6 %fusion.7 = f32[2,128,128]{2,1,0:T(8,128)S(1)} fusion(f32[2,512,128]{2,1,0:T(8,128)} %param.8, f32[512,128]{1,0:T(8,128)S(1)} %copy-done), kind=kOutput, calls=%fused_computation.12 | convolution fusion | flops 100663296 | bytes 917504 | tf_op jit(solution)/shard_map/kbq,bp->kqp/dot_general | solution.py:14
  11.5 3.7 %collective-permute-start.6 = (f32[2,128,128]{2,1,0:T(8,128)S(1)}, f32[2,128,128]{2,1,0:T(8,128)}, u32[]{:S(2)}, u32[]{:S(2)}) collective-permute-start(f32[2,128,128]{2,1,0:T(8,128)S(1)} %fusion.7), channel_id=1, source_target_pairs={{0,1},{1,0},{2,3},{3,2},{4,5},{5,4},{6,7},{7,6},{8,9},{9,8},{10,11... | collective-permute-start | bytes 393224 | tf_op jit(solution)/shard_map/ppermute | solution.py:282
  15.2 1.6 %fusion.2 = f32[2,128,128]{2,1,0:T(8,128)S(1)} fusion(f32[2,512,128]{2,1,0:T(8,128)} %param.9, f32[2,4,512,128]{3,2,1,0:T(8,128)S(1)} %bitcast.41, s32[]{:T(128)S(6)} %select_n.42), kind=kOutput, calls=%fused_computation.6 | convolution fusion | flops 100663296 | bytes 1179652 | tf_op jit(solution)/shard_map/kbr,kbq->krq/dot_general | solution.py:14
  16.8 1.9 %pad_maximum_fusion.own = f32[4,256,128]{2,1,0:T(8,128)} fusion(f32[2,256,128]{2,1,0:T(8,128)} %collective-permute-done.16, f32[2,256,128]{2,1,0:T(8,128)} %get-tuple-element.46), kind=kLoop, calls=%fused_computation.3 | loop fusion | flops 131072 | bytes 1048576 | tf_op jit(solution)/shard_map/concatenate | solution.py:311
  19.5 6.1 %collective-permute-start.4 = (f32[2,512,128]{2,1,0:T(8,128)S(1)}, f32[2,512,128]{2,1,0:T(8,128)S(1)}, u32[]{:S(2)}, u32[]{:S(2)}) collective-permute-start(f32[2,512,128]{2,1,0:T(8,128)S(1)} %bitcast_select_fusion), channel_id=1, source_target_pairs={{0,1},{1,0},{2,3},{3,2},{4,5},{5,4},{6,7},{7,6},{8,9},{9,8},{10,11... | collective-permute-start | bytes 1572872 | tf_op jit(solution)/shard_map/ppermute | solution.py:282
  25.6 1.6 %convolution_add_fusion.1 = f32[2,128,128]{2,1,0:T(8,128)S(1)} fusion(f32[2,128,128]{2,1,0:T(8,128)S(1)} %fusion.2, f32[2,512,128]{2,1,0:T(8,128)} %collective-permute-done.1, f32[2,4,512,128]{3,2,1,0:T(8,128)S(1)} %bitcast.43, s32[]{:T(128)S(6)} %select_n.43), kind=kOutput, calls=%fused_computation.1 | convolution fusion | flops 100696064 | bytes 1310724 | tf_op jit(solution)/shard_map/kbr,kbq->krq/dot_general | solution.py:14
  27.2 2.3 %convolution_add_fusion.part = f32[2,128,128]{2,1,0:T(8,128)} fusion(f32[2,128,128]{2,1,0:T(8,128)S(1)} %convolution_add_fusion.1, f32[2,512,128]{2,1,0:T(8,128)} %collective-permute-done.2, f32[2,4,512,128]{3,2,1,0:T(8,128)S(1)} %bitcast.44, s32[]{:T(128)S(6)} %select_n.45), kind=kOutput, calls=%fused_computation | convolution fusion | flops 100696064 | bytes 1310724 | tf_op jit(solution)/shard_map/kbr,kbq->krq/dot_general | solution.py:14
  29.5 1.4 %collective-permute-start.18 = (f32[4,256,128]{2,1,0:T(8,128)}, f32[4,256,128]{2,1,0:T(8,128)}, u32[]{:S(2)}, u32[]{:S(2)}) collective-permute-start(f32[4,256,128]{2,1,0:T(8,128)} %pad_maximum_fusion.own), channel_id=1, source_target_pairs={{1,2},{2,1},{5,6},{6,5},{9,10},{10,9},{13,14},{14,13},{17,18},{18,... | collective-permute-start | bytes 1572872 | tf_op jit(solution)/shard_map/ppermute | solution.py:282
  32.0 6.9 %collective-permute-start.7 = (f32[2,128,128]{2,1,0:T(8,128)S(1)}, f32[2,128,128]{2,1,0:T(8,128)}, u32[]{:S(2)}, u32[]{:S(2)}) collective-permute-start(f32[2,128,128]{2,1,0:T(8,128)S(1)} %add.54.probe_here), channel_id=1, source_target_pairs={{0,2},{1,3},{2,0},{3,1},{4,6},{5,7},{6,4},{7,5},{8,10},{9,11},{10,... | collective-permute-start | bytes 393224 | tf_op jit(solution)/shard_map/ppermute | solution.py:24
  40.5 1.3 %collective-permute-start.5 = (f32[2,128,128]{2,1,0:T(8,128)}, f32[2,128,128]{2,1,0:T(8,128)}, u32[]{:S(2)}, u32[]{:S(2)}) collective-permute-start(f32[2,128,128]{2,1,0:T(8,128)} %shard_map.78), channel_id=1, source_target_pairs={{1,0},{2,3},{5,4},{6,7},{9,8},{10,11},{13,12},{14,15},{17,16},{18,... | collective-permute-start | bytes 393224 | tf_op jit(solution)/shard_map/ppermute | solution.py:282
  45.3 6.9 %collective-permute-done.7.probe_far = f32[2,128,128]{2,1,0:T(8,128)} collective-permute-done((f32[2,128,128]{2,1,0:T(8,128)S(1)}, f32[2,128,128]{2,1,0:T(8,128)}, u32[]{:S(2)}, u32[]{:S(2)}) %collective-permute-start.7) | collective-permute-done | bytes 131104 | tf_op jit(solution)/shard_map/ppermute | solution.py:24
  53.0 1.2 %shard_map.79.both = f32[4,128,128]{2,1,0:T(8,128)S(1)} custom-call(f32[2,128,128]{2,1,0:T(8,128)S(1)} %shard_map.77.core, f32[2,128,128]{2,1,0:T(8,128)} %collective-permute-done.5.lent, f32[2,128,128]{2,1,0:T(8,128)S(1)} %add.54.probe_here, f32[2,128,128]{2,1,0:T(8,128)} %collective-permute-done.7.probe_far, s32[2,1]{1,0:T(2,128)S(1)} %copy.14.pattern), custom_call_target="tpu_custom_call" | custom-call | tf_op jit(solution)/shard_map/pallas_call | solution.py:78
  54.9 1.3 %collective-permute-start.20 = (f32[4,256,128]{2,1,0:T(8,128)}, f32[4,256,128]{2,1,0:T(8,128)S(1)}, u32[]{:S(2)}, u32[]{:S(2)}) collective-permute-start(f32[4,256,128]{2,1,0:T(8,128)} %collective-permute-done.18.inner), channel_id=1, source_target_pairs={{1,0},{2,3},{5,4},{6,7},{9,8},{10,11},{13,12},{14,15},{17,16},{18,... | collective-permute-start | bytes 1572872 | tf_op jit(solution)/shard_map/ppermute | solution.py:282
  56.3 1.1 %shard_map.80 = (f32[256,128]{1,0:T(8,128)S(1)}, f32[256,128]{1,0:T(8,128)S(1)}, f32[256,128]{1,0:T(8,128)S(1)}, f32[256,128]{1,0:T(8,128)S(1)}) custom-call(f32[2,1,2048,128]{3,2,1,0:T(8,128)S(1)} %copy-done.1, f32[4,128,128]{2,1,0:T(8,128)S(1)} %shard_map.79.both), custom_call_target="tpu_custom_call" | custom-call | tf_op jit(solution)/shard_map/pallas_call | solution.py:78
  58.9 1.6 %collective-permute-start.11 = (f32[256,128]{1,0:T(8,128)S(1)}, f32[256,128]{1,0:T(8,128)S(1)}, u32[]{:S(2)}, u32[]{:S(2)}) collective-permute-start(f32[256,128]{1,0:T(8,128)S(1)} %get-tuple-element.34), channel_id=1, source_target_pairs={{0,8},{4,12},{8,0},{12,4},{16,24},{20,28},{24,16},{28,20},{1,9},{5... | collective-permute-start | bytes 393224 | tf_op jit(solution)/shard_map/ppermute | solution.py:24
  60.4 1.5 %collective-permute-start.10 = (f32[256,128]{1,0:T(8,128)S(1)}, f32[256,128]{1,0:T(8,128)S(1)}, u32[]{:S(2)}, u32[]{:S(2)}) collective-permute-start(f32[256,128]{1,0:T(8,128)S(1)} %get-tuple-element.33), channel_id=1, source_target_pairs={{0,16},{4,20},{8,24},{12,28},{16,0},{20,4},{24,8},{28,12},{1,17},{... | collective-permute-start | bytes 393224 | tf_op jit(solution)/shard_map/ppermute | solution.py:24
  62.4 4.8 %collective-permute-done.20.outer = f32[4,256,128]{2,1,0:T(8,128)S(1)} collective-permute-done((f32[4,256,128]{2,1,0:T(8,128)}, f32[4,256,128]{2,1,0:T(8,128)S(1)}, u32[]{:S(2)}, u32[]{:S(2)}) %collective-permute-start.20) | collective-permute-done | bytes 524320 | tf_op jit(solution)/shard_map/ppermute | solution.py:282
  67.2 1.3 %collective-permute-start.21 = (f32[4,256,128]{2,1,0:T(8,128)S(1)}, f32[4,256,128]{2,1,0:T(8,128)S(1)}, u32[]{:S(2)}, u32[]{:S(2)}) collective-permute-start(f32[4,256,128]{2,1,0:T(8,128)S(1)} %collective-permute-done.19.inner_far), channel_id=1, source_target_pairs={{1,0},{2,3},{5,4},{6,7},{9,8},{10,11},{13,12},{14,15},{17,16},{18,... | collective-permute-start | bytes 1572872 | tf_op jit(solution)/shard_map/ppermute | solution.py:282
  68.6 1.6 %collective-permute-start.12 = (f32[256,128]{1,0:T(8,128)S(1)}, f32[256,128]{1,0:T(8,128)S(1)}, u32[]{:S(2)}, u32[]{:S(2)}) collective-permute-start(f32[256,128]{1,0:T(8,128)S(1)} %add_add_fusion.y.y_rows), channel_id=1, source_target_pairs={{0,8},{4,12},{8,0},{12,4},{16,24},{20,28},{24,16},{28,20},{1,9},{5... | collective-permute-start | bytes 393224 | tf_op jit(solution)/shard_map/ppermute | solution.py:24
  70.1 1.5 %collective-permute-start.13 = (f32[256,128]{1,0:T(8,128)S(1)}, f32[256,128]{1,0:T(8,128)S(1)}, u32[]{:S(2)}, u32[]{:S(2)}) collective-permute-start(f32[256,128]{1,0:T(8,128)S(1)} %add_add_fusion.y.y_rows), channel_id=1, source_target_pairs={{0,16},{4,20},{8,24},{12,28},{16,0},{20,4},{24,8},{28,12},{1,17},{... | collective-permute-start | bytes 393224 | tf_op jit(solution)/shard_map/ppermute | solution.py:24
  72.6 2.0 %collective-permute-done.12.rest_0_ = f32[256,128]{1,0:T(8,128)S(1)} collective-permute-done((f32[256,128]{1,0:T(8,128)S(1)}, f32[256,128]{1,0:T(8,128)S(1)}, u32[]{:S(2)}, u32[]{:S(2)}) %collective-permute-start.12) | collective-permute-done | bytes 131104 | tf_op jit(solution)/shard_map/ppermute | solution.py:24
  74.6 1.7 %collective-permute-done.13.rest_1_ = f32[256,128]{1,0:T(8,128)S(1)} collective-permute-done((f32[256,128]{1,0:T(8,128)S(1)}, f32[256,128]{1,0:T(8,128)S(1)}, u32[]{:S(2)}, u32[]{:S(2)}) %collective-permute-start.13) | collective-permute-done | bytes 131104 | tf_op jit(solution)/shard_map/ppermute | solution.py:24
  76.4 1.2 %collective-permute-done.14.rest_2_ = f32[256,128]{1,0:T(8,128)S(1)} collective-permute-done((f32[256,128]{1,0:T(8,128)S(1)}, f32[256,128]{1,0:T(8,128)S(1)}, u32[]{:S(2)}, u32[]{:S(2)}) %collective-permute-start.14) | collective-permute-done | bytes 131104 | tf_op jit(solution)/shard_map/ppermute | solution.py:24
  77.5 1.4 %shard_map.83.sent = f32[5,128,128]{2,1,0:T(8,128)S(1)} custom-call(f32[2,1,2048,128]{3,2,1,0:T(8,128)S(1)} %copy-done.1, f32[2,4,256,128]{3,2,1,0:T(8,128)S(1)} %collective-permute-done.left_other, f32[256,128]{1,0:T(8,128)S(1)} %collective-permute-done.12.rest_0_, f32[256,128]{1,0:T(8,128)S(1)} %collective-permute-done.13.rest_1_, ...), custom_call_target="tpu_custom_call" | custom-call | tf_op jit(solution)/shard_map/pallas_call | solution.py:78
  79.0 1.6 %collective-permute-done.15.got = f32[5,128,128]{2,1,0:T(8,128)S(1)} collective-permute-done((f32[5,128,128]{2,1,0:T(8,128)S(1)}, f32[5,128,128]{2,1,0:T(8,128)S(1)}, u32[]{:S(2)}, u32[]{:S(2)}) %collective-permute-start.15) | collective-permute-done | bytes 327712 | tf_op jit(solution)/shard_map/ppermute | solution.py:24
  80.6 2.4 %shard_map.85 = (f32[256,128]{1,0:T(8,128)S(1)}, f32[256,128]{1,0:T(8,128)S(1)}, f32[256,128]{1,0:T(8,128)S(1)}, f32[256,128]{1,0:T(8,128)S(1)}) custom-call(f32[5,128,128]{2,1,0:T(8,128)S(1)} %shard_map.83.sent, f32[5,128,128]{2,1,0:T(8,128)S(1)} %collective-permute-done.15.got, f32[4,128,128]{2,1,0:T(8,128)S(1)} %shard_map.79.both, ...), custom_call_target="tpu_custom_call" | custom-call | tf_op jit(solution)/shard_map/pallas_call | solution.py:78
  84.2 2.4 %collective-permute-start.24 = (f32[256,128]{1,0:T(8,128)S(1)}, f32[256,128]{1,0:T(8,128)S(1)}, u32[]{:S(2)}, u32[]{:S(2)}) collective-permute-start(f32[256,128]{1,0:T(8,128)S(1)} %get-tuple-element.44), channel_id=1, source_target_pairs={{0,24},{4,28},{8,16},{12,20},{16,8},{20,12},{24,0},{28,4},{1,25},{... | collective-permute-start | bytes 393224 | tf_op jit(solution)/shard_map/ppermute | solution.py:24
  86.6 4.4 %shard_map.84 = (f32[256,128]{1,0:T(8,128)}, f32[128,128]{1,0:T(8,128)S(1)}) custom-call(f32[5,128,128]{2,1,0:T(8,128)S(1)} %shard_map.83.sent, f32[5,128,128]{2,1,0:T(8,128)S(1)} %collective-permute-done.15.got, f32[256,128]{1,0:T(8,128)S(1)} %add_add_fusion.y.y_rows), custom_call_target="tpu_custom_call" | custom-call | flops 1000000000 | tf_op jit(solution)/shard_map/pallas_call | solution.py:78
  (59 shorter events, 15.1 us)
Async XLA Ops:
  0.6 9.2 %copy-start = (f32[512,128]{1,0:T(8,128)S(1)}, f32[512,128]{1,0:T(8,128)}, u32[]{:S(2)}) copy-start(f32[512,128]{1,0:T(8,128)} %param.10) | copy-start | bytes 786436
  0.6 14.6 %copy-start.2 = (f32[2,1,2048,128]{3,2,1,0:T(8,128)S(1)}, f32[2,1,2048,128]{3,2,1,0:T(8,128)}, u32[]{:S(2)}) copy-start(f32[2,1,2048,128]{3,2,1,0:T(8,128)} %right.1) | copy-start | bytes 6291460
  0.7 18.1 %collective-permute-start.1 = (f32[2,512,128]{2,1,0:T(8,128)}, f32[2,512,128]{2,1,0:T(8,128)}, u32[]{:S(2)}, u32[]{:S(2)}) collective-permute-start(f32[2,512,128]{2,1,0:T(8,128)} %param.9), channel_id=1, source_target_pairs={{0,1},{1,0},{2,3},{3,2},{4,5},{5,4},{6,7},{7,6},{8,9},{9,8},{10,11... | collective-permute-start | bytes 1572872 | tf_op jit(solution)/shard_map/ppermute | solution.py:282
  3.7 15.0 %collective-permute-start.2 = (f32[2,512,128]{2,1,0:T(8,128)}, f32[2,512,128]{2,1,0:T(8,128)}, u32[]{:S(2)}, u32[]{:S(2)}) collective-permute-start(f32[2,512,128]{2,1,0:T(8,128)} %param.9), channel_id=1, source_target_pairs={{1,2},{2,1},{5,6},{6,5},{9,10},{10,9},{13,14},{14,13},{17,18},{18,... | collective-permute-start | bytes 1572872 | tf_op jit(solution)/shard_map/ppermute | solution.py:282
  7.5 49.9 %collective-permute-start = (f32[2,4,256,128]{3,2,1,0:T(8,128)}, f32[2,4,256,128]{3,2,1,0:T(8,128)S(1)}, u32[]{:S(2)}, u32[]{:S(2)}) collective-permute-start(f32[2,4,256,128]{3,2,1,0:T(8,128)} %dynamic-slice_bitcast_fusion), channel_id=1, source_target_pairs={{0,4},{4,0},{8,12},{12,8},{16,20},{20,16},{24,28},{28,24},{1,5},{5... | collective-permute-start | bytes 3145736 | tf_op jit(solution)/shard_map/ppermute | solution.py:24
  9.4 7.5 %collective-permute-start.16 = (f32[2,256,128]{2,1,0:T(8,128)}, f32[2,256,128]{2,1,0:T(8,128)}, u32[]{:S(2)}, u32[]{:S(2)}) collective-permute-start(f32[2,256,128]{2,1,0:T(8,128)} %get-tuple-element.47), channel_id=1, source_target_pairs={{0,4},{4,0},{8,12},{12,8},{16,20},{20,16},{24,28},{28,24},{1,5},{5... | collective-permute-start | bytes 786440 | tf_op jit(solution)/shard_map/ppermute | solution.py:24
  11.5 15.7 %copy-start.8 = (f32[2,128,128]{2,1,0:T(8,128)}, f32[2,128,128]{2,1,0:T(8,128)S(1)}, u32[]{:S(2)}) copy-start(f32[2,128,128]{2,1,0:T(8,128)S(1)} %fusion.7) | copy-start | bytes 393220
  11.5 18.0 %collective-permute-start.6 = (f32[2,128,128]{2,1,0:T(8,128)S(1)}, f32[2,128,128]{2,1,0:T(8,128)}, u32[]{:S(2)}, u32[]{:S(2)}) collective-permute-start(f32[2,128,128]{2,1,0:T(8,128)S(1)} %fusion.7), channel_id=1, source_target_pairs={{0,1},{1,0},{2,3},{3,2},{4,5},{5,4},{6,7},{7,6},{8,9},{9,8},{10,11... | collective-permute-start | bytes 393224 | tf_op jit(solution)/shard_map/ppermute | solution.py:282
  18.7 13.3 %collective-permute-start.3 = (f32[2,512,128]{2,1,0:T(8,128)}, f32[2,512,128]{2,1,0:T(8,128)S(1)}, u32[]{:S(2)}, u32[]{:S(2)}) collective-permute-start(f32[2,512,128]{2,1,0:T(8,128)} %collective-permute-done.1), channel_id=1, source_target_pairs={{1,2},{2,1},{5,6},{6,5},{9,10},{10,9},{13,14},{14,13},{17,18},{18,... | collective-permute-start | bytes 1572872 | tf_op jit(solution)/shard_map/ppermute | solution.py:282
  19.5 22.3 %copy-start.9 = (s32[2,1]{0,1:T(1,128)S(1)}, s32[2,1]{0,1:T(1,128)}, u32[]{:S(2)}) copy-start(s32[2,1]{0,1:T(1,128)} %param.11) | copy-start | bytes 28
  19.5 19.4 %collective-permute-start.4 = (f32[2,512,128]{2,1,0:T(8,128)S(1)}, f32[2,512,128]{2,1,0:T(8,128)S(1)}, u32[]{:S(2)}, u32[]{:S(2)}) collective-permute-start(f32[2,512,128]{2,1,0:T(8,128)S(1)} %bitcast_select_fusion), channel_id=1, source_target_pairs={{0,1},{1,0},{2,3},{3,2},{4,5},{5,4},{6,7},{7,6},{8,9},{9,8},{10,11... | collective-permute-start | bytes 1572872 | tf_op jit(solution)/shard_map/ppermute | solution.py:282
  29.5 24.7 %collective-permute-start.17 = (f32[4,256,128]{2,1,0:T(8,128)}, f32[4,256,128]{2,1,0:T(8,128)}, u32[]{:S(2)}, u32[]{:S(2)}) collective-permute-start(f32[4,256,128]{2,1,0:T(8,128)} %pad_maximum_fusion.own), channel_id=1, source_target_pairs={{0,1},{1,0},{2,3},{3,2},{4,5},{5,4},{6,7},{7,6},{8,9},{9,8},{10,11... | collective-permute-start | bytes 1572872 | tf_op jit(solution)/shard_map/ppermute | solution.py:282
  29.5 24.6 %collective-permute-start.18 = (f32[4,256,128]{2,1,0:T(8,128)}, f32[4,256,128]{2,1,0:T(8,128)}, u32[]{:S(2)}, u32[]{:S(2)}) collective-permute-start(f32[4,256,128]{2,1,0:T(8,128)} %pad_maximum_fusion.own), channel_id=1, source_target_pairs={{1,2},{2,1},{5,6},{6,5},{9,10},{10,9},{13,14},{14,13},{17,18},{18,... | collective-permute-start | bytes 1572872 | tf_op jit(solution)/shard_map/ppermute | solution.py:282
  32.0 20.2 %collective-permute-start.7 = (f32[2,128,128]{2,1,0:T(8,128)S(1)}, f32[2,128,128]{2,1,0:T(8,128)}, u32[]{:S(2)}, u32[]{:S(2)}) collective-permute-start(f32[2,128,128]{2,1,0:T(8,128)S(1)} %add.54.probe_here), channel_id=1, source_target_pairs={{0,2},{1,3},{2,0},{3,1},{4,6},{5,7},{6,4},{7,5},{8,10},{9,11},{10,... | collective-permute-start | bytes 393224 | tf_op jit(solution)/shard_map/ppermute | solution.py:24
  40.5 12.5 %collective-permute-start.5 = (f32[2,128,128]{2,1,0:T(8,128)}, f32[2,128,128]{2,1,0:T(8,128)}, u32[]{:S(2)}, u32[]{:S(2)}) collective-permute-start(f32[2,128,128]{2,1,0:T(8,128)} %shard_map.78), channel_id=1, source_target_pairs={{1,0},{2,3},{5,4},{6,7},{9,8},{10,11},{13,12},{14,15},{17,16},{18,... | collective-permute-start | bytes 393224 | tf_op jit(solution)/shard_map/ppermute | solution.py:282
  41.9 1.0 %copy-start.4 = (f32[2,512,128]{2,1,0:T(8,128)S(1)}, f32[2,512,128]{2,1,0:T(8,128)}, u32[]{:S(2)}) copy-start(f32[2,512,128]{2,1,0:T(8,128)} %copy-done.3) | copy-start | bytes 1572868
  43.0 1.0 %copy-start.6 = (f32[2,512,128]{2,1,0:T(8,128)S(1)}, f32[2,512,128]{2,1,0:T(8,128)}, u32[]{:S(2)}) copy-start(f32[2,512,128]{2,1,0:T(8,128)} %copy-done.5) | copy-start | bytes 1572868
  44.9 11.4 %copy-start.1 = (f32[2,1,2048,128]{3,2,1,0:T(8,128)S(1)}, f32[2,1,2048,128]{3,2,1,0:T(8,128)}, u32[]{:S(2)}) copy-start(f32[2,1,2048,128]{3,2,1,0:T(8,128)} %left.5) | copy-start | bytes 6291460
  54.2 8.3 %collective-permute-start.19 = (f32[4,256,128]{2,1,0:T(8,128)}, f32[4,256,128]{2,1,0:T(8,128)S(1)}, u32[]{:S(2)}, u32[]{:S(2)}) collective-permute-start(f32[4,256,128]{2,1,0:T(8,128)} %collective-permute-done.17.near), channel_id=1, source_target_pairs={{1,2},{2,1},{5,6},{6,5},{9,10},{10,9},{13,14},{14,13},{17,18},{18,... | collective-permute-start | bytes 1572872 | tf_op jit(solution)/shard_map/ppermute | solution.py:282
  54.9 12.3 %collective-permute-start.20 = (f32[4,256,128]{2,1,0:T(8,128)}, f32[4,256,128]{2,1,0:T(8,128)S(1)}, u32[]{:S(2)}, u32[]{:S(2)}) collective-permute-start(f32[4,256,128]{2,1,0:T(8,128)} %collective-permute-done.18.inner), channel_id=1, source_target_pairs={{1,0},{2,3},{5,4},{6,7},{9,8},{10,11},{13,12},{14,15},{17,16},{18,... | collective-permute-start | bytes 1572872 | tf_op jit(solution)/shard_map/ppermute | solution.py:282
  56.2 1.6 %collective-permute-start.8 = (f32[4,128,128]{2,1,0:T(8,128)S(1)}, f32[4,128,128]{2,1,0:T(8,128)S(1)}, u32[]{:S(2)}, u32[]{:S(2)}) collective-permute-start(f32[4,128,128]{2,1,0:T(8,128)S(1)} %shard_map.79.both), channel_id=1, source_target_pairs={{0,4},{4,0},{8,12},{12,8},{16,20},{20,16},{24,28},{28,24},{1,5},{5... | collective-permute-start | bytes 786440 | tf_op jit(solution)/shard_map/ppermute | solution.py:24
  58.9 9.6 %collective-permute-start.11 = (f32[256,128]{1,0:T(8,128)S(1)}, f32[256,128]{1,0:T(8,128)S(1)}, u32[]{:S(2)}, u32[]{:S(2)}) collective-permute-start(f32[256,128]{1,0:T(8,128)S(1)} %get-tuple-element.34), channel_id=1, source_target_pairs={{0,8},{4,12},{8,0},{12,4},{16,24},{20,28},{24,16},{28,20},{1,9},{5... | collective-permute-start | bytes 393224 | tf_op jit(solution)/shard_map/ppermute | solution.py:24
  60.4 8.1 %collective-permute-start.10 = (f32[256,128]{1,0:T(8,128)S(1)}, f32[256,128]{1,0:T(8,128)S(1)}, u32[]{:S(2)}, u32[]{:S(2)}) collective-permute-start(f32[256,128]{1,0:T(8,128)S(1)} %get-tuple-element.33), channel_id=1, source_target_pairs={{0,16},{4,20},{8,24},{12,28},{16,0},{20,4},{24,8},{28,12},{1,17},{... | collective-permute-start | bytes 393224 | tf_op jit(solution)/shard_map/ppermute | solution.py:24
  62.0 6.6 %collective-permute-start.9 = (f32[256,128]{1,0:T(8,128)S(1)}, f32[256,128]{1,0:T(8,128)S(1)}, u32[]{:S(2)}, u32[]{:S(2)}) collective-permute-start(f32[256,128]{1,0:T(8,128)S(1)} %get-tuple-element.32), channel_id=1, source_target_pairs={{0,24},{4,28},{8,16},{12,20},{16,8},{20,12},{24,0},{28,4},{1,25},{... | collective-permute-start | bytes 393224 | tf_op jit(solution)/shard_map/ppermute | solution.py:24
  67.2 13.4 %collective-permute-start.21 = (f32[4,256,128]{2,1,0:T(8,128)S(1)}, f32[4,256,128]{2,1,0:T(8,128)S(1)}, u32[]{:S(2)}, u32[]{:S(2)}) collective-permute-start(f32[4,256,128]{2,1,0:T(8,128)S(1)} %collective-permute-done.19.inner_far), channel_id=1, source_target_pairs={{1,0},{2,3},{5,4},{6,7},{9,8},{10,11},{13,12},{14,15},{17,16},{18,... | collective-permute-start | bytes 1572872 | tf_op jit(solution)/shard_map/ppermute | solution.py:282
  68.6 6.0 %collective-permute-start.12 = (f32[256,128]{1,0:T(8,128)S(1)}, f32[256,128]{1,0:T(8,128)S(1)}, u32[]{:S(2)}, u32[]{:S(2)}) collective-permute-start(f32[256,128]{1,0:T(8,128)S(1)} %add_add_fusion.y.y_rows), channel_id=1, source_target_pairs={{0,8},{4,12},{8,0},{12,4},{16,24},{20,28},{24,16},{28,20},{1,9},{5... | collective-permute-start | bytes 393224 | tf_op jit(solution)/shard_map/ppermute | solution.py:24
  70.1 6.2 %collective-permute-start.13 = (f32[256,128]{1,0:T(8,128)S(1)}, f32[256,128]{1,0:T(8,128)S(1)}, u32[]{:S(2)}, u32[]{:S(2)}) collective-permute-start(f32[256,128]{1,0:T(8,128)S(1)} %add_add_fusion.y.y_rows), channel_id=1, source_target_pairs={{0,16},{4,20},{8,24},{12,28},{16,0},{20,4},{24,8},{28,12},{1,17},{... | collective-permute-start | bytes 393224 | tf_op jit(solution)/shard_map/ppermute | solution.py:24
  71.6 5.9 %collective-permute-start.14 = (f32[256,128]{1,0:T(8,128)S(1)}, f32[256,128]{1,0:T(8,128)S(1)}, u32[]{:S(2)}, u32[]{:S(2)}) collective-permute-start(f32[256,128]{1,0:T(8,128)S(1)} %add_add_fusion.y.y_rows), channel_id=1, source_target_pairs={{0,24},{4,28},{8,16},{12,20},{16,8},{20,12},{24,0},{28,4},{1,25},{... | collective-permute-start | bytes 393224 | tf_op jit(solution)/shard_map/ppermute | solution.py:24
  78.9 1.7 %collective-permute-start.15 = (f32[5,128,128]{2,1,0:T(8,128)S(1)}, f32[5,128,128]{2,1,0:T(8,128)S(1)}, u32[]{:S(2)}, u32[]{:S(2)}) collective-permute-start(f32[5,128,128]{2,1,0:T(8,128)S(1)} %shard_map.83.sent), channel_id=1, source_target_pairs={{0,4},{4,0},{8,12},{12,8},{16,20},{20,16},{24,28},{28,24},{1,5},{5... | collective-permute-start | bytes 983048 | tf_op jit(solution)/shard_map/ppermute | solution.py:24
  83.0 7.9 %collective-permute-start.22 = (f32[256,128]{1,0:T(8,128)S(1)}, f32[256,128]{1,0:T(8,128)S(1)}, u32[]{:S(2)}, u32[]{:S(2)}) collective-permute-start(f32[256,128]{1,0:T(8,128)S(1)} %get-tuple-element.42), channel_id=1, source_target_pairs={{0,8},{4,12},{8,0},{12,4},{16,24},{20,28},{24,16},{28,20},{1,9},{5... | collective-permute-start | bytes 393224 | tf_op jit(solution)/shard_map/ppermute | solution.py:24
  83.9 8.1 %collective-permute-start.23 = (f32[256,128]{1,0:T(8,128)S(1)}, f32[256,128]{1,0:T(8,128)S(1)}, u32[]{:S(2)}, u32[]{:S(2)}) collective-permute-start(f32[256,128]{1,0:T(8,128)S(1)} %get-tuple-element.43), channel_id=1, source_target_pairs={{0,16},{4,20},{8,24},{12,28},{16,0},{20,4},{24,8},{28,12},{1,17},{... | collective-permute-start | bytes 393224 | tf_op jit(solution)/shard_map/ppermute | solution.py:24
  84.2 7.8 %collective-permute-start.24 = (f32[256,128]{1,0:T(8,128)S(1)}, f32[256,128]{1,0:T(8,128)S(1)}, u32[]{:S(2)}, u32[]{:S(2)}) collective-permute-start(f32[256,128]{1,0:T(8,128)S(1)} %get-tuple-element.44), channel_id=1, source_target_pairs={{0,24},{4,28},{8,16},{12,20},{16,8},{20,12},{24,0},{28,4},{1,25},{... | collective-permute-start | bytes 393224 | tf_op jit(solution)/shard_map/ppermute | solution.py:24
  (3 other events, 2.5 us)
